TPU v7x, 32 devices: a whole 2x2x4 slice. The times are simulated.
32 devices in a mesh: row: 8 (over z, y), col: 4 (over x, core).
Axes of the slice: x: 2, y: 2, z: 4, core: 2. Of those that a mesh axis runs over, the one named last changes fastest.
Arguments:
- spectra: bfloat16 [2, 2, 10240, 256], P(None, None, ('row', 'col')), may hold values from -40 to 40
- delays_s: int32 [10240, 512], P('row'), may hold values from 0 to 1023
- delays_r: int32 [10240, 512], P('col'), may hold values from 0 to 1023
- wl_index: int32 [2], replicated, may hold values from 0 to 10239
Outputs:
- beam_field: float32 [2, 2, 512, 512], P(None, None, 'col', 'row')
All inputs are finite; a program needn't handle non-finite values.
Results may differ from a plain program's by a relative error of at most 0.0071.
Values may be sent and summed in bfloat16 or wider, within the bound.
No kernel may reach another device: no remote copies, remote signals or barrier semaphores. Data moves between devices by JAX's collectives and lax.ppermute only.
A program may use at most 128 MiB of HBM per device.

v0:
```python
import math

import jax
import jax.numpy as jnp
from jax import lax
from jax.sharding import PartitionSpec as P

STATIONS = 10240
WINDOWS = 256


cycle_rates = (0.0361, 0.0596)
two_pi = 2.0 * math.pi


def steering(delays):
    rates = jnp.array(cycle_rates, jnp.float32)
    phase = (two_pi * rates)[:, None, None] * delays.astype(jnp.float32)[None]
    return (jnp.cos(phase).astype(jnp.bfloat16), jnp.sin(phase).astype(jnp.bfloat16))


def lowprod(form, left, right):
    return jnp.einsum(form, left, right, preferred_element_type=jnp.float32)


def station_power(block):
    return jnp.sum(jnp.square(block.astype(jnp.float32)), axis=(1, 3))


def to_sources(beams, src_cos, src_sin):
    width = src_cos.shape[2]
    steer = jnp.concatenate([src_cos, src_sin], axis=2)
    high = beams.astype(jnp.bfloat16)
    low = (beams - high.astype(jnp.float32)).astype(jnp.bfloat16)
    joined = lowprod("fcbi,fia->fcba", high, steer) + lowprod("fcbi,fia->fcba", low, steer)
    out_re = joined[:, 0, :, :width] - joined[:, 1, :, width:]
    out_im = joined[:, 1, :, :width] + joined[:, 0, :, width:]
    return jnp.stack([out_re, out_im], axis=1)


def body(spectra, delays_s, delays_r, wl_index):
    row_spec = lax.all_gather(spectra, "col", axis=2, tiled=True)
    local_count = spectra.shape[2]
    first_station = (
        lax.axis_index("row") * lax.axis_size("col") + lax.axis_index("col")
    ) * local_count
    station_ids = first_station + jnp.arange(local_count, dtype=jnp.int32)
    picked = jnp.sum(
        jnp.where(station_ids[None, :] == wl_index[:, None], station_power(spectra), 0.0), axis=1
    )
    level = 0.5 * lax.psum(picked, ("row", "col"))
    row_gain = lax.rsqrt(station_power(row_spec) + level[:, None])
    rec_cos, rec_sin = steering(delays_r)
    src_cos, src_sin = steering(delays_s)
    piece = lax.all_gather(spectra, "row", axis=2, tiled=True)
    col_gain = lax.rsqrt(station_power(piece) + level[:, None])
    cross_re = lowprod("fiw,fjw->fij", row_spec[:, 0], piece[:, 0]) + lowprod(
        "fiw,fjw->fij", row_spec[:, 1], piece[:, 1]
    )
    cross_im = lowprod("fiw,fjw->fij", row_spec[:, 1], piece[:, 0]) - lowprod(
        "fiw,fjw->fij", row_spec[:, 0], piece[:, 1]
    )
    weight = row_gain[:, :, None] * col_gain[:, None, :]
    coh_re = (cross_re * weight).astype(jnp.bfloat16)
    coh_im = (cross_im * weight).astype(jnp.bfloat16)
    part_re = lowprod("fjb,fij->fbi", rec_cos, coh_re) + lowprod("fjb,fij->fbi", rec_sin, coh_im)
    part_im = lowprod("fjb,fij->fbi", rec_cos, coh_im) - lowprod("fjb,fij->fbi", rec_sin, coh_re)
    partial_value = jnp.stack([part_re, part_im], axis=1)
    whole_block = to_sources(partial_value, src_cos, src_sin)
    summed = lax.psum_scatter(whole_block, "col", scatter_dimension=2, tiled=True)
    field = lax.psum_scatter(summed, "row", scatter_dimension=3, tiled=True)
    return field * (math.sqrt(WINDOWS) / STATIONS)


def solution(mesh):
    in_specs = (P(None, None, ("row", "col"), None), P("row", None), P("col", None), P())
    out_specs = P(None, None, "col", "row")
    return jax.shard_map(body, mesh=mesh, in_specs=in_specs, out_specs=out_specs, check_vma=False)
```

profile of v0, /device:TPU:0, one launch (start us, length us, event | category | flops | bytes accessed | tf_op | source)
XLA Modules:
  0.0 563.6 jit_solution(16043585059814933433)
XLA Ops:
  6.5 0.0 all-gather.3.cloned.1.call-start
  6.5 2.0 copy.28
  8.5 0.0 all-gather.3.cloned.1.call-update
  8.6 0.0 all-gather.5.cloned.1.call-start
  8.6 0.7 all-gather.5.cloned.1.call-update
  9.3 0.0 reduce-scatter.2.cloned.1.call-start
  9.4 1.3 multiply_reduce_fusion.2
  10.7 0.8 fusion.36
  11.5 42.2 %psum.7 = f32[2]{0:T(128)S(1)} all-reduce(f32[2]{0:T(128)S(1)} %fusion.36), channel_id=1, replica_groups=mesh['row'=8,'col'=4] {'row','col'}, use_global_device_ids=true, to_apply=%region_3.4 | all-reduce | flops 2 | bytes 16 | tf_op jit(solution)/shard_map/psum | solution.py:51
  53.7 5.4 convert_element_type.42
  59.2 0.0 copy-start.2
  59.2 6.1 %copy.27 = f32[2560,512]{0,1:T(8,128)} copy(f32[2560,512]{1,0:T(8,128)} %convert_element_type.42) | data formatting | bytes 10485760 | tf_op jit(solution)/shard_map/convert_element_type | solution.py:18
  65.2 0.0 copy-done.2
  65.2 0.0 copy-start.4
  65.2 0.3 convert_element_type.51
  65.5 0.3 copy-done.4
  65.9 20.8 %fusion.13 = (bf16[2,1280,512]{2,1,0:T(8,128)(2,1)}, bf16[2,1280,512]{2,1,0:T(8,128)(2,1)}) fusion(f32[1280,512]{1,0:T(8,128)S(1)} %convert_element_type.51, f32[2]{0:T(128)S(1)} %copy-done.4), kind=kLoop, calls=%fused_computation.18 | loop fusion | flops 3932160 | bytes 7864328 | tf_op jit(solution)/shard_map/convert_element_type | solution.py:19
  86.7 0.0 all-gather.3.cloned.1.call-done
  86.7 0.0 copy-start.1
  86.7 2.5 multiply_reduce_fusion.1
  89.2 0.1 add_rsqrt_fusion.1
  89.3 36.8 %all-gather.5.cloned.1.call-done = bf16[2,2,2560,256]{3,2,0,1:T(8,128)(2,1)} async-done(((bf16[2,2,320,256]{3,2,0,1:T(8,128)(2,1)}), bf16[2,2,2560,256]{3,2,0,1:T(8,128)(2,1)}) %all-gather.5.cloned.1.call-update) | async-done | bytes 5242896 | tf_op jit(solution)/shard_map/all_gather | solution.py:55
  126.0 0.0 copy-start
  126.0 3.8 multiply_reduce_fusion
  129.8 0.1 add_rsqrt_fusion
  129.9 0.0 copy-done.1
  129.9 0.2 copy-done
  130.1 10.5 %fusion.34 = f32[2,1280,2560]{2,1,0:T(8,128)} fusion(bf16[2,2,2560,256]{3,2,0,1:T(8,128)(2,1)S(1)} %copy-done, bf16[2,2,1280,256]{3,2,0,1:T(8,128)(2,1)S(1)} %copy-done.1), kind=kOutput, calls=%fused_computation.40 | convolution fusion | flops 3355443200 | bytes 30146560 | tf_op jit(solution)/shard_map/fiw,fjw->fij/dot_general | solution.py:23
  140.6 15.8 %fusion.1 = bf16[2,1280,2560]{2,1,0:T(8,128)(2,1)} fusion(f32[2,1280,2560]{2,1,0:T(8,128)} %fusion.34, f32[2,2560]{1,0:T(2,128)S(1)} %add_rsqrt_fusion, f32[2,1280]{1,0:T(2,128)S(1)} %add_rsqrt_fusion.1, bf16[2,2,2560,256]{3,2,0,1:T(8,128)(2,1)} %all-gather.5.cloned.1.call-done, bf16[2,2,1280,256]{3,2,0,1:T(8,128)(2,1)S(1)} %copy-done.1), kind=kOutput, calls=%fused_computation.3 | convolution fusion | flops 3381657600 | bytes 43284480 | tf_op jit(solution)/shard_map/fiw,fjw->fij/dot_general | solution.py:23
  156.4 46.0 %fusion.7 = f32[2,512,1280]{2,1,0:T(8,128)} fusion(bf16[2,1280,2560]{2,1,0:T(8,128)(2,1)} %fusion.1, f32[2560,512]{0,1:T(8,128)} %copy.27, f32[2]{0:T(128)S(1)} %copy-done.4), kind=kOutput, calls=%fused_computation.15 | convolution fusion | flops 6716129280 | bytes 23592968 | tf_op jit(solution)/shard_map/fjb,fij->fbi/dot_general | solution.py:23
  202.4 12.4 %fusion.35 = f32[2,1280,2560]{2,1,0:T(8,128)} fusion(bf16[2,2,2560,256]{3,2,0,1:T(8,128)(2,1)} %all-gather.5.cloned.1.call-done, bf16[2,2,1280,256]{3,2,0,1:T(8,128)(2,1)S(1)} %copy-done.1), kind=kOutput, calls=%fused_computation.41 | convolution fusion | flops 3355443200 | bytes 30146560 | tf_op jit(solution)/shard_map/fiw,fjw->fij/dot_general | solution.py:23
  214.8 15.7 %fusion = bf16[2,1280,2560]{2,1,0:T(8,128)(2,1)} fusion(f32[2,1280,2560]{2,1,0:T(8,128)} %fusion.35, f32[2,2560]{1,0:T(2,128)S(1)} %add_rsqrt_fusion, f32[2,1280]{1,0:T(2,128)S(1)} %add_rsqrt_fusion.1, bf16[2,2,2560,256]{3,2,0,1:T(8,128)(2,1)} %all-gather.5.cloned.1.call-done, bf16[2,2,1280,256]{3,2,0,1:T(8,128)(2,1)S(1)} %copy-done.1), kind=kOutput, calls=%fused_computation.2 | convolution fusion | flops 3381657600 | bytes 43284480 | tf_op jit(solution)/shard_map/fiw,fjw->fij/dot_general | solution.py:23
  230.5 58.6 %fusion.5 = f32[2,512,1280]{2,1,0:T(8,128)} fusion(bf16[2,1280,2560]{2,1,0:T(8,128)(2,1)} %fusion, f32[2560,512]{0,1:T(8,128)} %copy.27, f32[2]{0:T(128)S(1)} %copy-done.4), kind=kOutput, calls=%fused_computation.14 | convolution fusion | flops 6716129280 | bytes 23592968 | tf_op jit(solution)/shard_map/fjb,fij->fbi/dot_general | solution.py:23
  289.1 58.8 %add_bitcast_fusion = f32[2,1,512,1280]{3,2,0,1:T(8,128)} fusion(f32[2,512,1280]{2,1,0:T(8,128)} %fusion.7, bf16[2,1280,2560]{2,1,0:T(8,128)(2,1)} %fusion, f32[2560,512]{0,1:T(8,128)} %copy.27, f32[2]{0:T(128)S(1)} %copy-done.4), kind=kOutput, calls=%fused_computation.26 | convolution fusion | flops 6717440000 | bytes 28835848 | tf_op jit(solution)/shard_map/fjb,fij->fbi/dot_general | solution.py:23
  347.9 0.0 copy-start.3
  347.9 46.0 %subtract_bitcast_fusion = f32[2,1,512,1280]{3,2,0,1:T(8,128)} fusion(f32[2,512,1280]{2,1,0:T(8,128)} %fusion.5, bf16[2,1280,2560]{2,1,0:T(8,128)(2,1)} %fusion.1, f32[2560,512]{0,1:T(8,128)} %copy.27, f32[2]{0:T(128)S(1)} %copy-done.4), kind=kOutput, calls=%fused_computation.25 | convolution fusion | flops 6717440000 | bytes 28835848 | tf_op jit(solution)/shard_map/fjb,fij->fbi/dot_general | solution.py:23
  393.9 0.0 copy-done.3
  393.9 13.6 %fusion.15 = f32[2,2,512,1024]{3,2,1,0:T(8,128)} fusion(bf16[2,1280,512]{2,1,0:T(8,128)(2,1)} %get-tuple-element.8, bf16[2,1280,512]{2,1,0:T(8,128)(2,1)S(1)} %copy-done.3, f32[2,1,512,1280]{3,2,0,1:T(8,128)} %subtract_bitcast_fusion, f32[2,1,512,1280]{3,2,0,1:T(8,128)} %add_bitcast_fusion), kind=kOutput, calls=%fused_computation.21 | convolution fusion | flops 5392302080 | bytes 24117248 | tf_op jit(solution)/shard_map/fcbi,fia->fcba/dot_general | solution.py:23
  407.5 16.0 %fusion.31 = f32[2,2,512,1024]{3,2,1,0:T(8,128)} fusion(f32[2,2,512,1024]{3,2,1,0:T(8,128)} %fusion.15, bf16[2,1280,512]{2,1,0:T(8,128)(2,1)} %get-tuple-element.8, bf16[2,1280,512]{2,1,0:T(8,128)(2,1)S(1)} %copy-done.3, f32[2,1,512,1280]{3,2,0,1:T(8,128)} %subtract_bitcast_fusion, f32[2,1,512,1280]{3,2,0,1:T(8,128)} %add_bitcast_fusion), kind=kOutput, calls=%fused_computation.37 | convolution fusion | flops 5383913472 | bytes 32505856 | tf_op jit(solution)/shard_map/fcbi,fia->fcba/dot_general | solution.py:23
  423.5 4.5 slice_subtract_fusion
  428.0 2.4 pad_maximum_fusion.1
  430.4 0.0 copy-start.5
  430.4 0.0 reduce-scatter.2.cloned.1.call-update
  430.4 0.0 all-reduce.3.cloned.1.call-start
  430.5 42.9 %reduce-scatter.2.cloned.1.call-done = f32[2,2,128,512]{3,2,1,0:T(8,128)} async-done(((f32[2,2,512,512]{3,2,1,0:T(8,128)}), f32[2,2,128,512]{3,2,1,0:T(8,128)}) %reduce-scatter.2.cloned.1.call-update) | async-done | bytes 1048592 | tf_op jit(solution)/shard_map/reduce_scatter | solution.py:70
  473.4 2.3 copy.32
  475.6 0.0 all-reduce.3.cloned.1.call-update
  475.7 0.0 copy-done.5
  475.7 0.6 dynamic-slice
  476.9 78.2 %all-reduce.3.cloned.1.call-done = f32[2,2,128,512]{2,1,0,3:T(2,128)} async-done(((f32[2,2,128,512]{2,1,0,3:T(2,128)}), f32[2,2,128,512]{2,1,0,3:T(2,128)}) %all-reduce.3.cloned.1.call-update) | async-done | bytes 1048592
  555.1 0.9 constant_dynamic-slice_fusion
  556.0 0.7 copy_multiply_fusion
  (2 shorter events, 0.0 us)
Async XLA Ops:
  6.5 80.1 %all-gather.3.cloned.1.call-start = ((), (), s32[]{:S(2)}) async-start(), calls=%async_computation.1 | async-start | bytes 3276800 | tf_op jit(solution)/shard_map/all_gather | solution.py:42
  8.6 117.5 %all-gather.5.cloned.1.call-start = ((), (), s32[]{:S(2)}) async-start(), calls=%async_computation.2 | async-start | bytes 5898240 | tf_op jit(solution)/shard_map/all_gather | solution.py:55
  9.3 464.1 %reduce-scatter.2.cloned.1.call-start = ((), (), s32[]{:S(2)}) async-start(), calls=%async_computation.3 | async-start | bytes 5242880 | tf_op jit(solution)/shard_map/reduce_scatter | solution.py:70
  59.2 6.1 %copy-start.2 = (s32[1280,512]{1,0:T(8,128)S(1)}, s32[1280,512]{1,0:T(8,128)}, u32[]{:S(2)}) copy-start(s32[1280,512]{1,0:T(8,128)} %param.7) | copy-start | bytes 7864324
  65.2 0.7 copy-start.4
  86.7 43.2 %copy-start.1 = (bf16[2,2,1280,256]{3,2,0,1:T(8,128)(2,1)S(1)}, bf16[2,2,1280,256]{3,2,0,1:T(8,128)(2,1)}, u32[]{:S(2)}) copy-start(bf16[2,2,1280,256]{3,2,0,1:T(8,128)(2,1)} %all-gather.3.cloned.1.call-done) | copy-start | bytes 7864324
  126.0 4.0 copy-start
  347.9 46.0 %copy-start.3 = (bf16[2,1280,512]{2,1,0:T(8,128)(2,1)S(1)}, bf16[2,1280,512]{2,1,0:T(8,128)(2,1)}, u32[]{:S(2)}) copy-start(bf16[2,1280,512]{2,1,0:T(8,128)(2,1)} %get-tuple-element.7) | copy-start | bytes 7864324
  430.4 45.3 %copy-start.5 = (u32[32]{0:T(128)S(1)}, u32[32]{0:T(128)}, u32[]{:S(2)}) copy-start(u32[32]{0:T(128)} %constant.27) | copy-start | bytes 388
  430.4 124.7 %all-reduce.3.cloned.1.call-start = ((), (), s32[]{:S(2)}) async-start(), calls=%async_computation.4 | async-start | bytes 2097152
Sparse Core Ops, SparseCore 0:
  8.9 28.5 all-gather.2
  39.7 86.2 all-gather.4
  430.5 42.7 reduce-scatter.1
  477.1 77.9 all-reduce.2
where the time goes:
time: 571 us; the launch traced here: 564 us
  matrix products  293 us (51%)
  waiting for transfers between devices  159 us (28%)
  other arithmetic  42.6 us (7%)
  blocking collectives  42.2 us (7%)
  between operations  14.3 us (3%)
  local copies, waits for them, and re-layouts  12.4 us (2%)
    dot_general x10, matrix products, lowprod(): return jnp.einsum(form, left, right, preferred_element_type=jnp.float32)  293 us
    unnamed x5, waiting for transfers between devices  79 us
    reduce_scatter x1, waiting for transfers between devices, body(): lax.psum_scatter(whole_block, 'col', scatter_dimension=2, tiled=True)  42.9 us
    psum x1, blocking collectives, body(): level = 0.5 * lax.psum(picked, ('row', 'col'))  42.2 us
    all_gather x1, waiting for transfers between devices, body(): piece = lax.all_gather(spectra, 'row', axis=2, tiled=True)  36.8 us
    convert_element_type x1, other arithmetic, steering(): jnp.cos(phase).astype(jnp.bfloat16)  20.8 us
  transfers between devices with their start and end apart: 4, of which 3 were waited for; matrix products, arithmetic and copies ran while one was open for 7% of the time, Pallas kernels for 0%

commit v1 on v0

v1 whole, which is shorter than its diff:
```python
import math

import jax
import jax.numpy as jnp
from jax import lax
from jax.sharding import PartitionSpec as P

cycle_rates = (0.0361, 0.0596)
SIN = (3.141592502593994, -5.1677069664001465, 2.5500314235687256, -0.5980451703071594, 0.0772201269865036)
COS = (0.9999999403953552, -4.934792995452881, 4.058412075042725, -1.3318800926208496, 0.2196967601776123)


def horner(z, terms):
    total = terms[-1]
    for term in terms[-2::-1]:
        total = total * z + term
    return total


def steering(delays, rate):
    turns = rate * delays.astype(jnp.float32)
    turns = turns - jnp.round(turns)
    z = turns * turns
    half_sin = turns * horner(z, SIN)
    half_cos = horner(z, COS)
    sin = 2.0 * half_sin * half_cos
    cos = 1.0 - 2.0 * half_sin * half_sin
    return cos.astype(jnp.bfloat16), sin.astype(jnp.bfloat16)


def swap(value, axis, bit):
    size = lax.axis_size(axis)
    return lax.ppermute(value, axis, [(i, i ^ bit) for i in range(size)])


def pick(value, index, axis):
    return lax.dynamic_index_in_dim(value, index, axis, keepdims=False)


def pair(own, other, bit, axis=0):
    first = jnp.where(bit == 0, own, other)
    second = jnp.where(bit == 0, other, own)
    return jnp.stack([first, second], axis=axis)


def bits(size, start):
    found = []
    while start < size:
        found.append(start)
        start *= 2
    return found


def beams(spec, gain, cos, sin):
    scaled = (spec.astype(jnp.float32) * gain[..., None, :, None]).astype(jnp.bfloat16)
    real, imag = scaled[..., 0, :, :], scaled[..., 1, :, :]
    width = real.shape[-1]
    real, imag = real.reshape(-1, width), imag.reshape(-1, width)
    straight = jnp.concatenate([real, imag], axis=1)
    turned = jnp.concatenate([-imag, real], axis=1)
    return jnp.einsum("sb,sw->bw", cos, straight, preferred_element_type=jnp.float32) + jnp.einsum(
        "sb,sw->bw", sin, turned, preferred_element_type=jnp.float32
    )


def halve(value, axis, bit, at):
    other = swap(pick(value, 1 - at, 1).astype(jnp.bfloat16), axis, bit)
    return pick(value, at, 1) + other.astype(jnp.float32)


def add(value, axis, bit):
    mine = value.astype(jnp.bfloat16)
    return value + swap(mine, axis, bit).astype(jnp.float32)


def body(spectra, delays_s, delays_r, wl_index):
    n_row, n_col = lax.axis_size("row"), lax.axis_size("col")
    row, col = lax.axis_index("row"), lax.axis_index("col")
    per, windows = spectra.shape[2:]
    half = windows // 2
    core, x, y = col & 1, (col >> 1) & 1, row & 1

    power = jnp.sum(jnp.square(spectra.astype(jnp.float32)), axis=(1, 3))
    ids = (row * n_col + col) * per + jnp.arange(per, dtype=jnp.int32)
    picked = jnp.sum(jnp.where(ids[None, :] == wl_index[:, None], power, 0.0), axis=1)

    spec = pair(pick(spectra, core, 0), swap(pick(spectra, 1 - core, 0), "col", 1), core)
    note = jnp.concatenate([power, picked[:, None]], axis=1)
    note = pair(pick(note, core, 0), swap(pick(note, 1 - core, 0), "col", 1), core)
    power, level = note[:, :per], jnp.sum(note[:, per])

    halves = spec.reshape(*spec.shape[:-1], 2, half)
    spec_x = pair(pick(halves, x, 3), swap(pick(halves, 1 - x, 3), "col", 2), x)
    spec_y = pair(pick(halves, y, 3), swap(pick(halves, 1 - y, 3), "row", 1), y)

    note = jnp.concatenate([power.reshape(-1), level[None]])
    other = swap(note, "col", 2)
    power_x = pair(power, other[:-1].reshape(power.shape), x)
    level = level + other[-1]
    note = jnp.concatenate([power.reshape(-1), level[None]])
    other = swap(note, "row", 1)
    power_y = pair(power, other[:-1].reshape(power.shape), y)
    level = level + other[-1]
    for bit in bits(n_row, 2):
        level = level + swap(level[None], "row", bit)[0]
    for bit in bits(n_col, 4):
        level = level + swap(level[None], "col", bit)[0]
    level = 0.5 * level

    rate = jnp.where(core == 0, cycle_rates[0], cycle_rates[1]).astype(jnp.float32)
    beams_s, beams_r = delays_s.shape[1], delays_r.shape[1]
    near_s = pick(delays_s.reshape(n_col // 4, 4 * per, beams_s), col >> 2, 0)
    near_r = pick(delays_r.reshape(n_row // 2, 2 * per, beams_r), row >> 1, 0)
    near_r = pair(near_r, swap(near_r, "col", 1), core).reshape(4 * per, beams_r)
    src_cos, src_sin = steering(near_s, rate)
    rec_cos, rec_sin = steering(near_r, rate)

    source = beams(spec_x, lax.rsqrt(power_x + level), src_cos, src_sin)
    spec_y, power_y = spec_y.swapaxes(0, 1), power_y.swapaxes(0, 1)
    receiver = beams(spec_y, lax.rsqrt(power_y + level), rec_cos, rec_sin)

    for bit in bits(n_row, 1):
        source = source.reshape(n_row // (2 * bit), 2, -1, 2 * half)
        source = halve(source, "row", bit, (row // bit) & 1)
    source = source.reshape(-1, 2 * half)
    for bit in bits(n_col, 4):
        source = add(source, "col", bit)
    source = source.astype(jnp.bfloat16)
    source = pair(source, swap(source, "col", 2), x)

    for bit in bits(n_col, 2):
        receiver = receiver.reshape(n_col // (2 * bit), 2, -1, 2 * half)
        receiver = halve(receiver, "col", bit, (col // bit) & 1)
    receiver = receiver.reshape(-1, 2 * half)
    for bit in bits(n_row, 2):
        receiver = add(receiver, "row", bit)
    receiver = receiver.astype(jnp.bfloat16)
    receiver = pair(receiver, swap(receiver, "row", 1), y)

    def joined(left, right):
        return jnp.einsum("hbw,haw->ba", left, right, preferred_element_type=jnp.float32)

    s_re, s_im = source[..., :half], source[..., half:]
    r_re, r_im = receiver[..., :half], receiver[..., half:]
    field = jnp.stack(
        [joined(r_re, s_re) + joined(r_im, s_im), joined(r_re, s_im) - joined(r_im, s_re)], axis=0
    )
    field = field * (math.sqrt(windows) / (per * n_row * n_col))
    field = field.reshape(2, 2, -1, field.shape[-1])
    return pair(pick(field, core, 1), swap(pick(field, 1 - core, 1), "col", 1), core)


def solution(mesh):
    in_specs = (P(None, None, ("row", "col"), None), P("row", None), P("col", None), P())
    out_specs = P(None, None, "col", "row")
    return jax.shard_map(body, mesh=mesh, in_specs=in_specs, out_specs=out_specs, check_vma=False)
```

time: 571 us -> 77 us (0.13); the launches traced: 564 us -> 76.6 us
  matrix products: 293 us -> 5.73 us
  waiting for transfers between devices: 159 us -> 21.7 us
  blocking collectives: 42.2 us -> 0 us
  other arithmetic: 42.6 us -> 11.1 us
  starting transfers between devices: 0.12 us -> 26 us
  between operations: 14.3 us -> 3.54 us
    dot_general x10 -> x8, matrix products: 293 us -> 5.73 us  [the longest x2 2.8 us: beams(): jnp.einsum('sb,sw->bw', sin, turned, preferred_element_type=jnp.float32)]
    unnamed x5 -> x0, waiting for transfers between devices: 79 us -> none
    reduce_scatter x1 -> x0, waiting for transfers between devices: 42.9 us -> none  [body(): lax.psum_scatter(whole_block, 'col', scatter_dimension=2, tiled=True)]
    psum x1 -> x0, blocking collectives: 42.2 us -> none  [body(): level = 0.5 * lax.psum(picked, ('row', 'col'))]
    all_gather x2 -> x0, waiting for transfers between devices: 36.8 us -> none  [the longest x1 36.8 us: body(): piece = lax.all_gather(spectra, 'row', axis=2, tiled=True)]
    ppermute x0 -> x18, starting transfers between devices: none -> 26 us  [swap(): return lax.ppermute(value, axis, [(i, i ^ bit) for i in range(size)])]
    convert_element_type x3 -> x7, other arithmetic: 26.5 us -> 2.98 us  [the longest x1 2.37 us: steering(): return (cos.astype(jnp.bfloat16), sin.astype(jnp.bfloat16))]
    ppermute x0 -> x18, waiting for transfers between devices: none -> 21.7 us  [swap(): return lax.ppermute(value, axis, [(i, i ^ bit) for i in range(size)])]
  transfers between devices with their start and end apart: 4 -> 18, of which waited for: 3 -> 9; matrix products, arithmetic and copies ran while one was open for 7% -> 28% of each run, Pallas kernels for 0% -> 0%
where the time goes in v1:
time: 77 us; the launch traced here: 76.6 us
  starting transfers between devices  26 us (34%)
  waiting for transfers between devices  21.7 us (28%)
  other arithmetic  11.1 us (14%)
  local copies, waits for them, and re-layouts  8.56 us (11%)
  matrix products  5.73 us (7%)
  between operations  3.54 us (5%)
    ppermute x18, starting transfers between devices, swap(): return lax.ppermute(value, axis, [(i, i ^ bit) for i in range(size)])  26 us
    ppermute x18, waiting for transfers between devices, swap(): return lax.ppermute(value, axis, [(i, i ^ bit) for i in range(size)])  21.7 us
    another operation x9, other arithmetic, pair(): return jnp.stack([first, second], axis=axis)  3.83 us
    dynamic_slice x2, local copies, waits for them, and re-layouts, pick(): return lax.dynamic_index_in_dim(value, index, axis, keepdims=False)  2.83 us
    dot_general x2, matrix products, beams(): jnp.einsum('sb,sw->bw', sin, turned, preferred_element_type=jnp.float32)  2.8 us
    squeeze x2, local copies, waits for them, and re-layouts, pick(): return lax.dynamic_index_in_dim(value, index, axis, keepdims=False)  2.4 us
    convert_element_type x1, other arithmetic, steering(): return (cos.astype(jnp.bfloat16), sin.astype(jnp.bfloat16))  2.37 us
    dot_general x2, matrix products, beams(): jnp.einsum('sb,sw->bw', cos, straight, preferred_element_type=jnp.float32)  2.24 us
  transfers between devices with their start and end apart: 18, of which 9 were waited for; matrix products, arithmetic and copies ran while one was open for 28% of the time, Pallas kernels for 0%

profile of v1, /device:TPU:0, one launch (start us, length us, event | category | flops | bytes accessed | tf_op | source)
XLA Modules:
  0.0 76.6 jit_solution(12278250196870207341)
XLA Ops:
  0.0 1.4 %multiply_reduce_fusion = f32[2,320]{1,0:T(2,128)S(1)} fusion(bf16[2,2,320,256]{3,2,1,0:T(8,128)(2,1)} %param.4), kind=kLoop, calls=%fused_computation.27 | loop fusion | flops 982400 | bytes 657920 | tf_op jit(solution)/shard_map/reduce_sum | solution.py:83
  1.4 0.8 %fusion.48 = f32[2]{0:T(128)S(1)} fusion(f32[2,320]{1,0:T(2,128)S(1)} %multiply_reduce_fusion, s32[320]{0:T(512)S(1)} %iota_add_fusion, s32[2]{0:T(128)} %param.7), kind=kLoop, calls=%fused_computation.119 | loop fusion | flops 1918 | bytes 3856 | tf_op jit(solution)/shard_map/reduce_sum | solution.py:85
  2.2 0.1 copy.16
  2.3 0.1 fusion.52
  2.4 0.5 collective-permute-start.3
  2.9 1.0 %dynamic-slice_bitcast_fusion.1 = bf16[2,320,256]{2,1,0:T(8,128)(2,1)S(1)} fusion(bf16[2,2,320,256]{3,2,1,0:T(8,128)(2,1)} %param.4, s32[]{:T(128)S(6)} %select_n.202), kind=kLoop, calls=%fused_computation.66 | loop fusion | bytes 655364 | tf_op jit(solution)/shard_map/jit(dynamic_index_in_dim)/squeeze | solution.py:37
  3.9 0.1 collective-permute-start.1
  4.1 0.7 fusion.53
  4.8 0.1 reshape.91
  4.8 0.7 pad_maximum_fusion.7
  5.5 3.0 %collective-permute-start.4 = (f32[641]{0:T(1024)S(1)}, f32[641]{0:T(1024)S(1)}, u32[]{:S(2)}, u32[]{:S(2)}) collective-permute-start(f32[641]{0:T(1024)S(1)} %pad_maximum_fusion.7), channel_id=1, source_target_pairs={{0,2},{1,3},{2,0},{3,1},{4,6},{5,7},{6,4},{7,5},{8,10},{9,11},{10,... | collective-permute-start | bytes 7700 | tf_op jit(solution)/shard_map/ppermute | solution.py:33
  8.5 1.4 %dynamic-slice_bitcast_fusion = s32[640,512]{1,0:T(8,128)S(1)} fusion(s32[4,640,512]{2,1,0:T(8,128)} %bitcast.159, s32[]{:T(128)S(6)} %select_n.196), kind=kLoop, calls=%fused_computation.30 | loop fusion | bytes 2621444 | tf_op jit(solution)/shard_map/jit(dynamic_index_in_dim)/squeeze | solution.py:37
  9.9 0.1 collective-permute-start
  10.0 0.1 collective-permute-done.4
  10.1 0.6 slice.44
  12.0 2.1 %collective-permute-start.5 = (f32[641]{0:T(1024)S(1)}, f32[641]{0:T(1024)S(1)}, u32[]{:S(2)}, u32[]{:S(2)}) collective-permute-start(f32[641]{0:T(1024)S(1)} %pad_maximum_fusion.8), channel_id=1, source_target_pairs={{0,4},{4,0},{8,12},{12,8},{16,20},{20,16},{24,28},{28,24},{1,5},{5... | collective-permute-start | bytes 7700 | tf_op jit(solution)/shard_map/ppermute | solution.py:33
  14.1 0.1 reshape.95
  14.2 1.5 %collective-permute-done.5 = f32[641]{0:T(1024)S(1)} collective-permute-done((f32[641]{0:T(1024)S(1)}, f32[641]{0:T(1024)S(1)}, u32[]{:S(2)}, u32[]{:S(2)}) %collective-permute-start.5) | collective-permute-done | bytes 2596 | tf_op jit(solution)/shard_map/ppermute | solution.py:33
  15.7 0.6 slice.46
  17.0 0.1 reshape.92
  17.1 3.4 %collective-permute-start.6 = (f32[1]{0:T(128)}, f32[1]{0:T(128)}, u32[]{:S(2)}, u32[]{:S(2)}) collective-permute-start(f32[1]{0:T(128)} %bitcast.17), channel_id=1, source_target_pairs={{0,8},{4,12},{8,0},{12,4},{16,24},{20,28},{24,16},{28,20},{1,9},{5... | collective-permute-start | bytes 20 | tf_op jit(solution)/shard_map/ppermute | solution.py:33
  20.5 0.1 stack.103
  20.6 0.1 stack.102
  20.7 0.2 constant_dynamic-update-slice_fusion.1
  20.9 0.3 constant_dynamic-update-slice_fusion
  21.2 2.7 %constant_dynamic-slice_fusion.9 = (bf16[2,2,320,1,128]{4,3,2,1,0:T(2,128)(2,1)S(1)}, bf16[2,2,320,1,128]{4,3,2,1,0:T(2,128)(2,1)S(1)}, bf16[2,2,320,1,128]{4,3,...) fusion(bf16[2,2,320,2,128]{4,3,2,1,0:T(2,128)(2,1)S(1)} %constant_dynamic-update-slice_fusion, s32[]{:T(128)S(6)} %select_n.205, ...), kind=kLoop, calls=%fused_computation.116 | loop fusion | bytes 2621456 | tf_op jit(solution)/shard_map/jit(dynamic_index_in_dim)/dynamic_slice | solution.py:37
  23.9 0.8 copy.33
  24.7 1.5 %collective-permute-start.12 = (bf16[2,2,320,128]{3,2,1,0:T(8,128)(2,1)}, bf16[2,2,320,128]{3,2,1,0:T(8,128)(2,1)}, u32[]{:S(2)}, u32[]{:S(2)}) collective-permute-start(bf16[2,2,320,128]{3,2,1,0:T(8,128)(2,1)} %bitcast.149), channel_id=1, source_target_pairs={{0,2},{1,3},{2,0},{3,1},{4,6},{5,7},{6,4},{7,5},{8,10},{9,11},{10,... | collective-permute-start | bytes 983048 | tf_op jit(solution)/shard_map/ppermute | solution.py:33
  26.7 4.0 %collective-permute-start.7 = (f32[1]{0:T(128)}, f32[1]{0:T(128)}, u32[]{:S(2)}, u32[]{:S(2)}) collective-permute-start(f32[1]{0:T(128)} %bitcast.19), channel_id=1, source_target_pairs={{0,16},{4,20},{8,24},{12,28},{16,0},{20,4},{24,8},{28,12},{1,17},{... | collective-permute-start | bytes 20 | tf_op jit(solution)/shard_map/ppermute | solution.py:33
  30.7 0.7 collective-permute-done.7
  32.0 1.6 %collective-permute-start.2 = (bf16[2,2,320,128]{3,2,1,0:T(8,128)(2,1)S(1)}, bf16[2,2,320,128]{3,2,1,0:T(8,128)(2,1)S(1)}, u32[]{:S(2)}, u32[]{:S(2)}) collective-permute-start(bf16[2,2,320,128]{3,2,1,0:T(8,128)(2,1)S(1)} %bitcast.167), channel_id=1, source_target_pairs={{0,4},{4,0},{8,12},{12,8},{16,20},{20,16},{24,28},{28,24},{1,5},{5... | collective-permute-start | bytes 983048 | tf_op jit(solution)/shard_map/ppermute | solution.py:33
  33.6 1.0 %fusion.34 = (bf16[1,2,2,320,128]{4,3,2,1,0:T(8,128)(2,1)S(1)}, bf16[1,2,2,320,128]{4,3,2,1,0:T(8,128)(2,1)S(1)}) fusion(bf16[2,2,320,128]{3,2,1,0:T(8,128)(2,1)} %collective-permute-done.12, pred[]{:T(512)S(6)} %eq.17, bf16[2,2,320,1,128]{4,3,2,1,0:T(2,128)(2,1)S(1)} %get-tuple-element.21), kind=kLoop, calls=%fused_computation.57 | loop fusion | flops 327680 | bytes 1310721 | tf_op jit(solution)/shard_map/stack | solution.py:43
  34.6 0.2 multiply_convert_fusion
  35.0 4.1 %collective-permute-done.2 = bf16[2,2,320,128]{3,2,1,0:T(8,128)(2,1)S(1)} collective-permute-done((bf16[2,2,320,128]{3,2,1,0:T(8,128)(2,1)S(1)}, bf16[2,2,320,128]{3,2,1,0:T(8,128)(2,1)S(1)}, u32[]{:S(2)}, u32[]{:S(2)}) %collective-permute-start.2) | collective-permute-done | bytes 327712 | tf_op jit(solution)/shard_map/ppermute | solution.py:33
  39.2 0.2 fusion.11
  39.4 2.3 %fusion.12 = f32[512,256]{1,0:T(8,128)S(1)} fusion(s32[1280,512]{1,0:T(8,128)S(1)} %copy-done.1, f32[]{:T(128)S(6)} %select_n.194, bf16[1280,128]{1,0:T(8,128)(2,1)S(1)} %bitcast.163, bf16[1280,128]{1,0:T(8,128)(2,1)S(1)} %bitcast_negate_fusion), kind=kOutput, calls=%fused_computation.31 | convolution fusion | flops 353239040 | bytes 3801092 | tf_op jit(solution)/shard_map/sb,sw->bw/dot_general | solution.py:61
  41.8 1.7 %fusion.16 = f32[512,256]{1,0:T(8,128)S(1)} fusion(f32[512,256]{1,0:T(8,128)S(1)} %fusion.12, s32[1280,512]{1,0:T(8,128)S(1)} %copy-done.1, f32[]{:T(128)S(6)} %select_n.194, bf16[1280,128]{1,0:T(8,128)(2,1)S(1)} %bitcast.157, bf16[1280,128]{1,0:T(8,128)(2,1)S(1)} %bitcast.164), kind=kOutput, calls=%fused_computation.34 | convolution fusion | flops 348782592 | bytes 4325380 | tf_op jit(solution)/shard_map/sb,sw->bw/dot_general | solution.py:61
  43.5 1.6 %collective-permute-start.13 = (bf16[4,64,256]{2,1,0:T(8,128)(2,1)S(1)}, bf16[4,64,256]{2,1,0:T(8,128)(2,1)S(1)}, u32[]{:S(2)}, u32[]{:S(2)}) collective-permute-start(bf16[4,64,256]{2,1,0:T(8,128)(2,1)S(1)} %fusion.40), channel_id=1, source_target_pairs={{0,4},{4,0},{8,12},{12,8},{16,20},{20,16},{24,28},{28,24},{1,5},{5... | collective-permute-start | bytes 393224 | tf_op jit(solution)/shard_map/ppermute | solution.py:33
  45.2 2.0 %select_bitcast_fusion.1 = (s32[1,640,512]{2,1,0:T(8,128)S(1)}, s32[1,640,512]{2,1,0:T(8,128)S(1)}) fusion(s32[640,512]{1,0:T(8,128)} %collective-permute-done, pred[]{:T(512)S(6)} %eq.12, s32[4,640,512]{2,1,0:T(8,128)} %bitcast.160, s32[]{:T(128)S(6)} %select_n.196), kind=kLoop, calls=%fused_computation.29 | loop fusion | flops 655360 | bytes 5242885 | tf_op jit(solution)/shard_map/stack | solution.py:43
  47.2 0.3 fusion.6
  47.6 2.4 %fusion.1 = (bf16[1280,512]{1,0:T(8,128)(2,1)S(1)}, bf16[1280,512]{1,0:T(8,128)(2,1)S(1)}) fusion(f32[2,640,512]{2,1,0:T(8,128)S(1)} %fusion.6), kind=kLoop, calls=%fused_computation.7 | loop fusion | flops 17039360 | bytes 5242880 | tf_op jit(solution)/shard_map/convert_element_type | solution.py:28
  49.9 0.5 fusion.24
  50.5 0.6 convolution_add_fusion
  51.1 0.6 collective-permute-start.8
  51.7 0.5 collective-permute-start.14
  52.2 3.9 %collective-permute-done.8 = bf16[1,256,256]{2,1,0:T(8,128)(2,1)S(1)} collective-permute-done((bf16[1,256,256]{2,1,0:T(8,128)(2,1)S(1)}, bf16[1,256,256]{2,1,0:T(8,128)(2,1)S(1)}, u32[]{:S(2)}, u32[]{:S(2)}) %collective-permute-start.8) | collective-permute-done | bytes 131104 | tf_op jit(solution)/shard_map/ppermute | solution.py:33
  56.1 0.5 collective-permute-start.9
  56.7 2.7 %collective-permute-start.15 = (bf16[1,64,256]{2,1,0:T(8,128)(2,1)S(1)}, bf16[1,64,256]{2,1,0:T(8,128)(2,1)S(1)}, u32[]{:S(2)}, u32[]{:S(2)}) collective-permute-start(bf16[1,64,256]{2,1,0:T(8,128)(2,1)S(1)} %dynamic-slice_convert_fusion.1), channel_id=1, source_target_pairs={{0,16},{4,20},{8,24},{12,28},{16,0},{20,4},{24,8},{28,12},{1,17},{... | collective-permute-start | bytes 98312 | tf_op jit(solution)/shard_map/ppermute | solution.py:33
  59.4 1.8 %collective-permute-done.9 = bf16[256,256]{1,0:T(8,128)(2,1)S(1)} collective-permute-done((bf16[256,256]{1,0:T(8,128)(2,1)S(1)}, bf16[256,256]{1,0:T(8,128)(2,1)S(1)}, u32[]{:S(2)}, u32[]{:S(2)}) %collective-permute-start.9) | collective-permute-done | bytes 131104 | tf_op jit(solution)/shard_map/ppermute | solution.py:33
  61.2 2.7 %collective-permute-start.10 = (bf16[256,256]{1,0:T(8,128)(2,1)S(1)}, bf16[256,256]{1,0:T(8,128)(2,1)S(1)}, u32[]{:S(2)}, u32[]{:S(2)}) collective-permute-start(bf16[256,256]{1,0:T(8,128)(2,1)S(1)} %fusion.38), channel_id=1, source_target_pairs={{0,16},{4,20},{8,24},{12,28},{16,0},{20,4},{24,8},{28,12},{1,17},{... | collective-permute-start | bytes 393224 | tf_op jit(solution)/shard_map/ppermute | solution.py:33
  63.9 0.6 collective-permute-start.16
  64.5 3.9 %collective-permute-done.10 = bf16[256,256]{1,0:T(8,128)(2,1)S(1)} collective-permute-done((bf16[256,256]{1,0:T(8,128)(2,1)S(1)}, bf16[256,256]{1,0:T(8,128)(2,1)S(1)}, u32[]{:S(2)}, u32[]{:S(2)}) %collective-permute-start.10) | collective-permute-done | bytes 131104 | tf_op jit(solution)/shard_map/ppermute | solution.py:33
  68.5 0.6 collective-permute-start.11
  69.1 4.4 %collective-permute-done.11 = bf16[256,256]{1,0:T(8,128)(2,1)S(1)} collective-permute-done((bf16[256,256]{1,0:T(8,128)(2,1)S(1)}, bf16[256,256]{1,0:T(8,128)(2,1)S(1)}, u32[]{:S(2)}, u32[]{:S(2)}) %collective-permute-start.11) | collective-permute-done | bytes 131104 | tf_op jit(solution)/shard_map/ppermute | solution.py:33
  73.6 0.2 convolution_bitcast_fusion.1
  73.7 0.2 convolution_bitcast_fusion.3
  73.9 0.2 fusion.19
  74.2 0.2 fusion.20
  74.3 0.1 stack.126
  74.4 0.1 maximum_multiply_fusion
  74.5 0.1 constant_dynamic-slice_fusion.3
  74.6 0.1 collective-permute-start.17
  74.7 1.2 %collective-permute-done.17 = f32[2,128,64]{1,2,0:T(8,128)S(1)} collective-permute-done((f32[2,128,64]{1,2,0:T(8,128)S(1)}, f32[2,128,64]{1,2,0:T(8,128)S(1)}, u32[]{:S(2)}, u32[]{:S(2)}) %collective-permute-start.17) | collective-permute-done | bytes 65568 | tf_op jit(solution)/shard_map/ppermute | solution.py:33
  76.0 0.7 pad_maximum_fusion.1
  (45 shorter events, 0.9 us)
Async XLA Ops:
  0.0 20.5 %copy-start = (bf16[2,2,320,256]{3,2,1,0:T(8,128)(2,1)S(1)}, bf16[2,2,320,256]{3,2,1,0:T(8,128)(2,1)}, u32[]{:S(2)}) copy-start(bf16[2,2,320,256]{3,2,1,0:T(8,128)(2,1)} %param.4) | copy-start | bytes 1966084
  2.4 1.6 %collective-permute-start.3 = (f32[321]{0:T(512)S(1)}, f32[321]{0:T(512)S(1)}, u32[]{:S(2)}, u32[]{:S(2)}) collective-permute-start(f32[321]{0:T(512)S(1)} %get-tuple-element.6), channel_id=1, source_target_pairs={{0,1},{1,0},{2,3},{3,2},{4,5},{5,4},{6,7},{7,6},{8,9},{9,8},{10,11... | collective-permute-start | bytes 3860 | tf_op jit(solution)/shard_map/ppermute | solution.py:33
  3.9 16.6 %collective-permute-start.1 = (bf16[2,320,256]{2,1,0:T(8,128)(2,1)S(1)}, bf16[2,320,256]{2,1,0:T(8,128)(2,1)S(1)}, u32[]{:S(2)}, u32[]{:S(2)}) collective-permute-start(bf16[2,320,256]{2,1,0:T(8,128)(2,1)S(1)} %dynamic-slice_bitcast_fusion.1), channel_id=1, source_target_pairs={{0,1},{1,0},{2,3},{3,2},{4,5},{5,4},{6,7},{7,6},{8,9},{9,8},{10,11... | collective-permute-start | bytes 983048 | tf_op jit(solution)/shard_map/ppermute | solution.py:33
  5.5 4.6 %collective-permute-start.4 = (f32[641]{0:T(1024)S(1)}, f32[641]{0:T(1024)S(1)}, u32[]{:S(2)}, u32[]{:S(2)}) collective-permute-start(f32[641]{0:T(1024)S(1)} %pad_maximum_fusion.7), channel_id=1, source_target_pairs={{0,2},{1,3},{2,0},{3,1},{4,6},{5,7},{6,4},{7,5},{8,10},{9,11},{10,... | collective-permute-start | bytes 7700 | tf_op jit(solution)/shard_map/ppermute | solution.py:33
  9.9 35.3 %collective-permute-start = (s32[640,512]{1,0:T(8,128)S(1)}, s32[640,512]{1,0:T(8,128)}, u32[]{:S(2)}, u32[]{:S(2)}) collective-permute-start(s32[640,512]{1,0:T(8,128)S(1)} %dynamic-slice_bitcast_fusion), channel_id=1, source_target_pairs={{0,1},{1,0},{2,3},{3,2},{4,5},{5,4},{6,7},{7,6},{8,9},{9,8},{10,11... | collective-permute-start | bytes 3932168 | tf_op jit(solution)/shard_map/ppermute | solution.py:33
  12.0 3.7 %collective-permute-start.5 = (f32[641]{0:T(1024)S(1)}, f32[641]{0:T(1024)S(1)}, u32[]{:S(2)}, u32[]{:S(2)}) collective-permute-start(f32[641]{0:T(1024)S(1)} %pad_maximum_fusion.8), channel_id=1, source_target_pairs={{0,4},{4,0},{8,12},{12,8},{16,20},{20,16},{24,28},{28,24},{1,5},{5... | collective-permute-start | bytes 7700 | tf_op jit(solution)/shard_map/ppermute | solution.py:33
  17.1 9.1 %collective-permute-start.6 = (f32[1]{0:T(128)}, f32[1]{0:T(128)}, u32[]{:S(2)}, u32[]{:S(2)}) collective-permute-start(f32[1]{0:T(128)} %bitcast.17), channel_id=1, source_target_pairs={{0,8},{4,12},{8,0},{12,4},{16,24},{20,28},{24,16},{28,20},{1,9},{5... | collective-permute-start | bytes 20 | tf_op jit(solution)/shard_map/ppermute | solution.py:33
  24.7 8.9 %collective-permute-start.12 = (bf16[2,2,320,128]{3,2,1,0:T(8,128)(2,1)}, bf16[2,2,320,128]{3,2,1,0:T(8,128)(2,1)}, u32[]{:S(2)}, u32[]{:S(2)}) collective-permute-start(bf16[2,2,320,128]{3,2,1,0:T(8,128)(2,1)} %bitcast.149), channel_id=1, source_target_pairs={{0,2},{1,3},{2,0},{3,1},{4,6},{5,7},{6,4},{7,5},{8,10},{9,11},{10,... | collective-permute-start | bytes 983048 | tf_op jit(solution)/shard_map/ppermute | solution.py:33
  26.7 4.6 %collective-permute-start.7 = (f32[1]{0:T(128)}, f32[1]{0:T(128)}, u32[]{:S(2)}, u32[]{:S(2)}) collective-permute-start(f32[1]{0:T(128)} %bitcast.19), channel_id=1, source_target_pairs={{0,16},{4,20},{8,24},{12,28},{16,0},{20,4},{24,8},{28,12},{1,17},{... | collective-permute-start | bytes 20 | tf_op jit(solution)/shard_map/ppermute | solution.py:33
  32.0 7.1 %collective-permute-start.2 = (bf16[2,2,320,128]{3,2,1,0:T(8,128)(2,1)S(1)}, bf16[2,2,320,128]{3,2,1,0:T(8,128)(2,1)S(1)}, u32[]{:S(2)}, u32[]{:S(2)}) collective-permute-start(bf16[2,2,320,128]{3,2,1,0:T(8,128)(2,1)S(1)} %bitcast.167), channel_id=1, source_target_pairs={{0,4},{4,0},{8,12},{12,8},{16,20},{20,16},{24,28},{28,24},{1,5},{5... | collective-permute-start | bytes 983048 | tf_op jit(solution)/shard_map/ppermute | solution.py:33
  34.9 4.6 %copy-start.1 = (s32[1280,512]{1,0:T(8,128)S(1)}, s32[1280,512]{1,0:T(8,128)}, u32[]{:S(2)}) copy-start(s32[1280,512]{1,0:T(8,128)} %param.5) | copy-start | bytes 7864324
  43.5 8.1 %collective-permute-start.13 = (bf16[4,64,256]{2,1,0:T(8,128)(2,1)S(1)}, bf16[4,64,256]{2,1,0:T(8,128)(2,1)S(1)}, u32[]{:S(2)}, u32[]{:S(2)}) collective-permute-start(bf16[4,64,256]{2,1,0:T(8,128)(2,1)S(1)} %fusion.40), channel_id=1, source_target_pairs={{0,4},{4,0},{8,12},{12,8},{16,20},{20,16},{24,28},{28,24},{1,5},{5... | collective-permute-start | bytes 393224 | tf_op jit(solution)/shard_map/ppermute | solution.py:33
  51.1 5.0 %collective-permute-start.8 = (bf16[1,256,256]{2,1,0:T(8,128)(2,1)S(1)}, bf16[1,256,256]{2,1,0:T(8,128)(2,1)S(1)}, u32[]{:S(2)}, u32[]{:S(2)}) collective-permute-start(bf16[1,256,256]{2,1,0:T(8,128)(2,1)S(1)} %fusion.39), channel_id=1, source_target_pairs={{0,2},{1,3},{2,0},{3,1},{4,6},{5,7},{6,4},{7,5},{8,10},{9,11},{10,... | collective-permute-start | bytes 393224 | tf_op jit(solution)/shard_map/ppermute | solution.py:33
  51.7 4.9 %collective-permute-start.14 = (bf16[2,64,256]{2,1,0:T(8,128)(2,1)S(1)}, bf16[2,64,256]{2,1,0:T(8,128)(2,1)S(1)}, u32[]{:S(2)}, u32[]{:S(2)}) collective-permute-start(bf16[2,64,256]{2,1,0:T(8,128)(2,1)S(1)} %fusion.42), channel_id=1, source_target_pairs={{0,8},{4,12},{8,0},{12,4},{16,24},{20,28},{24,16},{28,20},{1,9},{5... | collective-permute-start | bytes 196616 | tf_op jit(solution)/shard_map/ppermute | solution.py:33
  56.1 5.0 %collective-permute-start.9 = (bf16[256,256]{1,0:T(8,128)(2,1)S(1)}, bf16[256,256]{1,0:T(8,128)(2,1)S(1)}, u32[]{:S(2)}, u32[]{:S(2)}) collective-permute-start(bf16[256,256]{1,0:T(8,128)(2,1)S(1)} %bitcast_convert_fusion.1), channel_id=1, source_target_pairs={{0,8},{4,12},{8,0},{12,4},{16,24},{20,28},{24,16},{28,20},{1,9},{5... | collective-permute-start | bytes 393224 | tf_op jit(solution)/shard_map/ppermute | solution.py:33
  56.7 7.2 %collective-permute-start.15 = (bf16[1,64,256]{2,1,0:T(8,128)(2,1)S(1)}, bf16[1,64,256]{2,1,0:T(8,128)(2,1)S(1)}, u32[]{:S(2)}, u32[]{:S(2)}) collective-permute-start(bf16[1,64,256]{2,1,0:T(8,128)(2,1)S(1)} %dynamic-slice_convert_fusion.1), channel_id=1, source_target_pairs={{0,16},{4,20},{8,24},{12,28},{16,0},{20,4},{24,8},{28,12},{1,17},{... | collective-permute-start | bytes 98312 | tf_op jit(solution)/shard_map/ppermute | solution.py:33
  61.2 7.2 %collective-permute-start.10 = (bf16[256,256]{1,0:T(8,128)(2,1)S(1)}, bf16[256,256]{1,0:T(8,128)(2,1)S(1)}, u32[]{:S(2)}, u32[]{:S(2)}) collective-permute-start(bf16[256,256]{1,0:T(8,128)(2,1)S(1)} %fusion.38), channel_id=1, source_target_pairs={{0,16},{4,20},{8,24},{12,28},{16,0},{20,4},{24,8},{28,12},{1,17},{... | collective-permute-start | bytes 393224 | tf_op jit(solution)/shard_map/ppermute | solution.py:33
  63.9 5.2 %collective-permute-start.16 = (bf16[64,256]{1,0:T(8,128)(2,1)S(1)}, bf16[64,256]{1,0:T(8,128)(2,1)S(1)}, u32[]{:S(2)}, u32[]{:S(2)}) collective-permute-start(bf16[64,256]{1,0:T(8,128)(2,1)S(1)} %fusion.43), channel_id=1, source_target_pairs={{0,2},{1,3},{2,0},{3,1},{4,6},{5,7},{6,4},{7,5},{8,10},{9,11},{10,... | collective-permute-start | bytes 98312 | tf_op jit(solution)/shard_map/ppermute | solution.py:33
  68.5 5.0 %collective-permute-start.11 = (bf16[256,256]{1,0:T(8,128)(2,1)S(1)}, bf16[256,256]{1,0:T(8,128)(2,1)S(1)}, u32[]{:S(2)}, u32[]{:S(2)}) collective-permute-start(bf16[256,256]{1,0:T(8,128)(2,1)S(1)} %add_convert_fusion.1), channel_id=1, source_target_pairs={{0,4},{4,0},{8,12},{12,8},{16,20},{20,16},{24,28},{28,24},{1,5},{5... | collective-permute-start | bytes 393224 | tf_op jit(solution)/shard_map/ppermute | solution.py:33
  74.6 1.3 %collective-permute-start.17 = (f32[2,128,64]{1,2,0:T(8,128)S(1)}, f32[2,128,64]{1,2,0:T(8,128)S(1)}, u32[]{:S(2)}, u32[]{:S(2)}) collective-permute-start(f32[2,128,64]{1,2,0:T(8,128)S(1)} %bitcast.171), channel_id=1, source_target_pairs={{0,1},{1,0},{2,3},{3,2},{4,5},{5,4},{6,7},{7,6},{8,9},{9,8},{10,11... | collective-permute-start | bytes 196616 | tf_op jit(solution)/shard_map/ppermute | solution.py:33

commit v2 on v0

v2 whole, which is shorter than its diff:
```python
import functools
import math

import jax
import jax.numpy as jnp
from jax import lax
from jax.experimental import pallas as pl
from jax.experimental.pallas import tpu as pltpu
from jax.sharding import PartitionSpec as P

cycle_rates = (0.0361, 0.0596)
ROOT = math.sqrt(2.0)
SIN = (3.1415820121765137, -5.167142868041992, 2.5418989658355713, -0.5546361207962036)
COS = (0.9999999403953552, -4.934792995452881, 4.058412075042725, -1.3318800926208496, 0.2196967601776123)


def horner(z, terms):
    total = ROOT * terms[-1]
    for term in terms[-2::-1]:
        total = total * z + ROOT * term
    return total


def steer_rows(rate, delays):
    turns = rate * delays.astype(jnp.float32)
    turns = turns - jnp.round(turns)
    z = turns * turns
    half_sin = turns * horner(z, SIN)
    half_cos = horner(z, COS)
    return (1.0 - half_sin * half_sin).astype(jnp.bfloat16), (half_sin * half_cos).astype(jnp.bfloat16)


CHUNK = 32
LANES = 128


def place():
    row, col = lax.axis_index("row"), lax.axis_index("col")
    return row, col, col & 1, (col >> 1) & 1, row & 1


def y_of():
    return place()[4]


def block_of(j, at):
    _, col, core, x, _ = place()
    return (col >> 2) * 4 + (x ^ j) * 2 + (core ^ at)


def vmem(shape, dtype):
    return pltpu.VMEM(shape, dtype)


def kernel_call(body, out, inputs, spaces, scratch=(), limit=8, cost=1):
    held = [
        pltpu.with_memory_space_constraint(v, space) if space in (pltpu.HBM, pltpu.VMEM) else v
        for v, space in zip(inputs, spaces)
    ]
    return pl.pallas_call(
        body,
        out_shape=out,
        in_specs=[pl.BlockSpec(memory_space=space) for space in spaces],
        out_specs=[pl.BlockSpec(memory_space=pltpu.VMEM)] * len(out),
        scratch_shapes=list(scratch),
        compiler_params=pltpu.CompilerParams(vmem_limit_bytes=limit * 2**20),
        cost_estimate=pl.CostEstimate(flops=1, bytes_accessed=cost, transcendentals=0),
    )(*held)


def power_kernel(wl_ref, spec_ref, note_ref, held_ref, wl_held, sems):
    row, col, *_ = place()
    n_col = lax.axis_size("col")
    freqs, _, per, windows = spec_ref.shape
    wl_copy = pltpu.make_async_copy(wl_ref, wl_held, sems.at[freqs])
    copies = [pltpu.make_async_copy(spec_ref.at[f], held_ref.at[f], sems.at[f]) for f in range(freqs)]
    wl_copy.start()
    for copy in copies:
        copy.start()
    note_ref[...] = jnp.zeros_like(note_ref)
    ids = (row * n_col + col) * per + lax.broadcasted_iota(jnp.int32, (1, per), 1)
    rest = jnp.zeros((note_ref.shape[2] - per, LANES), jnp.float32)
    wl_copy.wait()
    for f, copy in enumerate(copies):
        copy.wait()
        squares = jnp.square(held_ref[f].astype(jnp.float32))
        squares = squares[0] + squares[1]
        squares = sum(squares[:, at : at + LANES] for at in range(0, windows, LANES))
        columns = jnp.transpose(jnp.concatenate([squares, rest], axis=0))
        power = jnp.sum(columns, axis=0, keepdims=True)[:, :per]
        level = jnp.sum(jnp.where(ids == wl_held[f], power, 0.0), axis=1, keepdims=True)
        note_ref[f, 0:1, :per] = power
        note_ref[f, 1:2, :] = jnp.broadcast_to(level, (1, note_ref.shape[2]))


def gate_kernel(n, *refs):
    out_ref, start = refs[-1], 0
    for ref in refs[:n]:
        out_ref[start : start + ref.shape[0], :] = ref[...]
        start += ref.shape[0]


def gated(values, others):
    rows, width = sum(v.shape[0] for v in values), values[0].shape[1]
    return kernel_call(
        functools.partial(gate_kernel, len(values)),
        [vmem((rows, width), values[0].dtype)],
        [*values, *others],
        [pltpu.VMEM] * (len(values) + len(others)),
    )[0]


def steer_blocks(blocks, delays_ref, cos_ref, sin_ref):
    core = place()[2]
    rate = jnp.where(core == 0, cycle_rates[0], cycle_rates[1]).astype(jnp.float32)
    size = cos_ref.shape[0] // len(blocks)
    chunk = math.gcd(CHUNK, size)
    for index, (start, copy) in enumerate(blocks):
        if copy is not None:
            copy.wait()

        @pl.loop(0, size // chunk)
        def _(i):
            here = pl.ds(pl.multiple_of(start + i * chunk, chunk), chunk)
            there = pl.ds(pl.multiple_of(index * size + i * chunk, chunk), chunk)
            cos, sin = steer_rows(rate, delays_ref[here, :])
            cos_ref[there, :] = cos
            sin_ref[there, :] = sin


def steer_kernel(starts, token_ref, delays_ref, cos_ref, sin_ref):
    steer_blocks([(start, None) for start in starts(delays_ref.shape[0])], delays_ref, cos_ref, sin_ref)


def steer_far_kernel(parts, token_ref, delays_ref, cos_ref, sin_ref, held_ref, sems):
    row, *_, y = place()
    per = cos_ref.shape[0] // 2
    rows = per // parts
    blocks = []
    for index in range(2 * parts):
        j, part = divmod(index, parts)
        start = pl.multiple_of((row ^ j) * per + part * rows, 8)
        here = pl.ds(index * rows, rows)
        copy = pltpu.make_async_copy(delays_ref.at[pl.ds(start, rows), :], held_ref.at[here, :], sems.at[index])
        copy.start()
        blocks.append((index * rows, copy))
    steer_blocks(blocks, held_ref, cos_ref, sin_ref)


def steering(starts, rows, token, delays):
    out = [vmem((rows, delays.shape[1]), jnp.bfloat16)] * 2
    return kernel_call(functools.partial(steer_kernel, starts), out, [token, delays], [pltpu.VMEM] * 2)


def steering_far(rows, token, delays):
    width = delays.shape[1]
    parts = math.gcd(rows // (2 * CHUNK), 5)
    return kernel_call(
        functools.partial(steer_far_kernel, parts),
        [vmem((rows, width), jnp.bfloat16)] * 2,
        [token, delays],
        [pltpu.VMEM, pltpu.HBM],
        scratch=[pltpu.VMEM((rows, width), delays.dtype), pltpu.SemaphoreType.DMA((2 * parts,))],
    )


def beams_kernel(axis, order, near_power_ref, far_ref, level_ref, near_ref, from_ref, *refs):
    *steer, out_ref = refs
    per, half = from_ref.shape[2:]
    _, _, _, x, y = place()
    mine = pl.ds(pl.multiple_of((x if axis == "x" else y) * half, half), half)
    level = 0.5 * level_ref[...]
    real, imag = [], []
    for at in range(4):
        power = near_power_ref[at : at + 1] if at < 2 else far_ref[at - 2 : at - 1]
        gain = jnp.transpose(jnp.broadcast_to(lax.rsqrt(power + level), (8, level.shape[1])))[:per, :1]
        for part, parts in enumerate((real, imag)):
            spec = near_ref[at, part, :, mine] if at < 2 else from_ref[at - 2, part]
            parts.append(spec.astype(jnp.float32) * gain)
    total = None
    count = len(steer) // 2
    for group in range(count):
        members = order[group * 4 // count : (group + 1) * 4 // count]
        re, im = (jnp.concatenate([p[m] for m in members], axis=0).astype(jnp.bfloat16) for p in (real, imag))
        for left, right in (((re, im), steer[2 * group]), ((-im, re), steer[2 * group + 1])):
            term = lax.dot_general(
                right[...],
                jnp.concatenate(left, axis=1),
                (((0,), (0,)), ((), ())),
                preferred_element_type=jnp.float32,
            )
            total = term if total is None else total + term
    out_ref[...] = total


def beams(axis, order, near_power, far, level, near, arrived, steer):
    inputs = [near_power, far, level, near, arrived, *steer]
    out = [vmem((steer[0].shape[1], 2 * arrived.shape[-1]), jnp.float32)]
    return kernel_call(functools.partial(beams_kernel, axis, order), out, inputs, [pltpu.VMEM] * len(inputs), limit=24)[0]


def swap(value, axis, bit):
    size = lax.axis_size(axis)
    return lax.ppermute(value, axis, [(i, i ^ bit) for i in range(size)])


def choose(bit, first, second):
    return jnp.where(bit == 0, first, second)


def ordered(bit, own, other):
    return choose(bit, own, other), choose(bit, other, own)


def bits(size, start):
    found = []
    while start < size:
        found.append(start)
        start *= 2
    return found


tie = lax.optimization_barrier


def halve(value, dim, axis, bit, at):
    first, second = lax.index_in_dim(value, 0, dim, False), lax.index_in_dim(value, 1, dim, False)
    return choose(at, first, second), swap(choose(at, second, first).astype(jnp.bfloat16), axis, bit)


def total(parts):
    own, other = parts
    return own + other.astype(jnp.float32)


def body(spectra, delays_s, delays_r, wl_index):
    n_row, n_col = lax.axis_size("row"), lax.axis_size("col")
    row, col, core, x, y = place()
    per, windows = spectra.shape[2:]
    half = windows // 2
    core, x, y = col & 1, (col >> 1) & 1, row & 1
    beams_r = delays_r.shape[1]

    partner = swap(spectra, "col", 1)
    freqs, padded = spectra.shape[0], -(-per // LANES) * LANES
    (note,) = kernel_call(
        power_kernel,
        [vmem((freqs, 2, padded), jnp.float32)],
        [wl_index, spectra],
        [pltpu.HBM, pltpu.HBM],
        scratch=[
            pltpu.VMEM(spectra.shape, spectra.dtype),
            pltpu.SMEM(wl_index.shape, wl_index.dtype),
            pltpu.SemaphoreType.DMA((freqs + 1,)),
        ],
        cost=2 * spectra.size * 2,
    )
    other = swap(note, "col", 1)
    note, other = choose(core, note[0], note[1]), choose(core, other[0], other[1])
    power = jnp.concatenate([note[:1], other[:1]])
    level = note[1:] + other[1:]

    spec = jnp.stack([choose(core, spectra[0], spectra[1]), choose(core, partner[0], partner[1])])
    low, high = spec[..., :half], spec[..., half:]
    from_x, from_y = swap(choose(x, high, low), "col", 2), swap(choose(y, high, low), "row", 1)

    near_r = lax.dynamic_slice_in_dim(delays_r, (row >> 1) * (2 * per), 2 * per, 0)
    other_r = swap(near_r.astype(jnp.int16), "col", 1)
    row_bits, col_bits = bits(n_row, 2), bits(n_col, 4)
    for bit in row_bits[:1]:
        level = level + swap(level, "row", bit)
    steer_r = steering_far(2 * per, level, delays_r)
    steer_r += steering(lambda rows: [(y_of() ^ j) * (rows // 2) for j in (0, 1)], 2 * per, level, other_r)
    for bit in row_bits[1:]:
        level = level + swap(level, "row", bit)
    for bit in col_bits:
        level = level + swap(level, "col", bit)
    steer_s = steering(lambda rows: [block_of(0, at) * per for at in (0, 1)], 2 * per, level, delays_s)
    far_x = swap(gated([power, level], [from_x, from_y]), "col", 2)
    level = level + far_x[2:]
    steer_s += steering(lambda rows: [block_of(1, at) * per for at in (0, 1)], 2 * per, level, delays_s)
    far_y = swap(jnp.concatenate([power, level]), "row", 1)
    level = level + far_y[2:]

    receiver = beams("y", (0, 2, 1, 3), power, far_y, level, spec, from_y, steer_r)
    source = beams("x", (0, 1, 2, 3), power, far_x, level, spec, from_x, steer_s)

    row_bits, col_bits = bits(n_row, 1), bits(n_col, 2)
    receiver = receiver.reshape((2,) * len(col_bits) + (-1, 2 * half))
    source = source.reshape((2,) * len(row_bits) + (-1, 2 * half))

    def scatter(axis, bit, dim):
        index = row if axis == "row" else col
        return (lambda v: halve(v, dim, axis, bit, (index // bit) & 1)), total

    def add(axis, bit):
        return (lambda v: (v, swap(v.astype(jnp.bfloat16), axis, bit))), total

    def gather(axis, bit, index):
        def send(v):
            v = v.astype(jnp.bfloat16)
            return v, swap(v, axis, bit)

        return send, lambda parts: jnp.stack(ordered(index, *parts), axis=-3)

    receiver_steps = [scatter("col", bit, 0) for bit in col_bits[::-1]]
    receiver_steps += [add("row", bit) for bit in row_bits[1:]] + [gather("row", 1, y)]
    source_steps = [scatter("row", 2, len(row_bits) - 2), scatter("row", 1, -3), gather("col", 2, x)]
    source_steps += [scatter("row", bit, 0) for bit in row_bits[:1:-1]]
    source_steps += [add("col", bit) for bit in col_bits[1:]]
    for index in range(max(len(receiver_steps), len(source_steps))):
        sent = []
        if index < len(receiver_steps):
            sent.append(receiver_steps[index][0](receiver))
        if index < len(source_steps):
            sent.append(source_steps[index][0](source))
        sent = tie(sent)
        if index < len(receiver_steps):
            receiver = receiver_steps[index][1](sent[0])
        if index < len(source_steps):
            source = source_steps[index][1](sent[-1])
    receiver, source = receiver.astype(jnp.bfloat16), source.astype(jnp.bfloat16)

    def flat(parts):
        return jnp.concatenate(parts, axis=1)

    left, real = flat(receiver), flat(source)
    imag = flat([v for s in source for v in (s[:, half:], -s[:, :half])])
    field = jnp.stack(
        [jnp.dot(left, right.T, preferred_element_type=jnp.float32) for right in (real, imag)]
    )
    field = field * (math.sqrt(windows) / (per * n_row * n_col))
    field = field.reshape(2, 2, -1, field.shape[-1])
    first, second = field[:, 0], field[:, 1]
    return jnp.stack(ordered(core, choose(core, first, second), swap(choose(core, second, first), "col", 1)))


def solution(mesh):
    in_specs = (P(None, None, ("row", "col"), None), P("row", None), P("col", None), P())
    out_specs = P(None, None, "col", "row")
    return jax.shard_map(body, mesh=mesh, in_specs=in_specs, out_specs=out_specs, check_vma=False)
```

time: 571 us -> 63.5 us (0.11); the launches traced: 564 us -> 63.3 us
  matrix products: 293 us -> 0.41 us
  waiting for transfers between devices: 159 us -> 20.7 us
  blocking collectives: 42.2 us -> 0 us
  other arithmetic: 42.6 us -> 5.98 us
  starting transfers between devices: 0.12 us -> 23.7 us
  between operations: 14.3 us -> 0.38 us
  local copies, waits for them, and re-layouts: 12.4 us -> 0.55 us
  Pallas kernels: 0 us -> 11.5 us
    dot_general x10 -> x2, matrix products: 293 us -> 0.41 us  [body(): jnp.dot(left, right.T, preferred_element_type=jnp.float32)]
    unnamed x5 -> x0, waiting for transfers between devices: 79 us -> none
    reduce_scatter x1 -> x0, waiting for transfers between devices: 42.9 us -> none  [body(): lax.psum_scatter(whole_block, 'col', scatter_dimension=2, tiled=True)]
    psum x1 -> x0, blocking collectives: 42.2 us -> none  [body(): level = 0.5 * lax.psum(picked, ('row', 'col'))]
    all_gather x2 -> x0, waiting for transfers between devices: 36.8 us -> none  [the longest x1 36.8 us: body(): piece = lax.all_gather(spectra, 'row', axis=2, tiled=True)]
    convert_element_type x3 -> x9, other arithmetic: 26.5 us -> 2.59 us  [the longest x1 2.4 us: body(): other_r = swap(near_r.astype(jnp.int16), 'col', 1)]
    ppermute x0 -> x18, starting transfers between devices: none -> 23.7 us  [swap(): return lax.ppermute(value, axis, [(i, i ^ bit) for i in range(size)])]
    ppermute x0 -> x18, waiting for transfers between devices: none -> 20.7 us  [swap(): return lax.ppermute(value, axis, [(i, i ^ bit) for i in range(size)])]
  transfers between devices with their start and end apart: 4 -> 18, of which waited for: 3 -> 10; matrix products, arithmetic and copies ran while one was open for 7% -> 8% of each run, Pallas kernels for 0% -> 16%
where the time goes in v2:
time: 63.5 us; the launch traced here: 63.3 us
  starting transfers between devices  23.7 us (37%)
  waiting for transfers between devices  20.7 us (33%)
  Pallas kernels  11.5 us (18%)
  other arithmetic  5.98 us (9%)
    ppermute x18, starting transfers between devices, swap(): return lax.ppermute(value, axis, [(i, i ^ bit) for i in range(size)])  23.7 us
    ppermute x18, waiting for transfers between devices, swap(): return lax.ppermute(value, axis, [(i, i ^ bit) for i in range(size)])  20.7 us
    pallas_call x8, Pallas kernels, kernel_call(): pl.pallas_call(body, out_shape=out, in_specs=[pl.BlockSpec(memory_space=s...  11.5 us
    select_n x10, other arithmetic, choose(): return jnp.where(bit == 0, first, second)  2.48 us
    convert_element_type x1, other arithmetic, body(): other_r = swap(near_r.astype(jnp.int16), 'col', 1)  2.4 us
  transfers between devices with their start and end apart: 18, of which 10 were waited for; matrix products, arithmetic and copies ran while one was open for 8% of the time, Pallas kernels for 16%

profile of v2, /device:TPU:0, one launch (start us, length us, event | category | flops | bytes accessed | tf_op | source)
XLA Modules:
  0.0 63.3 jit_solution(15087230535398390129)
XLA Ops:
  0.0 0.5 collective-permute-start.3
  0.5 1.5 %shard_map.46 = f32[2,2,384]{2,1,0:T(2,128)S(1)} custom-call(s32[2]{0:T(128)} %wl_ref.1, bf16[2,2,320,256]{3,2,1,0:T(8,128)(2,1)} %spec_ref.1), custom_call_target="tpu_custom_call" | custom-call | flops 1 | bytes 1310720 | tf_op jit(solution)/shard_map/pallas_call | solution.py:60
  1.9 0.1 collective-permute-start
  2.1 0.0 copy-start
  2.1 2.4 %dynamic-slice_convert_fusion = s16[640,512]{1,0:T(8,128)(2,1)} fusion(s32[2560,512]{1,0:T(8,128)} %delays_ref.3, s32[]{:T(128)S(6)} %select_n.184), kind=kLoop, calls=%fused_computation | loop fusion | flops 327680 | bytes 1966084 | tf_op jit(solution)/shard_map/convert_element_type | solution.py:268
  4.5 0.5 collective-permute-start.8
  4.9 1.1 %slice_select_fusion.1 = bf16[1,2,320,256]{3,2,1,0:T(8,128)(2,1)S(1)} fusion(bf16[2,2,320,256]{3,2,1,0:T(8,128)(2,1)} %spec_ref.1, pred[]{:T(512)S(6)} %eq.12), kind=kLoop, calls=%fused_computation.11 | loop fusion | flops 163840 | bytes 983041 | tf_op jit(solution)/shard_map/jit(_where)/select_n | solution.py:208
  6.0 0.0 copy-start.1
  6.1 0.0 collective-permute-done
  6.1 0.0 collective-permute-done.3
  6.1 1.2 %slice_select_fusion = bf16[1,2,320,256]{3,2,1,0:T(8,128)(2,1)S(1)} fusion(bf16[2,2,320,256]{3,2,1,0:T(8,128)(2,1)} %collective-permute-done.3, pred[]{:T(512)S(6)} %eq.12), kind=kLoop, calls=%fused_computation.10 | loop fusion | flops 163840 | bytes 983041 | tf_op jit(solution)/shard_map/jit(_where)/select_n | solution.py:208
  7.3 0.0 copy-start.3
  7.3 0.1 broadcast_select_fusion
  7.4 0.0 copy-done.1
  7.4 2.6 %collective-permute-start.4 = (bf16[2,2,320,128]{3,2,1,0:T(8,128)(2,1)S(1)}, bf16[2,2,320,128]{3,2,1,0:T(8,128)(2,1)S(1)}, u32[]{:S(2)}, u32[]{:S(2)}) collective-permute-start(bf16[2,2,320,128]{3,2,1,0:T(8,128)(2,1)S(1)} %get-tuple-element.58), channel_id=1, source_target_pairs={{0,2},{1,3},{2,0},{3,1},{4,6},{5,7},{6,4},{7,5},{8,10},{9,11},{10,... | collective-permute-start | bytes 983048 | tf_op jit(solution)/shard_map/ppermute | solution.py:204
  10.0 1.5 %collective-permute-start.5 = (bf16[2,2,320,128]{3,2,1,0:T(8,128)(2,1)S(1)}, bf16[2,2,320,128]{3,2,1,0:T(8,128)(2,1)S(1)}, u32[]{:S(2)}, u32[]{:S(2)}) collective-permute-start(bf16[2,2,320,128]{3,2,1,0:T(8,128)(2,1)S(1)} %get-tuple-element.57), channel_id=1, source_target_pairs={{0,4},{4,0},{8,12},{12,8},{16,20},{20,16},{24,28},{28,24},{1,5},{5... | collective-permute-start | bytes 983048 | tf_op jit(solution)/shard_map/ppermute | solution.py:204
  11.5 1.6 %collective-permute-start.1 = (f32[1,384]{1,0:T(1,128)S(1)}, f32[1,384]{1,0:T(1,128)S(1)}, u32[]{:S(2)}, u32[]{:S(2)}) collective-permute-start(f32[1,384]{1,0:T(1,128)S(1)} %get-tuple-element.75), channel_id=1, source_target_pairs={{0,8},{4,12},{8,0},{12,4},{16,24},{20,28},{24,16},{28,20},{1,9},{5... | collective-permute-start | bytes 4616 | tf_op jit(solution)/shard_map/ppermute | solution.py:204
  13.1 2.0 %collective-permute-done.1 = f32[1,384]{1,0:T(1,128)S(1)} collective-permute-done((f32[1,384]{1,0:T(1,128)S(1)}, f32[1,384]{1,0:T(1,128)S(1)}, u32[]{:S(2)}, u32[]{:S(2)}) %collective-permute-start.1) | collective-permute-done | bytes 1568 | tf_op jit(solution)/shard_map/ppermute | solution.py:204
  15.1 2.6 %collective-permute-start.2 = (f32[1,384]{1,0:T(1,128)S(1)}, f32[1,384]{1,0:T(1,128)S(1)}, u32[]{:S(2)}, u32[]{:S(2)}) collective-permute-start(f32[1,384]{1,0:T(1,128)S(1)} %add.45.token_ref), channel_id=1, source_target_pairs={{0,16},{4,20},{8,24},{12,28},{16,0},{20,4},{24,8},{28,12},{1,17},{... | collective-permute-start | bytes 4616 | tf_op jit(solution)/shard_map/ppermute | solution.py:204
  17.7 1.9 %collective-permute-done.2 = f32[1,384]{1,0:T(1,128)S(1)} collective-permute-done((f32[1,384]{1,0:T(1,128)S(1)}, f32[1,384]{1,0:T(1,128)S(1)}, u32[]{:S(2)}, u32[]{:S(2)}) %collective-permute-start.2) | collective-permute-done | bytes 1568 | tf_op jit(solution)/shard_map/ppermute | solution.py:204
  19.5 0.0 collective-permute-done.4.refs_2_.from_ref
  19.6 0.2 collective-permute-done.5.refs_3_.from_ref
  19.8 0.0 copy-done.3
  19.8 0.4 collective-permute-start.6
  20.2 0.0 copy-start.2
  20.2 0.0 copy-start.4
  20.2 2.2 %shard_map.48 = (bf16[640,512]{1,0:T(8,128)(2,1)S(1)}, bf16[640,512]{1,0:T(8,128)(2,1)S(1)}) custom-call(f32[1,384]{1,0:T(1,128)S(1)} %add.45.token_ref, s32[2560,512]{1,0:T(8,128)} %delays_ref.3), custom_call_target="tpu_custom_call" | custom-call | flops 1 | bytes 1 | tf_op jit(solution)/shard_map/pallas_call | solution.py:60
  22.4 0.0 copy-done
  22.4 1.2 %shard_map.51 = (bf16[640,512]{1,0:T(8,128)(2,1)S(1)}, bf16[640,512]{1,0:T(8,128)(2,1)S(1)}) custom-call(f32[1,384]{1,0:T(1,128)S(1)} %add.46.refs_1_.token_ref, s32[1280,512]{1,0:T(8,128)S(1)} %copy-done), custom_call_target="tpu_custom_call" | custom-call | flops 1 | bytes 1 | tf_op jit(solution)/shard_map/pallas_call | solution.py:60
  23.6 0.0 collective-permute-done.6.far_ref
  23.7 1.7 %collective-permute-start.7 = (f32[3,384]{1,0:T(4,128)S(1)}, f32[3,384]{1,0:T(4,128)S(1)}, u32[]{:S(2)}, u32[]{:S(2)}) collective-permute-start(f32[3,384]{1,0:T(4,128)S(1)} %pad_maximum_fusion.3), channel_id=1, source_target_pairs={{0,4},{4,0},{8,12},{12,8},{16,20},{20,16},{24,28},{28,24},{1,5},{5... | collective-permute-start | bytes 13832 | tf_op jit(solution)/shard_map/ppermute | solution.py:204
  25.4 0.0 copy-done.2
  25.4 0.0 copy-done.4
  25.4 0.1 pad_maximum_fusion.near_ref
  25.5 0.0 collective-permute-done.8.delays_ref
  25.5 2.3 %shard_map.49 = (bf16[640,512]{1,0:T(8,128)(2,1)S(1)}, bf16[640,512]{1,0:T(8,128)(2,1)S(1)}) custom-call(f32[1,384]{1,0:T(1,128)S(1)} %add.45.token_ref, s16[640,512]{1,0:T(8,128)(2,1)} %collective-permute-done.8.delays_ref), custom_call_target="tpu_custom_call" | custom-call | flops 1 | bytes 1 | tf_op jit(solution)/shard_map/pallas_call | solution.py:60
  27.8 1.2 %shard_map.52 = (bf16[640,512]{1,0:T(8,128)(2,1)S(1)}, bf16[640,512]{1,0:T(8,128)(2,1)S(1)}) custom-call(f32[1,384]{1,0:T(1,128)S(1)} %slice_add_fusion.1.token_ref, s32[1280,512]{1,0:T(8,128)S(1)} %copy-done), custom_call_target="tpu_custom_call" | custom-call | flops 1 | bytes 1 | tf_op jit(solution)/shard_map/pallas_call | solution.py:60
  29.0 0.0 collective-permute-done.7.far_ref
  29.0 1.5 %shard_map.53 = f32[512,256]{1,0:T(8,128)S(1)} custom-call(f32[2,384]{1,0:T(2,128)S(1)} %pad_maximum_fusion.4.refs_0_.near_power_ref, f32[3,384]{1,0:T(4,128)S(1)} %collective-permute-done.6.far_ref, f32[1,384]{1,0:T(1,128)S(1)} %slice_add_fusion.level_ref, bf16[2,2,320,256]{3,2,1,0:T(8,128)(2,1)S(1)} %pad_maximum_fusion.near_ref, ...), custom_call_target="tpu_custom_call" | custom-call | flops 1 | bytes 1 | tf_op jit(solution)/shard_map/pallas_call | solution.py:60
  30.7 1.6 %collective-permute-start.10 = (bf16[2,2,64,256]{3,2,0,1:T(8,128)(2,1)S(1)}, bf16[2,2,64,256]{3,2,0,1:T(8,128)(2,1)S(1)}, u32[]{:S(2)}, u32[]{:S(2)}) collective-permute-start(bf16[2,2,64,256]{3,2,0,1:T(8,128)(2,1)S(1)} %fusion.2), channel_id=1, source_target_pairs={{0,8},{4,12},{8,0},{12,4},{16,24},{20,28},{24,16},{28,20},{1,9},{5... | collective-permute-start | bytes 393224 | tf_op jit(solution)/shard_map/ppermute | solution.py:204
  32.3 1.6 %shard_map.50 = f32[512,256]{1,0:T(8,128)S(1)} custom-call(f32[2,384]{1,0:T(2,128)S(1)} %pad_maximum_fusion.4.refs_0_.near_power_ref, f32[3,384]{1,0:T(4,128)S(1)} %collective-permute-done.7.far_ref, f32[1,384]{1,0:T(1,128)S(1)} %slice_add_fusion.level_ref, bf16[2,2,320,256]{3,2,1,0:T(8,128)(2,1)S(1)} %pad_maximum_fusion.near_ref, ...), custom_call_target="tpu_custom_call" | custom-call | flops 1 | bytes 1 | tf_op jit(solution)/shard_map/pallas_call | solution.py:60
  33.9 1.6 %collective-permute-start.9 = (bf16[256,256]{1,0:T(8,128)(2,1)S(1)}, bf16[256,256]{1,0:T(8,128)(2,1)S(1)}, u32[]{:S(2)}, u32[]{:S(2)}) collective-permute-start(bf16[256,256]{1,0:T(8,128)(2,1)S(1)} %select_convert_fusion.1), channel_id=1, source_target_pairs={{0,2},{1,3},{2,0},{3,1},{4,6},{5,7},{6,4},{7,5},{8,10},{9,11},{10,... | collective-permute-start | bytes 393224 | tf_op jit(solution)/shard_map/ppermute | solution.py:204
  35.5 0.2 collective-permute-done.10
  35.7 3.3 %collective-permute-done.9 = bf16[256,256]{1,0:T(8,128)(2,1)S(1)} collective-permute-done((bf16[256,256]{1,0:T(8,128)(2,1)S(1)}, bf16[256,256]{1,0:T(8,128)(2,1)S(1)}, u32[]{:S(2)}, u32[]{:S(2)}) %collective-permute-start.9) | collective-permute-done | bytes 131104 | tf_op jit(solution)/shard_map/ppermute | solution.py:204
  39.0 0.6 collective-permute-start.12
  39.6 0.4 collective-permute-start.11
  40.0 3.3 %collective-permute-done.12 = bf16[2,64,256]{2,1,0:T(8,128)(2,1)S(1)} collective-permute-done((bf16[2,64,256]{2,1,0:T(8,128)(2,1)S(1)}, bf16[2,64,256]{2,1,0:T(8,128)(2,1)S(1)}, u32[]{:S(2)}, u32[]{:S(2)}) %collective-permute-start.12) | collective-permute-done | bytes 65568 | tf_op jit(solution)/shard_map/ppermute | solution.py:204
  43.3 1.6 %collective-permute-done.11 = bf16[256,256]{1,0:T(8,128)(2,1)S(1)} collective-permute-done((bf16[256,256]{1,0:T(8,128)(2,1)S(1)}, bf16[256,256]{1,0:T(8,128)(2,1)S(1)}, u32[]{:S(2)}, u32[]{:S(2)}) %collective-permute-start.11) | collective-permute-done | bytes 131104 | tf_op jit(solution)/shard_map/ppermute | solution.py:204
  45.0 3.0 %collective-permute-start.13 = (bf16[256,256]{1,0:T(8,128)(2,1)S(1)}, bf16[256,256]{1,0:T(8,128)(2,1)S(1)}, u32[]{:S(2)}, u32[]{:S(2)}) collective-permute-start(bf16[256,256]{1,0:T(8,128)(2,1)S(1)} %get-tuple-element.53), channel_id=1, source_target_pairs={{0,16},{4,20},{8,24},{12,28},{16,0},{20,4},{24,8},{28,12},{1,17},{... | collective-permute-start | bytes 393224 | tf_op jit(solution)/shard_map/ppermute | solution.py:204
  48.0 1.4 %collective-permute-start.14 = (bf16[2,64,256]{2,1,0:T(8,128)(2,1)S(1)}, bf16[2,64,256]{2,1,0:T(8,128)(2,1)S(1)}, u32[]{:S(2)}, u32[]{:S(2)}) collective-permute-start(bf16[2,64,256]{2,1,0:T(8,128)(2,1)S(1)} %add_convert_fusion.2), channel_id=1, source_target_pairs={{0,2},{1,3},{2,0},{3,1},{4,6},{5,7},{6,4},{7,5},{8,10},{9,11},{10,... | collective-permute-start | bytes 196616 | tf_op jit(solution)/shard_map/ppermute | solution.py:204
  49.4 2.9 %collective-permute-done.14 = bf16[2,64,256]{2,1,0:T(8,128)(2,1)S(1)} collective-permute-done((bf16[2,64,256]{2,1,0:T(8,128)(2,1)S(1)}, bf16[2,64,256]{2,1,0:T(8,128)(2,1)S(1)}, u32[]{:S(2)}, u32[]{:S(2)}) %collective-permute-start.14) | collective-permute-done | bytes 65568 | tf_op jit(solution)/shard_map/ppermute | solution.py:204
  52.4 0.0 collective-permute-done.13
  52.4 2.5 %collective-permute-start.15 = (bf16[256,256]{1,0:T(8,128)(2,1)S(1)}, bf16[256,256]{1,0:T(8,128)(2,1)S(1)}, u32[]{:S(2)}, u32[]{:S(2)}) collective-permute-start(bf16[256,256]{1,0:T(8,128)(2,1)S(1)} %add_convert_fusion), channel_id=1, source_target_pairs={{0,4},{4,0},{8,12},{12,8},{16,20},{20,16},{24,28},{28,24},{1,5},{5... | collective-permute-start | bytes 393224 | tf_op jit(solution)/shard_map/ppermute | solution.py:204
  55.0 1.1 %collective-permute-start.16 = (bf16[2,64,256]{2,1,0:T(8,128)(2,1)S(1)}, bf16[2,64,256]{2,1,0:T(8,128)(2,1)S(1)}, u32[]{:S(2)}, u32[]{:S(2)}) collective-permute-start(bf16[2,64,256]{2,1,0:T(8,128)(2,1)S(1)} %get-tuple-element.65), channel_id=1, source_target_pairs={{0,16},{4,20},{8,24},{12,28},{16,0},{20,4},{24,8},{28,12},{1,17},{... | collective-permute-start | bytes 196616 | tf_op jit(solution)/shard_map/ppermute | solution.py:204
  56.1 4.1 %collective-permute-done.16 = bf16[2,64,256]{2,1,0:T(8,128)(2,1)S(1)} collective-permute-done((bf16[2,64,256]{2,1,0:T(8,128)(2,1)S(1)}, bf16[2,64,256]{2,1,0:T(8,128)(2,1)S(1)}, u32[]{:S(2)}, u32[]{:S(2)}) %collective-permute-start.16) | collective-permute-done | bytes 65568 | tf_op jit(solution)/shard_map/ppermute | solution.py:204
  60.2 0.0 collective-permute-done.15
  60.3 0.2 convolution_bitcast_fusion.1
  60.6 0.3 copy.16
  60.8 0.2 reshape.58
  61.0 0.2 convolution_bitcast_fusion
  61.3 0.1 collective-permute-start.17
  61.4 1.2 %collective-permute-done.17 = f32[2,128,64]{1,2,0:T(8,128)S(1)} collective-permute-done((f32[2,128,64]{1,2,0:T(8,128)S(1)}, f32[2,128,64]{1,2,0:T(8,128)S(1)}, u32[]{:S(2)}, u32[]{:S(2)}) %collective-permute-start.17) | collective-permute-done | bytes 65568 | tf_op jit(solution)/shard_map/ppermute | solution.py:204
  62.6 0.7 %pad_maximum_fusion.1 = f32[2,2,128,64]{2,3,1,0:T(8,128)} fusion(f32[1,2,128,64]{2,3,1,0:T(8,128)S(1)} %get-tuple-element.64, f32[1,2,128,64]{2,3,1,0:T(8,128)S(1)} %get-tuple-element.63), kind=kLoop, calls=%fused_computation.27 | loop fusion | flops 32768 | bytes 262144 | tf_op jit(solution)/shard_map/stack | solution.py:335
  (34 shorter events, 0.6 us)
Async XLA Ops:
  0.0 6.1 %collective-permute-start.3 = (bf16[2,2,320,256]{3,2,1,0:T(8,128)(2,1)}, bf16[2,2,320,256]{3,2,1,0:T(8,128)(2,1)}, u32[]{:S(2)}, u32[]{:S(2)}) collective-permute-start(bf16[2,2,320,256]{3,2,1,0:T(8,128)(2,1)} %spec_ref.1), channel_id=1, source_target_pairs={{0,1},{1,0},{2,3},{3,2},{4,5},{5,4},{6,7},{7,6},{8,9},{9,8},{10,11... | collective-permute-start | bytes 1966088 | tf_op jit(solution)/shard_map/ppermute | solution.py:204
  1.9 4.1 %collective-permute-start = (f32[2,2,384]{2,1,0:T(2,128)S(1)}, f32[2,2,384]{2,1,0:T(2,128)S(1)}, u32[]{:S(2)}, u32[]{:S(2)}) collective-permute-start(f32[2,2,384]{2,1,0:T(2,128)S(1)} %shard_map.46), channel_id=1, source_target_pairs={{0,1},{1,0},{2,3},{3,2},{4,5},{5,4},{6,7},{7,6},{8,9},{9,8},{10,11... | collective-permute-start | bytes 18440 | tf_op jit(solution)/shard_map/ppermute | solution.py:204
  2.1 20.4 %copy-start = (s32[1280,512]{1,0:T(8,128)S(1)}, s32[1280,512]{1,0:T(8,128)}, u32[]{:S(2)}) copy-start(s32[1280,512]{1,0:T(8,128)} %delays_ref.5) | copy-start | bytes 7864324
  4.5 21.0 %collective-permute-start.8 = (s16[640,512]{1,0:T(8,128)(2,1)}, s16[640,512]{1,0:T(8,128)(2,1)}, u32[]{:S(2)}, u32[]{:S(2)}) collective-permute-start(s16[640,512]{1,0:T(8,128)(2,1)} %dynamic-slice_convert_fusion), channel_id=1, source_target_pairs={{0,1},{1,0},{2,3},{3,2},{4,5},{5,4},{6,7},{7,6},{8,9},{9,8},{10,11... | collective-permute-start | bytes 1966088 | tf_op jit(solution)/shard_map/ppermute | solution.py:204
  6.0 1.3 %copy-start.1 = (bf16[1,2,320,256]{3,2,1,0:T(8,128)(2,1)}, bf16[1,2,320,256]{3,2,1,0:T(8,128)(2,1)S(1)}, u32[]{:S(2)}) copy-start(bf16[1,2,320,256]{3,2,1,0:T(8,128)(2,1)S(1)} %slice_select_fusion.1) | copy-start | bytes 983044
  7.3 12.5 %copy-start.3 = (bf16[1,2,320,256]{3,2,1,0:T(8,128)(2,1)}, bf16[1,2,320,256]{3,2,1,0:T(8,128)(2,1)S(1)}, u32[]{:S(2)}) copy-start(bf16[1,2,320,256]{3,2,1,0:T(8,128)(2,1)S(1)} %slice_select_fusion) | copy-start | bytes 983044
  7.4 12.2 %collective-permute-start.4 = (bf16[2,2,320,128]{3,2,1,0:T(8,128)(2,1)S(1)}, bf16[2,2,320,128]{3,2,1,0:T(8,128)(2,1)S(1)}, u32[]{:S(2)}, u32[]{:S(2)}) collective-permute-start(bf16[2,2,320,128]{3,2,1,0:T(8,128)(2,1)S(1)} %get-tuple-element.58), channel_id=1, source_target_pairs={{0,2},{1,3},{2,0},{3,1},{4,6},{5,7},{6,4},{7,5},{8,10},{9,11},{10,... | collective-permute-start | bytes 983048 | tf_op jit(solution)/shard_map/ppermute | solution.py:204
  10.0 9.8 %collective-permute-start.5 = (bf16[2,2,320,128]{3,2,1,0:T(8,128)(2,1)S(1)}, bf16[2,2,320,128]{3,2,1,0:T(8,128)(2,1)S(1)}, u32[]{:S(2)}, u32[]{:S(2)}) collective-permute-start(bf16[2,2,320,128]{3,2,1,0:T(8,128)(2,1)S(1)} %get-tuple-element.57), channel_id=1, source_target_pairs={{0,4},{4,0},{8,12},{12,8},{16,20},{20,16},{24,28},{28,24},{1,5},{5... | collective-permute-start | bytes 983048 | tf_op jit(solution)/shard_map/ppermute | solution.py:204
  11.5 3.6 %collective-permute-start.1 = (f32[1,384]{1,0:T(1,128)S(1)}, f32[1,384]{1,0:T(1,128)S(1)}, u32[]{:S(2)}, u32[]{:S(2)}) collective-permute-start(f32[1,384]{1,0:T(1,128)S(1)} %get-tuple-element.75), channel_id=1, source_target_pairs={{0,8},{4,12},{8,0},{12,4},{16,24},{20,28},{24,16},{28,20},{1,9},{5... | collective-permute-start | bytes 4616 | tf_op jit(solution)/shard_map/ppermute | solution.py:204
  15.1 4.5 %collective-permute-start.2 = (f32[1,384]{1,0:T(1,128)S(1)}, f32[1,384]{1,0:T(1,128)S(1)}, u32[]{:S(2)}, u32[]{:S(2)}) collective-permute-start(f32[1,384]{1,0:T(1,128)S(1)} %add.45.token_ref), channel_id=1, source_target_pairs={{0,16},{4,20},{8,24},{12,28},{16,0},{20,4},{24,8},{28,12},{1,17},{... | collective-permute-start | bytes 4616 | tf_op jit(solution)/shard_map/ppermute | solution.py:204
  19.8 3.9 %collective-permute-start.6 = (f32[3,384]{1,0:T(4,128)S(1)}, f32[3,384]{1,0:T(4,128)S(1)}, u32[]{:S(2)}, u32[]{:S(2)}) collective-permute-start(f32[3,384]{1,0:T(4,128)S(1)} %shard_map.47), channel_id=1, source_target_pairs={{0,2},{1,3},{2,0},{3,1},{4,6},{5,7},{6,4},{7,5},{8,10},{9,11},{10,... | collective-permute-start | bytes 13832 | tf_op jit(solution)/shard_map/ppermute | solution.py:204
  20.2 5.2 %copy-start.2 = (bf16[1,2,320,256]{3,2,1,0:T(8,128)(2,1)S(1)}, bf16[1,2,320,256]{3,2,1,0:T(8,128)(2,1)}, u32[]{:S(2)}) copy-start(bf16[1,2,320,256]{3,2,1,0:T(8,128)(2,1)} %copy-done.1) | copy-start | bytes 983044
  20.2 5.2 %copy-start.4 = (bf16[1,2,320,256]{3,2,1,0:T(8,128)(2,1)S(1)}, bf16[1,2,320,256]{3,2,1,0:T(8,128)(2,1)}, u32[]{:S(2)}) copy-start(bf16[1,2,320,256]{3,2,1,0:T(8,128)(2,1)} %copy-done.3) | copy-start | bytes 983044
  23.7 5.3 %collective-permute-start.7 = (f32[3,384]{1,0:T(4,128)S(1)}, f32[3,384]{1,0:T(4,128)S(1)}, u32[]{:S(2)}, u32[]{:S(2)}) collective-permute-start(f32[3,384]{1,0:T(4,128)S(1)} %pad_maximum_fusion.3), channel_id=1, source_target_pairs={{0,4},{4,0},{8,12},{12,8},{16,20},{20,16},{24,28},{28,24},{1,5},{5... | collective-permute-start | bytes 13832 | tf_op jit(solution)/shard_map/ppermute | solution.py:204
  30.7 5.0 %collective-permute-start.10 = (bf16[2,2,64,256]{3,2,0,1:T(8,128)(2,1)S(1)}, bf16[2,2,64,256]{3,2,0,1:T(8,128)(2,1)S(1)}, u32[]{:S(2)}, u32[]{:S(2)}) collective-permute-start(bf16[2,2,64,256]{3,2,0,1:T(8,128)(2,1)S(1)} %fusion.2), channel_id=1, source_target_pairs={{0,8},{4,12},{8,0},{12,4},{16,24},{20,28},{24,16},{28,20},{1,9},{5... | collective-permute-start | bytes 393224 | tf_op jit(solution)/shard_map/ppermute | solution.py:204
  33.9 5.0 %collective-permute-start.9 = (bf16[256,256]{1,0:T(8,128)(2,1)S(1)}, bf16[256,256]{1,0:T(8,128)(2,1)S(1)}, u32[]{:S(2)}, u32[]{:S(2)}) collective-permute-start(bf16[256,256]{1,0:T(8,128)(2,1)S(1)} %select_convert_fusion.1), channel_id=1, source_target_pairs={{0,2},{1,3},{2,0},{3,1},{4,6},{5,7},{6,4},{7,5},{8,10},{9,11},{10,... | collective-permute-start | bytes 393224 | tf_op jit(solution)/shard_map/ppermute | solution.py:204
  39.0 4.3 %collective-permute-start.12 = (bf16[2,64,256]{2,1,0:T(8,128)(2,1)S(1)}, bf16[2,64,256]{2,1,0:T(8,128)(2,1)S(1)}, u32[]{:S(2)}, u32[]{:S(2)}) collective-permute-start(bf16[2,64,256]{2,1,0:T(8,128)(2,1)S(1)} %fusion.3), channel_id=1, source_target_pairs={{0,4},{4,0},{8,12},{12,8},{16,20},{20,16},{24,28},{28,24},{1,5},{5... | collective-permute-start | bytes 196616 | tf_op jit(solution)/shard_map/ppermute | solution.py:204
  39.6 5.3 %collective-permute-start.11 = (bf16[256,256]{1,0:T(8,128)(2,1)S(1)}, bf16[256,256]{1,0:T(8,128)(2,1)S(1)}, u32[]{:S(2)}, u32[]{:S(2)}) collective-permute-start(bf16[256,256]{1,0:T(8,128)(2,1)S(1)} %get-tuple-element.55), channel_id=1, source_target_pairs={{0,8},{4,12},{8,0},{12,4},{16,24},{20,28},{24,16},{28,20},{1,9},{5... | collective-permute-start | bytes 393224 | tf_op jit(solution)/shard_map/ppermute | solution.py:204
  45.0 7.4 %collective-permute-start.13 = (bf16[256,256]{1,0:T(8,128)(2,1)S(1)}, bf16[256,256]{1,0:T(8,128)(2,1)S(1)}, u32[]{:S(2)}, u32[]{:S(2)}) collective-permute-start(bf16[256,256]{1,0:T(8,128)(2,1)S(1)} %get-tuple-element.53), channel_id=1, source_target_pairs={{0,16},{4,20},{8,24},{12,28},{16,0},{20,4},{24,8},{28,12},{1,17},{... | collective-permute-start | bytes 393224 | tf_op jit(solution)/shard_map/ppermute | solution.py:204
  48.0 4.3 %collective-permute-start.14 = (bf16[2,64,256]{2,1,0:T(8,128)(2,1)S(1)}, bf16[2,64,256]{2,1,0:T(8,128)(2,1)S(1)}, u32[]{:S(2)}, u32[]{:S(2)}) collective-permute-start(bf16[2,64,256]{2,1,0:T(8,128)(2,1)S(1)} %add_convert_fusion.2), channel_id=1, source_target_pairs={{0,2},{1,3},{2,0},{3,1},{4,6},{5,7},{6,4},{7,5},{8,10},{9,11},{10,... | collective-permute-start | bytes 196616 | tf_op jit(solution)/shard_map/ppermute | solution.py:204
  52.4 7.8 %collective-permute-start.15 = (bf16[256,256]{1,0:T(8,128)(2,1)S(1)}, bf16[256,256]{1,0:T(8,128)(2,1)S(1)}, u32[]{:S(2)}, u32[]{:S(2)}) collective-permute-start(bf16[256,256]{1,0:T(8,128)(2,1)S(1)} %add_convert_fusion), channel_id=1, source_target_pairs={{0,4},{4,0},{8,12},{12,8},{16,20},{20,16},{24,28},{28,24},{1,5},{5... | collective-permute-start | bytes 393224 | tf_op jit(solution)/shard_map/ppermute | solution.py:204
  55.0 5.2 %collective-permute-start.16 = (bf16[2,64,256]{2,1,0:T(8,128)(2,1)S(1)}, bf16[2,64,256]{2,1,0:T(8,128)(2,1)S(1)}, u32[]{:S(2)}, u32[]{:S(2)}) collective-permute-start(bf16[2,64,256]{2,1,0:T(8,128)(2,1)S(1)} %get-tuple-element.65), channel_id=1, source_target_pairs={{0,16},{4,20},{8,24},{12,28},{16,0},{20,4},{24,8},{28,12},{1,17},{... | collective-permute-start | bytes 196616 | tf_op jit(solution)/shard_map/ppermute | solution.py:204
  61.3 1.3 %collective-permute-start.17 = (f32[2,128,64]{1,2,0:T(8,128)S(1)}, f32[2,128,64]{1,2,0:T(8,128)S(1)}, u32[]{:S(2)}, u32[]{:S(2)}) collective-permute-start(f32[2,128,64]{1,2,0:T(8,128)S(1)} %select_bitcast_fusion.6), channel_id=1, source_target_pairs={{0,1},{1,0},{2,3},{3,2},{4,5},{5,4},{6,7},{7,6},{8,9},{9,8},{10,11... | collective-permute-start | bytes 196616 | tf_op jit(solution)/shard_map/ppermute | solution.py:204

commit v3 on v2

v3 whole, which is shorter than its diff:
```python
import functools
import math

import jax
import jax.numpy as jnp
from jax import lax
from jax.experimental import pallas as pl
from jax.experimental.pallas import tpu as pltpu
from jax.sharding import PartitionSpec as P

cycle_rates = (0.0361, 0.0596)
ROOT = math.sqrt(2.0)
SIN = (3.1415820121765137, -5.167142868041992, 2.5418989658355713, -0.5546361207962036)
COS = (0.9999999403953552, -4.934792995452881, 4.058412075042725, -1.3318800926208496, 0.2196967601776123)


def horner(z, terms):
    total = ROOT * terms[-1]
    for term in terms[-2::-1]:
        total = total * z + ROOT * term
    return total


def steer_rows(rate, delays):
    turns = rate * delays.astype(jnp.float32)
    turns = turns - jnp.round(turns)
    z = turns * turns
    half_sin = turns * horner(z, SIN)
    half_cos = horner(z, COS)
    return (1.0 - half_sin * half_sin).astype(jnp.bfloat16), (half_sin * half_cos).astype(jnp.bfloat16)


CHUNK = 32
LANES = 128


def place():
    row, col = lax.axis_index("row"), lax.axis_index("col")
    return row, col, col & 1, (col >> 1) & 1, row & 1


def y_of():
    return place()[4]


def block_of(j, at):
    _, col, core, x, _ = place()
    return (col >> 2) * 4 + (x ^ j) * 2 + (core ^ at)


def vmem(shape, dtype):
    return pltpu.VMEM(shape, dtype)


def kernel_call(body, out, inputs, spaces, scratch=(), limit=8, cost=1, name=None):
    held = [
        pltpu.with_memory_space_constraint(v, space) if space in (pltpu.HBM, pltpu.VMEM) else v
        for v, space in zip(inputs, spaces)
    ]
    return pl.pallas_call(
        body,
        out_shape=out,
        in_specs=[pl.BlockSpec(memory_space=space) for space in spaces],
        out_specs=[pl.BlockSpec(memory_space=pltpu.VMEM)] * len(out),
        scratch_shapes=list(scratch),
        compiler_params=pltpu.CompilerParams(vmem_limit_bytes=limit * 2**20),
        cost_estimate=pl.CostEstimate(flops=1, bytes_accessed=cost, transcendentals=0),
        name=name,
    )(*held)


def power_kernel(wl_ref, spec_ref, own_note, away_note, own_ref, away_ref, wl_held, sems):
    row, col, core, *_ = place()
    n_col = lax.axis_size("col")
    _, parts, per, windows = spec_ref.shape
    wl_copy = pltpu.make_async_copy(wl_ref, wl_held, sems.at[2])
    wl_copy.start()
    both = ((core, own_note, own_ref), (1 - core, away_note, away_ref))
    copies = [pltpu.make_async_copy(spec_ref.at[f], held, sems.at[i]) for i, (f, _, held) in enumerate(both)]
    for copy in copies:
        copy.start()
    ids = (row * n_col + col) * per + lax.broadcasted_iota(jnp.int32, (1, per), 1)
    rest = jnp.zeros((own_note.shape[1] - per, LANES), jnp.float32)
    wl_copy.wait()
    for (f, note, held), copy in zip(both, copies):
        copy.wait()
        squares = jnp.square(held[...].astype(jnp.float32))
        squares = squares[0] + squares[1]
        squares = sum(squares[:, at : at + LANES] for at in range(0, windows, LANES))
        columns = jnp.transpose(jnp.concatenate([squares, rest], axis=0))
        power = jnp.sum(columns, axis=0, keepdims=True)
        level = jnp.sum(jnp.where(ids == wl_held[f], power[:, :per], 0.0), axis=1, keepdims=True)
        note[0:1, :] = power
        note[1:2, :] = jnp.broadcast_to(level, power.shape)


def gate_kernel(n, *refs):
    out_ref, start = refs[-1], 0
    for ref in refs[:n]:
        out_ref[start : start + ref.shape[0], :] = ref[...]
        start += ref.shape[0]


def gated(values, others):
    rows, width = sum(v.shape[0] for v in values), values[0].shape[1]
    return kernel_call(
        functools.partial(gate_kernel, len(values)),
        [vmem((rows, width), values[0].dtype)],
        [*values, *others],
        [pltpu.VMEM] * (len(values) + len(others)),
        name="gate",
    )[0]


def send_kernel(token_ref, own_ref, other_ref, to_x_ref, to_y_ref):
    y = place()[4]
    half = to_y_ref.shape[-1]
    theirs = pl.ds(pl.multiple_of((1 - y) * half, half), half)
    for at, ref in enumerate((own_ref, other_ref)):
        to_x_ref[at] = ref[...]
        for part in range(ref.shape[0]):
            to_y_ref[at, part] = ref[part, :, theirs]


def steer_blocks(blocks, delays_ref, cos_ref, sin_ref, copy_ref=None):
    core = place()[2]
    rate = jnp.where(core == 0, cycle_rates[0], cycle_rates[1]).astype(jnp.float32)
    size = cos_ref.shape[0] // len(blocks)
    chunk = math.gcd(CHUNK, size)
    for index, (start, arrival) in enumerate(blocks):
        if arrival is not None:
            arrival.wait()

        @pl.loop(0, size // chunk)
        def _(i):
            here = pl.ds(pl.multiple_of(start + i * chunk, chunk), chunk)
            there = pl.ds(pl.multiple_of(index * size + i * chunk, chunk), chunk)
            delays = delays_ref[here, :]
            cos, sin = steer_rows(rate, delays)
            cos_ref[there, :] = cos
            sin_ref[there, :] = sin
            if copy_ref is not None:
                copy_ref[there, :] = delays.astype(copy_ref.dtype)


def steer_kernel(token_ref, delays_ref, cos_ref, sin_ref, out_ref):
    out_ref[...] = token_ref[...]
    steer_blocks([(0, None)], delays_ref, cos_ref, sin_ref)


def steer_far_kernel(starts, parts, token_ref, delays_ref, cos_ref, sin_ref, out_ref, *refs):
    *copy_ref, held_ref, sems = refs
    out_ref[...] = token_ref[...]
    per = cos_ref.shape[0] // 2
    rows = per // parts
    blocks = []
    for j, first in enumerate(starts()):
        for part in range(parts):
            index = j * parts + part
            here = pl.ds(index * rows, rows)
            there = pl.ds(pl.multiple_of(first + part * rows, 8), rows)
            arrival = pltpu.make_async_copy(delays_ref.at[there, :], held_ref.at[here, :], sems.at[index])
            arrival.start()
            blocks.append((index * rows, arrival))
    steer_blocks(blocks, held_ref, cos_ref, sin_ref, *copy_ref)


def steering(token, delays):
    out = [vmem(delays.shape, jnp.bfloat16)] * 2 + [vmem(token.shape, token.dtype)]
    return kernel_call(steer_kernel, out, [token, delays], [pltpu.VMEM] * 2, name="steering")


def steering_far(starts, rows, token, delays, copied=()):
    width = delays.shape[1]
    parts = math.gcd(rows // (2 * CHUNK), 5)
    return kernel_call(
        functools.partial(steer_far_kernel, starts, parts),
        [vmem((rows, width), jnp.bfloat16)] * 2
        + [vmem(token.shape, token.dtype)]
        + [vmem((rows, width), t) for t in copied],
        [token, delays],
        [pltpu.VMEM, pltpu.HBM],
        scratch=[pltpu.VMEM((rows, width), delays.dtype), pltpu.SemaphoreType.DMA((2 * parts,))],
        name="steering_far",
    )


def halves(total, block, bit, keep_ref, send_ref):
    for pair in range(keep_ref.shape[0] // block):
        out = pl.ds(pair * block, block)
        for ref, at in ((keep_ref, bit), (send_ref, 1 - bit)):
            rows = pl.ds(pl.multiple_of((2 * pair + at) * block, block), block)
            ref[out, :] = total[rows, :].astype(ref.dtype)


def beams_kernel(order, mine, block, kept, near_power_ref, far_ref, level_ref, own_ref, other_ref, from_ref, *refs):
    *steer, keep_ref, send_ref, token_ref, total_ref = refs
    token_ref[...] = level_ref[...]
    per = from_ref.shape[2]
    windows = mine(from_ref.shape[3])
    level = 0.5 * level_ref[...]
    real, imag = [], []
    for at in range(4):
        power = near_power_ref[at : at + 1] if at < 2 else far_ref[at - 2 : at - 1]
        gain = jnp.transpose(jnp.broadcast_to(lax.rsqrt(power + level), (8, level.shape[1])))[:per, :1]
        for part, parts in enumerate((real, imag)):
            near_ref = (own_ref, other_ref)[at % 2]
            spec = near_ref[part, :, windows] if at < 2 else from_ref[at - 2, part]
            parts.append(spec.astype(jnp.float32) * gain)
    total = None
    count = len(steer) // 2
    for group in range(count):
        members = order[group * 4 // count : (group + 1) * 4 // count]
        re, im = (jnp.concatenate([p[m] for m in members], axis=0).astype(jnp.bfloat16) for p in (real, imag))
        for left, right in (((re, im), steer[2 * group]), ((-im, re), steer[2 * group + 1])):
            term = lax.dot_general(
                right[...],
                jnp.concatenate(left, axis=1),
                (((0,), (0,)), ((), ())),
                preferred_element_type=jnp.float32,
            )
            total = term if total is None else total + term
    total_ref[...] = total
    halves(total_ref, block, kept(), keep_ref, send_ref)


def beams(order, mine, block, kept, near_power, far, level, own, other, arrived, steer, name):
    inputs = [near_power, far, level, own, other, arrived, *steer]
    rows, width = steer[0].shape[1], 2 * arrived.shape[-1]
    return kernel_call(
        functools.partial(beams_kernel, order, mine, block, kept),
        [
            vmem((rows // 2, width), jnp.float32),
            vmem((rows // 2, width), jnp.bfloat16),
            vmem(level.shape, level.dtype),
        ],
        inputs,
        [pltpu.VMEM] * len(inputs),
        scratch=[pltpu.VMEM((rows, width), jnp.float32)],
        limit=24,
        name=name,
    )


def step_kernel(block, axis, bit, given, keep_ref, other_ref, token_ref, *outs):
    if given:
        *outs, out_token_ref = outs if bit is None else (*outs[:2], outs[3], outs[2])
        out_token_ref[...] = token_ref[...]
    if bit is None:
        total = keep_ref[...] + other_ref[...].astype(jnp.float32)
        for ref in outs:
            ref[...] = total.astype(ref.dtype)
    else:
        keep_out, send_out, total_ref = outs
        total_ref[...] = keep_ref[...] + other_ref[...].astype(jnp.float32)
        index = lax.axis_index(axis)
        halves(total_ref, block, (index // bit) & 1, keep_out, send_out)


def exchange(keep, send, block, steps, given, name):
    token = yield
    for index, (axis, bit, _) in enumerate(steps):
        other = swap(send, axis, bit)
        rows, width = keep.shape
        scratch, cut = [], (None, None)
        if index + 1 == len(steps):
            out = [vmem((rows, width), jnp.bfloat16)]
        elif steps[index + 1][2]:
            out, cut = [vmem((rows // 2, width), t) for t in (jnp.float32, jnp.bfloat16)], steps[index + 1][:2]
            scratch = [pltpu.VMEM((rows, width), jnp.float32)]
        else:
            out = [vmem((rows, width), t) for t in (jnp.float32, jnp.bfloat16)]
        if index in given:
            out.append(vmem(token.shape, token.dtype))
        results = kernel_call(
            functools.partial(step_kernel, block, *cut, index in given),
            out,
            [keep, other, token],
            [pltpu.VMEM] * 3,
            scratch=scratch,
            name=name,
        )
        if index + 1 == len(steps):
            yield results[0]
        else:
            keep, send = results[:2]
            token = yield results[-1]


def field_kernel(scale, source_ref, near_r, far_r, keep_ref, send_ref):
    _, _, core, _, y = place()
    half = near_r.shape[1] // 2
    block = keep_ref.shape[2]

    def product(left, right):
        return lax.dot_general(left, right, (((1,), (1,)), ((), ())), preferred_element_type=jnp.float32)

    for ref, at in ((keep_ref, core), (send_ref, 1 - core)):
        rows = pl.ds(pl.multiple_of(at * block, block), block)
        real = imag = 0.0
        for bit, receiver in ((y, near_r), (1 - y, far_r)):
            s_re, s_im = (
                source_ref[:, pl.ds(pl.multiple_of((2 * part + bit) * half, half), half)] for part in (0, 1)
            )
            r_re, r_im = receiver[rows, :half], receiver[rows, half:]
            real += product(s_re, r_re) + product(s_im, r_im)
            imag += product(s_im, r_re) - product(s_re, r_im)
        ref[0] = real * scale
        ref[1] = imag * scale


def swap(value, axis, bit):
    size = lax.axis_size(axis)
    return lax.ppermute(value, axis, [(i, i ^ bit) for i in range(size)])


def choose(bit, first, second):
    return jnp.where(bit == 0, first, second)


def ordered(bit, own, other):
    return choose(bit, own, other), choose(bit, other, own)


def bits(size, start):
    found = []
    while start < size:
        found.append(start)
        start *= 2
    return found


def body(spectra, delays_s, delays_r, wl_index):
    n_row, n_col = lax.axis_size("row"), lax.axis_size("col")
    row, col, core, x, y = place()
    freqs, parts, per, windows = spectra.shape
    half = windows // 2
    padded = -(-per // LANES) * LANES

    spec_shape, note_shape = vmem((parts, per, windows), spectra.dtype), vmem((2, padded), jnp.float32)
    note, away_note, own, away = kernel_call(
        power_kernel,
        [note_shape, note_shape, spec_shape, spec_shape],
        [wl_index, spectra],
        [pltpu.HBM, pltpu.HBM],
        scratch=[pltpu.SMEM(wl_index.shape, wl_index.dtype), pltpu.SemaphoreType.DMA((3,))],
        name="power",
    )
    other_note, other = swap(away_note, "col", 1), swap(away, "col", 1)
    power = jnp.concatenate([note[:1], other_note[:1]])
    level = note[1:] + other_note[1:]

    def rows_r():
        return [(place()[0] ^ j) * per for j in (0, 1)]

    def rows_s(j):
        return lambda: [block_of(j, at) * per for at in (0, 1)]

    far_x = swap(jnp.concatenate([power, level]), "col", 2)
    *steer_r, token, near_r = steering_far(rows_r, 2 * per, note[1:], delays_r, [jnp.int16])
    other_r = swap(near_r, "col", 1)
    level = gated([level + far_x[2:]], [token])

    sent = [vmem((2, parts, per, w), spectra.dtype) for w in (windows, half)]
    to_x, to_y = kernel_call(send_kernel, sent, [level, own, other], [pltpu.VMEM] * 3, name="send")
    from_x, from_y = swap(to_x, "col", 2), swap(to_y, "row", 1)

    row_bits, col_bits = bits(n_row, 2), bits(n_col, 4)
    *steer_s, token = steering_far(rows_s(0), 2 * per, level, delays_s)
    first, *others = [("row", bit) for bit in row_bits] + [("col", bit) for bit in col_bits]
    level = level + swap(level, *first)
    cos, sin, next_token = steering_far(rows_s(1), 2 * per, level, delays_s)
    steer_s += [cos, sin]
    for step in others:
        level = gated([level], [token])
        level = level + swap(level, *step)
    cos, sin, token = steering(level, other_r)
    steer_r += [cos, sin]
    far_y = swap(gated([power, level], [from_y, next_token]), "row", 1)
    level = gated([level + far_y[2:]], [token])

    block_r, block_s = 2 * delays_r.shape[1] // n_col, delays_s.shape[1] // n_row
    keep_r, send_r, token = beams(
        (0, 2, 1, 3),
        lambda half: pl.ds(pl.multiple_of(y_of() * half, half), half),
        block_r,
        lambda: place()[3],
        power,
        far_y,
        level,
        own,
        other,
        from_y,
        steer_r,
        "beams_r",
    )
    keep_s, send_s, _ = beams(
        (0, 1, 2, 3), lambda windows: slice(None), block_s, y_of, power, far_x, token, own, other, from_x, steer_s, "beams_s"
    )
    r_steps = [("col", bit, True) for bit in [2, *col_bits]] + [("row", bit, False) for bit in row_bits]
    s_steps = [("row", bit, True) for bit in [1, *row_bits]] + [("col", bit, False) for bit in col_bits]
    late = 1
    r_chain = exchange(keep_r, send_r, block_r, r_steps, (), "step_r")
    s_chain = exchange(keep_s, send_s, block_s, s_steps, (late - 1,), "step_s")
    next(r_chain), next(s_chain)
    token = level
    for index in range(max(len(r_steps), len(s_steps))):
        if index < len(r_steps):
            receiver = r_chain.send(token if index == late else level)
        if index < len(s_steps):
            source = s_chain.send(level)
            if index == late - 1:
                token = source
    r_far = swap(receiver, "row", 1)

    block = delays_r.shape[1] // n_col
    shape = vmem((2, block_s, block), jnp.float32)
    scale = math.sqrt(windows) / (per * n_row * n_col)
    near, away = kernel_call(
        functools.partial(field_kernel, scale),
        [shape, shape],
        [source, receiver, r_far],
        [pltpu.VMEM] * 3,
        name="field",
    )
    far = swap(away, "col", 1)
    return jnp.stack(ordered(core, near, far)).swapaxes(2, 3)


def solution(mesh):
    in_specs = (P(None, None, ("row", "col"), None), P("row", None), P("col", None), P())
    out_specs = P(None, None, "col", "row")
    return jax.shard_map(body, mesh=mesh, in_specs=in_specs, out_specs=out_specs, check_vma=False)
```

time: 63.5 us -> 54.1 us (0.85)
  other arithmetic: 5.98 us -> 0.73 us
  waiting for transfers between devices: 20.7 us -> 16.6 us
  Pallas kernels: 11.5 us -> 14.5 us
  starting transfers between devices: 23.7 us -> 21.9 us
    ppermute x18 -> x17, waiting for transfers between devices: 20.7 us -> 16.6 us  [swap(): return lax.ppermute(value, axis, [(i, i ^ bit) for i in range(size)])]
    pallas_call x8 -> x19, Pallas kernels: 11.5 us -> 14.5 us  [kernel_call(): pl.pallas_call(body, out_shape=out, in_specs=[pl.BlockSpec(memory_space=s...]
    convert_element_type x9 -> x0, other arithmetic: 2.59 us -> none  [the longest x1 2.4 us: body(): other_r = swap(near_r.astype(jnp.int16), 'col', 1)]
    select_n x10 -> x0, other arithmetic: 2.48 us -> none  [choose(): return jnp.where(bit == 0, first, second)]
    ppermute x18 -> x17, starting transfers between devices: 23.7 us -> 21.9 us  [swap(): return lax.ppermute(value, axis, [(i, i ^ bit) for i in range(size)])]
    another operation x5 -> x1, other arithmetic: 0.78 us -> 0.01 us  [body(): return jnp.stack(ordered(core, near, far)).swapaxes(2, 3)]
    transpose x0 -> x1, other arithmetic: none -> 0.67 us  [body(): return jnp.stack(ordered(core, near, far)).swapaxes(2, 3)]
  transfers between devices with their start and end apart: 18 -> 17, of which waited for: 10 -> 7; matrix products, arithmetic and copies ran while one was open for 8% -> 0% of each run, Pallas kernels for 16% -> 23%
where the time goes in v3:
time: 54.1 us; the launch traced here: 54 us
  starting transfers between devices  21.9 us (40%)
  waiting for transfers between devices  16.6 us (31%)
  Pallas kernels  14.5 us (27%)
  other arithmetic  0.73 us (1%)
    ppermute x17, starting transfers between devices, swap(): return lax.ppermute(value, axis, [(i, i ^ bit) for i in range(size)])  21.9 us
    ppermute x17, waiting for transfers between devices, swap(): return lax.ppermute(value, axis, [(i, i ^ bit) for i in range(size)])  16.6 us
    pallas_call x19, Pallas kernels, kernel_call(): pl.pallas_call(body, out_shape=out, in_specs=[pl.BlockSpec(memory_space=s...  14.5 us
  transfers between devices with their start and end apart: 17, of which 7 were waited for; matrix products, arithmetic and copies ran while one was open for 0% of the time, Pallas kernels for 23%

profile of v3, /device:TPU:0, one launch (start us, length us, event | category | flops | bytes accessed | tf_op | source)
XLA Modules:
  0.0 54.0 jit_solution(1982661560227439113)
XLA Ops:
  0.0 1.5 %power.1 = (f32[2,384]{1,0:T(2,128)S(1)}, f32[2,384]{1,0:T(2,128)S(1)}, bf16[2,320,256]{2,1,0:T(8,128)(2,1)S(1)}, bf16[2,320,256]{2,1,0:T(8,128)(2,1)S(1)}) custom-call(s32[2]{0:T(128)} %wl_ref.1, bf16[2,2,320,256]{3,2,1,0:T(8,128)(2,1)} %spec_ref.1), custom_call_target="tpu_custom_call" | custom-call | flops 1 | bytes 1 | tf_op jit(solution)/shard_map/power/pallas_call | solution.py:60
  1.5 0.5 collective-permute-start
  2.0 0.1 collective-permute-start.4
  2.1 0.7 %collective-permute-done = f32[2,384]{1,0:T(2,128)S(1)} collective-permute-done((f32[2,384]{1,0:T(2,128)S(1)}, f32[2,384]{1,0:T(2,128)S(1)}, u32[]{:S(2)}, u32[]{:S(2)}) %collective-permute-start) | collective-permute-done | bytes 3104 | tf_op jit(solution)/shard_map/ppermute | solution.py:314
  2.8 2.9 %collective-permute-start.1 = (f32[3,384]{1,0:T(4,128)S(1)}, f32[3,384]{1,0:T(4,128)S(1)}, u32[]{:S(2)}, u32[]{:S(2)}) collective-permute-start(f32[3,384]{1,0:T(4,128)S(1)} %pad_maximum_fusion), channel_id=1, source_target_pairs={{0,2},{1,3},{2,0},{3,1},{4,6},{5,7},{6,4},{7,5},{8,10},{9,11},{10,... | collective-permute-start | bytes 13832 | tf_op jit(solution)/shard_map/ppermute | solution.py:314
  5.7 2.2 %steering_far.3 = (bf16[640,512]{1,0:T(8,128)(2,1)S(1)}, bf16[640,512]{1,0:T(8,128)(2,1)S(1)}, f32[1,384]{1,0:T(1,128)S(1)}, s16[640,512]{1,0:T(8,128)(2,1)S(1)}) custom-call(f32[1,384]{1,0:T(1,128)S(1)} %get-tuple-element.77.token_ref, s32[2560,512]{1,0:T(8,128)} %delays_ref.3), custom_call_target="tpu_custom_call" | custom-call | flops 1 | bytes 1 | tf_op jit(solution)/shard_map/steering_far/pallas_call | solution.py:60
  7.9 0.1 collective-permute-start.7
  8.0 0.0 collective-permute-done.1.far_ref
  8.0 0.0 collective-permute-done.4.other_ref
  8.0 0.1 send.1
  8.2 1.4 %collective-permute-start.8 = (bf16[2,2,320,256]{3,2,1,0:T(8,128)(2,1)S(1)}, bf16[2,2,320,256]{3,2,1,0:T(8,128)(2,1)S(1)}, u32[]{:S(2)}, u32[]{:S(2)}) collective-permute-start(bf16[2,2,320,256]{3,2,1,0:T(8,128)(2,1)S(1)} %get-tuple-element.55), channel_id=1, source_target_pairs={{0,2},{1,3},{2,0},{3,1},{4,6},{5,7},{6,4},{7,5},{8,10},{9,11},{10,... | collective-permute-start | bytes 1966088 | tf_op jit(solution)/shard_map/ppermute | solution.py:314
  9.6 1.5 %collective-permute-start.5 = (bf16[2,2,320,128]{3,2,1,0:T(8,128)(2,1)S(1)}, bf16[2,2,320,128]{3,2,1,0:T(8,128)(2,1)S(1)}, u32[]{:S(2)}, u32[]{:S(2)}) collective-permute-start(bf16[2,2,320,128]{3,2,1,0:T(8,128)(2,1)S(1)} %get-tuple-element.46), channel_id=1, source_target_pairs={{0,4},{4,0},{8,12},{12,8},{16,20},{20,16},{24,28},{28,24},{1,5},{5... | collective-permute-start | bytes 983048 | tf_op jit(solution)/shard_map/ppermute | solution.py:314
  11.1 1.6 %collective-permute-start.2 = (f32[1,384]{1,0:T(1,128)S(1)}, f32[1,384]{1,0:T(1,128)S(1)}, u32[]{:S(2)}, u32[]{:S(2)}) collective-permute-start(f32[1,384]{1,0:T(1,128)S(1)} %gate.4.token_ref), channel_id=1, source_target_pairs={{0,8},{4,12},{8,0},{12,4},{16,24},{20,28},{24,16},{28,20},{1,9},{5... | collective-permute-start | bytes 4616 | tf_op jit(solution)/shard_map/ppermute | solution.py:314
  12.7 2.2 %steering_far.4 = (bf16[640,512]{1,0:T(8,128)(2,1)S(1)}, bf16[640,512]{1,0:T(8,128)(2,1)S(1)}, f32[1,384]{1,0:T(1,128)S(1)}) custom-call(f32[1,384]{1,0:T(1,128)S(1)} %gate.4.token_ref, s32[1280,512]{1,0:T(8,128)} %delays_ref.5), custom_call_target="tpu_custom_call" | custom-call | flops 1 | bytes 1 | tf_op jit(solution)/shard_map/steering_far/pallas_call | solution.py:60
  14.8 0.0 collective-permute-done.2
  14.9 2.7 %collective-permute-start.3 = (f32[1,384]{1,0:T(1,128)S(1)}, f32[1,384]{1,0:T(1,128)S(1)}, u32[]{:S(2)}, u32[]{:S(2)}) collective-permute-start(f32[1,384]{1,0:T(1,128)S(1)} %gate.5), channel_id=1, source_target_pairs={{0,16},{4,20},{8,24},{12,28},{16,0},{20,4},{24,8},{28,12},{1,17},{... | collective-permute-start | bytes 4616 | tf_op jit(solution)/shard_map/ppermute | solution.py:314
  17.5 2.2 %steering_far.5 = (bf16[640,512]{1,0:T(8,128)(2,1)S(1)}, bf16[640,512]{1,0:T(8,128)(2,1)S(1)}, f32[1,384]{1,0:T(1,128)S(1)}) custom-call(f32[1,384]{1,0:T(1,128)S(1)} %add.17.refs_0_.token_ref, s32[1280,512]{1,0:T(8,128)} %delays_ref.5), custom_call_target="tpu_custom_call" | custom-call | flops 1 | bytes 1 | tf_op jit(solution)/shard_map/steering_far/pallas_call | solution.py:60
  19.7 0.0 collective-permute-done.3
  19.8 0.0 collective-permute-done.5.refs_2_.from_ref
  19.8 0.6 %collective-permute-start.6 = (f32[3,384]{1,0:T(4,128)S(1)}, f32[3,384]{1,0:T(4,128)S(1)}, u32[]{:S(2)}, u32[]{:S(2)}) collective-permute-start(f32[3,384]{1,0:T(4,128)S(1)} %gate.6), channel_id=1, source_target_pairs={{0,4},{4,0},{8,12},{12,8},{16,20},{20,16},{24,28},{28,24},{1,5},{5... | collective-permute-start | bytes 13832 | tf_op jit(solution)/shard_map/ppermute | solution.py:314
  20.3 0.0 collective-permute-done.7.delays_ref
  20.4 1.2 %steering.1 = (bf16[640,512]{1,0:T(8,128)(2,1)S(1)}, bf16[640,512]{1,0:T(8,128)(2,1)S(1)}, f32[1,384]{1,0:T(1,128)S(1)}) custom-call(f32[1,384]{1,0:T(1,128)S(1)} %add.18.refs_1_.token_ref, s16[640,512]{1,0:T(8,128)(2,1)S(1)} %collective-permute-done.7.delays_ref), custom_call_target="tpu_custom_call" | custom-call | flops 1 | bytes 1 | tf_op jit(solution)/shard_map/steering/pallas_call | solution.py:60
  21.6 1.9 %collective-permute-done.6.far_ref = f32[3,384]{1,0:T(4,128)S(1)} collective-permute-done((f32[3,384]{1,0:T(4,128)S(1)}, f32[3,384]{1,0:T(4,128)S(1)}, u32[]{:S(2)}, u32[]{:S(2)}) %collective-permute-start.6) | collective-permute-done | bytes 4640 | tf_op jit(solution)/shard_map/ppermute | solution.py:314
  23.5 1.7 %beams_r.1 = (f32[256,256]{1,0:T(8,128)S(1)}, bf16[256,256]{1,0:T(8,128)(2,1)S(1)}, f32[1,384]{1,0:T(1,128)S(1)}) custom-call(f32[2,384]{1,0:T(2,128)S(1)} %pad_maximum_fusion.1.refs_0_.near_power_ref, f32[3,384]{1,0:T(4,128)S(1)} %collective-permute-done.6.far_ref, f32[1,384]{1,0:T(1,128)S(1)} %gate.7.level_ref.token_ref, ...), custom_call_target="tpu_custom_call" | custom-call | flops 1 | bytes 1 | tf_op jit(solution)/shard_map/beams_r/pallas_call | solution.py:60
  25.2 0.8 %collective-permute-start.12 = (bf16[256,256]{1,0:T(8,128)(2,1)S(1)}, bf16[256,256]{1,0:T(8,128)(2,1)S(1)}, u32[]{:S(2)}, u32[]{:S(2)}) collective-permute-start(bf16[256,256]{1,0:T(8,128)(2,1)S(1)} %get-tuple-element.67), channel_id=1, source_target_pairs={{0,2},{1,3},{2,0},{3,1},{4,6},{5,7},{6,4},{7,5},{8,10},{9,11},{10,... | collective-permute-start | bytes 393224 | tf_op jit(solution)/shard_map/ppermute | solution.py:314
  25.9 0.0 collective-permute-done.8.from_ref
  25.9 2.7 %beams_s.1 = (f32[256,512]{1,0:T(8,128)S(1)}, bf16[256,512]{1,0:T(8,128)(2,1)S(1)}, f32[1,384]{1,0:T(1,128)}) custom-call(f32[2,384]{1,0:T(2,128)S(1)} %pad_maximum_fusion.1.refs_0_.near_power_ref, f32[3,384]{1,0:T(4,128)S(1)} %collective-permute-done.1.far_ref, f32[1,384]{1,0:T(1,128)S(1)} %get-tuple-element.54.level_ref, ...), custom_call_target="tpu_custom_call" | custom-call | flops 1 | bytes 1 | tf_op jit(solution)/shard_map/beams_s/pallas_call | solution.py:60
  28.6 1.3 %collective-permute-start.9 = (bf16[256,512]{1,0:T(8,128)(2,1)S(1)}, bf16[256,512]{1,0:T(8,128)(2,1)S(1)}, u32[]{:S(2)}, u32[]{:S(2)}) collective-permute-start(bf16[256,512]{1,0:T(8,128)(2,1)S(1)} %get-tuple-element.61), channel_id=1, source_target_pairs={{0,4},{4,0},{8,12},{12,8},{16,20},{20,16},{24,28},{28,24},{1,5},{5... | collective-permute-start | bytes 786440 | tf_op jit(solution)/shard_map/ppermute | solution.py:314
  30.0 0.2 collective-permute-done.12.other_ref
  30.3 1.4 %collective-permute-start.13 = (bf16[256,256]{1,0:T(8,128)(2,1)S(1)}, bf16[256,256]{1,0:T(8,128)(2,1)S(1)}, u32[]{:S(2)}, u32[]{:S(2)}) collective-permute-start(bf16[256,256]{1,0:T(8,128)(2,1)S(1)} %get-tuple-element.69), channel_id=1, source_target_pairs={{0,8},{4,12},{8,0},{12,4},{16,24},{20,28},{24,16},{28,20},{1,9},{5... | collective-permute-start | bytes 393224 | tf_op jit(solution)/shard_map/ppermute | solution.py:314
  31.7 4.3 %collective-permute-done.9.other_ref = bf16[256,512]{1,0:T(8,128)(2,1)S(1)} collective-permute-done((bf16[256,512]{1,0:T(8,128)(2,1)S(1)}, bf16[256,512]{1,0:T(8,128)(2,1)S(1)}, u32[]{:S(2)}, u32[]{:S(2)}) %collective-permute-start.9) | collective-permute-done | bytes 262176 | tf_op jit(solution)/shard_map/ppermute | solution.py:314
  36.0 0.1 step_s.3
  36.1 0.0 collective-permute-done.13.other_ref
  36.1 2.6 %collective-permute-start.14 = (bf16[256,256]{1,0:T(8,128)(2,1)S(1)}, bf16[256,256]{1,0:T(8,128)(2,1)S(1)}, u32[]{:S(2)}, u32[]{:S(2)}) collective-permute-start(bf16[256,256]{1,0:T(8,128)(2,1)S(1)} %get-tuple-element.72), channel_id=1, source_target_pairs={{0,16},{4,20},{8,24},{12,28},{16,0},{20,4},{24,8},{28,12},{1,17},{... | collective-permute-start | bytes 393224 | tf_op jit(solution)/shard_map/ppermute | solution.py:314
  38.8 1.6 %collective-permute-start.10 = (bf16[128,512]{1,0:T(8,128)(2,1)S(1)}, bf16[128,512]{1,0:T(8,128)(2,1)S(1)}, u32[]{:S(2)}, u32[]{:S(2)}) collective-permute-start(bf16[128,512]{1,0:T(8,128)(2,1)S(1)} %get-tuple-element.63), channel_id=1, source_target_pairs={{0,8},{4,12},{8,0},{12,4},{16,24},{20,28},{24,16},{28,20},{1,9},{5... | collective-permute-start | bytes 393224 | tf_op jit(solution)/shard_map/ppermute | solution.py:314
  40.4 3.4 %collective-permute-done.14.other_ref = bf16[256,256]{1,0:T(8,128)(2,1)S(1)} collective-permute-done((bf16[256,256]{1,0:T(8,128)(2,1)S(1)}, bf16[256,256]{1,0:T(8,128)(2,1)S(1)}, u32[]{:S(2)}, u32[]{:S(2)}) %collective-permute-start.14) | collective-permute-done | bytes 131104 | tf_op jit(solution)/shard_map/ppermute | solution.py:314
  43.8 1.6 %collective-permute-start.15 = (bf16[256,256]{1,0:T(8,128)(2,1)S(1)}, bf16[256,256]{1,0:T(8,128)(2,1)S(1)}, u32[]{:S(2)}, u32[]{:S(2)}) collective-permute-start(bf16[256,256]{1,0:T(8,128)(2,1)S(1)} %step_r.5.near_r), channel_id=1, source_target_pairs={{0,4},{4,0},{8,12},{12,8},{16,20},{20,16},{24,28},{28,24},{1,5},{5... | collective-permute-start | bytes 393224 | tf_op jit(solution)/shard_map/ppermute | solution.py:314
  45.5 0.0 collective-permute-done.10.other_ref
  45.5 1.2 %collective-permute-start.11 = (bf16[64,512]{1,0:T(8,128)(2,1)S(1)}, bf16[64,512]{1,0:T(8,128)(2,1)S(1)}, u32[]{:S(2)}, u32[]{:S(2)}) collective-permute-start(bf16[64,512]{1,0:T(8,128)(2,1)S(1)} %get-tuple-element.65), channel_id=1, source_target_pairs={{0,16},{4,20},{8,24},{12,28},{16,0},{20,4},{24,8},{28,12},{1,17},{... | collective-permute-start | bytes 196616 | tf_op jit(solution)/shard_map/ppermute | solution.py:314
  46.7 4.7 %collective-permute-done.11.other_ref = bf16[64,512]{1,0:T(8,128)(2,1)S(1)} collective-permute-done((bf16[64,512]{1,0:T(8,128)(2,1)S(1)}, bf16[64,512]{1,0:T(8,128)(2,1)S(1)}, u32[]{:S(2)}, u32[]{:S(2)}) %collective-permute-start.11) | collective-permute-done | bytes 65568 | tf_op jit(solution)/shard_map/ppermute | solution.py:314
  51.5 0.0 collective-permute-done.15.far_r
  51.5 0.5 field.1
  51.9 0.1 collective-permute-start.16
  52.0 1.2 %collective-permute-done.16 = f32[2,64,128]{2,1,0:T(8,128)S(1)} collective-permute-done((f32[2,64,128]{2,1,0:T(8,128)S(1)}, f32[2,64,128]{2,1,0:T(8,128)S(1)}, u32[]{:S(2)}, u32[]{:S(2)}) %collective-permute-start.16) | collective-permute-done | bytes 65568 | tf_op jit(solution)/shard_map/ppermute | solution.py:314
  53.3 0.7 %maximum_bitcast_fusion = f32[2,2,128,64]{2,3,1,0:T(8,128)} fusion(f32[1,2,64,128]{3,2,1,0:T(8,128)S(1)} %get-tuple-element.76, f32[1,2,64,128]{3,2,1,0:T(8,128)S(1)} %get-tuple-element.75), kind=kLoop, calls=%fused_computation | loop fusion | flops 32768 | bytes 262144 | tf_op jit(solution)/shard_map/transpose | solution.py:427
  (17 shorter events, 0.2 us)
Async XLA Ops:
  1.5 1.3 %collective-permute-start = (f32[2,384]{1,0:T(2,128)S(1)}, f32[2,384]{1,0:T(2,128)S(1)}, u32[]{:S(2)}, u32[]{:S(2)}) collective-permute-start(f32[2,384]{1,0:T(2,128)S(1)} %get-tuple-element.41), channel_id=1, source_target_pairs={{0,1},{1,0},{2,3},{3,2},{4,5},{5,4},{6,7},{7,6},{8,9},{9,8},{10,11... | collective-permute-start | bytes 9224 | tf_op jit(solution)/shard_map/ppermute | solution.py:314
  2.0 6.0 %collective-permute-start.4 = (bf16[2,320,256]{2,1,0:T(8,128)(2,1)S(1)}, bf16[2,320,256]{2,1,0:T(8,128)(2,1)S(1)}, u32[]{:S(2)}, u32[]{:S(2)}) collective-permute-start(bf16[2,320,256]{2,1,0:T(8,128)(2,1)S(1)} %get-tuple-element.45), channel_id=1, source_target_pairs={{0,1},{1,0},{2,3},{3,2},{4,5},{5,4},{6,7},{7,6},{8,9},{9,8},{10,11... | collective-permute-start | bytes 983048 | tf_op jit(solution)/shard_map/ppermute | solution.py:314
  2.8 5.2 %collective-permute-start.1 = (f32[3,384]{1,0:T(4,128)S(1)}, f32[3,384]{1,0:T(4,128)S(1)}, u32[]{:S(2)}, u32[]{:S(2)}) collective-permute-start(f32[3,384]{1,0:T(4,128)S(1)} %pad_maximum_fusion), channel_id=1, source_target_pairs={{0,2},{1,3},{2,0},{3,1},{4,6},{5,7},{6,4},{7,5},{8,10},{9,11},{10,... | collective-permute-start | bytes 13832 | tf_op jit(solution)/shard_map/ppermute | solution.py:314
  7.9 12.4 %collective-permute-start.7 = (s16[640,512]{1,0:T(8,128)(2,1)S(1)}, s16[640,512]{1,0:T(8,128)(2,1)S(1)}, u32[]{:S(2)}, u32[]{:S(2)}) collective-permute-start(s16[640,512]{1,0:T(8,128)(2,1)S(1)} %get-tuple-element.48), channel_id=1, source_target_pairs={{0,1},{1,0},{2,3},{3,2},{4,5},{5,4},{6,7},{7,6},{8,9},{9,8},{10,11... | collective-permute-start | bytes 1966088 | tf_op jit(solution)/shard_map/ppermute | solution.py:314
  8.2 17.8 %collective-permute-start.8 = (bf16[2,2,320,256]{3,2,1,0:T(8,128)(2,1)S(1)}, bf16[2,2,320,256]{3,2,1,0:T(8,128)(2,1)S(1)}, u32[]{:S(2)}, u32[]{:S(2)}) collective-permute-start(bf16[2,2,320,256]{3,2,1,0:T(8,128)(2,1)S(1)} %get-tuple-element.55), channel_id=1, source_target_pairs={{0,2},{1,3},{2,0},{3,1},{4,6},{5,7},{6,4},{7,5},{8,10},{9,11},{10,... | collective-permute-start | bytes 1966088 | tf_op jit(solution)/shard_map/ppermute | solution.py:314
  9.6 10.2 %collective-permute-start.5 = (bf16[2,2,320,128]{3,2,1,0:T(8,128)(2,1)S(1)}, bf16[2,2,320,128]{3,2,1,0:T(8,128)(2,1)S(1)}, u32[]{:S(2)}, u32[]{:S(2)}) collective-permute-start(bf16[2,2,320,128]{3,2,1,0:T(8,128)(2,1)S(1)} %get-tuple-element.46), channel_id=1, source_target_pairs={{0,4},{4,0},{8,12},{12,8},{16,20},{20,16},{24,28},{28,24},{1,5},{5... | collective-permute-start | bytes 983048 | tf_op jit(solution)/shard_map/ppermute | solution.py:314
  11.1 3.8 %collective-permute-start.2 = (f32[1,384]{1,0:T(1,128)S(1)}, f32[1,384]{1,0:T(1,128)S(1)}, u32[]{:S(2)}, u32[]{:S(2)}) collective-permute-start(f32[1,384]{1,0:T(1,128)S(1)} %gate.4.token_ref), channel_id=1, source_target_pairs={{0,8},{4,12},{8,0},{12,4},{16,24},{20,28},{24,16},{28,20},{1,9},{5... | collective-permute-start | bytes 4616 | tf_op jit(solution)/shard_map/ppermute | solution.py:314
  14.9 4.9 %collective-permute-start.3 = (f32[1,384]{1,0:T(1,128)S(1)}, f32[1,384]{1,0:T(1,128)S(1)}, u32[]{:S(2)}, u32[]{:S(2)}) collective-permute-start(f32[1,384]{1,0:T(1,128)S(1)} %gate.5), channel_id=1, source_target_pairs={{0,16},{4,20},{8,24},{12,28},{16,0},{20,4},{24,8},{28,12},{1,17},{... | collective-permute-start | bytes 4616 | tf_op jit(solution)/shard_map/ppermute | solution.py:314
  19.8 3.7 %collective-permute-start.6 = (f32[3,384]{1,0:T(4,128)S(1)}, f32[3,384]{1,0:T(4,128)S(1)}, u32[]{:S(2)}, u32[]{:S(2)}) collective-permute-start(f32[3,384]{1,0:T(4,128)S(1)} %gate.6), channel_id=1, source_target_pairs={{0,4},{4,0},{8,12},{12,8},{16,20},{20,16},{24,28},{28,24},{1,5},{5... | collective-permute-start | bytes 13832 | tf_op jit(solution)/shard_map/ppermute | solution.py:314
  25.2 5.0 %collective-permute-start.12 = (bf16[256,256]{1,0:T(8,128)(2,1)S(1)}, bf16[256,256]{1,0:T(8,128)(2,1)S(1)}, u32[]{:S(2)}, u32[]{:S(2)}) collective-permute-start(bf16[256,256]{1,0:T(8,128)(2,1)S(1)} %get-tuple-element.67), channel_id=1, source_target_pairs={{0,2},{1,3},{2,0},{3,1},{4,6},{5,7},{6,4},{7,5},{8,10},{9,11},{10,... | collective-permute-start | bytes 393224 | tf_op jit(solution)/shard_map/ppermute | solution.py:314
  28.6 7.3 %collective-permute-start.9 = (bf16[256,512]{1,0:T(8,128)(2,1)S(1)}, bf16[256,512]{1,0:T(8,128)(2,1)S(1)}, u32[]{:S(2)}, u32[]{:S(2)}) collective-permute-start(bf16[256,512]{1,0:T(8,128)(2,1)S(1)} %get-tuple-element.61), channel_id=1, source_target_pairs={{0,4},{4,0},{8,12},{12,8},{16,20},{20,16},{24,28},{28,24},{1,5},{5... | collective-permute-start | bytes 786440 | tf_op jit(solution)/shard_map/ppermute | solution.py:314
  30.3 5.8 %collective-permute-start.13 = (bf16[256,256]{1,0:T(8,128)(2,1)S(1)}, bf16[256,256]{1,0:T(8,128)(2,1)S(1)}, u32[]{:S(2)}, u32[]{:S(2)}) collective-permute-start(bf16[256,256]{1,0:T(8,128)(2,1)S(1)} %get-tuple-element.69), channel_id=1, source_target_pairs={{0,8},{4,12},{8,0},{12,4},{16,24},{20,28},{24,16},{28,20},{1,9},{5... | collective-permute-start | bytes 393224 | tf_op jit(solution)/shard_map/ppermute | solution.py:314
  36.1 7.6 %collective-permute-start.14 = (bf16[256,256]{1,0:T(8,128)(2,1)S(1)}, bf16[256,256]{1,0:T(8,128)(2,1)S(1)}, u32[]{:S(2)}, u32[]{:S(2)}) collective-permute-start(bf16[256,256]{1,0:T(8,128)(2,1)S(1)} %get-tuple-element.72), channel_id=1, source_target_pairs={{0,16},{4,20},{8,24},{12,28},{16,0},{20,4},{24,8},{28,12},{1,17},{... | collective-permute-start | bytes 393224 | tf_op jit(solution)/shard_map/ppermute | solution.py:314
  38.8 6.7 %collective-permute-start.10 = (bf16[128,512]{1,0:T(8,128)(2,1)S(1)}, bf16[128,512]{1,0:T(8,128)(2,1)S(1)}, u32[]{:S(2)}, u32[]{:S(2)}) collective-permute-start(bf16[128,512]{1,0:T(8,128)(2,1)S(1)} %get-tuple-element.63), channel_id=1, source_target_pairs={{0,8},{4,12},{8,0},{12,4},{16,24},{20,28},{24,16},{28,20},{1,9},{5... | collective-permute-start | bytes 393224 | tf_op jit(solution)/shard_map/ppermute | solution.py:314
  43.8 7.7 %collective-permute-start.15 = (bf16[256,256]{1,0:T(8,128)(2,1)S(1)}, bf16[256,256]{1,0:T(8,128)(2,1)S(1)}, u32[]{:S(2)}, u32[]{:S(2)}) collective-permute-start(bf16[256,256]{1,0:T(8,128)(2,1)S(1)} %step_r.5.near_r), channel_id=1, source_target_pairs={{0,4},{4,0},{8,12},{12,8},{16,20},{20,16},{24,28},{28,24},{1,5},{5... | collective-permute-start | bytes 393224 | tf_op jit(solution)/shard_map/ppermute | solution.py:314
  45.5 5.9 %collective-permute-start.11 = (bf16[64,512]{1,0:T(8,128)(2,1)S(1)}, bf16[64,512]{1,0:T(8,128)(2,1)S(1)}, u32[]{:S(2)}, u32[]{:S(2)}) collective-permute-start(bf16[64,512]{1,0:T(8,128)(2,1)S(1)} %get-tuple-element.65), channel_id=1, source_target_pairs={{0,16},{4,20},{8,24},{12,28},{16,0},{20,4},{24,8},{28,12},{1,17},{... | collective-permute-start | bytes 196616 | tf_op jit(solution)/shard_map/ppermute | solution.py:314
  51.9 1.3 %collective-permute-start.16 = (f32[2,64,128]{2,1,0:T(8,128)S(1)}, f32[2,64,128]{2,1,0:T(8,128)S(1)}, u32[]{:S(2)}, u32[]{:S(2)}) collective-permute-start(f32[2,64,128]{2,1,0:T(8,128)S(1)} %get-tuple-element.74), channel_id=1, source_target_pairs={{0,1},{1,0},{2,3},{3,2},{4,5},{5,4},{6,7},{7,6},{8,9},{9,8},{10,11... | collective-permute-start | bytes 196616 | tf_op jit(solution)/shard_map/ppermute | solution.py:314

commit v4 on v3

--- a/solution.py
+++ b/solution.py
@@ -69,20 +69,20 @@
     )(*held)
 
 
-def power_kernel(wl_ref, spec_ref, own_note, away_note, own_ref, away_ref, wl_held, sems):
+def power_kernel(wl_ref, spec_ref, notes_ref, own_ref, away_ref, wl_held, sems):
     row, col, core, *_ = place()
     n_col = lax.axis_size("col")
     _, parts, per, windows = spec_ref.shape
     wl_copy = pltpu.make_async_copy(wl_ref, wl_held, sems.at[2])
     wl_copy.start()
-    both = ((core, own_note, own_ref), (1 - core, away_note, away_ref))
-    copies = [pltpu.make_async_copy(spec_ref.at[f], held, sems.at[i]) for i, (f, _, held) in enumerate(both)]
+    both = ((core, own_ref), (1 - core, away_ref))
+    copies = [pltpu.make_async_copy(spec_ref.at[f], held, sems.at[i]) for i, (f, held) in enumerate(both)]
     for copy in copies:
         copy.start()
     ids = (row * n_col + col) * per + lax.broadcasted_iota(jnp.int32, (1, per), 1)
-    rest = jnp.zeros((own_note.shape[1] - per, LANES), jnp.float32)
+    rest = jnp.zeros((notes_ref.shape[1] - per, LANES), jnp.float32)
     wl_copy.wait()
-    for (f, note, held), copy in zip(both, copies):
+    for at, ((f, held), copy) in enumerate(zip(both, copies)):
         copy.wait()
         squares = jnp.square(held[...].astype(jnp.float32))
         squares = squares[0] + squares[1]
@@ -90,8 +90,8 @@
         columns = jnp.transpose(jnp.concatenate([squares, rest], axis=0))
         power = jnp.sum(columns, axis=0, keepdims=True)
         level = jnp.sum(jnp.where(ids == wl_held[f], power[:, :per], 0.0), axis=1, keepdims=True)
-        note[0:1, :] = power
-        note[1:2, :] = jnp.broadcast_to(level, power.shape)
+        notes_ref[2 * at : 2 * at + 1, :] = power
+        notes_ref[2 * at + 1 : 2 * at + 2, :] = jnp.broadcast_to(level, power.shape)
 
 
 def gate_kernel(n, *refs):
@@ -151,10 +151,11 @@
 def steer_far_kernel(starts, parts, token_ref, delays_ref, cos_ref, sin_ref, out_ref, *refs):
     *copy_ref, held_ref, sems = refs
     out_ref[...] = token_ref[...]
-    per = cos_ref.shape[0] // 2
+    firsts = starts()
+    per = cos_ref.shape[0] // len(firsts)
     rows = per // parts
     blocks = []
-    for j, first in enumerate(starts()):
+    for j, first in enumerate(firsts):
         for part in range(parts):
             index = j * parts + part
             here = pl.ds(index * rows, rows)
@@ -170,17 +171,17 @@
     return kernel_call(steer_kernel, out, [token, delays], [pltpu.VMEM] * 2, name="steering")
 
 
-def steering_far(starts, rows, token, delays, copied=()):
-    width = delays.shape[1]
-    parts = math.gcd(rows // (2 * CHUNK), 5)
+def steering_far(starts, per, blocks, token, delays, copied=()):
+    parts = math.gcd(per // CHUNK, 5)
+    shape = (per * blocks, delays.shape[1])
     return kernel_call(
         functools.partial(steer_far_kernel, starts, parts),
-        [vmem((rows, width), jnp.bfloat16)] * 2
+        [vmem(shape, jnp.bfloat16)] * 2
         + [vmem(token.shape, token.dtype)]
-        + [vmem((rows, width), t) for t in copied],
+        + [vmem(shape, t) for t in copied],
         [token, delays],
         [pltpu.VMEM, pltpu.HBM],
-        scratch=[pltpu.VMEM((rows, width), delays.dtype), pltpu.SemaphoreType.DMA((2 * parts,))],
+        scratch=[pltpu.VMEM(shape, delays.dtype), pltpu.SemaphoreType.DMA((blocks * parts,))],
         name="steering_far",
     )
 
@@ -208,9 +209,7 @@
             spec = near_ref[part, :, windows] if at < 2 else from_ref[at - 2, part]
             parts.append(spec.astype(jnp.float32) * gain)
     total = None
-    count = len(steer) // 2
-    for group in range(count):
-        members = order[group * 4 // count : (group + 1) * 4 // count]
+    for group, members in enumerate(order):
         re, im = (jnp.concatenate([p[m] for m in members], axis=0).astype(jnp.bfloat16) for p in (real, imag))
         for left, right in (((re, im), steer[2 * group]), ((-im, re), steer[2 * group + 1])):
             term = lax.dot_general(
@@ -337,39 +336,39 @@
     half = windows // 2
     padded = -(-per // LANES) * LANES
 
-    spec_shape, note_shape = vmem((parts, per, windows), spectra.dtype), vmem((2, padded), jnp.float32)
-    note, away_note, own, away = kernel_call(
+    spec_shape = vmem((parts, per, windows), spectra.dtype)
+    notes, own, away = kernel_call(
         power_kernel,
-        [note_shape, note_shape, spec_shape, spec_shape],
+        [vmem((4, padded), jnp.float32), spec_shape, spec_shape],
         [wl_index, spectra],
         [pltpu.HBM, pltpu.HBM],
         scratch=[pltpu.SMEM(wl_index.shape, wl_index.dtype), pltpu.SemaphoreType.DMA((3,))],
         name="power",
     )
-    other_note, other = swap(away_note, "col", 1), swap(away, "col", 1)
-    power = jnp.concatenate([note[:1], other_note[:1]])
-    level = note[1:] + other_note[1:]
-
-    def rows_r():
+    other = swap(away, "col", 1)
+
+    def starts_r():
         return [(place()[0] ^ j) * per for j in (0, 1)]
 
-    def rows_s(j):
-        return lambda: [block_of(j, at) * per for at in (0, 1)]
-
-    far_x = swap(jnp.concatenate([power, level]), "col", 2)
-    *steer_r, token, near_r = steering_far(rows_r, 2 * per, note[1:], delays_r, [jnp.int16])
+    def starts_s(first, last):
+        return lambda: [block_of(j, at) * per for j, at in ((0, 0), (0, 1), (1, 0), (1, 1))[first:last]]
+
+    far = swap(notes, "col", 2)
+    *steer_r, token, near_r = steering_far(starts_r, per, 2, notes[:1], delays_r, [jnp.int16])
     other_r = swap(near_r, "col", 1)
-    level = gated([level + far_x[2:]], [token])
+    across = swap(gated([notes[2:], far[2:]], [token]), "col", 1)
+    power, far_x = jnp.concatenate([notes[:1], across[:1]]), jnp.concatenate([far[:1], across[2:3]])
+    level = (notes[1:2] + far[1:2]) + (across[1:2] + across[3:])
 
     sent = [vmem((2, parts, per, w), spectra.dtype) for w in (windows, half)]
     to_x, to_y = kernel_call(send_kernel, sent, [level, own, other], [pltpu.VMEM] * 3, name="send")
     from_x, from_y = swap(to_x, "col", 2), swap(to_y, "row", 1)
 
     row_bits, col_bits = bits(n_row, 2), bits(n_col, 4)
-    *steer_s, token = steering_far(rows_s(0), 2 * per, level, delays_s)
     first, *others = [("row", bit) for bit in row_bits] + [("col", bit) for bit in col_bits]
+    *steer_s, token = steering_far(starts_s(0, 2), per, 2, level, delays_s)
     level = level + swap(level, *first)
-    cos, sin, next_token = steering_far(rows_s(1), 2 * per, level, delays_s)
+    cos, sin, next_token = steering_far(starts_s(2, 4), per, 2, level, delays_s)
     steer_s += [cos, sin]
     for step in others:
         level = gated([level], [token])
@@ -381,7 +380,7 @@
 
     block_r, block_s = 2 * delays_r.shape[1] // n_col, delays_s.shape[1] // n_row
     keep_r, send_r, token = beams(
-        (0, 2, 1, 3),
+        ((0, 2), (1, 3)),
         lambda half: pl.ds(pl.multiple_of(y_of() * half, half), half),
         block_r,
         lambda: place()[3],
@@ -395,7 +394,7 @@
         "beams_r",
     )
     keep_s, send_s, _ = beams(
-        (0, 1, 2, 3), lambda windows: slice(None), block_s, y_of, power, far_x, token, own, other, from_x, steer_s, "beams_s"
+        ((0, 1), (2, 3)), lambda windows: slice(None), block_s, y_of, power, far_x, token, own, other, from_x, steer_s, "beams_s"
     )
     r_steps = [("col", bit, True) for bit in [2, *col_bits]] + [("row", bit, False) for bit in row_bits]
     s_steps = [("row", bit, True) for bit in [1, *row_bits]] + [("col", bit, False) for bit in col_bits]

time: 54.1 us -> 52.7 us (0.974)
  starting transfers between devices: 21.9 us -> 21.1 us
  waiting for transfers between devices: 16.6 us -> 15.9 us
    ppermute x17, starting transfers between devices: 21.9 us -> 21.1 us  [swap(): return lax.ppermute(value, axis, [(i, i ^ bit) for i in range(size)])]
    ppermute x17, waiting for transfers between devices: 16.6 us -> 15.9 us  [swap(): return lax.ppermute(value, axis, [(i, i ^ bit) for i in range(size)])]
  transfers between devices with their start and end apart: 17 -> 17, of which waited for: 7 -> 8; matrix products, arithmetic and copies ran while one was open for 0% -> 0% of each run, Pallas kernels for 23% -> 24%
where the time goes in v4:
time: 52.7 us; the launch traced here: 52.5 us
  starting transfers between devices  21.1 us (40%)
  waiting for transfers between devices  15.9 us (30%)
  Pallas kernels  14.5 us (28%)
  other arithmetic  0.72 us (1%)
    ppermute x17, starting transfers between devices, swap(): return lax.ppermute(value, axis, [(i, i ^ bit) for i in range(size)])  21.1 us
    ppermute x17, waiting for transfers between devices, swap(): return lax.ppermute(value, axis, [(i, i ^ bit) for i in range(size)])  15.9 us
    pallas_call x19, Pallas kernels, kernel_call(): pl.pallas_call(body, out_shape=out, in_specs=[pl.BlockSpec(memory_space=s...  14.5 us
  transfers between devices with their start and end apart: 17, of which 8 were waited for; matrix products, arithmetic and copies ran while one was open for 0% of the time, Pallas kernels for 24%

profile of v4, /device:TPU:0, one launch (start us, length us, event | category | flops | bytes accessed | tf_op | source)
XLA Modules:
  0.0 52.5 jit_solution(13154661295437091092)
XLA Ops:
  0.0 1.5 %power.1 = (f32[4,384]{1,0:T(4,128)S(1)}, bf16[2,320,256]{2,1,0:T(8,128)(2,1)S(1)}, bf16[2,320,256]{2,1,0:T(8,128)(2,1)S(1)}) custom-call(s32[2]{0:T(128)} %wl_ref.1, bf16[2,2,320,256]{3,2,1,0:T(8,128)(2,1)} %spec_ref.1), custom_call_target="tpu_custom_call" | custom-call | flops 1 | bytes 1 | tf_op jit(solution)/shard_map/power/pallas_call | solution.py:60
  1.5 0.5 collective-permute-start.4
  2.0 2.6 %collective-permute-start = (f32[4,384]{1,0:T(4,128)S(1)}, f32[4,384]{1,0:T(4,128)S(1)}, u32[]{:S(2)}, u32[]{:S(2)}) collective-permute-start(f32[4,384]{1,0:T(4,128)S(1)} %get-tuple-element.39), channel_id=1, source_target_pairs={{0,2},{1,3},{2,0},{3,1},{4,6},{5,7},{6,4},{7,5},{8,10},{9,11},{10,... | collective-permute-start | bytes 18440 | tf_op jit(solution)/shard_map/ppermute | solution.py:313
  4.6 2.2 %steering_far.3 = (bf16[640,512]{1,0:T(8,128)(2,1)S(1)}, bf16[640,512]{1,0:T(8,128)(2,1)S(1)}, f32[1,384]{1,0:T(1,128)S(1)}, s16[640,512]{1,0:T(8,128)(2,1)S(1)}) custom-call(f32[1,384]{1,0:T(1,128)S(1)} %slice.34.token_ref, s32[2560,512]{1,0:T(8,128)} %delays_ref.3), custom_call_target="tpu_custom_call" | custom-call | flops 1 | bytes 1 | tf_op jit(solution)/shard_map/steering_far/pallas_call | solution.py:60
  6.8 0.0 collective-permute-done
  6.8 0.2 collective-permute-start.1
  7.0 0.3 collective-permute-start.7
  7.4 0.7 %collective-permute-done.1 = f32[4,384]{1,0:T(4,128)S(1)} collective-permute-done((f32[4,384]{1,0:T(4,128)S(1)}, f32[4,384]{1,0:T(4,128)S(1)}, u32[]{:S(2)}, u32[]{:S(2)}) %collective-permute-start.1) | collective-permute-done | bytes 6176 | tf_op jit(solution)/shard_map/ppermute | solution.py:313
  8.0 0.0 collective-permute-done.4.other_ref
  8.1 0.1 send.1
  8.2 1.6 %collective-permute-start.5 = (bf16[2,2,320,128]{3,2,1,0:T(8,128)(2,1)S(1)}, bf16[2,2,320,128]{3,2,1,0:T(8,128)(2,1)S(1)}, u32[]{:S(2)}, u32[]{:S(2)}) collective-permute-start(bf16[2,2,320,128]{3,2,1,0:T(8,128)(2,1)S(1)} %get-tuple-element.44), channel_id=1, source_target_pairs={{0,4},{4,0},{8,12},{12,8},{16,20},{20,16},{24,28},{28,24},{1,5},{5... | collective-permute-start | bytes 983048 | tf_op jit(solution)/shard_map/ppermute | solution.py:313
  9.8 1.4 %collective-permute-start.8 = (bf16[2,2,320,256]{3,2,1,0:T(8,128)(2,1)S(1)}, bf16[2,2,320,256]{3,2,1,0:T(8,128)(2,1)S(1)}, u32[]{:S(2)}, u32[]{:S(2)}) collective-permute-start(bf16[2,2,320,256]{3,2,1,0:T(8,128)(2,1)S(1)} %get-tuple-element.53), channel_id=1, source_target_pairs={{0,2},{1,3},{2,0},{3,1},{4,6},{5,7},{6,4},{7,5},{8,10},{9,11},{10,... | collective-permute-start | bytes 1966088 | tf_op jit(solution)/shard_map/ppermute | solution.py:313
  11.2 1.6 %collective-permute-start.2 = (f32[1,384]{1,0:T(1,128)S(1)}, f32[1,384]{1,0:T(1,128)S(1)}, u32[]{:S(2)}, u32[]{:S(2)}) collective-permute-start(f32[1,384]{1,0:T(1,128)S(1)} %get-tuple-element.75.token_ref), channel_id=1, source_target_pairs={{0,8},{4,12},{8,0},{12,4},{16,24},{20,28},{24,16},{28,20},{1,9},{5... | collective-permute-start | bytes 4616 | tf_op jit(solution)/shard_map/ppermute | solution.py:313
  12.7 2.2 %steering_far.4 = (bf16[640,512]{1,0:T(8,128)(2,1)S(1)}, bf16[640,512]{1,0:T(8,128)(2,1)S(1)}, f32[1,384]{1,0:T(1,128)S(1)}) custom-call(f32[1,384]{1,0:T(1,128)S(1)} %get-tuple-element.75.token_ref, s32[1280,512]{1,0:T(8,128)} %delays_ref.5), custom_call_target="tpu_custom_call" | custom-call | flops 1 | bytes 1 | tf_op jit(solution)/shard_map/steering_far/pallas_call | solution.py:60
  14.9 0.0 collective-permute-done.2
  15.0 2.7 %collective-permute-start.3 = (f32[1,384]{1,0:T(1,128)S(1)}, f32[1,384]{1,0:T(1,128)S(1)}, u32[]{:S(2)}, u32[]{:S(2)}) collective-permute-start(f32[1,384]{1,0:T(1,128)S(1)} %gate.5), channel_id=1, source_target_pairs={{0,16},{4,20},{8,24},{12,28},{16,0},{20,4},{24,8},{28,12},{1,17},{... | collective-permute-start | bytes 4616 | tf_op jit(solution)/shard_map/ppermute | solution.py:313
  17.6 2.2 %steering_far.5 = (bf16[640,512]{1,0:T(8,128)(2,1)S(1)}, bf16[640,512]{1,0:T(8,128)(2,1)S(1)}, f32[1,384]{1,0:T(1,128)S(1)}) custom-call(f32[1,384]{1,0:T(1,128)S(1)} %add.21.refs_0_.token_ref, s32[1280,512]{1,0:T(8,128)} %delays_ref.5), custom_call_target="tpu_custom_call" | custom-call | flops 1 | bytes 1 | tf_op jit(solution)/shard_map/steering_far/pallas_call | solution.py:60
  19.8 0.0 collective-permute-done.3
  19.8 0.0 collective-permute-done.5.refs_2_.from_ref
  19.9 0.6 %collective-permute-start.6 = (f32[3,384]{1,0:T(4,128)S(1)}, f32[3,384]{1,0:T(4,128)S(1)}, u32[]{:S(2)}, u32[]{:S(2)}) collective-permute-start(f32[3,384]{1,0:T(4,128)S(1)} %gate.6), channel_id=1, source_target_pairs={{0,4},{4,0},{8,12},{12,8},{16,20},{20,16},{24,28},{28,24},{1,5},{5... | collective-permute-start | bytes 13832 | tf_op jit(solution)/shard_map/ppermute | solution.py:313
  20.4 0.0 collective-permute-done.7.delays_ref
  20.4 1.2 %steering.1 = (bf16[640,512]{1,0:T(8,128)(2,1)S(1)}, bf16[640,512]{1,0:T(8,128)(2,1)S(1)}, f32[1,384]{1,0:T(1,128)S(1)}) custom-call(f32[1,384]{1,0:T(1,128)S(1)} %add.22.refs_1_.token_ref, s16[640,512]{1,0:T(8,128)(2,1)S(1)} %collective-permute-done.7.delays_ref), custom_call_target="tpu_custom_call" | custom-call | flops 1 | bytes 1 | tf_op jit(solution)/shard_map/steering/pallas_call | solution.py:60
  21.7 1.9 %collective-permute-done.6.far_ref = f32[3,384]{1,0:T(4,128)S(1)} collective-permute-done((f32[3,384]{1,0:T(4,128)S(1)}, f32[3,384]{1,0:T(4,128)S(1)}, u32[]{:S(2)}, u32[]{:S(2)}) %collective-permute-start.6) | collective-permute-done | bytes 4640 | tf_op jit(solution)/shard_map/ppermute | solution.py:313
  23.6 1.7 %beams_r.1 = (f32[256,256]{1,0:T(8,128)S(1)}, bf16[256,256]{1,0:T(8,128)(2,1)S(1)}, f32[1,384]{1,0:T(1,128)S(1)}) custom-call(f32[2,384]{1,0:T(2,128)S(1)} %pad_maximum_fusion.refs_0_.near_power_ref, f32[3,384]{1,0:T(4,128)S(1)} %collective-permute-done.6.far_ref, f32[1,384]{1,0:T(1,128)S(1)} %gate.7.level_ref.token_ref, ...), custom_call_target="tpu_custom_call" | custom-call | flops 1 | bytes 1 | tf_op jit(solution)/shard_map/beams_r/pallas_call | solution.py:60
  25.3 0.7 %collective-permute-start.12 = (bf16[256,256]{1,0:T(8,128)(2,1)S(1)}, bf16[256,256]{1,0:T(8,128)(2,1)S(1)}, u32[]{:S(2)}, u32[]{:S(2)}) collective-permute-start(bf16[256,256]{1,0:T(8,128)(2,1)S(1)} %get-tuple-element.65), channel_id=1, source_target_pairs={{0,2},{1,3},{2,0},{3,1},{4,6},{5,7},{6,4},{7,5},{8,10},{9,11},{10,... | collective-permute-start | bytes 393224 | tf_op jit(solution)/shard_map/ppermute | solution.py:313
  26.0 0.4 collective-permute-done.8.from_ref
  26.4 2.7 %beams_s.1 = (f32[256,512]{1,0:T(8,128)S(1)}, bf16[256,512]{1,0:T(8,128)(2,1)S(1)}, f32[1,384]{1,0:T(1,128)}) custom-call(f32[2,384]{1,0:T(2,128)S(1)} %pad_maximum_fusion.refs_0_.near_power_ref, f32[2,384]{1,0:T(2,128)S(1)} %pad_maximum_fusion.1.far_ref, f32[1,384]{1,0:T(1,128)S(1)} %get-tuple-element.52.level_ref, ...), custom_call_target="tpu_custom_call" | custom-call | flops 1 | bytes 1 | tf_op jit(solution)/shard_map/beams_s/pallas_call | solution.py:60
  29.1 0.5 collective-permute-start.9
  29.6 0.7 %collective-permute-done.12.other_ref = bf16[256,256]{1,0:T(8,128)(2,1)S(1)} collective-permute-done((bf16[256,256]{1,0:T(8,128)(2,1)S(1)}, bf16[256,256]{1,0:T(8,128)(2,1)S(1)}, u32[]{:S(2)}, u32[]{:S(2)}) %collective-permute-start.12) | collective-permute-done | bytes 131104 | tf_op jit(solution)/shard_map/ppermute | solution.py:313
  30.3 1.5 %collective-permute-start.13 = (bf16[256,256]{1,0:T(8,128)(2,1)S(1)}, bf16[256,256]{1,0:T(8,128)(2,1)S(1)}, u32[]{:S(2)}, u32[]{:S(2)}) collective-permute-start(bf16[256,256]{1,0:T(8,128)(2,1)S(1)} %get-tuple-element.67), channel_id=1, source_target_pairs={{0,8},{4,12},{8,0},{12,4},{16,24},{20,28},{24,16},{28,20},{1,9},{5... | collective-permute-start | bytes 393224 | tf_op jit(solution)/shard_map/ppermute | solution.py:313
  31.8 4.3 %collective-permute-done.9.other_ref = bf16[256,512]{1,0:T(8,128)(2,1)S(1)} collective-permute-done((bf16[256,512]{1,0:T(8,128)(2,1)S(1)}, bf16[256,512]{1,0:T(8,128)(2,1)S(1)}, u32[]{:S(2)}, u32[]{:S(2)}) %collective-permute-start.9) | collective-permute-done | bytes 262176 | tf_op jit(solution)/shard_map/ppermute | solution.py:313
  36.2 0.1 step_s.3
  36.3 0.0 collective-permute-done.13.other_ref
  36.4 2.9 %collective-permute-start.14 = (bf16[256,256]{1,0:T(8,128)(2,1)S(1)}, bf16[256,256]{1,0:T(8,128)(2,1)S(1)}, u32[]{:S(2)}, u32[]{:S(2)}) collective-permute-start(bf16[256,256]{1,0:T(8,128)(2,1)S(1)} %get-tuple-element.70), channel_id=1, source_target_pairs={{0,16},{4,20},{8,24},{12,28},{16,0},{20,4},{24,8},{28,12},{1,17},{... | collective-permute-start | bytes 393224 | tf_op jit(solution)/shard_map/ppermute | solution.py:313
  39.3 1.6 %collective-permute-start.10 = (bf16[128,512]{1,0:T(8,128)(2,1)S(1)}, bf16[128,512]{1,0:T(8,128)(2,1)S(1)}, u32[]{:S(2)}, u32[]{:S(2)}) collective-permute-start(bf16[128,512]{1,0:T(8,128)(2,1)S(1)} %get-tuple-element.61), channel_id=1, source_target_pairs={{0,8},{4,12},{8,0},{12,4},{16,24},{20,28},{24,16},{28,20},{1,9},{5... | collective-permute-start | bytes 393224 | tf_op jit(solution)/shard_map/ppermute | solution.py:313
  40.8 3.0 %collective-permute-done.14.other_ref = bf16[256,256]{1,0:T(8,128)(2,1)S(1)} collective-permute-done((bf16[256,256]{1,0:T(8,128)(2,1)S(1)}, bf16[256,256]{1,0:T(8,128)(2,1)S(1)}, u32[]{:S(2)}, u32[]{:S(2)}) %collective-permute-start.14) | collective-permute-done | bytes 131104 | tf_op jit(solution)/shard_map/ppermute | solution.py:313
  43.8 0.9 %collective-permute-start.15 = (bf16[256,256]{1,0:T(8,128)(2,1)S(1)}, bf16[256,256]{1,0:T(8,128)(2,1)S(1)}, u32[]{:S(2)}, u32[]{:S(2)}) collective-permute-start(bf16[256,256]{1,0:T(8,128)(2,1)S(1)} %step_r.5.near_r), channel_id=1, source_target_pairs={{0,4},{4,0},{8,12},{12,8},{16,20},{20,16},{24,28},{28,24},{1,5},{5... | collective-permute-start | bytes 393224 | tf_op jit(solution)/shard_map/ppermute | solution.py:313
  44.7 0.0 collective-permute-done.10.other_ref
  44.8 1.6 %collective-permute-start.11 = (bf16[64,512]{1,0:T(8,128)(2,1)S(1)}, bf16[64,512]{1,0:T(8,128)(2,1)S(1)}, u32[]{:S(2)}, u32[]{:S(2)}) collective-permute-start(bf16[64,512]{1,0:T(8,128)(2,1)S(1)} %get-tuple-element.63), channel_id=1, source_target_pairs={{0,16},{4,20},{8,24},{12,28},{16,0},{20,4},{24,8},{28,12},{1,17},{... | collective-permute-start | bytes 196616 | tf_op jit(solution)/shard_map/ppermute | solution.py:313
  46.3 3.7 %collective-permute-done.11.other_ref = bf16[64,512]{1,0:T(8,128)(2,1)S(1)} collective-permute-done((bf16[64,512]{1,0:T(8,128)(2,1)S(1)}, bf16[64,512]{1,0:T(8,128)(2,1)S(1)}, u32[]{:S(2)}, u32[]{:S(2)}) %collective-permute-start.11) | collective-permute-done | bytes 65568 | tf_op jit(solution)/shard_map/ppermute | solution.py:313
  50.0 0.0 collective-permute-done.15.far_r
  50.0 0.5 field.1
  50.5 0.1 collective-permute-start.16
  50.6 1.2 %collective-permute-done.16 = f32[2,64,128]{2,1,0:T(8,128)S(1)} collective-permute-done((f32[2,64,128]{2,1,0:T(8,128)S(1)}, f32[2,64,128]{2,1,0:T(8,128)S(1)}, u32[]{:S(2)}, u32[]{:S(2)}) %collective-permute-start.16) | collective-permute-done | bytes 65568 | tf_op jit(solution)/shard_map/ppermute | solution.py:313
  51.8 0.7 %maximum_bitcast_fusion = f32[2,2,128,64]{2,3,1,0:T(8,128)} fusion(f32[1,2,64,128]{3,2,1,0:T(8,128)S(1)} %get-tuple-element.74, f32[1,2,64,128]{3,2,1,0:T(8,128)S(1)} %get-tuple-element.73), kind=kLoop, calls=%fused_computation | loop fusion | flops 32768 | bytes 262144 | tf_op jit(solution)/shard_map/transpose | solution.py:426
  (19 shorter events, 0.2 us)
Async XLA Ops:
  1.5 6.6 %collective-permute-start.4 = (bf16[2,320,256]{2,1,0:T(8,128)(2,1)S(1)}, bf16[2,320,256]{2,1,0:T(8,128)(2,1)S(1)}, u32[]{:S(2)}, u32[]{:S(2)}) collective-permute-start(bf16[2,320,256]{2,1,0:T(8,128)(2,1)S(1)} %get-tuple-element.43), channel_id=1, source_target_pairs={{0,1},{1,0},{2,3},{3,2},{4,5},{5,4},{6,7},{7,6},{8,9},{9,8},{10,11... | collective-permute-start | bytes 983048 | tf_op jit(solution)/shard_map/ppermute | solution.py:313
  2.0 4.8 %collective-permute-start = (f32[4,384]{1,0:T(4,128)S(1)}, f32[4,384]{1,0:T(4,128)S(1)}, u32[]{:S(2)}, u32[]{:S(2)}) collective-permute-start(f32[4,384]{1,0:T(4,128)S(1)} %get-tuple-element.39), channel_id=1, source_target_pairs={{0,2},{1,3},{2,0},{3,1},{4,6},{5,7},{6,4},{7,5},{8,10},{9,11},{10,... | collective-permute-start | bytes 18440 | tf_op jit(solution)/shard_map/ppermute | solution.py:313
  6.8 1.2 %collective-permute-start.1 = (f32[4,384]{1,0:T(4,128)S(1)}, f32[4,384]{1,0:T(4,128)S(1)}, u32[]{:S(2)}, u32[]{:S(2)}) collective-permute-start(f32[4,384]{1,0:T(4,128)S(1)} %gate.4), channel_id=1, source_target_pairs={{0,1},{1,0},{2,3},{3,2},{4,5},{5,4},{6,7},{7,6},{8,9},{9,8},{10,11... | collective-permute-start | bytes 18440 | tf_op jit(solution)/shard_map/ppermute | solution.py:313
  7.0 13.4 %collective-permute-start.7 = (s16[640,512]{1,0:T(8,128)(2,1)S(1)}, s16[640,512]{1,0:T(8,128)(2,1)S(1)}, u32[]{:S(2)}, u32[]{:S(2)}) collective-permute-start(s16[640,512]{1,0:T(8,128)(2,1)S(1)} %get-tuple-element.46), channel_id=1, source_target_pairs={{0,1},{1,0},{2,3},{3,2},{4,5},{5,4},{6,7},{7,6},{8,9},{9,8},{10,11... | collective-permute-start | bytes 1966088 | tf_op jit(solution)/shard_map/ppermute | solution.py:313
  8.2 11.7 %collective-permute-start.5 = (bf16[2,2,320,128]{3,2,1,0:T(8,128)(2,1)S(1)}, bf16[2,2,320,128]{3,2,1,0:T(8,128)(2,1)S(1)}, u32[]{:S(2)}, u32[]{:S(2)}) collective-permute-start(bf16[2,2,320,128]{3,2,1,0:T(8,128)(2,1)S(1)} %get-tuple-element.44), channel_id=1, source_target_pairs={{0,4},{4,0},{8,12},{12,8},{16,20},{20,16},{24,28},{28,24},{1,5},{5... | collective-permute-start | bytes 983048 | tf_op jit(solution)/shard_map/ppermute | solution.py:313
  9.8 16.6 %collective-permute-start.8 = (bf16[2,2,320,256]{3,2,1,0:T(8,128)(2,1)S(1)}, bf16[2,2,320,256]{3,2,1,0:T(8,128)(2,1)S(1)}, u32[]{:S(2)}, u32[]{:S(2)}) collective-permute-start(bf16[2,2,320,256]{3,2,1,0:T(8,128)(2,1)S(1)} %get-tuple-element.53), channel_id=1, source_target_pairs={{0,2},{1,3},{2,0},{3,1},{4,6},{5,7},{6,4},{7,5},{8,10},{9,11},{10,... | collective-permute-start | bytes 1966088 | tf_op jit(solution)/shard_map/ppermute | solution.py:313
  11.2 3.8 %collective-permute-start.2 = (f32[1,384]{1,0:T(1,128)S(1)}, f32[1,384]{1,0:T(1,128)S(1)}, u32[]{:S(2)}, u32[]{:S(2)}) collective-permute-start(f32[1,384]{1,0:T(1,128)S(1)} %get-tuple-element.75.token_ref), channel_id=1, source_target_pairs={{0,8},{4,12},{8,0},{12,4},{16,24},{20,28},{24,16},{28,20},{1,9},{5... | collective-permute-start | bytes 4616 | tf_op jit(solution)/shard_map/ppermute | solution.py:313
  15.0 4.9 %collective-permute-start.3 = (f32[1,384]{1,0:T(1,128)S(1)}, f32[1,384]{1,0:T(1,128)S(1)}, u32[]{:S(2)}, u32[]{:S(2)}) collective-permute-start(f32[1,384]{1,0:T(1,128)S(1)} %gate.5), channel_id=1, source_target_pairs={{0,16},{4,20},{8,24},{12,28},{16,0},{20,4},{24,8},{28,12},{1,17},{... | collective-permute-start | bytes 4616 | tf_op jit(solution)/shard_map/ppermute | solution.py:313
  19.9 3.7 %collective-permute-start.6 = (f32[3,384]{1,0:T(4,128)S(1)}, f32[3,384]{1,0:T(4,128)S(1)}, u32[]{:S(2)}, u32[]{:S(2)}) collective-permute-start(f32[3,384]{1,0:T(4,128)S(1)} %gate.6), channel_id=1, source_target_pairs={{0,4},{4,0},{8,12},{12,8},{16,20},{20,16},{24,28},{28,24},{1,5},{5... | collective-permute-start | bytes 13832 | tf_op jit(solution)/shard_map/ppermute | solution.py:313
  25.3 5.0 %collective-permute-start.12 = (bf16[256,256]{1,0:T(8,128)(2,1)S(1)}, bf16[256,256]{1,0:T(8,128)(2,1)S(1)}, u32[]{:S(2)}, u32[]{:S(2)}) collective-permute-start(bf16[256,256]{1,0:T(8,128)(2,1)S(1)} %get-tuple-element.65), channel_id=1, source_target_pairs={{0,2},{1,3},{2,0},{3,1},{4,6},{5,7},{6,4},{7,5},{8,10},{9,11},{10,... | collective-permute-start | bytes 393224 | tf_op jit(solution)/shard_map/ppermute | solution.py:313
  29.1 7.1 %collective-permute-start.9 = (bf16[256,512]{1,0:T(8,128)(2,1)S(1)}, bf16[256,512]{1,0:T(8,128)(2,1)S(1)}, u32[]{:S(2)}, u32[]{:S(2)}) collective-permute-start(bf16[256,512]{1,0:T(8,128)(2,1)S(1)} %get-tuple-element.59), channel_id=1, source_target_pairs={{0,4},{4,0},{8,12},{12,8},{16,20},{20,16},{24,28},{28,24},{1,5},{5... | collective-permute-start | bytes 786440 | tf_op jit(solution)/shard_map/ppermute | solution.py:313
  30.3 6.0 %collective-permute-start.13 = (bf16[256,256]{1,0:T(8,128)(2,1)S(1)}, bf16[256,256]{1,0:T(8,128)(2,1)S(1)}, u32[]{:S(2)}, u32[]{:S(2)}) collective-permute-start(bf16[256,256]{1,0:T(8,128)(2,1)S(1)} %get-tuple-element.67), channel_id=1, source_target_pairs={{0,8},{4,12},{8,0},{12,4},{16,24},{20,28},{24,16},{28,20},{1,9},{5... | collective-permute-start | bytes 393224 | tf_op jit(solution)/shard_map/ppermute | solution.py:313
  36.4 7.4 %collective-permute-start.14 = (bf16[256,256]{1,0:T(8,128)(2,1)S(1)}, bf16[256,256]{1,0:T(8,128)(2,1)S(1)}, u32[]{:S(2)}, u32[]{:S(2)}) collective-permute-start(bf16[256,256]{1,0:T(8,128)(2,1)S(1)} %get-tuple-element.70), channel_id=1, source_target_pairs={{0,16},{4,20},{8,24},{12,28},{16,0},{20,4},{24,8},{28,12},{1,17},{... | collective-permute-start | bytes 393224 | tf_op jit(solution)/shard_map/ppermute | solution.py:313
  39.3 5.5 %collective-permute-start.10 = (bf16[128,512]{1,0:T(8,128)(2,1)S(1)}, bf16[128,512]{1,0:T(8,128)(2,1)S(1)}, u32[]{:S(2)}, u32[]{:S(2)}) collective-permute-start(bf16[128,512]{1,0:T(8,128)(2,1)S(1)} %get-tuple-element.61), channel_id=1, source_target_pairs={{0,8},{4,12},{8,0},{12,4},{16,24},{20,28},{24,16},{28,20},{1,9},{5... | collective-permute-start | bytes 393224 | tf_op jit(solution)/shard_map/ppermute | solution.py:313
  43.8 6.2 %collective-permute-start.15 = (bf16[256,256]{1,0:T(8,128)(2,1)S(1)}, bf16[256,256]{1,0:T(8,128)(2,1)S(1)}, u32[]{:S(2)}, u32[]{:S(2)}) collective-permute-start(bf16[256,256]{1,0:T(8,128)(2,1)S(1)} %step_r.5.near_r), channel_id=1, source_target_pairs={{0,4},{4,0},{8,12},{12,8},{16,20},{20,16},{24,28},{28,24},{1,5},{5... | collective-permute-start | bytes 393224 | tf_op jit(solution)/shard_map/ppermute | solution.py:313
  44.8 5.2 %collective-permute-start.11 = (bf16[64,512]{1,0:T(8,128)(2,1)S(1)}, bf16[64,512]{1,0:T(8,128)(2,1)S(1)}, u32[]{:S(2)}, u32[]{:S(2)}) collective-permute-start(bf16[64,512]{1,0:T(8,128)(2,1)S(1)} %get-tuple-element.63), channel_id=1, source_target_pairs={{0,16},{4,20},{8,24},{12,28},{16,0},{20,4},{24,8},{28,12},{1,17},{... | collective-permute-start | bytes 196616 | tf_op jit(solution)/shard_map/ppermute | solution.py:313
  50.5 1.3 %collective-permute-start.16 = (f32[2,64,128]{2,1,0:T(8,128)S(1)}, f32[2,64,128]{2,1,0:T(8,128)S(1)}, u32[]{:S(2)}, u32[]{:S(2)}) collective-permute-start(f32[2,64,128]{2,1,0:T(8,128)S(1)} %get-tuple-element.72), channel_id=1, source_target_pairs={{0,1},{1,0},{2,3},{3,2},{4,5},{5,4},{6,7},{7,6},{8,9},{9,8},{10,11... | collective-permute-start | bytes 196616 | tf_op jit(solution)/shard_map/ppermute | solution.py:313

commit v5 on v4

--- a/solution.py
+++ b/solution.py
@@ -122,7 +122,21 @@
             to_y_ref[at, part] = ref[part, :, theirs]
 
 
-def steer_blocks(blocks, delays_ref, cos_ref, sin_ref, copy_ref=None):
+def by_parity(values, block):
+    width = values.shape[1]
+    if 2 * block != LANES or width % (2 * LANES):
+        order = [at for parity in (0, 1) for at in range(parity * block, width, 2 * block)]
+        return jnp.concatenate([values[:, at : at + block] for at in order], axis=1)
+    low = lax.broadcasted_iota(jnp.int32, (values.shape[0], LANES), 1) < block
+    even, odd = [], []
+    for at in range(0, width, 2 * LANES):
+        first, second = values[:, at : at + LANES], values[:, at + LANES : at + 2 * LANES]
+        even.append(jnp.where(low, first, pltpu.roll(second, block, 1)))
+        odd.append(jnp.where(low, pltpu.roll(first, block, 1), second))
+    return jnp.concatenate(even + odd, axis=1)
+
+
+def steer_blocks(blocks, delays_ref, cos_ref, sin_ref, copy_ref=None, block=None):
     core = place()[2]
     rate = jnp.where(core == 0, cycle_rates[0], cycle_rates[1]).astype(jnp.float32)
     size = cos_ref.shape[0] // len(blocks)
@@ -131,11 +145,13 @@
         if arrival is not None:
             arrival.wait()
 
-        @pl.loop(0, size // chunk)
+        @pl.loop(0, size // chunk, unroll=math.gcd(size // chunk, 10) if block else 1)
         def _(i):
             here = pl.ds(pl.multiple_of(start + i * chunk, chunk), chunk)
             there = pl.ds(pl.multiple_of(index * size + i * chunk, chunk), chunk)
             delays = delays_ref[here, :]
+            if block:
+                delays = by_parity(delays, block)
             cos, sin = steer_rows(rate, delays)
             cos_ref[there, :] = cos
             sin_ref[there, :] = sin
@@ -148,7 +164,7 @@
     steer_blocks([(0, None)], delays_ref, cos_ref, sin_ref)
 
 
-def steer_far_kernel(starts, parts, token_ref, delays_ref, cos_ref, sin_ref, out_ref, *refs):
+def steer_far_kernel(starts, parts, block, token_ref, delays_ref, cos_ref, sin_ref, out_ref, *refs):
     *copy_ref, held_ref, sems = refs
     out_ref[...] = token_ref[...]
     firsts = starts()
@@ -163,7 +179,7 @@
             arrival = pltpu.make_async_copy(delays_ref.at[there, :], held_ref.at[here, :], sems.at[index])
             arrival.start()
             blocks.append((index * rows, arrival))
-    steer_blocks(blocks, held_ref, cos_ref, sin_ref, *copy_ref)
+    steer_blocks(blocks, held_ref, cos_ref, sin_ref, *(copy_ref or [None]), block)
 
 
 def steering(token, delays):
@@ -171,11 +187,11 @@
     return kernel_call(steer_kernel, out, [token, delays], [pltpu.VMEM] * 2, name="steering")
 
 
-def steering_far(starts, per, blocks, token, delays, copied=()):
-    parts = math.gcd(per // CHUNK, 5)
+def steering_far(starts, per, blocks, token, delays, copied=(), block=None):
+    parts = math.gcd(per // CHUNK, 1 if block else 5)
     shape = (per * blocks, delays.shape[1])
     return kernel_call(
-        functools.partial(steer_far_kernel, starts, parts),
+        functools.partial(steer_far_kernel, starts, parts, block),
         [vmem(shape, jnp.bfloat16)] * 2
         + [vmem(token.shape, token.dtype)]
         + [vmem(shape, t) for t in copied],
@@ -194,48 +210,48 @@
             ref[out, :] = total[rows, :].astype(ref.dtype)
 
 
-def beams_kernel(order, mine, block, kept, near_power_ref, far_ref, level_ref, own_ref, other_ref, from_ref, *refs):
-    *steer, keep_ref, send_ref, token_ref, total_ref = refs
-    token_ref[...] = level_ref[...]
+def beams_kernel(order, mine, block, kept, only, near_power_ref, far_ref, level_ref, own_ref, other_ref, from_ref, *refs):
+    if only is None:
+        *steer, keep_ref, send_ref, total_ref = refs
+        beams_of = slice(None)
+    else:
+        *steer, total_ref = refs
+        beams_of = pl.ds(pl.multiple_of(only() * total_ref.shape[0], total_ref.shape[0]), total_ref.shape[0])
     per = from_ref.shape[2]
     windows = mine(from_ref.shape[3])
-    level = 0.5 * level_ref[...]
-    real, imag = [], []
+    width = total_ref.shape[1] // 2
+    powers = jnp.concatenate([near_power_ref[...], far_ref[:2]], axis=0)
+    gains = lax.rsqrt(powers + 0.5 * level_ref[...])
+    gains = jnp.transpose(jnp.concatenate([gains, gains], axis=0))[:per]
+    scaled = []
     for at in range(4):
-        power = near_power_ref[at : at + 1] if at < 2 else far_ref[at - 2 : at - 1]
-        gain = jnp.transpose(jnp.broadcast_to(lax.rsqrt(power + level), (8, level.shape[1])))[:per, :1]
-        for part, parts in enumerate((real, imag)):
-            near_ref = (own_ref, other_ref)[at % 2]
-            spec = near_ref[part, :, windows] if at < 2 else from_ref[at - 2, part]
-            parts.append(spec.astype(jnp.float32) * gain)
-    total = None
+        near_ref = (own_ref, other_ref)[at % 2]
+        spec = [near_ref[part, :, windows] if at < 2 else from_ref[at - 2, part] for part in (0, 1)]
+        scaled.append(jnp.concatenate(spec, axis=1).astype(jnp.float32) * gains[:, at : at + 1])
+    sums = [0.0, 0.0]
     for group, members in enumerate(order):
-        re, im = (jnp.concatenate([p[m] for m in members], axis=0).astype(jnp.bfloat16) for p in (real, imag))
-        for left, right in (((re, im), steer[2 * group]), ((-im, re), steer[2 * group + 1])):
-            term = lax.dot_general(
-                right[...],
-                jnp.concatenate(left, axis=1),
-                (((0,), (0,)), ((), ())),
-                preferred_element_type=jnp.float32,
+        right = jnp.concatenate([scaled[m] for m in members], axis=0).astype(jnp.bfloat16)
+        for at in (0, 1):
+            sums[at] += lax.dot_general(
+                steer[2 * group + at][:, beams_of], right, (((0,), (0,)), ((), ())), preferred_element_type=jnp.float32
             )
-            total = term if total is None else total + term
-    total_ref[...] = total
-    halves(total_ref, block, kept(), keep_ref, send_ref)
-
-
-def beams(order, mine, block, kept, near_power, far, level, own, other, arrived, steer, name):
+    with_cos, with_sin = sums
+    total_ref[:, :width] = (with_cos[:, :width] - with_sin[:, width:]).astype(total_ref.dtype)
+    total_ref[:, width:] = (with_cos[:, width:] + with_sin[:, :width]).astype(total_ref.dtype)
+    if only is None:
+        halves(total_ref, block, kept(), keep_ref, send_ref)
+
+
+def beams(order, mine, block, kept, near_power, far, level, own, other, arrived, steer, name, only=None, dtype=None):
     inputs = [near_power, far, level, own, other, arrived, *steer]
     rows, width = steer[0].shape[1], 2 * arrived.shape[-1]
+    out = [vmem((rows // 2, width), t) for t in ((jnp.float32, jnp.bfloat16) if only is None else (dtype,))]
     return kernel_call(
-        functools.partial(beams_kernel, order, mine, block, kept),
-        [
-            vmem((rows // 2, width), jnp.float32),
-            vmem((rows // 2, width), jnp.bfloat16),
-            vmem(level.shape, level.dtype),
-        ],
+        functools.partial(beams_kernel, order, mine, block, kept, only),
+        out,
         inputs,
         [pltpu.VMEM] * len(inputs),
-        scratch=[pltpu.VMEM((rows, width), jnp.float32)],
+        scratch=[pltpu.VMEM((rows, width), jnp.float32)] if only is None else [],
         limit=24,
         name=name,
     )
@@ -337,6 +353,7 @@
     padded = -(-per // LANES) * LANES
 
     spec_shape = vmem((parts, per, windows), spectra.dtype)
+    block_r, block_s = 2 * delays_r.shape[1] // n_col, delays_s.shape[1] // n_row
     notes, own, away = kernel_call(
         power_kernel,
         [vmem((4, padded), jnp.float32), spec_shape, spec_shape],
@@ -366,9 +383,9 @@
 
     row_bits, col_bits = bits(n_row, 2), bits(n_col, 4)
     first, *others = [("row", bit) for bit in row_bits] + [("col", bit) for bit in col_bits]
-    *steer_s, token = steering_far(starts_s(0, 2), per, 2, level, delays_s)
+    *steer_s, token = steering_far(starts_s(0, 2), per, 2, level, delays_s, block=block_s)
     level = level + swap(level, *first)
-    cos, sin, next_token = steering_far(starts_s(2, 4), per, 2, level, delays_s)
+    cos, sin, next_token = steering_far(starts_s(2, 4), per, 2, level, delays_s, block=block_s)
     steer_s += [cos, sin]
     for step in others:
         level = gated([level], [token])
@@ -378,8 +395,7 @@
     far_y = swap(gated([power, level], [from_y, next_token]), "row", 1)
     level = gated([level + far_y[2:]], [token])
 
-    block_r, block_s = 2 * delays_r.shape[1] // n_col, delays_s.shape[1] // n_row
-    keep_r, send_r, token = beams(
+    keep_r, send_r = beams(
         ((0, 2), (1, 3)),
         lambda half: pl.ds(pl.multiple_of(y_of() * half, half), half),
         block_r,
@@ -393,8 +409,24 @@
         steer_r,
         "beams_r",
     )
-    keep_s, send_s, _ = beams(
-        ((0, 1), (2, 3)), lambda windows: slice(None), block_s, y_of, power, far_x, token, own, other, from_x, steer_s, "beams_s"
+    (send_s,), (keep_s,) = (
+        beams(
+            ((0, 1), (2, 3)),
+            lambda windows: slice(None),
+            None,
+            None,
+            power,
+            far_x,
+            level,
+            own,
+            other,
+            from_x,
+            steer_s,
+            "beams_s",
+            only,
+            dtype,
+        )
+        for only, dtype in ((lambda: 1 - y_of(), jnp.bfloat16), (y_of, jnp.float32))
     )
     r_steps = [("col", bit, True) for bit in [2, *col_bits]] + [("row", bit, False) for bit in row_bits]
     s_steps = [("row", bit, True) for bit in [1, *row_bits]] + [("col", bit, False) for bit in col_bits]

time: 52.7 us -> 52.1 us (0.989)
  waiting for transfers between devices: 15.9 us -> 15.3 us
    ppermute x17, waiting for transfers between devices: 15.9 us -> 15.3 us  [swap(): return lax.ppermute(value, axis, [(i, i ^ bit) for i in range(size)])]
    pallas_call x19 -> x20, Pallas kernels: 14.5 us -> 14.4 us  [kernel_call(): pl.pallas_call(body, out_shape=out, in_specs=[pl.BlockSpec(memory_space=s...]
  transfers between devices with their start and end apart: 17 -> 17, of which waited for: 8 -> 9; matrix products, arithmetic and copies ran while one was open for 0% -> 0% of each run, Pallas kernels for 24% -> 24%
where the time goes in v5:
time: 52.1 us; the launch traced here: 51.7 us
  starting transfers between devices  20.9 us (40%)
  waiting for transfers between devices  15.3 us (29%)
  Pallas kernels  14.4 us (28%)
  other arithmetic  0.72 us (1%)
    ppermute x17, starting transfers between devices, swap(): return lax.ppermute(value, axis, [(i, i ^ bit) for i in range(size)])  20.9 us
    ppermute x17, waiting for transfers between devices, swap(): return lax.ppermute(value, axis, [(i, i ^ bit) for i in range(size)])  15.3 us
    pallas_call x20, Pallas kernels, kernel_call(): pl.pallas_call(body, out_shape=out, in_specs=[pl.BlockSpec(memory_space=s...  14.4 us
  transfers between devices with their start and end apart: 17, of which 9 were waited for; matrix products, arithmetic and copies ran while one was open for 0% of the time, Pallas kernels for 24%

profile of v5, /device:TPU:0, one launch (start us, length us, event | category | flops | bytes accessed | tf_op | source)
XLA Modules:
  0.0 51.7 jit_solution(17487711501602171185)
XLA Ops:
  0.0 1.5 %power.1 = (f32[4,384]{1,0:T(4,128)S(1)}, bf16[2,320,256]{2,1,0:T(8,128)(2,1)S(1)}, bf16[2,320,256]{2,1,0:T(8,128)(2,1)S(1)}) custom-call(s32[2]{0:T(128)} %wl_ref.1, bf16[2,2,320,256]{3,2,1,0:T(8,128)(2,1)} %spec_ref.1), custom_call_target="tpu_custom_call" | custom-call | flops 1 | bytes 1 | tf_op jit(solution)/shard_map/power/pallas_call | solution.py:60
  1.5 0.5 %collective-permute-start.4 = (bf16[2,320,256]{2,1,0:T(8,128)(2,1)S(1)}, bf16[2,320,256]{2,1,0:T(8,128)(2,1)S(1)}, u32[]{:S(2)}, u32[]{:S(2)}) collective-permute-start(bf16[2,320,256]{2,1,0:T(8,128)(2,1)S(1)} %get-tuple-element.40), channel_id=1, source_target_pairs={{0,1},{1,0},{2,3},{3,2},{4,5},{5,4},{6,7},{7,6},{8,9},{9,8},{10,11... | collective-permute-start | bytes 983048 | tf_op jit(solution)/shard_map/ppermute | solution.py:329
  2.0 2.6 %collective-permute-start = (f32[4,384]{1,0:T(4,128)S(1)}, f32[4,384]{1,0:T(4,128)S(1)}, u32[]{:S(2)}, u32[]{:S(2)}) collective-permute-start(f32[4,384]{1,0:T(4,128)S(1)} %get-tuple-element.36), channel_id=1, source_target_pairs={{0,2},{1,3},{2,0},{3,1},{4,6},{5,7},{6,4},{7,5},{8,10},{9,11},{10,... | collective-permute-start | bytes 18440 | tf_op jit(solution)/shard_map/ppermute | solution.py:329
  4.6 2.2 %steering_far.3 = (bf16[640,512]{1,0:T(8,128)(2,1)S(1)}, bf16[640,512]{1,0:T(8,128)(2,1)S(1)}, f32[1,384]{1,0:T(1,128)S(1)}, s16[640,512]{1,0:T(8,128)(2,1)S(1)}) custom-call(f32[1,384]{1,0:T(1,128)S(1)} %slice.34.token_ref, s32[2560,512]{1,0:T(8,128)} %delays_ref.3), custom_call_target="tpu_custom_call" | custom-call | flops 1 | bytes 1 | tf_op jit(solution)/shard_map/steering_far/pallas_call | solution.py:60
  6.8 0.0 collective-permute-done
  6.8 0.2 collective-permute-start.1
  7.0 0.3 collective-permute-start.7
  7.4 0.7 %collective-permute-done.1 = f32[4,384]{1,0:T(4,128)S(1)} collective-permute-done((f32[4,384]{1,0:T(4,128)S(1)}, f32[4,384]{1,0:T(4,128)S(1)}, u32[]{:S(2)}, u32[]{:S(2)}) %collective-permute-start.1) | collective-permute-done | bytes 6176 | tf_op jit(solution)/shard_map/ppermute | solution.py:329
  8.0 0.0 collective-permute-done.4.other_ref
  8.1 0.1 send.1
  8.2 1.6 %collective-permute-start.5 = (bf16[2,2,320,128]{3,2,1,0:T(8,128)(2,1)S(1)}, bf16[2,2,320,128]{3,2,1,0:T(8,128)(2,1)S(1)}, u32[]{:S(2)}, u32[]{:S(2)}) collective-permute-start(bf16[2,2,320,128]{3,2,1,0:T(8,128)(2,1)S(1)} %get-tuple-element.41), channel_id=1, source_target_pairs={{0,4},{4,0},{8,12},{12,8},{16,20},{20,16},{24,28},{28,24},{1,5},{5... | collective-permute-start | bytes 983048 | tf_op jit(solution)/shard_map/ppermute | solution.py:329
  9.8 1.4 %collective-permute-start.8 = (bf16[2,2,320,256]{3,2,1,0:T(8,128)(2,1)S(1)}, bf16[2,2,320,256]{3,2,1,0:T(8,128)(2,1)S(1)}, u32[]{:S(2)}, u32[]{:S(2)}) collective-permute-start(bf16[2,2,320,256]{3,2,1,0:T(8,128)(2,1)S(1)} %get-tuple-element.45), channel_id=1, source_target_pairs={{0,2},{1,3},{2,0},{3,1},{4,6},{5,7},{6,4},{7,5},{8,10},{9,11},{10,... | collective-permute-start | bytes 1966088 | tf_op jit(solution)/shard_map/ppermute | solution.py:329
  11.2 1.6 %collective-permute-start.2 = (f32[1,384]{1,0:T(1,128)S(1)}, f32[1,384]{1,0:T(1,128)S(1)}, u32[]{:S(2)}, u32[]{:S(2)}) collective-permute-start(f32[1,384]{1,0:T(1,128)S(1)} %get-tuple-element.69.token_ref), channel_id=1, source_target_pairs={{0,8},{4,12},{8,0},{12,4},{16,24},{20,28},{24,16},{28,20},{1,9},{5... | collective-permute-start | bytes 4616 | tf_op jit(solution)/shard_map/ppermute | solution.py:329
  12.7 2.3 %steering_far.4 = (bf16[640,512]{1,0:T(8,128)(2,1)S(1)}, bf16[640,512]{1,0:T(8,128)(2,1)S(1)}, f32[1,384]{1,0:T(1,128)S(1)}) custom-call(f32[1,384]{1,0:T(1,128)S(1)} %get-tuple-element.69.token_ref, s32[1280,512]{1,0:T(8,128)} %delays_ref.5), custom_call_target="tpu_custom_call" | custom-call | flops 1 | bytes 1 | tf_op jit(solution)/shard_map/steering_far/pallas_call | solution.py:60
  15.1 0.0 collective-permute-done.2
  15.1 2.7 %collective-permute-start.3 = (f32[1,384]{1,0:T(1,128)S(1)}, f32[1,384]{1,0:T(1,128)S(1)}, u32[]{:S(2)}, u32[]{:S(2)}) collective-permute-start(f32[1,384]{1,0:T(1,128)S(1)} %gate.5), channel_id=1, source_target_pairs={{0,16},{4,20},{8,24},{12,28},{16,0},{20,4},{24,8},{28,12},{1,17},{... | collective-permute-start | bytes 4616 | tf_op jit(solution)/shard_map/ppermute | solution.py:329
  17.8 2.3 %steering_far.5 = (bf16[640,512]{1,0:T(8,128)(2,1)S(1)}, bf16[640,512]{1,0:T(8,128)(2,1)S(1)}, f32[1,384]{1,0:T(1,128)S(1)}) custom-call(f32[1,384]{1,0:T(1,128)S(1)} %add.21.refs_0_.token_ref, s32[1280,512]{1,0:T(8,128)} %delays_ref.5), custom_call_target="tpu_custom_call" | custom-call | flops 1 | bytes 1 | tf_op jit(solution)/shard_map/steering_far/pallas_call | solution.py:60
  20.1 0.0 collective-permute-done.3
  20.1 0.0 collective-permute-done.5.refs_2_.from_ref
  20.1 0.6 %collective-permute-start.6 = (f32[3,384]{1,0:T(4,128)S(1)}, f32[3,384]{1,0:T(4,128)S(1)}, u32[]{:S(2)}, u32[]{:S(2)}) collective-permute-start(f32[3,384]{1,0:T(4,128)S(1)} %gate.6), channel_id=1, source_target_pairs={{0,4},{4,0},{8,12},{12,8},{16,20},{20,16},{24,28},{28,24},{1,5},{5... | collective-permute-start | bytes 13832 | tf_op jit(solution)/shard_map/ppermute | solution.py:329
  20.7 0.0 collective-permute-done.7.delays_ref
  20.7 1.2 %steering.1 = (bf16[640,512]{1,0:T(8,128)(2,1)S(1)}, bf16[640,512]{1,0:T(8,128)(2,1)S(1)}, f32[1,384]{1,0:T(1,128)S(1)}) custom-call(f32[1,384]{1,0:T(1,128)S(1)} %add.22.refs_1_.token_ref, s16[640,512]{1,0:T(8,128)(2,1)S(1)} %collective-permute-done.7.delays_ref), custom_call_target="tpu_custom_call" | custom-call | flops 1 | bytes 1 | tf_op jit(solution)/shard_map/steering/pallas_call | solution.py:60
  21.9 1.9 %collective-permute-done.6.far_ref = f32[3,384]{1,0:T(4,128)S(1)} collective-permute-done((f32[3,384]{1,0:T(4,128)S(1)}, f32[3,384]{1,0:T(4,128)S(1)}, u32[]{:S(2)}, u32[]{:S(2)}) %collective-permute-start.6) | collective-permute-done | bytes 4640 | tf_op jit(solution)/shard_map/ppermute | solution.py:329
  23.8 1.4 %beams_r.1 = (f32[256,256]{1,0:T(8,128)S(1)}, bf16[256,256]{1,0:T(8,128)(2,1)S(1)}) custom-call(f32[2,384]{1,0:T(2,128)S(1)} %pad_maximum_fusion.refs_0_.near_power_ref, f32[3,384]{1,0:T(4,128)S(1)} %collective-permute-done.6.far_ref, f32[1,384]{1,0:T(1,128)S(1)} %gate.7.level_ref.token_ref, bf16[2,320,256]{2,1,0:T(8,128)(2,1)S(1)} %get-tuple-element.39.own_ref, ...), custom_call_target="tpu_custom_call" | custom-call | flops 1 | bytes 1 | tf_op jit(solution)/shard_map/beams_r/pallas_call | solution.py:60
  25.2 0.7 %collective-permute-start.12 = (bf16[256,256]{1,0:T(8,128)(2,1)S(1)}, bf16[256,256]{1,0:T(8,128)(2,1)S(1)}, u32[]{:S(2)}, u32[]{:S(2)}) collective-permute-start(bf16[256,256]{1,0:T(8,128)(2,1)S(1)} %get-tuple-element.59), channel_id=1, source_target_pairs={{0,2},{1,3},{2,0},{3,1},{4,6},{5,7},{6,4},{7,5},{8,10},{9,11},{10,... | collective-permute-start | bytes 393224 | tf_op jit(solution)/shard_map/ppermute | solution.py:329
  25.9 0.5 collective-permute-done.8.from_ref
  26.4 1.3 %beams_s.3 = bf16[256,512]{1,0:T(8,128)(2,1)S(1)} custom-call(f32[2,384]{1,0:T(2,128)S(1)} %pad_maximum_fusion.refs_0_.near_power_ref, f32[2,384]{1,0:T(2,128)S(1)} %pad_maximum_fusion.1.far_ref, f32[1,384]{1,0:T(1,128)S(1)} %gate.7.level_ref.token_ref, bf16[2,320,256]{2,1,0:T(8,128)(2,1)S(1)} %get-tuple-element.39.own_ref, ...), custom_call_target="tpu_custom_call" | custom-call | flops 1 | bytes 1 | tf_op jit(solution)/shard_map/beams_s/pallas_call | solution.py:60
  27.8 0.6 %collective-permute-start.9 = (bf16[256,512]{1,0:T(8,128)(2,1)S(1)}, bf16[256,512]{1,0:T(8,128)(2,1)S(1)}, u32[]{:S(2)}, u32[]{:S(2)}) collective-permute-start(bf16[256,512]{1,0:T(8,128)(2,1)S(1)} %beams_s.3), channel_id=1, source_target_pairs={{0,4},{4,0},{8,12},{12,8},{16,20},{20,16},{24,28},{28,24},{1,5},{5... | collective-permute-start | bytes 786440 | tf_op jit(solution)/shard_map/ppermute | solution.py:329
  28.3 1.9 %collective-permute-done.12.other_ref = bf16[256,256]{1,0:T(8,128)(2,1)S(1)} collective-permute-done((bf16[256,256]{1,0:T(8,128)(2,1)S(1)}, bf16[256,256]{1,0:T(8,128)(2,1)S(1)}, u32[]{:S(2)}, u32[]{:S(2)}) %collective-permute-start.12) | collective-permute-done | bytes 131104 | tf_op jit(solution)/shard_map/ppermute | solution.py:329
  30.3 1.2 %collective-permute-start.13 = (bf16[256,256]{1,0:T(8,128)(2,1)S(1)}, bf16[256,256]{1,0:T(8,128)(2,1)S(1)}, u32[]{:S(2)}, u32[]{:S(2)}) collective-permute-start(bf16[256,256]{1,0:T(8,128)(2,1)S(1)} %get-tuple-element.61), channel_id=1, source_target_pairs={{0,8},{4,12},{8,0},{12,4},{16,24},{20,28},{24,16},{28,20},{1,9},{5... | collective-permute-start | bytes 393224 | tf_op jit(solution)/shard_map/ppermute | solution.py:329
  31.5 1.3 %beams_s.2.keep_ref = f32[256,512]{1,0:T(8,128)S(1)} custom-call(f32[2,384]{1,0:T(2,128)S(1)} %pad_maximum_fusion.refs_0_.near_power_ref, f32[2,384]{1,0:T(2,128)S(1)} %pad_maximum_fusion.1.far_ref, f32[1,384]{1,0:T(1,128)S(1)} %gate.7.level_ref.token_ref, bf16[2,320,256]{2,1,0:T(8,128)(2,1)S(1)} %get-tuple-element.39.own_ref, ...), custom_call_target="tpu_custom_call" | custom-call | flops 1 | bytes 1 | tf_op jit(solution)/shard_map/beams_s/pallas_call | solution.py:60
  32.9 2.0 %collective-permute-done.9.other_ref = bf16[256,512]{1,0:T(8,128)(2,1)S(1)} collective-permute-done((bf16[256,512]{1,0:T(8,128)(2,1)S(1)}, bf16[256,512]{1,0:T(8,128)(2,1)S(1)}, u32[]{:S(2)}, u32[]{:S(2)}) %collective-permute-start.9) | collective-permute-done | bytes 262176 | tf_op jit(solution)/shard_map/ppermute | solution.py:329
  34.9 0.1 step_s.3
  35.0 0.3 collective-permute-done.13.other_ref
  35.4 2.6 %collective-permute-start.14 = (bf16[256,256]{1,0:T(8,128)(2,1)S(1)}, bf16[256,256]{1,0:T(8,128)(2,1)S(1)}, u32[]{:S(2)}, u32[]{:S(2)}) collective-permute-start(bf16[256,256]{1,0:T(8,128)(2,1)S(1)} %get-tuple-element.64), channel_id=1, source_target_pairs={{0,16},{4,20},{8,24},{12,28},{16,0},{20,4},{24,8},{28,12},{1,17},{... | collective-permute-start | bytes 393224 | tf_op jit(solution)/shard_map/ppermute | solution.py:329
  38.0 1.6 %collective-permute-start.10 = (bf16[128,512]{1,0:T(8,128)(2,1)S(1)}, bf16[128,512]{1,0:T(8,128)(2,1)S(1)}, u32[]{:S(2)}, u32[]{:S(2)}) collective-permute-start(bf16[128,512]{1,0:T(8,128)(2,1)S(1)} %get-tuple-element.51), channel_id=1, source_target_pairs={{0,8},{4,12},{8,0},{12,4},{16,24},{20,28},{24,16},{28,20},{1,9},{5... | collective-permute-start | bytes 393224 | tf_op jit(solution)/shard_map/ppermute | solution.py:329
  39.6 3.3 %collective-permute-done.14.other_ref = bf16[256,256]{1,0:T(8,128)(2,1)S(1)} collective-permute-done((bf16[256,256]{1,0:T(8,128)(2,1)S(1)}, bf16[256,256]{1,0:T(8,128)(2,1)S(1)}, u32[]{:S(2)}, u32[]{:S(2)}) %collective-permute-start.14) | collective-permute-done | bytes 131104 | tf_op jit(solution)/shard_map/ppermute | solution.py:329
  42.8 1.0 %collective-permute-start.15 = (bf16[256,256]{1,0:T(8,128)(2,1)S(1)}, bf16[256,256]{1,0:T(8,128)(2,1)S(1)}, u32[]{:S(2)}, u32[]{:S(2)}) collective-permute-start(bf16[256,256]{1,0:T(8,128)(2,1)S(1)} %step_r.5.near_r), channel_id=1, source_target_pairs={{0,4},{4,0},{8,12},{12,8},{16,20},{20,16},{24,28},{28,24},{1,5},{5... | collective-permute-start | bytes 393224 | tf_op jit(solution)/shard_map/ppermute | solution.py:329
  43.9 0.0 collective-permute-done.10.other_ref
  43.9 1.7 %collective-permute-start.11 = (bf16[64,512]{1,0:T(8,128)(2,1)S(1)}, bf16[64,512]{1,0:T(8,128)(2,1)S(1)}, u32[]{:S(2)}, u32[]{:S(2)}) collective-permute-start(bf16[64,512]{1,0:T(8,128)(2,1)S(1)} %get-tuple-element.53), channel_id=1, source_target_pairs={{0,16},{4,20},{8,24},{12,28},{16,0},{20,4},{24,8},{28,12},{1,17},{... | collective-permute-start | bytes 196616 | tf_op jit(solution)/shard_map/ppermute | solution.py:329
  45.6 3.5 %collective-permute-done.11.other_ref = bf16[64,512]{1,0:T(8,128)(2,1)S(1)} collective-permute-done((bf16[64,512]{1,0:T(8,128)(2,1)S(1)}, bf16[64,512]{1,0:T(8,128)(2,1)S(1)}, u32[]{:S(2)}, u32[]{:S(2)}) %collective-permute-start.11) | collective-permute-done | bytes 65568 | tf_op jit(solution)/shard_map/ppermute | solution.py:329
  49.2 0.0 collective-permute-done.15.far_r
  49.2 0.5 field.1
  49.7 0.1 collective-permute-start.16
  49.7 1.2 %collective-permute-done.16 = f32[2,64,128]{2,1,0:T(8,128)S(1)} collective-permute-done((f32[2,64,128]{2,1,0:T(8,128)S(1)}, f32[2,64,128]{2,1,0:T(8,128)S(1)}, u32[]{:S(2)}, u32[]{:S(2)}) %collective-permute-start.16) | collective-permute-done | bytes 65568 | tf_op jit(solution)/shard_map/ppermute | solution.py:329
  51.0 0.7 %maximum_bitcast_fusion = f32[2,2,128,64]{2,3,1,0:T(8,128)} fusion(f32[1,2,64,128]{3,2,1,0:T(8,128)S(1)} %get-tuple-element.68, f32[1,2,64,128]{3,2,1,0:T(8,128)S(1)} %get-tuple-element.67), kind=kLoop, calls=%fused_computation | loop fusion | flops 32768 | bytes 262144 | tf_op jit(solution)/shard_map/transpose | solution.py:458
  (19 shorter events, 0.2 us)
Async XLA Ops:
  1.5 6.6 %collective-permute-start.4 = (bf16[2,320,256]{2,1,0:T(8,128)(2,1)S(1)}, bf16[2,320,256]{2,1,0:T(8,128)(2,1)S(1)}, u32[]{:S(2)}, u32[]{:S(2)}) collective-permute-start(bf16[2,320,256]{2,1,0:T(8,128)(2,1)S(1)} %get-tuple-element.40), channel_id=1, source_target_pairs={{0,1},{1,0},{2,3},{3,2},{4,5},{5,4},{6,7},{7,6},{8,9},{9,8},{10,11... | collective-permute-start | bytes 983048 | tf_op jit(solution)/shard_map/ppermute | solution.py:329
  2.0 4.8 %collective-permute-start = (f32[4,384]{1,0:T(4,128)S(1)}, f32[4,384]{1,0:T(4,128)S(1)}, u32[]{:S(2)}, u32[]{:S(2)}) collective-permute-start(f32[4,384]{1,0:T(4,128)S(1)} %get-tuple-element.36), channel_id=1, source_target_pairs={{0,2},{1,3},{2,0},{3,1},{4,6},{5,7},{6,4},{7,5},{8,10},{9,11},{10,... | collective-permute-start | bytes 18440 | tf_op jit(solution)/shard_map/ppermute | solution.py:329
  6.8 1.2 %collective-permute-start.1 = (f32[4,384]{1,0:T(4,128)S(1)}, f32[4,384]{1,0:T(4,128)S(1)}, u32[]{:S(2)}, u32[]{:S(2)}) collective-permute-start(f32[4,384]{1,0:T(4,128)S(1)} %gate.4), channel_id=1, source_target_pairs={{0,1},{1,0},{2,3},{3,2},{4,5},{5,4},{6,7},{7,6},{8,9},{9,8},{10,11... | collective-permute-start | bytes 18440 | tf_op jit(solution)/shard_map/ppermute | solution.py:329
  7.0 13.7 %collective-permute-start.7 = (s16[640,512]{1,0:T(8,128)(2,1)S(1)}, s16[640,512]{1,0:T(8,128)(2,1)S(1)}, u32[]{:S(2)}, u32[]{:S(2)}) collective-permute-start(s16[640,512]{1,0:T(8,128)(2,1)S(1)} %get-tuple-element.43), channel_id=1, source_target_pairs={{0,1},{1,0},{2,3},{3,2},{4,5},{5,4},{6,7},{7,6},{8,9},{9,8},{10,11... | collective-permute-start | bytes 1966088 | tf_op jit(solution)/shard_map/ppermute | solution.py:329
  8.2 11.9 %collective-permute-start.5 = (bf16[2,2,320,128]{3,2,1,0:T(8,128)(2,1)S(1)}, bf16[2,2,320,128]{3,2,1,0:T(8,128)(2,1)S(1)}, u32[]{:S(2)}, u32[]{:S(2)}) collective-permute-start(bf16[2,2,320,128]{3,2,1,0:T(8,128)(2,1)S(1)} %get-tuple-element.41), channel_id=1, source_target_pairs={{0,4},{4,0},{8,12},{12,8},{16,20},{20,16},{24,28},{28,24},{1,5},{5... | collective-permute-start | bytes 983048 | tf_op jit(solution)/shard_map/ppermute | solution.py:329
  9.8 16.7 %collective-permute-start.8 = (bf16[2,2,320,256]{3,2,1,0:T(8,128)(2,1)S(1)}, bf16[2,2,320,256]{3,2,1,0:T(8,128)(2,1)S(1)}, u32[]{:S(2)}, u32[]{:S(2)}) collective-permute-start(bf16[2,2,320,256]{3,2,1,0:T(8,128)(2,1)S(1)} %get-tuple-element.45), channel_id=1, source_target_pairs={{0,2},{1,3},{2,0},{3,1},{4,6},{5,7},{6,4},{7,5},{8,10},{9,11},{10,... | collective-permute-start | bytes 1966088 | tf_op jit(solution)/shard_map/ppermute | solution.py:329
  11.2 3.9 %collective-permute-start.2 = (f32[1,384]{1,0:T(1,128)S(1)}, f32[1,384]{1,0:T(1,128)S(1)}, u32[]{:S(2)}, u32[]{:S(2)}) collective-permute-start(f32[1,384]{1,0:T(1,128)S(1)} %get-tuple-element.69.token_ref), channel_id=1, source_target_pairs={{0,8},{4,12},{8,0},{12,4},{16,24},{20,28},{24,16},{28,20},{1,9},{5... | collective-permute-start | bytes 4616 | tf_op jit(solution)/shard_map/ppermute | solution.py:329
  15.1 5.0 %collective-permute-start.3 = (f32[1,384]{1,0:T(1,128)S(1)}, f32[1,384]{1,0:T(1,128)S(1)}, u32[]{:S(2)}, u32[]{:S(2)}) collective-permute-start(f32[1,384]{1,0:T(1,128)S(1)} %gate.5), channel_id=1, source_target_pairs={{0,16},{4,20},{8,24},{12,28},{16,0},{20,4},{24,8},{28,12},{1,17},{... | collective-permute-start | bytes 4616 | tf_op jit(solution)/shard_map/ppermute | solution.py:329
  20.1 3.7 %collective-permute-start.6 = (f32[3,384]{1,0:T(4,128)S(1)}, f32[3,384]{1,0:T(4,128)S(1)}, u32[]{:S(2)}, u32[]{:S(2)}) collective-permute-start(f32[3,384]{1,0:T(4,128)S(1)} %gate.6), channel_id=1, source_target_pairs={{0,4},{4,0},{8,12},{12,8},{16,20},{20,16},{24,28},{28,24},{1,5},{5... | collective-permute-start | bytes 13832 | tf_op jit(solution)/shard_map/ppermute | solution.py:329
  25.2 5.0 %collective-permute-start.12 = (bf16[256,256]{1,0:T(8,128)(2,1)S(1)}, bf16[256,256]{1,0:T(8,128)(2,1)S(1)}, u32[]{:S(2)}, u32[]{:S(2)}) collective-permute-start(bf16[256,256]{1,0:T(8,128)(2,1)S(1)} %get-tuple-element.59), channel_id=1, source_target_pairs={{0,2},{1,3},{2,0},{3,1},{4,6},{5,7},{6,4},{7,5},{8,10},{9,11},{10,... | collective-permute-start | bytes 393224 | tf_op jit(solution)/shard_map/ppermute | solution.py:329
  27.8 7.2 %collective-permute-start.9 = (bf16[256,512]{1,0:T(8,128)(2,1)S(1)}, bf16[256,512]{1,0:T(8,128)(2,1)S(1)}, u32[]{:S(2)}, u32[]{:S(2)}) collective-permute-start(bf16[256,512]{1,0:T(8,128)(2,1)S(1)} %beams_s.3), channel_id=1, source_target_pairs={{0,4},{4,0},{8,12},{12,8},{16,20},{20,16},{24,28},{28,24},{1,5},{5... | collective-permute-start | bytes 786440 | tf_op jit(solution)/shard_map/ppermute | solution.py:329
  30.3 5.0 %collective-permute-start.13 = (bf16[256,256]{1,0:T(8,128)(2,1)S(1)}, bf16[256,256]{1,0:T(8,128)(2,1)S(1)}, u32[]{:S(2)}, u32[]{:S(2)}) collective-permute-start(bf16[256,256]{1,0:T(8,128)(2,1)S(1)} %get-tuple-element.61), channel_id=1, source_target_pairs={{0,8},{4,12},{8,0},{12,4},{16,24},{20,28},{24,16},{28,20},{1,9},{5... | collective-permute-start | bytes 393224 | tf_op jit(solution)/shard_map/ppermute | solution.py:329
  35.4 7.4 %collective-permute-start.14 = (bf16[256,256]{1,0:T(8,128)(2,1)S(1)}, bf16[256,256]{1,0:T(8,128)(2,1)S(1)}, u32[]{:S(2)}, u32[]{:S(2)}) collective-permute-start(bf16[256,256]{1,0:T(8,128)(2,1)S(1)} %get-tuple-element.64), channel_id=1, source_target_pairs={{0,16},{4,20},{8,24},{12,28},{16,0},{20,4},{24,8},{28,12},{1,17},{... | collective-permute-start | bytes 393224 | tf_op jit(solution)/shard_map/ppermute | solution.py:329
  38.0 5.9 %collective-permute-start.10 = (bf16[128,512]{1,0:T(8,128)(2,1)S(1)}, bf16[128,512]{1,0:T(8,128)(2,1)S(1)}, u32[]{:S(2)}, u32[]{:S(2)}) collective-permute-start(bf16[128,512]{1,0:T(8,128)(2,1)S(1)} %get-tuple-element.51), channel_id=1, source_target_pairs={{0,8},{4,12},{8,0},{12,4},{16,24},{20,28},{24,16},{28,20},{1,9},{5... | collective-permute-start | bytes 393224 | tf_op jit(solution)/shard_map/ppermute | solution.py:329
  42.8 6.3 %collective-permute-start.15 = (bf16[256,256]{1,0:T(8,128)(2,1)S(1)}, bf16[256,256]{1,0:T(8,128)(2,1)S(1)}, u32[]{:S(2)}, u32[]{:S(2)}) collective-permute-start(bf16[256,256]{1,0:T(8,128)(2,1)S(1)} %step_r.5.near_r), channel_id=1, source_target_pairs={{0,4},{4,0},{8,12},{12,8},{16,20},{20,16},{24,28},{28,24},{1,5},{5... | collective-permute-start | bytes 393224 | tf_op jit(solution)/shard_map/ppermute | solution.py:329
  43.9 5.2 %collective-permute-start.11 = (bf16[64,512]{1,0:T(8,128)(2,1)S(1)}, bf16[64,512]{1,0:T(8,128)(2,1)S(1)}, u32[]{:S(2)}, u32[]{:S(2)}) collective-permute-start(bf16[64,512]{1,0:T(8,128)(2,1)S(1)} %get-tuple-element.53), channel_id=1, source_target_pairs={{0,16},{4,20},{8,24},{12,28},{16,0},{20,4},{24,8},{28,12},{1,17},{... | collective-permute-start | bytes 196616 | tf_op jit(solution)/shard_map/ppermute | solution.py:329
  49.7 1.3 %collective-permute-start.16 = (f32[2,64,128]{2,1,0:T(8,128)S(1)}, f32[2,64,128]{2,1,0:T(8,128)S(1)}, u32[]{:S(2)}, u32[]{:S(2)}) collective-permute-start(f32[2,64,128]{2,1,0:T(8,128)S(1)} %get-tuple-element.66), channel_id=1, source_target_pairs={{0,1},{1,0},{2,3},{3,2},{4,5},{5,4},{6,7},{7,6},{8,9},{9,8},{10,11... | collective-permute-start | bytes 196616 | tf_op jit(solution)/shard_map/ppermute | solution.py:329

commit v6 on v5

--- a/solution.py
+++ b/solution.py
@@ -145,7 +145,7 @@
         if arrival is not None:
             arrival.wait()
 
-        @pl.loop(0, size // chunk, unroll=math.gcd(size // chunk, 10) if block else 1)
+        @pl.loop(0, size // chunk, unroll=math.gcd(size // chunk, 10))
         def _(i):
             here = pl.ds(pl.multiple_of(start + i * chunk, chunk), chunk)
             there = pl.ds(pl.multiple_of(index * size + i * chunk, chunk), chunk)
@@ -188,7 +188,7 @@
 
 
 def steering_far(starts, per, blocks, token, delays, copied=(), block=None):
-    parts = math.gcd(per // CHUNK, 1 if block else 5)
+    parts = math.gcd(per // CHUNK, 1 if block else 2)
     shape = (per * blocks, delays.shape[1])
     return kernel_call(
         functools.partial(steer_far_kernel, starts, parts, block),
@@ -302,26 +302,25 @@
             token = yield results[-1]
 
 
-def field_kernel(scale, source_ref, near_r, far_r, keep_ref, send_ref):
+def field_kernel(scale, mine, source_ref, near_r, far_r, field_ref):
     _, _, core, _, y = place()
     half = near_r.shape[1] // 2
-    block = keep_ref.shape[2]
+    block = field_ref.shape[2]
 
     def product(left, right):
         return lax.dot_general(left, right, (((1,), (1,)), ((), ())), preferred_element_type=jnp.float32)
 
-    for ref, at in ((keep_ref, core), (send_ref, 1 - core)):
-        rows = pl.ds(pl.multiple_of(at * block, block), block)
-        real = imag = 0.0
-        for bit, receiver in ((y, near_r), (1 - y, far_r)):
-            s_re, s_im = (
-                source_ref[:, pl.ds(pl.multiple_of((2 * part + bit) * half, half), half)] for part in (0, 1)
-            )
-            r_re, r_im = receiver[rows, :half], receiver[rows, half:]
-            real += product(s_re, r_re) + product(s_im, r_im)
-            imag += product(s_im, r_re) - product(s_re, r_im)
-        ref[0] = real * scale
-        ref[1] = imag * scale
+    rows = pl.ds(pl.multiple_of((core if mine else 1 - core) * block, block), block)
+    real = imag = 0.0
+    for bit, receiver in ((y, near_r), (1 - y, far_r)):
+        s_re, s_im = (
+            source_ref[:, pl.ds(pl.multiple_of((2 * part + bit) * half, half), half)] for part in (0, 1)
+        )
+        r_re, r_im = receiver[rows, :half], receiver[rows, half:]
+        real += product(s_re, r_re) + product(s_im, r_im)
+        imag += product(s_im, r_re) - product(s_re, r_im)
+    field_ref[0] = real * scale
+    field_ref[1] = imag * scale
 
 
 def swap(value, axis, bit):
@@ -447,12 +446,15 @@
     block = delays_r.shape[1] // n_col
     shape = vmem((2, block_s, block), jnp.float32)
     scale = math.sqrt(windows) / (per * n_row * n_col)
-    near, away = kernel_call(
-        functools.partial(field_kernel, scale),
-        [shape, shape],
-        [source, receiver, r_far],
-        [pltpu.VMEM] * 3,
-        name="field",
+    away, near = (
+        kernel_call(
+            functools.partial(field_kernel, scale, mine),
+            [shape],
+            [source, receiver, r_far],
+            [pltpu.VMEM] * 3,
+            name="field",
+        )[0]
+        for mine in (False, True)
     )
     far = swap(away, "col", 1)
     return jnp.stack(ordered(core, near, far)).swapaxes(2, 3)

time: 52.1 us -> 51.9 us (level)
    pallas_call x20 -> x21, Pallas kernels: 14.4 us -> 14.3 us  [kernel_call(): pl.pallas_call(body, out_shape=out, in_specs=[pl.BlockSpec(memory_space=s...]
where the time goes in v6:
time: 51.9 us; the launch traced here: 51.4 us
  starting transfers between devices  20.6 us (40%)
  waiting for transfers between devices  15.4 us (30%)
  Pallas kernels  14.3 us (28%)
  other arithmetic  0.72 us (1%)
    ppermute x17, starting transfers between devices, swap(): return lax.ppermute(value, axis, [(i, i ^ bit) for i in range(size)])  20.6 us
    ppermute x17, waiting for transfers between devices, swap(): return lax.ppermute(value, axis, [(i, i ^ bit) for i in range(size)])  15.4 us
    pallas_call x21, Pallas kernels, kernel_call(): pl.pallas_call(body, out_shape=out, in_specs=[pl.BlockSpec(memory_space=s...  14.3 us
  transfers between devices with their start and end apart: 17, of which 9 were waited for; matrix products, arithmetic and copies ran while one was open for 0% of the time, Pallas kernels for 24%

profile of v6, /device:TPU:0, one launch (start us, length us, event | category | flops | bytes accessed | tf_op | source)
XLA Modules:
  0.0 51.4 jit_solution(16788099306010131876)
XLA Ops:
  0.0 1.5 %power.1 = (f32[4,384]{1,0:T(4,128)S(1)}, bf16[2,320,256]{2,1,0:T(8,128)(2,1)S(1)}, bf16[2,320,256]{2,1,0:T(8,128)(2,1)S(1)}) custom-call(s32[2]{0:T(128)} %wl_ref.1, bf16[2,2,320,256]{3,2,1,0:T(8,128)(2,1)} %spec_ref.1), custom_call_target="tpu_custom_call" | custom-call | flops 1 | bytes 1 | tf_op jit(solution)/shard_map/power/pallas_call | solution.py:60
  1.5 0.5 %collective-permute-start.4 = (bf16[2,320,256]{2,1,0:T(8,128)(2,1)S(1)}, bf16[2,320,256]{2,1,0:T(8,128)(2,1)S(1)}, u32[]{:S(2)}, u32[]{:S(2)}) collective-permute-start(bf16[2,320,256]{2,1,0:T(8,128)(2,1)S(1)} %get-tuple-element.38), channel_id=1, source_target_pairs={{0,1},{1,0},{2,3},{3,2},{4,5},{5,4},{6,7},{7,6},{8,9},{9,8},{10,11... | collective-permute-start | bytes 983048 | tf_op jit(solution)/shard_map/ppermute | solution.py:328
  2.0 2.6 %collective-permute-start = (f32[4,384]{1,0:T(4,128)S(1)}, f32[4,384]{1,0:T(4,128)S(1)}, u32[]{:S(2)}, u32[]{:S(2)}) collective-permute-start(f32[4,384]{1,0:T(4,128)S(1)} %get-tuple-element.34), channel_id=1, source_target_pairs={{0,2},{1,3},{2,0},{3,1},{4,6},{5,7},{6,4},{7,5},{8,10},{9,11},{10,... | collective-permute-start | bytes 18440 | tf_op jit(solution)/shard_map/ppermute | solution.py:328
  4.6 2.1 %steering_far.3 = (bf16[640,512]{1,0:T(8,128)(2,1)S(1)}, bf16[640,512]{1,0:T(8,128)(2,1)S(1)}, f32[1,384]{1,0:T(1,128)S(1)}, s16[640,512]{1,0:T(8,128)(2,1)S(1)}) custom-call(f32[1,384]{1,0:T(1,128)S(1)} %slice.34.token_ref, s32[2560,512]{1,0:T(8,128)} %delays_ref.3), custom_call_target="tpu_custom_call" | custom-call | flops 1 | bytes 1 | tf_op jit(solution)/shard_map/steering_far/pallas_call | solution.py:60
  6.7 0.0 collective-permute-done
  6.7 0.2 collective-permute-start.1
  6.9 0.3 collective-permute-start.7
  7.3 0.7 %collective-permute-done.1 = f32[4,384]{1,0:T(4,128)S(1)} collective-permute-done((f32[4,384]{1,0:T(4,128)S(1)}, f32[4,384]{1,0:T(4,128)S(1)}, u32[]{:S(2)}, u32[]{:S(2)}) %collective-permute-start.1) | collective-permute-done | bytes 6176 | tf_op jit(solution)/shard_map/ppermute | solution.py:328
  7.9 0.0 collective-permute-done.4.other_ref
  8.0 0.1 send.1
  8.1 1.6 %collective-permute-start.5 = (bf16[2,2,320,128]{3,2,1,0:T(8,128)(2,1)S(1)}, bf16[2,2,320,128]{3,2,1,0:T(8,128)(2,1)S(1)}, u32[]{:S(2)}, u32[]{:S(2)}) collective-permute-start(bf16[2,2,320,128]{3,2,1,0:T(8,128)(2,1)S(1)} %get-tuple-element.39), channel_id=1, source_target_pairs={{0,4},{4,0},{8,12},{12,8},{16,20},{20,16},{24,28},{28,24},{1,5},{5... | collective-permute-start | bytes 983048 | tf_op jit(solution)/shard_map/ppermute | solution.py:328
  9.7 1.5 %collective-permute-start.8 = (bf16[2,2,320,256]{3,2,1,0:T(8,128)(2,1)S(1)}, bf16[2,2,320,256]{3,2,1,0:T(8,128)(2,1)S(1)}, u32[]{:S(2)}, u32[]{:S(2)}) collective-permute-start(bf16[2,2,320,256]{3,2,1,0:T(8,128)(2,1)S(1)} %get-tuple-element.43), channel_id=1, source_target_pairs={{0,2},{1,3},{2,0},{3,1},{4,6},{5,7},{6,4},{7,5},{8,10},{9,11},{10,... | collective-permute-start | bytes 1966088 | tf_op jit(solution)/shard_map/ppermute | solution.py:328
  11.2 1.6 %collective-permute-start.2 = (f32[1,384]{1,0:T(1,128)S(1)}, f32[1,384]{1,0:T(1,128)S(1)}, u32[]{:S(2)}, u32[]{:S(2)}) collective-permute-start(f32[1,384]{1,0:T(1,128)S(1)} %get-tuple-element.65.token_ref), channel_id=1, source_target_pairs={{0,8},{4,12},{8,0},{12,4},{16,24},{20,28},{24,16},{28,20},{1,9},{5... | collective-permute-start | bytes 4616 | tf_op jit(solution)/shard_map/ppermute | solution.py:328
  12.7 2.3 %steering_far.4 = (bf16[640,512]{1,0:T(8,128)(2,1)S(1)}, bf16[640,512]{1,0:T(8,128)(2,1)S(1)}, f32[1,384]{1,0:T(1,128)S(1)}) custom-call(f32[1,384]{1,0:T(1,128)S(1)} %get-tuple-element.65.token_ref, s32[1280,512]{1,0:T(8,128)} %delays_ref.5), custom_call_target="tpu_custom_call" | custom-call | flops 1 | bytes 1 | tf_op jit(solution)/shard_map/steering_far/pallas_call | solution.py:60
  15.1 0.0 collective-permute-done.2
  15.1 2.7 %collective-permute-start.3 = (f32[1,384]{1,0:T(1,128)S(1)}, f32[1,384]{1,0:T(1,128)S(1)}, u32[]{:S(2)}, u32[]{:S(2)}) collective-permute-start(f32[1,384]{1,0:T(1,128)S(1)} %gate.5), channel_id=1, source_target_pairs={{0,16},{4,20},{8,24},{12,28},{16,0},{20,4},{24,8},{28,12},{1,17},{... | collective-permute-start | bytes 4616 | tf_op jit(solution)/shard_map/ppermute | solution.py:328
  17.8 2.3 %steering_far.5 = (bf16[640,512]{1,0:T(8,128)(2,1)S(1)}, bf16[640,512]{1,0:T(8,128)(2,1)S(1)}, f32[1,384]{1,0:T(1,128)S(1)}) custom-call(f32[1,384]{1,0:T(1,128)S(1)} %add.21.refs_0_.token_ref, s32[1280,512]{1,0:T(8,128)} %delays_ref.5), custom_call_target="tpu_custom_call" | custom-call | flops 1 | bytes 1 | tf_op jit(solution)/shard_map/steering_far/pallas_call | solution.py:60
  20.1 0.0 collective-permute-done.3
  20.1 0.0 collective-permute-done.5.refs_2_.from_ref
  20.1 0.6 %collective-permute-start.6 = (f32[3,384]{1,0:T(4,128)S(1)}, f32[3,384]{1,0:T(4,128)S(1)}, u32[]{:S(2)}, u32[]{:S(2)}) collective-permute-start(f32[3,384]{1,0:T(4,128)S(1)} %gate.6), channel_id=1, source_target_pairs={{0,4},{4,0},{8,12},{12,8},{16,20},{20,16},{24,28},{28,24},{1,5},{5... | collective-permute-start | bytes 13832 | tf_op jit(solution)/shard_map/ppermute | solution.py:328
  20.7 0.0 collective-permute-done.7.delays_ref
  20.7 1.1 %steering.1 = (bf16[640,512]{1,0:T(8,128)(2,1)S(1)}, bf16[640,512]{1,0:T(8,128)(2,1)S(1)}, f32[1,384]{1,0:T(1,128)S(1)}) custom-call(f32[1,384]{1,0:T(1,128)S(1)} %add.22.refs_1_.token_ref, s16[640,512]{1,0:T(8,128)(2,1)S(1)} %collective-permute-done.7.delays_ref), custom_call_target="tpu_custom_call" | custom-call | flops 1 | bytes 1 | tf_op jit(solution)/shard_map/steering/pallas_call | solution.py:60
  21.9 2.0 %collective-permute-done.6.far_ref = f32[3,384]{1,0:T(4,128)S(1)} collective-permute-done((f32[3,384]{1,0:T(4,128)S(1)}, f32[3,384]{1,0:T(4,128)S(1)}, u32[]{:S(2)}, u32[]{:S(2)}) %collective-permute-start.6) | collective-permute-done | bytes 4640 | tf_op jit(solution)/shard_map/ppermute | solution.py:328
  23.8 1.4 %beams_r.1 = (f32[256,256]{1,0:T(8,128)S(1)}, bf16[256,256]{1,0:T(8,128)(2,1)S(1)}) custom-call(f32[2,384]{1,0:T(2,128)S(1)} %pad_maximum_fusion.refs_0_.near_power_ref, f32[3,384]{1,0:T(4,128)S(1)} %collective-permute-done.6.far_ref, f32[1,384]{1,0:T(1,128)S(1)} %gate.7.level_ref.token_ref, bf16[2,320,256]{2,1,0:T(8,128)(2,1)S(1)} %get-tuple-element.37.own_ref, ...), custom_call_target="tpu_custom_call" | custom-call | flops 1 | bytes 1 | tf_op jit(solution)/shard_map/beams_r/pallas_call | solution.py:60
  25.2 0.6 %collective-permute-start.12 = (bf16[256,256]{1,0:T(8,128)(2,1)S(1)}, bf16[256,256]{1,0:T(8,128)(2,1)S(1)}, u32[]{:S(2)}, u32[]{:S(2)}) collective-permute-start(bf16[256,256]{1,0:T(8,128)(2,1)S(1)} %get-tuple-element.57), channel_id=1, source_target_pairs={{0,2},{1,3},{2,0},{3,1},{4,6},{5,7},{6,4},{7,5},{8,10},{9,11},{10,... | collective-permute-start | bytes 393224 | tf_op jit(solution)/shard_map/ppermute | solution.py:328
  25.8 0.4 collective-permute-done.8.from_ref
  26.2 1.3 %beams_s.3 = bf16[256,512]{1,0:T(8,128)(2,1)S(1)} custom-call(f32[2,384]{1,0:T(2,128)S(1)} %pad_maximum_fusion.refs_0_.near_power_ref, f32[2,384]{1,0:T(2,128)S(1)} %pad_maximum_fusion.1.far_ref, f32[1,384]{1,0:T(1,128)S(1)} %gate.7.level_ref.token_ref, bf16[2,320,256]{2,1,0:T(8,128)(2,1)S(1)} %get-tuple-element.37.own_ref, ...), custom_call_target="tpu_custom_call" | custom-call | flops 1 | bytes 1 | tf_op jit(solution)/shard_map/beams_s/pallas_call | solution.py:60
  27.6 0.6 %collective-permute-start.9 = (bf16[256,512]{1,0:T(8,128)(2,1)S(1)}, bf16[256,512]{1,0:T(8,128)(2,1)S(1)}, u32[]{:S(2)}, u32[]{:S(2)}) collective-permute-start(bf16[256,512]{1,0:T(8,128)(2,1)S(1)} %beams_s.3), channel_id=1, source_target_pairs={{0,4},{4,0},{8,12},{12,8},{16,20},{20,16},{24,28},{28,24},{1,5},{5... | collective-permute-start | bytes 786440 | tf_op jit(solution)/shard_map/ppermute | solution.py:328
  28.1 2.1 %collective-permute-done.12.other_ref = bf16[256,256]{1,0:T(8,128)(2,1)S(1)} collective-permute-done((bf16[256,256]{1,0:T(8,128)(2,1)S(1)}, bf16[256,256]{1,0:T(8,128)(2,1)S(1)}, u32[]{:S(2)}, u32[]{:S(2)}) %collective-permute-start.12) | collective-permute-done | bytes 131104 | tf_op jit(solution)/shard_map/ppermute | solution.py:328
  30.3 1.2 %collective-permute-start.13 = (bf16[256,256]{1,0:T(8,128)(2,1)S(1)}, bf16[256,256]{1,0:T(8,128)(2,1)S(1)}, u32[]{:S(2)}, u32[]{:S(2)}) collective-permute-start(bf16[256,256]{1,0:T(8,128)(2,1)S(1)} %get-tuple-element.59), channel_id=1, source_target_pairs={{0,8},{4,12},{8,0},{12,4},{16,24},{20,28},{24,16},{28,20},{1,9},{5... | collective-permute-start | bytes 393224 | tf_op jit(solution)/shard_map/ppermute | solution.py:328
  31.5 1.3 %beams_s.2.keep_ref = f32[256,512]{1,0:T(8,128)S(1)} custom-call(f32[2,384]{1,0:T(2,128)S(1)} %pad_maximum_fusion.refs_0_.near_power_ref, f32[2,384]{1,0:T(2,128)S(1)} %pad_maximum_fusion.1.far_ref, f32[1,384]{1,0:T(1,128)S(1)} %gate.7.level_ref.token_ref, bf16[2,320,256]{2,1,0:T(8,128)(2,1)S(1)} %get-tuple-element.37.own_ref, ...), custom_call_target="tpu_custom_call" | custom-call | flops 1 | bytes 1 | tf_op jit(solution)/shard_map/beams_s/pallas_call | solution.py:60
  32.9 1.9 %collective-permute-done.9.other_ref = bf16[256,512]{1,0:T(8,128)(2,1)S(1)} collective-permute-done((bf16[256,512]{1,0:T(8,128)(2,1)S(1)}, bf16[256,512]{1,0:T(8,128)(2,1)S(1)}, u32[]{:S(2)}, u32[]{:S(2)}) %collective-permute-start.9) | collective-permute-done | bytes 262176 | tf_op jit(solution)/shard_map/ppermute | solution.py:328
  34.8 0.1 step_s.3
  35.0 0.4 collective-permute-done.13.other_ref
  35.4 2.5 %collective-permute-start.14 = (bf16[256,256]{1,0:T(8,128)(2,1)S(1)}, bf16[256,256]{1,0:T(8,128)(2,1)S(1)}, u32[]{:S(2)}, u32[]{:S(2)}) collective-permute-start(bf16[256,256]{1,0:T(8,128)(2,1)S(1)} %get-tuple-element.62), channel_id=1, source_target_pairs={{0,16},{4,20},{8,24},{12,28},{16,0},{20,4},{24,8},{28,12},{1,17},{... | collective-permute-start | bytes 393224 | tf_op jit(solution)/shard_map/ppermute | solution.py:328
  37.9 1.6 %collective-permute-start.10 = (bf16[128,512]{1,0:T(8,128)(2,1)S(1)}, bf16[128,512]{1,0:T(8,128)(2,1)S(1)}, u32[]{:S(2)}, u32[]{:S(2)}) collective-permute-start(bf16[128,512]{1,0:T(8,128)(2,1)S(1)} %get-tuple-element.49), channel_id=1, source_target_pairs={{0,8},{4,12},{8,0},{12,4},{16,24},{20,28},{24,16},{28,20},{1,9},{5... | collective-permute-start | bytes 393224 | tf_op jit(solution)/shard_map/ppermute | solution.py:328
  39.5 3.4 %collective-permute-done.14.other_ref = bf16[256,256]{1,0:T(8,128)(2,1)S(1)} collective-permute-done((bf16[256,256]{1,0:T(8,128)(2,1)S(1)}, bf16[256,256]{1,0:T(8,128)(2,1)S(1)}, u32[]{:S(2)}, u32[]{:S(2)}) %collective-permute-start.14) | collective-permute-done | bytes 131104 | tf_op jit(solution)/shard_map/ppermute | solution.py:328
  42.8 0.9 %collective-permute-start.15 = (bf16[256,256]{1,0:T(8,128)(2,1)S(1)}, bf16[256,256]{1,0:T(8,128)(2,1)S(1)}, u32[]{:S(2)}, u32[]{:S(2)}) collective-permute-start(bf16[256,256]{1,0:T(8,128)(2,1)S(1)} %step_r.5.near_r), channel_id=1, source_target_pairs={{0,4},{4,0},{8,12},{12,8},{16,20},{20,16},{24,28},{28,24},{1,5},{5... | collective-permute-start | bytes 393224 | tf_op jit(solution)/shard_map/ppermute | solution.py:328
  43.8 0.0 collective-permute-done.10.other_ref
  43.8 1.6 %collective-permute-start.11 = (bf16[64,512]{1,0:T(8,128)(2,1)S(1)}, bf16[64,512]{1,0:T(8,128)(2,1)S(1)}, u32[]{:S(2)}, u32[]{:S(2)}) collective-permute-start(bf16[64,512]{1,0:T(8,128)(2,1)S(1)} %get-tuple-element.51), channel_id=1, source_target_pairs={{0,16},{4,20},{8,24},{12,28},{16,0},{20,4},{24,8},{28,12},{1,17},{... | collective-permute-start | bytes 196616 | tf_op jit(solution)/shard_map/ppermute | solution.py:328
  45.4 3.6 %collective-permute-done.11.other_ref = bf16[64,512]{1,0:T(8,128)(2,1)S(1)} collective-permute-done((bf16[64,512]{1,0:T(8,128)(2,1)S(1)}, bf16[64,512]{1,0:T(8,128)(2,1)S(1)}, u32[]{:S(2)}, u32[]{:S(2)}) %collective-permute-start.11) | collective-permute-done | bytes 65568 | tf_op jit(solution)/shard_map/ppermute | solution.py:328
  49.1 0.0 collective-permute-done.15.far_r
  49.1 0.3 field.3
  49.4 0.1 collective-permute-start.16
  49.5 0.3 field.2
  49.8 0.9 %collective-permute-done.16 = f32[2,64,128]{2,1,0:T(8,128)S(1)} collective-permute-done((f32[2,64,128]{2,1,0:T(8,128)S(1)}, f32[2,64,128]{2,1,0:T(8,128)S(1)}, u32[]{:S(2)}, u32[]{:S(2)}) %collective-permute-start.16) | collective-permute-done | bytes 65568 | tf_op jit(solution)/shard_map/ppermute | solution.py:328
  50.7 0.7 %maximum_bitcast_fusion = f32[2,2,128,64]{2,3,1,0:T(8,128)} fusion(f32[1,2,64,128]{3,2,1,0:T(8,128)S(1)} %get-tuple-element.64, f32[1,2,64,128]{3,2,1,0:T(8,128)S(1)} %get-tuple-element.63), kind=kLoop, calls=%fused_computation | loop fusion | flops 32768 | bytes 262144 | tf_op jit(solution)/shard_map/transpose | solution.py:460
  (19 shorter events, 0.2 us)
Async XLA Ops:
  1.5 6.5 %collective-permute-start.4 = (bf16[2,320,256]{2,1,0:T(8,128)(2,1)S(1)}, bf16[2,320,256]{2,1,0:T(8,128)(2,1)S(1)}, u32[]{:S(2)}, u32[]{:S(2)}) collective-permute-start(bf16[2,320,256]{2,1,0:T(8,128)(2,1)S(1)} %get-tuple-element.38), channel_id=1, source_target_pairs={{0,1},{1,0},{2,3},{3,2},{4,5},{5,4},{6,7},{7,6},{8,9},{9,8},{10,11... | collective-permute-start | bytes 983048 | tf_op jit(solution)/shard_map/ppermute | solution.py:328
  2.0 4.7 %collective-permute-start = (f32[4,384]{1,0:T(4,128)S(1)}, f32[4,384]{1,0:T(4,128)S(1)}, u32[]{:S(2)}, u32[]{:S(2)}) collective-permute-start(f32[4,384]{1,0:T(4,128)S(1)} %get-tuple-element.34), channel_id=1, source_target_pairs={{0,2},{1,3},{2,0},{3,1},{4,6},{5,7},{6,4},{7,5},{8,10},{9,11},{10,... | collective-permute-start | bytes 18440 | tf_op jit(solution)/shard_map/ppermute | solution.py:328
  6.7 1.2 %collective-permute-start.1 = (f32[4,384]{1,0:T(4,128)S(1)}, f32[4,384]{1,0:T(4,128)S(1)}, u32[]{:S(2)}, u32[]{:S(2)}) collective-permute-start(f32[4,384]{1,0:T(4,128)S(1)} %gate.4), channel_id=1, source_target_pairs={{0,1},{1,0},{2,3},{3,2},{4,5},{5,4},{6,7},{7,6},{8,9},{9,8},{10,11... | collective-permute-start | bytes 18440 | tf_op jit(solution)/shard_map/ppermute | solution.py:328
  6.9 13.8 %collective-permute-start.7 = (s16[640,512]{1,0:T(8,128)(2,1)S(1)}, s16[640,512]{1,0:T(8,128)(2,1)S(1)}, u32[]{:S(2)}, u32[]{:S(2)}) collective-permute-start(s16[640,512]{1,0:T(8,128)(2,1)S(1)} %get-tuple-element.41), channel_id=1, source_target_pairs={{0,1},{1,0},{2,3},{3,2},{4,5},{5,4},{6,7},{7,6},{8,9},{9,8},{10,11... | collective-permute-start | bytes 1966088 | tf_op jit(solution)/shard_map/ppermute | solution.py:328
  8.1 12.0 %collective-permute-start.5 = (bf16[2,2,320,128]{3,2,1,0:T(8,128)(2,1)S(1)}, bf16[2,2,320,128]{3,2,1,0:T(8,128)(2,1)S(1)}, u32[]{:S(2)}, u32[]{:S(2)}) collective-permute-start(bf16[2,2,320,128]{3,2,1,0:T(8,128)(2,1)S(1)} %get-tuple-element.39), channel_id=1, source_target_pairs={{0,4},{4,0},{8,12},{12,8},{16,20},{20,16},{24,28},{28,24},{1,5},{5... | collective-permute-start | bytes 983048 | tf_op jit(solution)/shard_map/ppermute | solution.py:328
  9.7 16.6 %collective-permute-start.8 = (bf16[2,2,320,256]{3,2,1,0:T(8,128)(2,1)S(1)}, bf16[2,2,320,256]{3,2,1,0:T(8,128)(2,1)S(1)}, u32[]{:S(2)}, u32[]{:S(2)}) collective-permute-start(bf16[2,2,320,256]{3,2,1,0:T(8,128)(2,1)S(1)} %get-tuple-element.43), channel_id=1, source_target_pairs={{0,2},{1,3},{2,0},{3,1},{4,6},{5,7},{6,4},{7,5},{8,10},{9,11},{10,... | collective-permute-start | bytes 1966088 | tf_op jit(solution)/shard_map/ppermute | solution.py:328
  11.2 3.9 %collective-permute-start.2 = (f32[1,384]{1,0:T(1,128)S(1)}, f32[1,384]{1,0:T(1,128)S(1)}, u32[]{:S(2)}, u32[]{:S(2)}) collective-permute-start(f32[1,384]{1,0:T(1,128)S(1)} %get-tuple-element.65.token_ref), channel_id=1, source_target_pairs={{0,8},{4,12},{8,0},{12,4},{16,24},{20,28},{24,16},{28,20},{1,9},{5... | collective-permute-start | bytes 4616 | tf_op jit(solution)/shard_map/ppermute | solution.py:328
  15.1 5.0 %collective-permute-start.3 = (f32[1,384]{1,0:T(1,128)S(1)}, f32[1,384]{1,0:T(1,128)S(1)}, u32[]{:S(2)}, u32[]{:S(2)}) collective-permute-start(f32[1,384]{1,0:T(1,128)S(1)} %gate.5), channel_id=1, source_target_pairs={{0,16},{4,20},{8,24},{12,28},{16,0},{20,4},{24,8},{28,12},{1,17},{... | collective-permute-start | bytes 4616 | tf_op jit(solution)/shard_map/ppermute | solution.py:328
  20.1 3.7 %collective-permute-start.6 = (f32[3,384]{1,0:T(4,128)S(1)}, f32[3,384]{1,0:T(4,128)S(1)}, u32[]{:S(2)}, u32[]{:S(2)}) collective-permute-start(f32[3,384]{1,0:T(4,128)S(1)} %gate.6), channel_id=1, source_target_pairs={{0,4},{4,0},{8,12},{12,8},{16,20},{20,16},{24,28},{28,24},{1,5},{5... | collective-permute-start | bytes 13832 | tf_op jit(solution)/shard_map/ppermute | solution.py:328
  25.2 5.0 %collective-permute-start.12 = (bf16[256,256]{1,0:T(8,128)(2,1)S(1)}, bf16[256,256]{1,0:T(8,128)(2,1)S(1)}, u32[]{:S(2)}, u32[]{:S(2)}) collective-permute-start(bf16[256,256]{1,0:T(8,128)(2,1)S(1)} %get-tuple-element.57), channel_id=1, source_target_pairs={{0,2},{1,3},{2,0},{3,1},{4,6},{5,7},{6,4},{7,5},{8,10},{9,11},{10,... | collective-permute-start | bytes 393224 | tf_op jit(solution)/shard_map/ppermute | solution.py:328
  27.6 7.3 %collective-permute-start.9 = (bf16[256,512]{1,0:T(8,128)(2,1)S(1)}, bf16[256,512]{1,0:T(8,128)(2,1)S(1)}, u32[]{:S(2)}, u32[]{:S(2)}) collective-permute-start(bf16[256,512]{1,0:T(8,128)(2,1)S(1)} %beams_s.3), channel_id=1, source_target_pairs={{0,4},{4,0},{8,12},{12,8},{16,20},{20,16},{24,28},{28,24},{1,5},{5... | collective-permute-start | bytes 786440 | tf_op jit(solution)/shard_map/ppermute | solution.py:328
  30.3 5.0 %collective-permute-start.13 = (bf16[256,256]{1,0:T(8,128)(2,1)S(1)}, bf16[256,256]{1,0:T(8,128)(2,1)S(1)}, u32[]{:S(2)}, u32[]{:S(2)}) collective-permute-start(bf16[256,256]{1,0:T(8,128)(2,1)S(1)} %get-tuple-element.59), channel_id=1, source_target_pairs={{0,8},{4,12},{8,0},{12,4},{16,24},{20,28},{24,16},{28,20},{1,9},{5... | collective-permute-start | bytes 393224 | tf_op jit(solution)/shard_map/ppermute | solution.py:328
  35.4 7.4 %collective-permute-start.14 = (bf16[256,256]{1,0:T(8,128)(2,1)S(1)}, bf16[256,256]{1,0:T(8,128)(2,1)S(1)}, u32[]{:S(2)}, u32[]{:S(2)}) collective-permute-start(bf16[256,256]{1,0:T(8,128)(2,1)S(1)} %get-tuple-element.62), channel_id=1, source_target_pairs={{0,16},{4,20},{8,24},{12,28},{16,0},{20,4},{24,8},{28,12},{1,17},{... | collective-permute-start | bytes 393224 | tf_op jit(solution)/shard_map/ppermute | solution.py:328
  37.9 5.9 %collective-permute-start.10 = (bf16[128,512]{1,0:T(8,128)(2,1)S(1)}, bf16[128,512]{1,0:T(8,128)(2,1)S(1)}, u32[]{:S(2)}, u32[]{:S(2)}) collective-permute-start(bf16[128,512]{1,0:T(8,128)(2,1)S(1)} %get-tuple-element.49), channel_id=1, source_target_pairs={{0,8},{4,12},{8,0},{12,4},{16,24},{20,28},{24,16},{28,20},{1,9},{5... | collective-permute-start | bytes 393224 | tf_op jit(solution)/shard_map/ppermute | solution.py:328
  42.8 6.2 %collective-permute-start.15 = (bf16[256,256]{1,0:T(8,128)(2,1)S(1)}, bf16[256,256]{1,0:T(8,128)(2,1)S(1)}, u32[]{:S(2)}, u32[]{:S(2)}) collective-permute-start(bf16[256,256]{1,0:T(8,128)(2,1)S(1)} %step_r.5.near_r), channel_id=1, source_target_pairs={{0,4},{4,0},{8,12},{12,8},{16,20},{20,16},{24,28},{28,24},{1,5},{5... | collective-permute-start | bytes 393224 | tf_op jit(solution)/shard_map/ppermute | solution.py:328
  43.8 5.2 %collective-permute-start.11 = (bf16[64,512]{1,0:T(8,128)(2,1)S(1)}, bf16[64,512]{1,0:T(8,128)(2,1)S(1)}, u32[]{:S(2)}, u32[]{:S(2)}) collective-permute-start(bf16[64,512]{1,0:T(8,128)(2,1)S(1)} %get-tuple-element.51), channel_id=1, source_target_pairs={{0,16},{4,20},{8,24},{12,28},{16,0},{20,4},{24,8},{28,12},{1,17},{... | collective-permute-start | bytes 196616 | tf_op jit(solution)/shard_map/ppermute | solution.py:328
  49.4 1.3 %collective-permute-start.16 = (f32[2,64,128]{2,1,0:T(8,128)S(1)}, f32[2,64,128]{2,1,0:T(8,128)S(1)}, u32[]{:S(2)}, u32[]{:S(2)}) collective-permute-start(f32[2,64,128]{2,1,0:T(8,128)S(1)} %field.3), channel_id=1, source_target_pairs={{0,1},{1,0},{2,3},{3,2},{4,5},{5,4},{6,7},{7,6},{8,9},{9,8},{10,11... | collective-permute-start | bytes 196616 | tf_op jit(solution)/shard_map/ppermute | solution.py:328

commit v7 on v6

--- a/solution.py
+++ b/solution.py
@@ -381,18 +381,20 @@
     from_x, from_y = swap(to_x, "col", 2), swap(to_y, "row", 1)
 
     row_bits, col_bits = bits(n_row, 2), bits(n_col, 4)
-    first, *others = [("row", bit) for bit in row_bits] + [("col", bit) for bit in col_bits]
+    first, *others = [("row", bit) for bit in row_bits[::-1]] + [("col", bit) for bit in col_bits]
     *steer_s, token = steering_far(starts_s(0, 2), per, 2, level, delays_s, block=block_s)
     level = level + swap(level, *first)
-    cos, sin, next_token = steering_far(starts_s(2, 4), per, 2, level, delays_s, block=block_s)
+    cos, sin, next_token = steering_far(starts_s(2, 3), per, 1, level, delays_s, block=block_s)
     steer_s += [cos, sin]
     for step in others:
         level = gated([level], [token])
         level = level + swap(level, *step)
     cos, sin, token = steering(level, other_r)
     steer_r += [cos, sin]
+    cos, sin, last_token = steering_far(starts_s(3, 4), per, 1, level, delays_s, block=block_s)
+    steer_s += [cos, sin]
     far_y = swap(gated([power, level], [from_y, next_token]), "row", 1)
-    level = gated([level + far_y[2:]], [token])
+    level = gated([level + far_y[2:]], [token, last_token])
 
     keep_r, send_r = beams(
         ((0, 2), (1, 3)),
@@ -410,7 +412,7 @@
     )
     (send_s,), (keep_s,) = (
         beams(
-            ((0, 1), (2, 3)),
+            ((0, 1), (2,), (3,)),
             lambda windows: slice(None),
             None,
             None,

time: 51.9 us -> 51.7 us (level)
  Pallas kernels: 14.3 us -> 15.7 us
  waiting for transfers between devices: 15.4 us -> 14.3 us
    pallas_call x21 -> x22, Pallas kernels: 14.3 us -> 15.7 us  [kernel_call(): pl.pallas_call(body, out_shape=out, in_specs=[pl.BlockSpec(memory_space=s...]
    ppermute x17, waiting for transfers between devices: 15.4 us -> 14.3 us  [swap(): return lax.ppermute(value, axis, [(i, i ^ bit) for i in range(size)])]
  transfers between devices with their start and end apart: 17 -> 17, of which waited for: 9 -> 9; matrix products, arithmetic and copies ran while one was open for 0% -> 0% of each run, Pallas kernels for 24% -> 27%
where the time goes in v7:
time: 51.7 us; the launch traced here: 51.4 us
  starting transfers between devices  20.4 us (39%)
  Pallas kernels  15.7 us (30%)
  waiting for transfers between devices  14.3 us (28%)
  other arithmetic  0.72 us (1%)
    ppermute x17, starting transfers between devices, swap(): return lax.ppermute(value, axis, [(i, i ^ bit) for i in range(size)])  20.4 us
    pallas_call x22, Pallas kernels, kernel_call(): pl.pallas_call(body, out_shape=out, in_specs=[pl.BlockSpec(memory_space=s...  15.7 us
    ppermute x17, waiting for transfers between devices, swap(): return lax.ppermute(value, axis, [(i, i ^ bit) for i in range(size)])  14.3 us
  transfers between devices with their start and end apart: 17, of which 9 were waited for; matrix products, arithmetic and copies ran while one was open for 0% of the time, Pallas kernels for 27%

profile of v7, /device:TPU:0, one launch (start us, length us, event | category | flops | bytes accessed | tf_op | source)
XLA Modules:
  0.0 51.4 jit_solution(6645640081283884695)
XLA Ops:
  0.0 1.5 %power.1 = (f32[4,384]{1,0:T(4,128)S(1)}, bf16[2,320,256]{2,1,0:T(8,128)(2,1)S(1)}, bf16[2,320,256]{2,1,0:T(8,128)(2,1)S(1)}) custom-call(s32[2]{0:T(128)} %wl_ref.1, bf16[2,2,320,256]{3,2,1,0:T(8,128)(2,1)} %spec_ref.1), custom_call_target="tpu_custom_call" | custom-call | flops 1 | bytes 1 | tf_op jit(solution)/shard_map/power/pallas_call | solution.py:60
  1.5 0.5 %collective-permute-start.4 = (bf16[2,320,256]{2,1,0:T(8,128)(2,1)S(1)}, bf16[2,320,256]{2,1,0:T(8,128)(2,1)S(1)}, u32[]{:S(2)}, u32[]{:S(2)}) collective-permute-start(bf16[2,320,256]{2,1,0:T(8,128)(2,1)S(1)} %get-tuple-element.41), channel_id=1, source_target_pairs={{0,1},{1,0},{2,3},{3,2},{4,5},{5,4},{6,7},{7,6},{8,9},{9,8},{10,11... | collective-permute-start | bytes 983048 | tf_op jit(solution)/shard_map/ppermute | solution.py:328
  2.0 2.6 %collective-permute-start = (f32[4,384]{1,0:T(4,128)S(1)}, f32[4,384]{1,0:T(4,128)S(1)}, u32[]{:S(2)}, u32[]{:S(2)}) collective-permute-start(f32[4,384]{1,0:T(4,128)S(1)} %get-tuple-element.37), channel_id=1, source_target_pairs={{0,2},{1,3},{2,0},{3,1},{4,6},{5,7},{6,4},{7,5},{8,10},{9,11},{10,... | collective-permute-start | bytes 18440 | tf_op jit(solution)/shard_map/ppermute | solution.py:328
  4.6 2.1 %steering_far.4 = (bf16[640,512]{1,0:T(8,128)(2,1)S(1)}, bf16[640,512]{1,0:T(8,128)(2,1)S(1)}, f32[1,384]{1,0:T(1,128)S(1)}, s16[640,512]{1,0:T(8,128)(2,1)S(1)}) custom-call(f32[1,384]{1,0:T(1,128)S(1)} %slice.34.token_ref, s32[2560,512]{1,0:T(8,128)} %delays_ref.4), custom_call_target="tpu_custom_call" | custom-call | flops 1 | bytes 1 | tf_op jit(solution)/shard_map/steering_far/pallas_call | solution.py:60
  6.7 0.0 collective-permute-done
  6.7 0.2 collective-permute-start.1
  6.9 0.3 collective-permute-start.7
  7.3 0.7 %collective-permute-done.1 = f32[4,384]{1,0:T(4,128)S(1)} collective-permute-done((f32[4,384]{1,0:T(4,128)S(1)}, f32[4,384]{1,0:T(4,128)S(1)}, u32[]{:S(2)}, u32[]{:S(2)}) %collective-permute-start.1) | collective-permute-done | bytes 6176 | tf_op jit(solution)/shard_map/ppermute | solution.py:328
  7.9 0.0 collective-permute-done.4.other_ref
  8.0 0.1 send.1
  8.1 1.6 %collective-permute-start.5 = (bf16[2,2,320,128]{3,2,1,0:T(8,128)(2,1)S(1)}, bf16[2,2,320,128]{3,2,1,0:T(8,128)(2,1)S(1)}, u32[]{:S(2)}, u32[]{:S(2)}) collective-permute-start(bf16[2,2,320,128]{3,2,1,0:T(8,128)(2,1)S(1)} %get-tuple-element.42), channel_id=1, source_target_pairs={{0,4},{4,0},{8,12},{12,8},{16,20},{20,16},{24,28},{28,24},{1,5},{5... | collective-permute-start | bytes 983048 | tf_op jit(solution)/shard_map/ppermute | solution.py:328
  9.7 1.5 %collective-permute-start.8 = (bf16[2,2,320,256]{3,2,1,0:T(8,128)(2,1)S(1)}, bf16[2,2,320,256]{3,2,1,0:T(8,128)(2,1)S(1)}, u32[]{:S(2)}, u32[]{:S(2)}) collective-permute-start(bf16[2,2,320,256]{3,2,1,0:T(8,128)(2,1)S(1)} %get-tuple-element.47), channel_id=1, source_target_pairs={{0,2},{1,3},{2,0},{3,1},{4,6},{5,7},{6,4},{7,5},{8,10},{9,11},{10,... | collective-permute-start | bytes 1966088 | tf_op jit(solution)/shard_map/ppermute | solution.py:328
  11.2 2.6 %collective-permute-start.2 = (f32[1,384]{1,0:T(1,128)S(1)}, f32[1,384]{1,0:T(1,128)S(1)}, u32[]{:S(2)}, u32[]{:S(2)}) collective-permute-start(f32[1,384]{1,0:T(1,128)S(1)} %get-tuple-element.71.token_ref), channel_id=1, source_target_pairs={{0,16},{4,20},{8,24},{12,28},{16,0},{20,4},{24,8},{28,12},{1,17},{... | collective-permute-start | bytes 4616 | tf_op jit(solution)/shard_map/ppermute | solution.py:328
  13.7 2.3 %steering_far.5 = (bf16[640,512]{1,0:T(8,128)(2,1)S(1)}, bf16[640,512]{1,0:T(8,128)(2,1)S(1)}, f32[1,384]{1,0:T(1,128)S(1)}) custom-call(f32[1,384]{1,0:T(1,128)S(1)} %get-tuple-element.71.token_ref, s32[1280,512]{1,0:T(8,128)} %delays_ref.7), custom_call_target="tpu_custom_call" | custom-call | flops 1 | bytes 1 | tf_op jit(solution)/shard_map/steering_far/pallas_call | solution.py:60
  16.1 0.0 collective-permute-done.2
  16.1 1.6 %collective-permute-start.3 = (f32[1,384]{1,0:T(1,128)S(1)}, f32[1,384]{1,0:T(1,128)S(1)}, u32[]{:S(2)}, u32[]{:S(2)}) collective-permute-start(f32[1,384]{1,0:T(1,128)S(1)} %gate.5), channel_id=1, source_target_pairs={{0,8},{4,12},{8,0},{12,4},{16,24},{20,28},{24,16},{28,20},{1,9},{5... | collective-permute-start | bytes 4616 | tf_op jit(solution)/shard_map/ppermute | solution.py:328
  17.8 1.7 %steering_far.6 = (bf16[320,512]{1,0:T(8,128)(2,1)S(1)}, bf16[320,512]{1,0:T(8,128)(2,1)S(1)}, f32[1,384]{1,0:T(1,128)S(1)}) custom-call(f32[1,384]{1,0:T(1,128)S(1)} %add.21.refs_0_.token_ref, s32[1280,512]{1,0:T(8,128)} %delays_ref.7), custom_call_target="tpu_custom_call" | custom-call | flops 1 | bytes 1 | tf_op jit(solution)/shard_map/steering_far/pallas_call | solution.py:60
  19.5 0.3 collective-permute-done.3
  19.8 0.0 collective-permute-done.5.refs_2_.from_ref
  19.8 0.6 %collective-permute-start.6 = (f32[3,384]{1,0:T(4,128)S(1)}, f32[3,384]{1,0:T(4,128)S(1)}, u32[]{:S(2)}, u32[]{:S(2)}) collective-permute-start(f32[3,384]{1,0:T(4,128)S(1)} %gate.6), channel_id=1, source_target_pairs={{0,4},{4,0},{8,12},{12,8},{16,20},{20,16},{24,28},{28,24},{1,5},{5... | collective-permute-start | bytes 13832 | tf_op jit(solution)/shard_map/ppermute | solution.py:328
  20.3 1.7 %steering_far.7 = (bf16[320,512]{1,0:T(8,128)(2,1)S(1)}, bf16[320,512]{1,0:T(8,128)(2,1)S(1)}, f32[1,384]{1,0:T(1,128)S(1)}) custom-call(f32[1,384]{1,0:T(1,128)S(1)} %add.22.refs_1_.token_ref, s32[1280,512]{1,0:T(8,128)} %delays_ref.7), custom_call_target="tpu_custom_call" | custom-call | flops 1 | bytes 1 | tf_op jit(solution)/shard_map/steering_far/pallas_call | solution.py:60
  22.1 0.0 collective-permute-done.7.delays_ref
  22.1 1.1 %steering.1 = (bf16[640,512]{1,0:T(8,128)(2,1)S(1)}, bf16[640,512]{1,0:T(8,128)(2,1)S(1)}, f32[1,384]{1,0:T(1,128)S(1)}) custom-call(f32[1,384]{1,0:T(1,128)S(1)} %add.22.refs_1_.token_ref, s16[640,512]{1,0:T(8,128)(2,1)S(1)} %collective-permute-done.7.delays_ref), custom_call_target="tpu_custom_call" | custom-call | flops 1 | bytes 1 | tf_op jit(solution)/shard_map/steering/pallas_call | solution.py:60
  23.2 0.2 collective-permute-done.6.far_ref
  23.5 1.4 %beams_r.1 = (f32[256,256]{1,0:T(8,128)S(1)}, bf16[256,256]{1,0:T(8,128)(2,1)S(1)}) custom-call(f32[2,384]{1,0:T(2,128)S(1)} %pad_maximum_fusion.refs_0_.near_power_ref, f32[3,384]{1,0:T(4,128)S(1)} %collective-permute-done.6.far_ref, f32[1,384]{1,0:T(1,128)S(1)} %gate.7.level_ref.token_ref, bf16[2,320,256]{2,1,0:T(8,128)(2,1)S(1)} %get-tuple-element.40.own_ref, ...), custom_call_target="tpu_custom_call" | custom-call | flops 1 | bytes 1 | tf_op jit(solution)/shard_map/beams_r/pallas_call | solution.py:60
  24.9 0.6 %collective-permute-start.12 = (bf16[256,256]{1,0:T(8,128)(2,1)S(1)}, bf16[256,256]{1,0:T(8,128)(2,1)S(1)}, u32[]{:S(2)}, u32[]{:S(2)}) collective-permute-start(bf16[256,256]{1,0:T(8,128)(2,1)S(1)} %get-tuple-element.63), channel_id=1, source_target_pairs={{0,2},{1,3},{2,0},{3,1},{4,6},{5,7},{6,4},{7,5},{8,10},{9,11},{10,... | collective-permute-start | bytes 393224 | tf_op jit(solution)/shard_map/ppermute | solution.py:328
  25.5 1.0 %collective-permute-done.8.from_ref = bf16[2,2,320,256]{3,2,1,0:T(8,128)(2,1)S(1)} collective-permute-done((bf16[2,2,320,256]{3,2,1,0:T(8,128)(2,1)S(1)}, bf16[2,2,320,256]{3,2,1,0:T(8,128)(2,1)S(1)}, u32[]{:S(2)}, u32[]{:S(2)}) %collective-permute-start.8) | collective-permute-done | bytes 655392 | tf_op jit(solution)/shard_map/ppermute | solution.py:328
  26.5 1.4 %beams_s.3 = bf16[256,512]{1,0:T(8,128)(2,1)S(1)} custom-call(f32[2,384]{1,0:T(2,128)S(1)} %pad_maximum_fusion.refs_0_.near_power_ref, f32[2,384]{1,0:T(2,128)S(1)} %pad_maximum_fusion.1.far_ref, f32[1,384]{1,0:T(1,128)S(1)} %gate.7.level_ref.token_ref, bf16[2,320,256]{2,1,0:T(8,128)(2,1)S(1)} %get-tuple-element.40.own_ref, ...), custom_call_target="tpu_custom_call" | custom-call | flops 1 | bytes 1 | tf_op jit(solution)/shard_map/beams_s/pallas_call | solution.py:60
  27.9 0.4 collective-permute-start.9
  28.3 1.6 %collective-permute-done.12.other_ref = bf16[256,256]{1,0:T(8,128)(2,1)S(1)} collective-permute-done((bf16[256,256]{1,0:T(8,128)(2,1)S(1)}, bf16[256,256]{1,0:T(8,128)(2,1)S(1)}, u32[]{:S(2)}, u32[]{:S(2)}) %collective-permute-start.12) | collective-permute-done | bytes 131104 | tf_op jit(solution)/shard_map/ppermute | solution.py:328
  29.9 1.6 %collective-permute-start.13 = (bf16[256,256]{1,0:T(8,128)(2,1)S(1)}, bf16[256,256]{1,0:T(8,128)(2,1)S(1)}, u32[]{:S(2)}, u32[]{:S(2)}) collective-permute-start(bf16[256,256]{1,0:T(8,128)(2,1)S(1)} %get-tuple-element.65), channel_id=1, source_target_pairs={{0,8},{4,12},{8,0},{12,4},{16,24},{20,28},{24,16},{28,20},{1,9},{5... | collective-permute-start | bytes 393224 | tf_op jit(solution)/shard_map/ppermute | solution.py:328
  31.6 1.5 %beams_s.2.keep_ref = f32[256,512]{1,0:T(8,128)S(1)} custom-call(f32[2,384]{1,0:T(2,128)S(1)} %pad_maximum_fusion.refs_0_.near_power_ref, f32[2,384]{1,0:T(2,128)S(1)} %pad_maximum_fusion.1.far_ref, f32[1,384]{1,0:T(1,128)S(1)} %gate.7.level_ref.token_ref, bf16[2,320,256]{2,1,0:T(8,128)(2,1)S(1)} %get-tuple-element.40.own_ref, ...), custom_call_target="tpu_custom_call" | custom-call | flops 1 | bytes 1 | tf_op jit(solution)/shard_map/beams_s/pallas_call | solution.py:60
  33.0 1.9 %collective-permute-done.9.other_ref = bf16[256,512]{1,0:T(8,128)(2,1)S(1)} collective-permute-done((bf16[256,512]{1,0:T(8,128)(2,1)S(1)}, bf16[256,512]{1,0:T(8,128)(2,1)S(1)}, u32[]{:S(2)}, u32[]{:S(2)}) %collective-permute-start.9) | collective-permute-done | bytes 262176 | tf_op jit(solution)/shard_map/ppermute | solution.py:328
  34.9 0.1 step_s.3
  35.1 0.0 collective-permute-done.13.other_ref
  35.1 2.7 %collective-permute-start.14 = (bf16[256,256]{1,0:T(8,128)(2,1)S(1)}, bf16[256,256]{1,0:T(8,128)(2,1)S(1)}, u32[]{:S(2)}, u32[]{:S(2)}) collective-permute-start(bf16[256,256]{1,0:T(8,128)(2,1)S(1)} %get-tuple-element.68), channel_id=1, source_target_pairs={{0,16},{4,20},{8,24},{12,28},{16,0},{20,4},{24,8},{28,12},{1,17},{... | collective-permute-start | bytes 393224 | tf_op jit(solution)/shard_map/ppermute | solution.py:328
  37.8 1.6 %collective-permute-start.10 = (bf16[128,512]{1,0:T(8,128)(2,1)S(1)}, bf16[128,512]{1,0:T(8,128)(2,1)S(1)}, u32[]{:S(2)}, u32[]{:S(2)}) collective-permute-start(bf16[128,512]{1,0:T(8,128)(2,1)S(1)} %get-tuple-element.55), channel_id=1, source_target_pairs={{0,8},{4,12},{8,0},{12,4},{16,24},{20,28},{24,16},{28,20},{1,9},{5... | collective-permute-start | bytes 393224 | tf_op jit(solution)/shard_map/ppermute | solution.py:328
  39.4 3.2 %collective-permute-done.14.other_ref = bf16[256,256]{1,0:T(8,128)(2,1)S(1)} collective-permute-done((bf16[256,256]{1,0:T(8,128)(2,1)S(1)}, bf16[256,256]{1,0:T(8,128)(2,1)S(1)}, u32[]{:S(2)}, u32[]{:S(2)}) %collective-permute-start.14) | collective-permute-done | bytes 131104 | tf_op jit(solution)/shard_map/ppermute | solution.py:328
  42.6 1.2 %collective-permute-start.15 = (bf16[256,256]{1,0:T(8,128)(2,1)S(1)}, bf16[256,256]{1,0:T(8,128)(2,1)S(1)}, u32[]{:S(2)}, u32[]{:S(2)}) collective-permute-start(bf16[256,256]{1,0:T(8,128)(2,1)S(1)} %step_r.5.near_r), channel_id=1, source_target_pairs={{0,4},{4,0},{8,12},{12,8},{16,20},{20,16},{24,28},{28,24},{1,5},{5... | collective-permute-start | bytes 393224 | tf_op jit(solution)/shard_map/ppermute | solution.py:328
  43.8 0.0 collective-permute-done.10.other_ref
  43.9 0.8 %collective-permute-start.11 = (bf16[64,512]{1,0:T(8,128)(2,1)S(1)}, bf16[64,512]{1,0:T(8,128)(2,1)S(1)}, u32[]{:S(2)}, u32[]{:S(2)}) collective-permute-start(bf16[64,512]{1,0:T(8,128)(2,1)S(1)} %get-tuple-element.57), channel_id=1, source_target_pairs={{0,16},{4,20},{8,24},{12,28},{16,0},{20,4},{24,8},{28,12},{1,17},{... | collective-permute-start | bytes 196616 | tf_op jit(solution)/shard_map/ppermute | solution.py:328
  44.6 4.5 %collective-permute-done.11.other_ref = bf16[64,512]{1,0:T(8,128)(2,1)S(1)} collective-permute-done((bf16[64,512]{1,0:T(8,128)(2,1)S(1)}, bf16[64,512]{1,0:T(8,128)(2,1)S(1)}, u32[]{:S(2)}, u32[]{:S(2)}) %collective-permute-start.11) | collective-permute-done | bytes 65568 | tf_op jit(solution)/shard_map/ppermute | solution.py:328
  49.1 0.0 collective-permute-done.15.far_r
  49.1 0.3 field.3
  49.4 0.1 collective-permute-start.16
  49.5 0.3 field.2
  49.8 0.9 %collective-permute-done.16 = f32[2,64,128]{2,1,0:T(8,128)S(1)} collective-permute-done((f32[2,64,128]{2,1,0:T(8,128)S(1)}, f32[2,64,128]{2,1,0:T(8,128)S(1)}, u32[]{:S(2)}, u32[]{:S(2)}) %collective-permute-start.16) | collective-permute-done | bytes 65568 | tf_op jit(solution)/shard_map/ppermute | solution.py:328
  50.8 0.7 %maximum_bitcast_fusion = f32[2,2,128,64]{2,3,1,0:T(8,128)} fusion(f32[1,2,64,128]{3,2,1,0:T(8,128)S(1)} %get-tuple-element.70, f32[1,2,64,128]{3,2,1,0:T(8,128)S(1)} %get-tuple-element.69), kind=kLoop, calls=%fused_computation | loop fusion | flops 32768 | bytes 262144 | tf_op jit(solution)/shard_map/transpose | solution.py:462
  (19 shorter events, 0.2 us)
Async XLA Ops:
  1.5 6.5 %collective-permute-start.4 = (bf16[2,320,256]{2,1,0:T(8,128)(2,1)S(1)}, bf16[2,320,256]{2,1,0:T(8,128)(2,1)S(1)}, u32[]{:S(2)}, u32[]{:S(2)}) collective-permute-start(bf16[2,320,256]{2,1,0:T(8,128)(2,1)S(1)} %get-tuple-element.41), channel_id=1, source_target_pairs={{0,1},{1,0},{2,3},{3,2},{4,5},{5,4},{6,7},{7,6},{8,9},{9,8},{10,11... | collective-permute-start | bytes 983048 | tf_op jit(solution)/shard_map/ppermute | solution.py:328
  2.0 4.7 %collective-permute-start = (f32[4,384]{1,0:T(4,128)S(1)}, f32[4,384]{1,0:T(4,128)S(1)}, u32[]{:S(2)}, u32[]{:S(2)}) collective-permute-start(f32[4,384]{1,0:T(4,128)S(1)} %get-tuple-element.37), channel_id=1, source_target_pairs={{0,2},{1,3},{2,0},{3,1},{4,6},{5,7},{6,4},{7,5},{8,10},{9,11},{10,... | collective-permute-start | bytes 18440 | tf_op jit(solution)/shard_map/ppermute | solution.py:328
  6.7 1.2 %collective-permute-start.1 = (f32[4,384]{1,0:T(4,128)S(1)}, f32[4,384]{1,0:T(4,128)S(1)}, u32[]{:S(2)}, u32[]{:S(2)}) collective-permute-start(f32[4,384]{1,0:T(4,128)S(1)} %gate.4), channel_id=1, source_target_pairs={{0,1},{1,0},{2,3},{3,2},{4,5},{5,4},{6,7},{7,6},{8,9},{9,8},{10,11... | collective-permute-start | bytes 18440 | tf_op jit(solution)/shard_map/ppermute | solution.py:328
  6.9 15.1 %collective-permute-start.7 = (s16[640,512]{1,0:T(8,128)(2,1)S(1)}, s16[640,512]{1,0:T(8,128)(2,1)S(1)}, u32[]{:S(2)}, u32[]{:S(2)}) collective-permute-start(s16[640,512]{1,0:T(8,128)(2,1)S(1)} %get-tuple-element.44), channel_id=1, source_target_pairs={{0,1},{1,0},{2,3},{3,2},{4,5},{5,4},{6,7},{7,6},{8,9},{9,8},{10,11... | collective-permute-start | bytes 1966088 | tf_op jit(solution)/shard_map/ppermute | solution.py:328
  8.1 11.7 %collective-permute-start.5 = (bf16[2,2,320,128]{3,2,1,0:T(8,128)(2,1)S(1)}, bf16[2,2,320,128]{3,2,1,0:T(8,128)(2,1)S(1)}, u32[]{:S(2)}, u32[]{:S(2)}) collective-permute-start(bf16[2,2,320,128]{3,2,1,0:T(8,128)(2,1)S(1)} %get-tuple-element.42), channel_id=1, source_target_pairs={{0,4},{4,0},{8,12},{12,8},{16,20},{20,16},{24,28},{28,24},{1,5},{5... | collective-permute-start | bytes 983048 | tf_op jit(solution)/shard_map/ppermute | solution.py:328
  9.7 16.8 %collective-permute-start.8 = (bf16[2,2,320,256]{3,2,1,0:T(8,128)(2,1)S(1)}, bf16[2,2,320,256]{3,2,1,0:T(8,128)(2,1)S(1)}, u32[]{:S(2)}, u32[]{:S(2)}) collective-permute-start(bf16[2,2,320,256]{3,2,1,0:T(8,128)(2,1)S(1)} %get-tuple-element.47), channel_id=1, source_target_pairs={{0,2},{1,3},{2,0},{3,1},{4,6},{5,7},{6,4},{7,5},{8,10},{9,11},{10,... | collective-permute-start | bytes 1966088 | tf_op jit(solution)/shard_map/ppermute | solution.py:328
  11.2 4.9 %collective-permute-start.2 = (f32[1,384]{1,0:T(1,128)S(1)}, f32[1,384]{1,0:T(1,128)S(1)}, u32[]{:S(2)}, u32[]{:S(2)}) collective-permute-start(f32[1,384]{1,0:T(1,128)S(1)} %get-tuple-element.71.token_ref), channel_id=1, source_target_pairs={{0,16},{4,20},{8,24},{12,28},{16,0},{20,4},{24,8},{28,12},{1,17},{... | collective-permute-start | bytes 4616 | tf_op jit(solution)/shard_map/ppermute | solution.py:328
  16.1 3.6 %collective-permute-start.3 = (f32[1,384]{1,0:T(1,128)S(1)}, f32[1,384]{1,0:T(1,128)S(1)}, u32[]{:S(2)}, u32[]{:S(2)}) collective-permute-start(f32[1,384]{1,0:T(1,128)S(1)} %gate.5), channel_id=1, source_target_pairs={{0,8},{4,12},{8,0},{12,4},{16,24},{20,28},{24,16},{28,20},{1,9},{5... | collective-permute-start | bytes 4616 | tf_op jit(solution)/shard_map/ppermute | solution.py:328
  19.8 3.7 %collective-permute-start.6 = (f32[3,384]{1,0:T(4,128)S(1)}, f32[3,384]{1,0:T(4,128)S(1)}, u32[]{:S(2)}, u32[]{:S(2)}) collective-permute-start(f32[3,384]{1,0:T(4,128)S(1)} %gate.6), channel_id=1, source_target_pairs={{0,4},{4,0},{8,12},{12,8},{16,20},{20,16},{24,28},{28,24},{1,5},{5... | collective-permute-start | bytes 13832 | tf_op jit(solution)/shard_map/ppermute | solution.py:328
  24.9 5.0 %collective-permute-start.12 = (bf16[256,256]{1,0:T(8,128)(2,1)S(1)}, bf16[256,256]{1,0:T(8,128)(2,1)S(1)}, u32[]{:S(2)}, u32[]{:S(2)}) collective-permute-start(bf16[256,256]{1,0:T(8,128)(2,1)S(1)} %get-tuple-element.63), channel_id=1, source_target_pairs={{0,2},{1,3},{2,0},{3,1},{4,6},{5,7},{6,4},{7,5},{8,10},{9,11},{10,... | collective-permute-start | bytes 393224 | tf_op jit(solution)/shard_map/ppermute | solution.py:328
  27.9 7.0 %collective-permute-start.9 = (bf16[256,512]{1,0:T(8,128)(2,1)S(1)}, bf16[256,512]{1,0:T(8,128)(2,1)S(1)}, u32[]{:S(2)}, u32[]{:S(2)}) collective-permute-start(bf16[256,512]{1,0:T(8,128)(2,1)S(1)} %beams_s.3), channel_id=1, source_target_pairs={{0,4},{4,0},{8,12},{12,8},{16,20},{20,16},{24,28},{28,24},{1,5},{5... | collective-permute-start | bytes 786440 | tf_op jit(solution)/shard_map/ppermute | solution.py:328
  29.9 5.1 %collective-permute-start.13 = (bf16[256,256]{1,0:T(8,128)(2,1)S(1)}, bf16[256,256]{1,0:T(8,128)(2,1)S(1)}, u32[]{:S(2)}, u32[]{:S(2)}) collective-permute-start(bf16[256,256]{1,0:T(8,128)(2,1)S(1)} %get-tuple-element.65), channel_id=1, source_target_pairs={{0,8},{4,12},{8,0},{12,4},{16,24},{20,28},{24,16},{28,20},{1,9},{5... | collective-permute-start | bytes 393224 | tf_op jit(solution)/shard_map/ppermute | solution.py:328
  35.1 7.4 %collective-permute-start.14 = (bf16[256,256]{1,0:T(8,128)(2,1)S(1)}, bf16[256,256]{1,0:T(8,128)(2,1)S(1)}, u32[]{:S(2)}, u32[]{:S(2)}) collective-permute-start(bf16[256,256]{1,0:T(8,128)(2,1)S(1)} %get-tuple-element.68), channel_id=1, source_target_pairs={{0,16},{4,20},{8,24},{12,28},{16,0},{20,4},{24,8},{28,12},{1,17},{... | collective-permute-start | bytes 393224 | tf_op jit(solution)/shard_map/ppermute | solution.py:328
  37.8 6.0 %collective-permute-start.10 = (bf16[128,512]{1,0:T(8,128)(2,1)S(1)}, bf16[128,512]{1,0:T(8,128)(2,1)S(1)}, u32[]{:S(2)}, u32[]{:S(2)}) collective-permute-start(bf16[128,512]{1,0:T(8,128)(2,1)S(1)} %get-tuple-element.55), channel_id=1, source_target_pairs={{0,8},{4,12},{8,0},{12,4},{16,24},{20,28},{24,16},{28,20},{1,9},{5... | collective-permute-start | bytes 393224 | tf_op jit(solution)/shard_map/ppermute | solution.py:328
  42.6 6.5 %collective-permute-start.15 = (bf16[256,256]{1,0:T(8,128)(2,1)S(1)}, bf16[256,256]{1,0:T(8,128)(2,1)S(1)}, u32[]{:S(2)}, u32[]{:S(2)}) collective-permute-start(bf16[256,256]{1,0:T(8,128)(2,1)S(1)} %step_r.5.near_r), channel_id=1, source_target_pairs={{0,4},{4,0},{8,12},{12,8},{16,20},{20,16},{24,28},{28,24},{1,5},{5... | collective-permute-start | bytes 393224 | tf_op jit(solution)/shard_map/ppermute | solution.py:328
  43.9 5.2 %collective-permute-start.11 = (bf16[64,512]{1,0:T(8,128)(2,1)S(1)}, bf16[64,512]{1,0:T(8,128)(2,1)S(1)}, u32[]{:S(2)}, u32[]{:S(2)}) collective-permute-start(bf16[64,512]{1,0:T(8,128)(2,1)S(1)} %get-tuple-element.57), channel_id=1, source_target_pairs={{0,16},{4,20},{8,24},{12,28},{16,0},{20,4},{24,8},{28,12},{1,17},{... | collective-permute-start | bytes 196616 | tf_op jit(solution)/shard_map/ppermute | solution.py:328
  49.4 1.3 %collective-permute-start.16 = (f32[2,64,128]{2,1,0:T(8,128)S(1)}, f32[2,64,128]{2,1,0:T(8,128)S(1)}, u32[]{:S(2)}, u32[]{:S(2)}) collective-permute-start(f32[2,64,128]{2,1,0:T(8,128)S(1)} %field.3), channel_id=1, source_target_pairs={{0,1},{1,0},{2,3},{3,2},{4,5},{5,4},{6,7},{7,6},{8,9},{9,8},{10,11... | collective-permute-start | bytes 196616 | tf_op jit(solution)/shard_map/ppermute | solution.py:328

commit v8 on v7

--- a/solution.py
+++ b/solution.py
@@ -159,16 +159,20 @@
                 copy_ref[there, :] = delays.astype(copy_ref.dtype)
 
 
-def steer_kernel(token_ref, delays_ref, cos_ref, sin_ref, out_ref):
+def steer_kernel(token_ref, *refs):
+    *delays, cos_ref, sin_ref, out_ref = refs
     out_ref[...] = token_ref[...]
-    steer_blocks([(0, None)], delays_ref, cos_ref, sin_ref)
-
-
-def steer_far_kernel(starts, parts, block, token_ref, delays_ref, cos_ref, sin_ref, out_ref, *refs):
-    *copy_ref, held_ref, sems = refs
+    rows = cos_ref.shape[0] // len(delays)
+    for index, delays_ref in enumerate(delays):
+        here = pl.ds(index * rows, rows)
+        steer_blocks([(0, None)], delays_ref, cos_ref.at[here, :], sin_ref.at[here, :])
+
+
+def steer_far_kernel(starts, parts, block, heads, token_ref, delays_ref, *refs):
+    head, (cos_ref, sin_ref, out_ref, *copy_ref, held_ref, sems) = refs[:heads], refs[heads:]
     out_ref[...] = token_ref[...]
     firsts = starts()
-    per = cos_ref.shape[0] // len(firsts)
+    per = held_ref.shape[0] // len(firsts)
     rows = per // parts
     blocks = []
     for j, first in enumerate(firsts):
@@ -179,24 +183,32 @@
             arrival = pltpu.make_async_copy(delays_ref.at[there, :], held_ref.at[here, :], sems.at[index])
             arrival.start()
             blocks.append((index * rows, arrival))
+    if head:
+        above = head[0].shape[0]
+        for ref, given in zip((cos_ref, sin_ref), head):
+            ref[:above, :] = given[...]
+        cos_ref, sin_ref = (ref.at[pl.ds(above, held_ref.shape[0]), :] for ref in (cos_ref, sin_ref))
     steer_blocks(blocks, held_ref, cos_ref, sin_ref, *(copy_ref or [None]), block)
 
 
 def steering(token, delays):
-    out = [vmem(delays.shape, jnp.bfloat16)] * 2 + [vmem(token.shape, token.dtype)]
-    return kernel_call(steer_kernel, out, [token, delays], [pltpu.VMEM] * 2, name="steering")
-
-
-def steering_far(starts, per, blocks, token, delays, copied=(), block=None):
+    shape = (sum(d.shape[0] for d in delays), delays[0].shape[1])
+    out = [vmem(shape, jnp.bfloat16)] * 2 + [vmem(token.shape, token.dtype)]
+    inputs = [token, *delays]
+    return kernel_call(steer_kernel, out, inputs, [pltpu.VMEM] * len(inputs), name="steering")
+
+
+def steering_far(starts, per, blocks, token, delays, copied=(), block=None, head=()):
     parts = math.gcd(per // CHUNK, 1 if block else 2)
     shape = (per * blocks, delays.shape[1])
+    whole = (shape[0] + (head[0].shape[0] if head else 0), shape[1])
     return kernel_call(
-        functools.partial(steer_far_kernel, starts, parts, block),
-        [vmem(shape, jnp.bfloat16)] * 2
+        functools.partial(steer_far_kernel, starts, parts, block, len(head)),
+        [vmem(whole, jnp.bfloat16)] * 2
         + [vmem(token.shape, token.dtype)]
         + [vmem(shape, t) for t in copied],
-        [token, delays],
-        [pltpu.VMEM, pltpu.HBM],
+        [token, delays, *head],
+        [pltpu.VMEM, pltpu.HBM] + [pltpu.VMEM] * len(head),
         scratch=[pltpu.VMEM(shape, delays.dtype), pltpu.SemaphoreType.DMA((blocks * parts,))],
         name="steering_far",
     )
@@ -212,7 +224,8 @@
 
 def beams_kernel(order, mine, block, kept, only, near_power_ref, far_ref, level_ref, own_ref, other_ref, from_ref, *refs):
     if only is None:
-        *steer, keep_ref, send_ref, total_ref = refs
+        *steer, keep_ref, send_ref, token_ref, total_ref = refs
+        token_ref[...] = level_ref[...]
         beams_of = slice(None)
     else:
         *steer, total_ref = refs
@@ -246,6 +259,8 @@
     inputs = [near_power, far, level, own, other, arrived, *steer]
     rows, width = steer[0].shape[1], 2 * arrived.shape[-1]
     out = [vmem((rows // 2, width), t) for t in ((jnp.float32, jnp.bfloat16) if only is None else (dtype,))]
+    if only is None:
+        out.append(vmem(level.shape, level.dtype))
     return kernel_call(
         functools.partial(beams_kernel, order, mine, block, kept, only),
         out,
@@ -319,8 +334,8 @@
         r_re, r_im = receiver[rows, :half], receiver[rows, half:]
         real += product(s_re, r_re) + product(s_im, r_im)
         imag += product(s_im, r_re) - product(s_re, r_im)
-    field_ref[0] = real * scale
-    field_ref[1] = imag * scale
+    field_ref[0] = (real * scale).astype(field_ref.dtype)
+    field_ref[1] = (imag * scale).astype(field_ref.dtype)
 
 
 def swap(value, axis, bit):
@@ -382,21 +397,19 @@
 
     row_bits, col_bits = bits(n_row, 2), bits(n_col, 4)
     first, *others = [("row", bit) for bit in row_bits[::-1]] + [("col", bit) for bit in col_bits]
-    *steer_s, token = steering_far(starts_s(0, 2), per, 2, level, delays_s, block=block_s)
+    *steer_s, token = steering_far(starts_s(0, 1), per, 1, level, delays_s, block=block_s)
     level = level + swap(level, *first)
-    cos, sin, next_token = steering_far(starts_s(2, 3), per, 1, level, delays_s, block=block_s)
-    steer_s += [cos, sin]
+    *steer_s, next_token = steering_far(starts_s(1, 2), per, 1, level, delays_s, block=block_s, head=steer_s)
     for step in others:
         level = gated([level], [token])
         level = level + swap(level, *step)
-    cos, sin, token = steering(level, other_r)
+    cos, sin, token = steering(level, [other_r])
     steer_r += [cos, sin]
-    cos, sin, last_token = steering_far(starts_s(3, 4), per, 1, level, delays_s, block=block_s)
-    steer_s += [cos, sin]
+    *more_s, last_token = steering_far(starts_s(2, 3), per, 1, level, delays_s, block=block_s)
     far_y = swap(gated([power, level], [from_y, next_token]), "row", 1)
     level = gated([level + far_y[2:]], [token, last_token])
 
-    keep_r, send_r = beams(
+    keep_r, send_r, token = beams(
         ((0, 2), (1, 3)),
         lambda half: pl.ds(pl.multiple_of(y_of() * half, half), half),
         block_r,
@@ -410,9 +423,10 @@
         steer_r,
         "beams_r",
     )
+    steer_s += steering_far(starts_s(3, 4), per, 1, token, delays_s, block=block_s, head=more_s)[:2]
     (send_s,), (keep_s,) = (
         beams(
-            ((0, 1), (2,), (3,)),
+            ((0, 1), (2, 3)),
             lambda windows: slice(None),
             None,
             None,
@@ -446,19 +460,18 @@
     r_far = swap(receiver, "row", 1)
 
     block = delays_r.shape[1] // n_col
-    shape = vmem((2, block_s, block), jnp.float32)
     scale = math.sqrt(windows) / (per * n_row * n_col)
     away, near = (
         kernel_call(
             functools.partial(field_kernel, scale, mine),
-            [shape],
+            [vmem((2, block_s, block), jnp.float32 if mine else jnp.bfloat16)],
             [source, receiver, r_far],
             [pltpu.VMEM] * 3,
             name="field",
         )[0]
         for mine in (False, True)
     )
-    far = swap(away, "col", 1)
+    far = swap(away, "col", 1).astype(jnp.float32)
     return jnp.stack(ordered(core, near, far)).swapaxes(2, 3)
 
 

time: 51.7 us -> 51.6 us (level)
  waiting for transfers between devices: 14.3 us -> 12.5 us
  Pallas kernels: 15.7 us -> 16.6 us
  starting transfers between devices: 20.4 us -> 21.3 us
    ppermute x17, waiting for transfers between devices: 14.3 us -> 12.5 us  [swap(): return lax.ppermute(value, axis, [(i, i ^ bit) for i in range(size)])]
    pallas_call x22 -> x23, Pallas kernels: 15.7 us -> 16.6 us  [kernel_call(): pl.pallas_call(body, out_shape=out, in_specs=[pl.BlockSpec(memory_space=s...]
    ppermute x17, starting transfers between devices: 20.4 us -> 21.3 us  [swap(): return lax.ppermute(value, axis, [(i, i ^ bit) for i in range(size)])]
  transfers between devices with their start and end apart: 17 -> 17, of which waited for: 9 -> 8; matrix products, arithmetic and copies ran while one was open for 0% -> 0% of each run, Pallas kernels for 27% -> 29%
where the time goes in v8:
time: 51.6 us; the launch traced here: 51.3 us
  starting transfers between devices  21.3 us (41%)
  Pallas kernels  16.6 us (32%)
  waiting for transfers between devices  12.5 us (24%)
  other arithmetic  0.72 us (1%)
    ppermute x17, starting transfers between devices, swap(): return lax.ppermute(value, axis, [(i, i ^ bit) for i in range(size)])  21.3 us
    pallas_call x23, Pallas kernels, kernel_call(): pl.pallas_call(body, out_shape=out, in_specs=[pl.BlockSpec(memory_space=s...  16.6 us
    ppermute x17, waiting for transfers between devices, swap(): return lax.ppermute(value, axis, [(i, i ^ bit) for i in range(size)])  12.5 us
  transfers between devices with their start and end apart: 17, of which 8 were waited for; matrix products, arithmetic and copies ran while one was open for 0% of the time, Pallas kernels for 29%

profile of v8, /device:TPU:0, one launch (start us, length us, event | category | flops | bytes accessed | tf_op | source)
XLA Modules:
  0.0 51.3 jit_solution(16299841046595345542)
XLA Ops:
  0.0 1.5 %power.1 = (f32[4,384]{1,0:T(4,128)S(1)}, bf16[2,320,256]{2,1,0:T(8,128)(2,1)S(1)}, bf16[2,320,256]{2,1,0:T(8,128)(2,1)S(1)}) custom-call(s32[2]{0:T(128)} %wl_ref.1, bf16[2,2,320,256]{3,2,1,0:T(8,128)(2,1)} %spec_ref.1), custom_call_target="tpu_custom_call" | custom-call | flops 1 | bytes 1 | tf_op jit(solution)/shard_map/power/pallas_call | solution.py:60
  1.5 0.5 %collective-permute-start.4 = (bf16[2,320,256]{2,1,0:T(8,128)(2,1)S(1)}, bf16[2,320,256]{2,1,0:T(8,128)(2,1)S(1)}, u32[]{:S(2)}, u32[]{:S(2)}) collective-permute-start(bf16[2,320,256]{2,1,0:T(8,128)(2,1)S(1)} %get-tuple-element.44), channel_id=1, source_target_pairs={{0,1},{1,0},{2,3},{3,2},{4,5},{5,4},{6,7},{7,6},{8,9},{9,8},{10,11... | collective-permute-start | bytes 983048 | tf_op jit(solution)/shard_map/ppermute | solution.py:343
  2.0 2.6 %collective-permute-start = (f32[4,384]{1,0:T(4,128)S(1)}, f32[4,384]{1,0:T(4,128)S(1)}, u32[]{:S(2)}, u32[]{:S(2)}) collective-permute-start(f32[4,384]{1,0:T(4,128)S(1)} %get-tuple-element.40), channel_id=1, source_target_pairs={{0,2},{1,3},{2,0},{3,1},{4,6},{5,7},{6,4},{7,5},{8,10},{9,11},{10,... | collective-permute-start | bytes 18440 | tf_op jit(solution)/shard_map/ppermute | solution.py:343
  4.6 2.1 %steering_far.5 = (bf16[640,512]{1,0:T(8,128)(2,1)S(1)}, bf16[640,512]{1,0:T(8,128)(2,1)S(1)}, f32[1,384]{1,0:T(1,128)S(1)}, s16[640,512]{1,0:T(8,128)(2,1)S(1)}) custom-call(f32[1,384]{1,0:T(1,128)S(1)} %slice.34.token_ref, s32[2560,512]{1,0:T(8,128)} %delays_ref.5), custom_call_target="tpu_custom_call" | custom-call | flops 1 | bytes 1 | tf_op jit(solution)/shard_map/steering_far/pallas_call | solution.py:60
  6.7 0.0 collective-permute-done
  6.7 0.2 collective-permute-start.1
  6.9 0.3 collective-permute-start.7
  7.3 0.7 %collective-permute-done.1 = f32[4,384]{1,0:T(4,128)S(1)} collective-permute-done((f32[4,384]{1,0:T(4,128)S(1)}, f32[4,384]{1,0:T(4,128)S(1)}, u32[]{:S(2)}, u32[]{:S(2)}) %collective-permute-start.1) | collective-permute-done | bytes 6176 | tf_op jit(solution)/shard_map/ppermute | solution.py:343
  7.9 0.0 collective-permute-done.4.other_ref
  8.0 0.1 send.1
  8.1 1.6 %collective-permute-start.5 = (bf16[2,2,320,128]{3,2,1,0:T(8,128)(2,1)S(1)}, bf16[2,2,320,128]{3,2,1,0:T(8,128)(2,1)S(1)}, u32[]{:S(2)}, u32[]{:S(2)}) collective-permute-start(bf16[2,2,320,128]{3,2,1,0:T(8,128)(2,1)S(1)} %get-tuple-element.45), channel_id=1, source_target_pairs={{0,4},{4,0},{8,12},{12,8},{16,20},{20,16},{24,28},{28,24},{1,5},{5... | collective-permute-start | bytes 983048 | tf_op jit(solution)/shard_map/ppermute | solution.py:343
  9.7 1.5 %collective-permute-start.8 = (bf16[2,2,320,256]{3,2,1,0:T(8,128)(2,1)S(1)}, bf16[2,2,320,256]{3,2,1,0:T(8,128)(2,1)S(1)}, u32[]{:S(2)}, u32[]{:S(2)}) collective-permute-start(bf16[2,2,320,256]{3,2,1,0:T(8,128)(2,1)S(1)} %get-tuple-element.52), channel_id=1, source_target_pairs={{0,2},{1,3},{2,0},{3,1},{4,6},{5,7},{6,4},{7,5},{8,10},{9,11},{10,... | collective-permute-start | bytes 1966088 | tf_op jit(solution)/shard_map/ppermute | solution.py:343
  11.2 2.6 %collective-permute-start.2 = (f32[1,384]{1,0:T(1,128)S(1)}, f32[1,384]{1,0:T(1,128)S(1)}, u32[]{:S(2)}, u32[]{:S(2)}) collective-permute-start(f32[1,384]{1,0:T(1,128)S(1)} %get-tuple-element.77.token_ref), channel_id=1, source_target_pairs={{0,16},{4,20},{8,24},{12,28},{16,0},{20,4},{24,8},{28,12},{1,17},{... | collective-permute-start | bytes 4616 | tf_op jit(solution)/shard_map/ppermute | solution.py:343
  13.7 1.7 %steering_far.6 = (bf16[320,512]{1,0:T(8,128)(2,1)S(1)}, bf16[320,512]{1,0:T(8,128)(2,1)S(1)}, f32[1,384]{1,0:T(1,128)S(1)}) custom-call(f32[1,384]{1,0:T(1,128)S(1)} %get-tuple-element.77.token_ref, s32[1280,512]{1,0:T(8,128)} %delays_ref.9), custom_call_target="tpu_custom_call" | custom-call | flops 1 | bytes 1 | tf_op jit(solution)/shard_map/steering_far/pallas_call | solution.py:60
  15.5 0.2 collective-permute-done.2
  15.6 1.6 %collective-permute-start.3 = (f32[1,384]{1,0:T(1,128)S(1)}, f32[1,384]{1,0:T(1,128)S(1)}, u32[]{:S(2)}, u32[]{:S(2)}) collective-permute-start(f32[1,384]{1,0:T(1,128)S(1)} %gate.5), channel_id=1, source_target_pairs={{0,8},{4,12},{8,0},{12,4},{16,24},{20,28},{24,16},{28,20},{1,9},{5... | collective-permute-start | bytes 4616 | tf_op jit(solution)/shard_map/ppermute | solution.py:343
  17.3 1.7 %steering_far.7 = (bf16[640,512]{1,0:T(8,128)(2,1)S(1)}, bf16[640,512]{1,0:T(8,128)(2,1)S(1)}, f32[1,384]{1,0:T(1,128)S(1)}) custom-call(f32[1,384]{1,0:T(1,128)S(1)} %add.21.refs_0_.token_ref, s32[1280,512]{1,0:T(8,128)} %delays_ref.9, bf16[320,512]{1,0:T(8,128)(2,1)S(1)} %get-tuple-element.46.refs_0_, bf16[320,512]{1,0:T(8,128)(2,1)S(1)} %get-tuple-element.47.refs_1_), custom_call_target="tpu_custom_call" | custom-call | flops 1 | bytes 1 | tf_op jit(solution)/shard_map/steering_far/pallas_call | solution.py:60
  19.0 0.3 collective-permute-done.3
  19.2 0.0 collective-permute-done.5.refs_2_.from_ref
  19.3 0.6 %collective-permute-start.6 = (f32[3,384]{1,0:T(4,128)S(1)}, f32[3,384]{1,0:T(4,128)S(1)}, u32[]{:S(2)}, u32[]{:S(2)}) collective-permute-start(f32[3,384]{1,0:T(4,128)S(1)} %gate.6), channel_id=1, source_target_pairs={{0,4},{4,0},{8,12},{12,8},{16,20},{20,16},{24,28},{28,24},{1,5},{5... | collective-permute-start | bytes 13832 | tf_op jit(solution)/shard_map/ppermute | solution.py:343
  19.8 1.7 %steering_far.8 = (bf16[320,512]{1,0:T(8,128)(2,1)S(1)}, bf16[320,512]{1,0:T(8,128)(2,1)S(1)}, f32[1,384]{1,0:T(1,128)S(1)}) custom-call(f32[1,384]{1,0:T(1,128)S(1)} %add.22.refs_1_.token_ref, s32[1280,512]{1,0:T(8,128)} %delays_ref.9), custom_call_target="tpu_custom_call" | custom-call | flops 1 | bytes 1 | tf_op jit(solution)/shard_map/steering_far/pallas_call | solution.py:60
  21.6 0.0 collective-permute-done.7.refs_0_
  21.6 1.1 %steering.1 = (bf16[640,512]{1,0:T(8,128)(2,1)S(1)}, bf16[640,512]{1,0:T(8,128)(2,1)S(1)}, f32[1,384]{1,0:T(1,128)S(1)}) custom-call(f32[1,384]{1,0:T(1,128)S(1)} %add.22.refs_1_.token_ref, s16[640,512]{1,0:T(8,128)(2,1)S(1)} %collective-permute-done.7.refs_0_), custom_call_target="tpu_custom_call" | custom-call | flops 1 | bytes 1 | tf_op jit(solution)/shard_map/steering/pallas_call | solution.py:60
  22.7 0.2 collective-permute-done.6.far_ref
  23.0 1.4 %beams_r.1 = (f32[256,256]{1,0:T(8,128)S(1)}, bf16[256,256]{1,0:T(8,128)(2,1)S(1)}, f32[1,384]{1,0:T(1,128)S(1)}) custom-call(f32[2,384]{1,0:T(2,128)S(1)} %pad_maximum_fusion.refs_0_.near_power_ref, f32[3,384]{1,0:T(4,128)S(1)} %collective-permute-done.6.far_ref, f32[1,384]{1,0:T(1,128)S(1)} %gate.7.level_ref.token_ref, ...), custom_call_target="tpu_custom_call" | custom-call | flops 1 | bytes 1 | tf_op jit(solution)/shard_map/beams_r/pallas_call | solution.py:60
  24.4 1.0 %collective-permute-start.12 = (bf16[256,256]{1,0:T(8,128)(2,1)S(1)}, bf16[256,256]{1,0:T(8,128)(2,1)S(1)}, u32[]{:S(2)}, u32[]{:S(2)}) collective-permute-start(bf16[256,256]{1,0:T(8,128)(2,1)S(1)} %get-tuple-element.69), channel_id=1, source_target_pairs={{0,2},{1,3},{2,0},{3,1},{4,6},{5,7},{6,4},{7,5},{8,10},{9,11},{10,... | collective-permute-start | bytes 393224 | tf_op jit(solution)/shard_map/ppermute | solution.py:343
  25.3 1.7 %steering_far.9 = (bf16[640,512]{1,0:T(8,128)(2,1)S(1)}, bf16[640,512]{1,0:T(8,128)(2,1)S(1)}, f32[1,384]{1,0:T(1,128)}) custom-call(f32[1,384]{1,0:T(1,128)S(1)} %get-tuple-element.59.token_ref, s32[1280,512]{1,0:T(8,128)} %delays_ref.9, bf16[320,512]{1,0:T(8,128)(2,1)S(1)} %get-tuple-element.60.refs_0_, bf16[320,512]{1,0:T(8,128)(2,1)S(1)} %get-tuple-element.61.refs_1_), custom_call_target="tpu_custom_call" | custom-call | flops 1 | bytes 1 | tf_op jit(solution)/shard_map/steering_far/pallas_call | solution.py:60
  27.0 0.0 collective-permute-done.8.from_ref
  27.1 1.3 %beams_s.3 = bf16[256,512]{1,0:T(8,128)(2,1)S(1)} custom-call(f32[2,384]{1,0:T(2,128)S(1)} %pad_maximum_fusion.refs_0_.near_power_ref, f32[2,384]{1,0:T(2,128)S(1)} %pad_maximum_fusion.1.far_ref, f32[1,384]{1,0:T(1,128)S(1)} %gate.7.level_ref.token_ref, bf16[2,320,256]{2,1,0:T(8,128)(2,1)S(1)} %get-tuple-element.43.own_ref, ...), custom_call_target="tpu_custom_call" | custom-call | flops 1 | bytes 1 | tf_op jit(solution)/shard_map/beams_s/pallas_call | solution.py:60
  28.4 1.0 %collective-permute-start.9 = (bf16[256,512]{1,0:T(8,128)(2,1)S(1)}, bf16[256,512]{1,0:T(8,128)(2,1)S(1)}, u32[]{:S(2)}, u32[]{:S(2)}) collective-permute-start(bf16[256,512]{1,0:T(8,128)(2,1)S(1)} %beams_s.3), channel_id=1, source_target_pairs={{0,4},{4,0},{8,12},{12,8},{16,20},{20,16},{24,28},{28,24},{1,5},{5... | collective-permute-start | bytes 786440 | tf_op jit(solution)/shard_map/ppermute | solution.py:343
  29.4 0.0 collective-permute-done.12.other_ref
  29.5 1.6 %collective-permute-start.13 = (bf16[256,256]{1,0:T(8,128)(2,1)S(1)}, bf16[256,256]{1,0:T(8,128)(2,1)S(1)}, u32[]{:S(2)}, u32[]{:S(2)}) collective-permute-start(bf16[256,256]{1,0:T(8,128)(2,1)S(1)} %get-tuple-element.71), channel_id=1, source_target_pairs={{0,8},{4,12},{8,0},{12,4},{16,24},{20,28},{24,16},{28,20},{1,9},{5... | collective-permute-start | bytes 393224 | tf_op jit(solution)/shard_map/ppermute | solution.py:343
  31.1 1.3 %beams_s.2.keep_ref = f32[256,512]{1,0:T(8,128)S(1)} custom-call(f32[2,384]{1,0:T(2,128)S(1)} %pad_maximum_fusion.refs_0_.near_power_ref, f32[2,384]{1,0:T(2,128)S(1)} %pad_maximum_fusion.1.far_ref, f32[1,384]{1,0:T(1,128)S(1)} %gate.7.level_ref.token_ref, bf16[2,320,256]{2,1,0:T(8,128)(2,1)S(1)} %get-tuple-element.43.own_ref, ...), custom_call_target="tpu_custom_call" | custom-call | flops 1 | bytes 1 | tf_op jit(solution)/shard_map/beams_s/pallas_call | solution.py:60
  32.5 3.0 %collective-permute-done.9.other_ref = bf16[256,512]{1,0:T(8,128)(2,1)S(1)} collective-permute-done((bf16[256,512]{1,0:T(8,128)(2,1)S(1)}, bf16[256,512]{1,0:T(8,128)(2,1)S(1)}, u32[]{:S(2)}, u32[]{:S(2)}) %collective-permute-start.9) | collective-permute-done | bytes 262176 | tf_op jit(solution)/shard_map/ppermute | solution.py:343
  35.5 0.1 step_s.3
  35.6 0.0 collective-permute-done.13.other_ref
  35.6 2.6 %collective-permute-start.14 = (bf16[256,256]{1,0:T(8,128)(2,1)S(1)}, bf16[256,256]{1,0:T(8,128)(2,1)S(1)}, u32[]{:S(2)}, u32[]{:S(2)}) collective-permute-start(bf16[256,256]{1,0:T(8,128)(2,1)S(1)} %get-tuple-element.74), channel_id=1, source_target_pairs={{0,16},{4,20},{8,24},{12,28},{16,0},{20,4},{24,8},{28,12},{1,17},{... | collective-permute-start | bytes 393224 | tf_op jit(solution)/shard_map/ppermute | solution.py:343
  38.3 1.6 %collective-permute-start.10 = (bf16[128,512]{1,0:T(8,128)(2,1)S(1)}, bf16[128,512]{1,0:T(8,128)(2,1)S(1)}, u32[]{:S(2)}, u32[]{:S(2)}) collective-permute-start(bf16[128,512]{1,0:T(8,128)(2,1)S(1)} %get-tuple-element.65), channel_id=1, source_target_pairs={{0,8},{4,12},{8,0},{12,4},{16,24},{20,28},{24,16},{28,20},{1,9},{5... | collective-permute-start | bytes 393224 | tf_op jit(solution)/shard_map/ppermute | solution.py:343
  39.9 3.2 %collective-permute-done.14.other_ref = bf16[256,256]{1,0:T(8,128)(2,1)S(1)} collective-permute-done((bf16[256,256]{1,0:T(8,128)(2,1)S(1)}, bf16[256,256]{1,0:T(8,128)(2,1)S(1)}, u32[]{:S(2)}, u32[]{:S(2)}) %collective-permute-start.14) | collective-permute-done | bytes 131104 | tf_op jit(solution)/shard_map/ppermute | solution.py:343
  43.1 0.6 %collective-permute-start.15 = (bf16[256,256]{1,0:T(8,128)(2,1)S(1)}, bf16[256,256]{1,0:T(8,128)(2,1)S(1)}, u32[]{:S(2)}, u32[]{:S(2)}) collective-permute-start(bf16[256,256]{1,0:T(8,128)(2,1)S(1)} %step_r.5.near_r), channel_id=1, source_target_pairs={{0,4},{4,0},{8,12},{12,8},{16,20},{20,16},{24,28},{28,24},{1,5},{5... | collective-permute-start | bytes 393224 | tf_op jit(solution)/shard_map/ppermute | solution.py:343
  43.7 0.0 collective-permute-done.10.other_ref
  43.7 1.2 %collective-permute-start.11 = (bf16[64,512]{1,0:T(8,128)(2,1)S(1)}, bf16[64,512]{1,0:T(8,128)(2,1)S(1)}, u32[]{:S(2)}, u32[]{:S(2)}) collective-permute-start(bf16[64,512]{1,0:T(8,128)(2,1)S(1)} %get-tuple-element.67), channel_id=1, source_target_pairs={{0,16},{4,20},{8,24},{12,28},{16,0},{20,4},{24,8},{28,12},{1,17},{... | collective-permute-start | bytes 196616 | tf_op jit(solution)/shard_map/ppermute | solution.py:343
  45.0 4.0 %collective-permute-done.11.other_ref = bf16[64,512]{1,0:T(8,128)(2,1)S(1)} collective-permute-done((bf16[64,512]{1,0:T(8,128)(2,1)S(1)}, bf16[64,512]{1,0:T(8,128)(2,1)S(1)}, u32[]{:S(2)}, u32[]{:S(2)}) %collective-permute-start.11) | collective-permute-done | bytes 65568 | tf_op jit(solution)/shard_map/ppermute | solution.py:343
  49.0 0.0 collective-permute-done.15.far_r
  49.0 0.3 field.3
  49.3 0.1 collective-permute-start.16
  49.4 0.3 field.2
  49.7 0.9 %collective-permute-done.16 = bf16[2,64,128]{2,1,0:T(8,128)(2,1)S(1)} collective-permute-done((bf16[2,64,128]{2,1,0:T(8,128)(2,1)S(1)}, bf16[2,64,128]{2,1,0:T(8,128)(2,1)S(1)}, u32[]{:S(2)}, u32[]{:S(2)}) %collective-permute-start.16) | collective-permute-done | bytes 32800 | tf_op jit(solution)/shard_map/ppermute | solution.py:343
  50.6 0.7 %maximum_bitcast_fusion = f32[2,2,128,64]{2,3,1,0:T(8,128)} fusion(f32[1,2,64,128]{3,2,1,0:T(8,128)S(1)} %get-tuple-element.76, f32[1,2,64,128]{3,2,1,0:T(8,128)S(1)} %get-tuple-element.75), kind=kLoop, calls=%fused_computation | loop fusion | flops 32768 | bytes 262144 | tf_op jit(solution)/shard_map/transpose | solution.py:475
  (19 shorter events, 0.3 us)
Async XLA Ops:
  1.5 6.5 %collective-permute-start.4 = (bf16[2,320,256]{2,1,0:T(8,128)(2,1)S(1)}, bf16[2,320,256]{2,1,0:T(8,128)(2,1)S(1)}, u32[]{:S(2)}, u32[]{:S(2)}) collective-permute-start(bf16[2,320,256]{2,1,0:T(8,128)(2,1)S(1)} %get-tuple-element.44), channel_id=1, source_target_pairs={{0,1},{1,0},{2,3},{3,2},{4,5},{5,4},{6,7},{7,6},{8,9},{9,8},{10,11... | collective-permute-start | bytes 983048 | tf_op jit(solution)/shard_map/ppermute | solution.py:343
  2.0 4.7 %collective-permute-start = (f32[4,384]{1,0:T(4,128)S(1)}, f32[4,384]{1,0:T(4,128)S(1)}, u32[]{:S(2)}, u32[]{:S(2)}) collective-permute-start(f32[4,384]{1,0:T(4,128)S(1)} %get-tuple-element.40), channel_id=1, source_target_pairs={{0,2},{1,3},{2,0},{3,1},{4,6},{5,7},{6,4},{7,5},{8,10},{9,11},{10,... | collective-permute-start | bytes 18440 | tf_op jit(solution)/shard_map/ppermute | solution.py:343
  6.7 1.2 %collective-permute-start.1 = (f32[4,384]{1,0:T(4,128)S(1)}, f32[4,384]{1,0:T(4,128)S(1)}, u32[]{:S(2)}, u32[]{:S(2)}) collective-permute-start(f32[4,384]{1,0:T(4,128)S(1)} %gate.4), channel_id=1, source_target_pairs={{0,1},{1,0},{2,3},{3,2},{4,5},{5,4},{6,7},{7,6},{8,9},{9,8},{10,11... | collective-permute-start | bytes 18440 | tf_op jit(solution)/shard_map/ppermute | solution.py:343
  6.9 14.6 %collective-permute-start.7 = (s16[640,512]{1,0:T(8,128)(2,1)S(1)}, s16[640,512]{1,0:T(8,128)(2,1)S(1)}, u32[]{:S(2)}, u32[]{:S(2)}) collective-permute-start(s16[640,512]{1,0:T(8,128)(2,1)S(1)} %get-tuple-element.49), channel_id=1, source_target_pairs={{0,1},{1,0},{2,3},{3,2},{4,5},{5,4},{6,7},{7,6},{8,9},{9,8},{10,11... | collective-permute-start | bytes 1966088 | tf_op jit(solution)/shard_map/ppermute | solution.py:343
  8.1 11.2 %collective-permute-start.5 = (bf16[2,2,320,128]{3,2,1,0:T(8,128)(2,1)S(1)}, bf16[2,2,320,128]{3,2,1,0:T(8,128)(2,1)S(1)}, u32[]{:S(2)}, u32[]{:S(2)}) collective-permute-start(bf16[2,2,320,128]{3,2,1,0:T(8,128)(2,1)S(1)} %get-tuple-element.45), channel_id=1, source_target_pairs={{0,4},{4,0},{8,12},{12,8},{16,20},{20,16},{24,28},{28,24},{1,5},{5... | collective-permute-start | bytes 983048 | tf_op jit(solution)/shard_map/ppermute | solution.py:343
  9.7 17.4 %collective-permute-start.8 = (bf16[2,2,320,256]{3,2,1,0:T(8,128)(2,1)S(1)}, bf16[2,2,320,256]{3,2,1,0:T(8,128)(2,1)S(1)}, u32[]{:S(2)}, u32[]{:S(2)}) collective-permute-start(bf16[2,2,320,256]{3,2,1,0:T(8,128)(2,1)S(1)} %get-tuple-element.52), channel_id=1, source_target_pairs={{0,2},{1,3},{2,0},{3,1},{4,6},{5,7},{6,4},{7,5},{8,10},{9,11},{10,... | collective-permute-start | bytes 1966088 | tf_op jit(solution)/shard_map/ppermute | solution.py:343
  11.2 4.5 %collective-permute-start.2 = (f32[1,384]{1,0:T(1,128)S(1)}, f32[1,384]{1,0:T(1,128)S(1)}, u32[]{:S(2)}, u32[]{:S(2)}) collective-permute-start(f32[1,384]{1,0:T(1,128)S(1)} %get-tuple-element.77.token_ref), channel_id=1, source_target_pairs={{0,16},{4,20},{8,24},{12,28},{16,0},{20,4},{24,8},{28,12},{1,17},{... | collective-permute-start | bytes 4616 | tf_op jit(solution)/shard_map/ppermute | solution.py:343
  15.6 3.6 %collective-permute-start.3 = (f32[1,384]{1,0:T(1,128)S(1)}, f32[1,384]{1,0:T(1,128)S(1)}, u32[]{:S(2)}, u32[]{:S(2)}) collective-permute-start(f32[1,384]{1,0:T(1,128)S(1)} %gate.5), channel_id=1, source_target_pairs={{0,8},{4,12},{8,0},{12,4},{16,24},{20,28},{24,16},{28,20},{1,9},{5... | collective-permute-start | bytes 4616 | tf_op jit(solution)/shard_map/ppermute | solution.py:343
  19.3 3.7 %collective-permute-start.6 = (f32[3,384]{1,0:T(4,128)S(1)}, f32[3,384]{1,0:T(4,128)S(1)}, u32[]{:S(2)}, u32[]{:S(2)}) collective-permute-start(f32[3,384]{1,0:T(4,128)S(1)} %gate.6), channel_id=1, source_target_pairs={{0,4},{4,0},{8,12},{12,8},{16,20},{20,16},{24,28},{28,24},{1,5},{5... | collective-permute-start | bytes 13832 | tf_op jit(solution)/shard_map/ppermute | solution.py:343
  24.4 5.1 %collective-permute-start.12 = (bf16[256,256]{1,0:T(8,128)(2,1)S(1)}, bf16[256,256]{1,0:T(8,128)(2,1)S(1)}, u32[]{:S(2)}, u32[]{:S(2)}) collective-permute-start(bf16[256,256]{1,0:T(8,128)(2,1)S(1)} %get-tuple-element.69), channel_id=1, source_target_pairs={{0,2},{1,3},{2,0},{3,1},{4,6},{5,7},{6,4},{7,5},{8,10},{9,11},{10,... | collective-permute-start | bytes 393224 | tf_op jit(solution)/shard_map/ppermute | solution.py:343
  28.4 7.1 %collective-permute-start.9 = (bf16[256,512]{1,0:T(8,128)(2,1)S(1)}, bf16[256,512]{1,0:T(8,128)(2,1)S(1)}, u32[]{:S(2)}, u32[]{:S(2)}) collective-permute-start(bf16[256,512]{1,0:T(8,128)(2,1)S(1)} %beams_s.3), channel_id=1, source_target_pairs={{0,4},{4,0},{8,12},{12,8},{16,20},{20,16},{24,28},{28,24},{1,5},{5... | collective-permute-start | bytes 786440 | tf_op jit(solution)/shard_map/ppermute | solution.py:343
  29.5 6.1 %collective-permute-start.13 = (bf16[256,256]{1,0:T(8,128)(2,1)S(1)}, bf16[256,256]{1,0:T(8,128)(2,1)S(1)}, u32[]{:S(2)}, u32[]{:S(2)}) collective-permute-start(bf16[256,256]{1,0:T(8,128)(2,1)S(1)} %get-tuple-element.71), channel_id=1, source_target_pairs={{0,8},{4,12},{8,0},{12,4},{16,24},{20,28},{24,16},{28,20},{1,9},{5... | collective-permute-start | bytes 393224 | tf_op jit(solution)/shard_map/ppermute | solution.py:343
  35.6 7.4 %collective-permute-start.14 = (bf16[256,256]{1,0:T(8,128)(2,1)S(1)}, bf16[256,256]{1,0:T(8,128)(2,1)S(1)}, u32[]{:S(2)}, u32[]{:S(2)}) collective-permute-start(bf16[256,256]{1,0:T(8,128)(2,1)S(1)} %get-tuple-element.74), channel_id=1, source_target_pairs={{0,16},{4,20},{8,24},{12,28},{16,0},{20,4},{24,8},{28,12},{1,17},{... | collective-permute-start | bytes 393224 | tf_op jit(solution)/shard_map/ppermute | solution.py:343
  38.3 5.4 %collective-permute-start.10 = (bf16[128,512]{1,0:T(8,128)(2,1)S(1)}, bf16[128,512]{1,0:T(8,128)(2,1)S(1)}, u32[]{:S(2)}, u32[]{:S(2)}) collective-permute-start(bf16[128,512]{1,0:T(8,128)(2,1)S(1)} %get-tuple-element.65), channel_id=1, source_target_pairs={{0,8},{4,12},{8,0},{12,4},{16,24},{20,28},{24,16},{28,20},{1,9},{5... | collective-permute-start | bytes 393224 | tf_op jit(solution)/shard_map/ppermute | solution.py:343
  43.1 5.9 %collective-permute-start.15 = (bf16[256,256]{1,0:T(8,128)(2,1)S(1)}, bf16[256,256]{1,0:T(8,128)(2,1)S(1)}, u32[]{:S(2)}, u32[]{:S(2)}) collective-permute-start(bf16[256,256]{1,0:T(8,128)(2,1)S(1)} %step_r.5.near_r), channel_id=1, source_target_pairs={{0,4},{4,0},{8,12},{12,8},{16,20},{20,16},{24,28},{28,24},{1,5},{5... | collective-permute-start | bytes 393224 | tf_op jit(solution)/shard_map/ppermute | solution.py:343
  43.7 5.2 %collective-permute-start.11 = (bf16[64,512]{1,0:T(8,128)(2,1)S(1)}, bf16[64,512]{1,0:T(8,128)(2,1)S(1)}, u32[]{:S(2)}, u32[]{:S(2)}) collective-permute-start(bf16[64,512]{1,0:T(8,128)(2,1)S(1)} %get-tuple-element.67), channel_id=1, source_target_pairs={{0,16},{4,20},{8,24},{12,28},{16,0},{20,4},{24,8},{28,12},{1,17},{... | collective-permute-start | bytes 196616 | tf_op jit(solution)/shard_map/ppermute | solution.py:343
  49.3 1.3 %collective-permute-start.16 = (bf16[2,64,128]{2,1,0:T(8,128)(2,1)S(1)}, bf16[2,64,128]{2,1,0:T(8,128)(2,1)S(1)}, u32[]{:S(2)}, u32[]{:S(2)}) collective-permute-start(bf16[2,64,128]{2,1,0:T(8,128)(2,1)S(1)} %field.3), channel_id=1, source_target_pairs={{0,1},{1,0},{2,3},{3,2},{4,5},{5,4},{6,7},{7,6},{8,9},{9,8},{10,11... | collective-permute-start | bytes 98312 | tf_op jit(solution)/shard_map/ppermute | solution.py:343

commit v9 on v8

--- a/solution.py
+++ b/solution.py
@@ -199,7 +199,7 @@
 
 
 def steering_far(starts, per, blocks, token, delays, copied=(), block=None, head=()):
-    parts = math.gcd(per // CHUNK, 1 if block else 2)
+    parts = 1
     shape = (per * blocks, delays.shape[1])
     whole = (shape[0] + (head[0].shape[0] if head else 0), shape[1])
     return kernel_call(
@@ -396,7 +396,7 @@
     from_x, from_y = swap(to_x, "col", 2), swap(to_y, "row", 1)
 
     row_bits, col_bits = bits(n_row, 2), bits(n_col, 4)
-    first, *others = [("row", bit) for bit in row_bits[::-1]] + [("col", bit) for bit in col_bits]
+    first, *others = [("row", bit) for bit in row_bits] + [("col", bit) for bit in col_bits]
     *steer_s, token = steering_far(starts_s(0, 1), per, 1, level, delays_s, block=block_s)
     level = level + swap(level, *first)
     *steer_s, next_token = steering_far(starts_s(1, 2), per, 1, level, delays_s, block=block_s, head=steer_s)

time: 51.6 us -> 51.6 us (level)
  no operation moved by 1% of the time
where the time goes in v9:
time: 51.6 us; the launch traced here: 51.3 us
  starting transfers between devices  21.2 us (41%)
  Pallas kernels  16.6 us (32%)
  waiting for transfers between devices  12.4 us (24%)
  other arithmetic  0.72 us (1%)
    ppermute x17, starting transfers between devices, swap(): return lax.ppermute(value, axis, [(i, i ^ bit) for i in range(size)])  21.2 us
    pallas_call x23, Pallas kernels, kernel_call(): pl.pallas_call(body, out_shape=out, in_specs=[pl.BlockSpec(memory_space=s...  16.6 us
    ppermute x17, waiting for transfers between devices, swap(): return lax.ppermute(value, axis, [(i, i ^ bit) for i in range(size)])  12.4 us
  transfers between devices with their start and end apart: 17, of which 8 were waited for; matrix products, arithmetic and copies ran while one was open for 0% of the time, Pallas kernels for 29%

profile of v9, /device:TPU:0, one launch (start us, length us, event | category | flops | bytes accessed | tf_op | source)
XLA Modules:
  0.0 51.3 jit_solution(9565110066091386007)
XLA Ops:
  0.0 1.5 %power.1 = (f32[4,384]{1,0:T(4,128)S(1)}, bf16[2,320,256]{2,1,0:T(8,128)(2,1)S(1)}, bf16[2,320,256]{2,1,0:T(8,128)(2,1)S(1)}) custom-call(s32[2]{0:T(128)} %wl_ref.1, bf16[2,2,320,256]{3,2,1,0:T(8,128)(2,1)} %spec_ref.1), custom_call_target="tpu_custom_call" | custom-call | flops 1 | bytes 1 | tf_op jit(solution)/shard_map/power/pallas_call | solution.py:60
  1.5 0.5 %collective-permute-start.4 = (bf16[2,320,256]{2,1,0:T(8,128)(2,1)S(1)}, bf16[2,320,256]{2,1,0:T(8,128)(2,1)S(1)}, u32[]{:S(2)}, u32[]{:S(2)}) collective-permute-start(bf16[2,320,256]{2,1,0:T(8,128)(2,1)S(1)} %get-tuple-element.44), channel_id=1, source_target_pairs={{0,1},{1,0},{2,3},{3,2},{4,5},{5,4},{6,7},{7,6},{8,9},{9,8},{10,11... | collective-permute-start | bytes 983048 | tf_op jit(solution)/shard_map/ppermute | solution.py:343
  2.0 2.6 %collective-permute-start = (f32[4,384]{1,0:T(4,128)S(1)}, f32[4,384]{1,0:T(4,128)S(1)}, u32[]{:S(2)}, u32[]{:S(2)}) collective-permute-start(f32[4,384]{1,0:T(4,128)S(1)} %get-tuple-element.40), channel_id=1, source_target_pairs={{0,2},{1,3},{2,0},{3,1},{4,6},{5,7},{6,4},{7,5},{8,10},{9,11},{10,... | collective-permute-start | bytes 18440 | tf_op jit(solution)/shard_map/ppermute | solution.py:343
  4.6 2.2 %steering_far.5 = (bf16[640,512]{1,0:T(8,128)(2,1)S(1)}, bf16[640,512]{1,0:T(8,128)(2,1)S(1)}, f32[1,384]{1,0:T(1,128)S(1)}, s16[640,512]{1,0:T(8,128)(2,1)S(1)}) custom-call(f32[1,384]{1,0:T(1,128)S(1)} %slice.34.token_ref, s32[2560,512]{1,0:T(8,128)} %delays_ref.5), custom_call_target="tpu_custom_call" | custom-call | flops 1 | bytes 1 | tf_op jit(solution)/shard_map/steering_far/pallas_call | solution.py:60
  6.7 0.0 collective-permute-done
  6.8 0.2 collective-permute-start.1
  7.0 0.3 collective-permute-start.7
  7.4 0.7 %collective-permute-done.1 = f32[4,384]{1,0:T(4,128)S(1)} collective-permute-done((f32[4,384]{1,0:T(4,128)S(1)}, f32[4,384]{1,0:T(4,128)S(1)}, u32[]{:S(2)}, u32[]{:S(2)}) %collective-permute-start.1) | collective-permute-done | bytes 6176 | tf_op jit(solution)/shard_map/ppermute | solution.py:343
  8.0 0.0 collective-permute-done.4.other_ref
  8.0 0.1 send.1
  8.2 1.6 %collective-permute-start.5 = (bf16[2,2,320,128]{3,2,1,0:T(8,128)(2,1)S(1)}, bf16[2,2,320,128]{3,2,1,0:T(8,128)(2,1)S(1)}, u32[]{:S(2)}, u32[]{:S(2)}) collective-permute-start(bf16[2,2,320,128]{3,2,1,0:T(8,128)(2,1)S(1)} %get-tuple-element.45), channel_id=1, source_target_pairs={{0,4},{4,0},{8,12},{12,8},{16,20},{20,16},{24,28},{28,24},{1,5},{5... | collective-permute-start | bytes 983048 | tf_op jit(solution)/shard_map/ppermute | solution.py:343
  9.7 1.4 %collective-permute-start.8 = (bf16[2,2,320,256]{3,2,1,0:T(8,128)(2,1)S(1)}, bf16[2,2,320,256]{3,2,1,0:T(8,128)(2,1)S(1)}, u32[]{:S(2)}, u32[]{:S(2)}) collective-permute-start(bf16[2,2,320,256]{3,2,1,0:T(8,128)(2,1)S(1)} %get-tuple-element.52), channel_id=1, source_target_pairs={{0,2},{1,3},{2,0},{3,1},{4,6},{5,7},{6,4},{7,5},{8,10},{9,11},{10,... | collective-permute-start | bytes 1966088 | tf_op jit(solution)/shard_map/ppermute | solution.py:343
  11.2 1.6 %collective-permute-start.2 = (f32[1,384]{1,0:T(1,128)S(1)}, f32[1,384]{1,0:T(1,128)S(1)}, u32[]{:S(2)}, u32[]{:S(2)}) collective-permute-start(f32[1,384]{1,0:T(1,128)S(1)} %get-tuple-element.77.token_ref), channel_id=1, source_target_pairs={{0,8},{4,12},{8,0},{12,4},{16,24},{20,28},{24,16},{28,20},{1,9},{5... | collective-permute-start | bytes 4616 | tf_op jit(solution)/shard_map/ppermute | solution.py:343
  12.7 1.7 %steering_far.6 = (bf16[320,512]{1,0:T(8,128)(2,1)S(1)}, bf16[320,512]{1,0:T(8,128)(2,1)S(1)}, f32[1,384]{1,0:T(1,128)S(1)}) custom-call(f32[1,384]{1,0:T(1,128)S(1)} %get-tuple-element.77.token_ref, s32[1280,512]{1,0:T(8,128)} %delays_ref.9), custom_call_target="tpu_custom_call" | custom-call | flops 1 | bytes 1 | tf_op jit(solution)/shard_map/steering_far/pallas_call | solution.py:60
  14.4 0.3 collective-permute-done.2
  14.7 2.6 %collective-permute-start.3 = (f32[1,384]{1,0:T(1,128)S(1)}, f32[1,384]{1,0:T(1,128)S(1)}, u32[]{:S(2)}, u32[]{:S(2)}) collective-permute-start(f32[1,384]{1,0:T(1,128)S(1)} %gate.5), channel_id=1, source_target_pairs={{0,16},{4,20},{8,24},{12,28},{16,0},{20,4},{24,8},{28,12},{1,17},{... | collective-permute-start | bytes 4616 | tf_op jit(solution)/shard_map/ppermute | solution.py:343
  17.3 1.7 %steering_far.7 = (bf16[640,512]{1,0:T(8,128)(2,1)S(1)}, bf16[640,512]{1,0:T(8,128)(2,1)S(1)}, f32[1,384]{1,0:T(1,128)S(1)}) custom-call(f32[1,384]{1,0:T(1,128)S(1)} %add.21.refs_0_.token_ref, s32[1280,512]{1,0:T(8,128)} %delays_ref.9, bf16[320,512]{1,0:T(8,128)(2,1)S(1)} %get-tuple-element.46.refs_0_, bf16[320,512]{1,0:T(8,128)(2,1)S(1)} %get-tuple-element.47.refs_1_), custom_call_target="tpu_custom_call" | custom-call | flops 1 | bytes 1 | tf_op jit(solution)/shard_map/steering_far/pallas_call | solution.py:60
  19.1 0.2 collective-permute-done.3
  19.2 0.0 collective-permute-done.5.refs_2_.from_ref
  19.2 0.6 %collective-permute-start.6 = (f32[3,384]{1,0:T(4,128)S(1)}, f32[3,384]{1,0:T(4,128)S(1)}, u32[]{:S(2)}, u32[]{:S(2)}) collective-permute-start(f32[3,384]{1,0:T(4,128)S(1)} %gate.6), channel_id=1, source_target_pairs={{0,4},{4,0},{8,12},{12,8},{16,20},{20,16},{24,28},{28,24},{1,5},{5... | collective-permute-start | bytes 13832 | tf_op jit(solution)/shard_map/ppermute | solution.py:343
  19.8 1.7 %steering_far.8 = (bf16[320,512]{1,0:T(8,128)(2,1)S(1)}, bf16[320,512]{1,0:T(8,128)(2,1)S(1)}, f32[1,384]{1,0:T(1,128)S(1)}) custom-call(f32[1,384]{1,0:T(1,128)S(1)} %add.22.refs_1_.token_ref, s32[1280,512]{1,0:T(8,128)} %delays_ref.9), custom_call_target="tpu_custom_call" | custom-call | flops 1 | bytes 1 | tf_op jit(solution)/shard_map/steering_far/pallas_call | solution.py:60
  21.5 0.0 collective-permute-done.7.refs_0_
  21.5 1.1 %steering.1 = (bf16[640,512]{1,0:T(8,128)(2,1)S(1)}, bf16[640,512]{1,0:T(8,128)(2,1)S(1)}, f32[1,384]{1,0:T(1,128)S(1)}) custom-call(f32[1,384]{1,0:T(1,128)S(1)} %add.22.refs_1_.token_ref, s16[640,512]{1,0:T(8,128)(2,1)S(1)} %collective-permute-done.7.refs_0_), custom_call_target="tpu_custom_call" | custom-call | flops 1 | bytes 1 | tf_op jit(solution)/shard_map/steering/pallas_call | solution.py:60
  22.7 0.2 collective-permute-done.6.far_ref
  22.9 1.4 %beams_r.1 = (f32[256,256]{1,0:T(8,128)S(1)}, bf16[256,256]{1,0:T(8,128)(2,1)S(1)}, f32[1,384]{1,0:T(1,128)S(1)}) custom-call(f32[2,384]{1,0:T(2,128)S(1)} %pad_maximum_fusion.refs_0_.near_power_ref, f32[3,384]{1,0:T(4,128)S(1)} %collective-permute-done.6.far_ref, f32[1,384]{1,0:T(1,128)S(1)} %gate.7.level_ref.token_ref, ...), custom_call_target="tpu_custom_call" | custom-call | flops 1 | bytes 1 | tf_op jit(solution)/shard_map/beams_r/pallas_call | solution.py:60
  24.3 1.0 %collective-permute-start.12 = (bf16[256,256]{1,0:T(8,128)(2,1)S(1)}, bf16[256,256]{1,0:T(8,128)(2,1)S(1)}, u32[]{:S(2)}, u32[]{:S(2)}) collective-permute-start(bf16[256,256]{1,0:T(8,128)(2,1)S(1)} %get-tuple-element.69), channel_id=1, source_target_pairs={{0,2},{1,3},{2,0},{3,1},{4,6},{5,7},{6,4},{7,5},{8,10},{9,11},{10,... | collective-permute-start | bytes 393224 | tf_op jit(solution)/shard_map/ppermute | solution.py:343
  25.3 1.7 %steering_far.9 = (bf16[640,512]{1,0:T(8,128)(2,1)S(1)}, bf16[640,512]{1,0:T(8,128)(2,1)S(1)}, f32[1,384]{1,0:T(1,128)}) custom-call(f32[1,384]{1,0:T(1,128)S(1)} %get-tuple-element.59.token_ref, s32[1280,512]{1,0:T(8,128)} %delays_ref.9, bf16[320,512]{1,0:T(8,128)(2,1)S(1)} %get-tuple-element.60.refs_0_, bf16[320,512]{1,0:T(8,128)(2,1)S(1)} %get-tuple-element.61.refs_1_), custom_call_target="tpu_custom_call" | custom-call | flops 1 | bytes 1 | tf_op jit(solution)/shard_map/steering_far/pallas_call | solution.py:60
  27.0 0.0 collective-permute-done.8.from_ref
  27.1 1.3 %beams_s.3 = bf16[256,512]{1,0:T(8,128)(2,1)S(1)} custom-call(f32[2,384]{1,0:T(2,128)S(1)} %pad_maximum_fusion.refs_0_.near_power_ref, f32[2,384]{1,0:T(2,128)S(1)} %pad_maximum_fusion.1.far_ref, f32[1,384]{1,0:T(1,128)S(1)} %gate.7.level_ref.token_ref, bf16[2,320,256]{2,1,0:T(8,128)(2,1)S(1)} %get-tuple-element.43.own_ref, ...), custom_call_target="tpu_custom_call" | custom-call | flops 1 | bytes 1 | tf_op jit(solution)/shard_map/beams_s/pallas_call | solution.py:60
  28.4 1.1 %collective-permute-start.9 = (bf16[256,512]{1,0:T(8,128)(2,1)S(1)}, bf16[256,512]{1,0:T(8,128)(2,1)S(1)}, u32[]{:S(2)}, u32[]{:S(2)}) collective-permute-start(bf16[256,512]{1,0:T(8,128)(2,1)S(1)} %beams_s.3), channel_id=1, source_target_pairs={{0,4},{4,0},{8,12},{12,8},{16,20},{20,16},{24,28},{28,24},{1,5},{5... | collective-permute-start | bytes 786440 | tf_op jit(solution)/shard_map/ppermute | solution.py:343
  29.5 0.0 collective-permute-done.12.other_ref
  29.5 1.6 %collective-permute-start.13 = (bf16[256,256]{1,0:T(8,128)(2,1)S(1)}, bf16[256,256]{1,0:T(8,128)(2,1)S(1)}, u32[]{:S(2)}, u32[]{:S(2)}) collective-permute-start(bf16[256,256]{1,0:T(8,128)(2,1)S(1)} %get-tuple-element.71), channel_id=1, source_target_pairs={{0,8},{4,12},{8,0},{12,4},{16,24},{20,28},{24,16},{28,20},{1,9},{5... | collective-permute-start | bytes 393224 | tf_op jit(solution)/shard_map/ppermute | solution.py:343
  31.2 1.3 %beams_s.2.keep_ref = f32[256,512]{1,0:T(8,128)S(1)} custom-call(f32[2,384]{1,0:T(2,128)S(1)} %pad_maximum_fusion.refs_0_.near_power_ref, f32[2,384]{1,0:T(2,128)S(1)} %pad_maximum_fusion.1.far_ref, f32[1,384]{1,0:T(1,128)S(1)} %gate.7.level_ref.token_ref, bf16[2,320,256]{2,1,0:T(8,128)(2,1)S(1)} %get-tuple-element.43.own_ref, ...), custom_call_target="tpu_custom_call" | custom-call | flops 1 | bytes 1 | tf_op jit(solution)/shard_map/beams_s/pallas_call | solution.py:60
  32.5 3.0 %collective-permute-done.9.other_ref = bf16[256,512]{1,0:T(8,128)(2,1)S(1)} collective-permute-done((bf16[256,512]{1,0:T(8,128)(2,1)S(1)}, bf16[256,512]{1,0:T(8,128)(2,1)S(1)}, u32[]{:S(2)}, u32[]{:S(2)}) %collective-permute-start.9) | collective-permute-done | bytes 262176 | tf_op jit(solution)/shard_map/ppermute | solution.py:343
  35.5 0.1 step_s.3
  35.6 0.0 collective-permute-done.13.other_ref
  35.6 2.6 %collective-permute-start.14 = (bf16[256,256]{1,0:T(8,128)(2,1)S(1)}, bf16[256,256]{1,0:T(8,128)(2,1)S(1)}, u32[]{:S(2)}, u32[]{:S(2)}) collective-permute-start(bf16[256,256]{1,0:T(8,128)(2,1)S(1)} %get-tuple-element.74), channel_id=1, source_target_pairs={{0,16},{4,20},{8,24},{12,28},{16,0},{20,4},{24,8},{28,12},{1,17},{... | collective-permute-start | bytes 393224 | tf_op jit(solution)/shard_map/ppermute | solution.py:343
  38.3 1.6 %collective-permute-start.10 = (bf16[128,512]{1,0:T(8,128)(2,1)S(1)}, bf16[128,512]{1,0:T(8,128)(2,1)S(1)}, u32[]{:S(2)}, u32[]{:S(2)}) collective-permute-start(bf16[128,512]{1,0:T(8,128)(2,1)S(1)} %get-tuple-element.65), channel_id=1, source_target_pairs={{0,8},{4,12},{8,0},{12,4},{16,24},{20,28},{24,16},{28,20},{1,9},{5... | collective-permute-start | bytes 393224 | tf_op jit(solution)/shard_map/ppermute | solution.py:343
  39.9 3.2 %collective-permute-done.14.other_ref = bf16[256,256]{1,0:T(8,128)(2,1)S(1)} collective-permute-done((bf16[256,256]{1,0:T(8,128)(2,1)S(1)}, bf16[256,256]{1,0:T(8,128)(2,1)S(1)}, u32[]{:S(2)}, u32[]{:S(2)}) %collective-permute-start.14) | collective-permute-done | bytes 131104 | tf_op jit(solution)/shard_map/ppermute | solution.py:343
  43.1 0.6 %collective-permute-start.15 = (bf16[256,256]{1,0:T(8,128)(2,1)S(1)}, bf16[256,256]{1,0:T(8,128)(2,1)S(1)}, u32[]{:S(2)}, u32[]{:S(2)}) collective-permute-start(bf16[256,256]{1,0:T(8,128)(2,1)S(1)} %step_r.5.near_r), channel_id=1, source_target_pairs={{0,4},{4,0},{8,12},{12,8},{16,20},{20,16},{24,28},{28,24},{1,5},{5... | collective-permute-start | bytes 393224 | tf_op jit(solution)/shard_map/ppermute | solution.py:343
  43.7 0.0 collective-permute-done.10.other_ref
  43.7 1.2 %collective-permute-start.11 = (bf16[64,512]{1,0:T(8,128)(2,1)S(1)}, bf16[64,512]{1,0:T(8,128)(2,1)S(1)}, u32[]{:S(2)}, u32[]{:S(2)}) collective-permute-start(bf16[64,512]{1,0:T(8,128)(2,1)S(1)} %get-tuple-element.67), channel_id=1, source_target_pairs={{0,16},{4,20},{8,24},{12,28},{16,0},{20,4},{24,8},{28,12},{1,17},{... | collective-permute-start | bytes 196616 | tf_op jit(solution)/shard_map/ppermute | solution.py:343
  45.0 4.0 %collective-permute-done.11.other_ref = bf16[64,512]{1,0:T(8,128)(2,1)S(1)} collective-permute-done((bf16[64,512]{1,0:T(8,128)(2,1)S(1)}, bf16[64,512]{1,0:T(8,128)(2,1)S(1)}, u32[]{:S(2)}, u32[]{:S(2)}) %collective-permute-start.11) | collective-permute-done | bytes 65568 | tf_op jit(solution)/shard_map/ppermute | solution.py:343
  49.0 0.0 collective-permute-done.15.far_r
  49.0 0.3 field.3
  49.3 0.1 collective-permute-start.16
  49.4 0.3 field.2
  49.7 0.9 %collective-permute-done.16 = bf16[2,64,128]{2,1,0:T(8,128)(2,1)S(1)} collective-permute-done((bf16[2,64,128]{2,1,0:T(8,128)(2,1)S(1)}, bf16[2,64,128]{2,1,0:T(8,128)(2,1)S(1)}, u32[]{:S(2)}, u32[]{:S(2)}) %collective-permute-start.16) | collective-permute-done | bytes 32800 | tf_op jit(solution)/shard_map/ppermute | solution.py:343
  50.6 0.7 %maximum_bitcast_fusion = f32[2,2,128,64]{2,3,1,0:T(8,128)} fusion(f32[1,2,64,128]{3,2,1,0:T(8,128)S(1)} %get-tuple-element.76, f32[1,2,64,128]{3,2,1,0:T(8,128)S(1)} %get-tuple-element.75), kind=kLoop, calls=%fused_computation | loop fusion | flops 32768 | bytes 262144 | tf_op jit(solution)/shard_map/transpose | solution.py:475
  (19 shorter events, 0.3 us)
Async XLA Ops:
  1.5 6.6 %collective-permute-start.4 = (bf16[2,320,256]{2,1,0:T(8,128)(2,1)S(1)}, bf16[2,320,256]{2,1,0:T(8,128)(2,1)S(1)}, u32[]{:S(2)}, u32[]{:S(2)}) collective-permute-start(bf16[2,320,256]{2,1,0:T(8,128)(2,1)S(1)} %get-tuple-element.44), channel_id=1, source_target_pairs={{0,1},{1,0},{2,3},{3,2},{4,5},{5,4},{6,7},{7,6},{8,9},{9,8},{10,11... | collective-permute-start | bytes 983048 | tf_op jit(solution)/shard_map/ppermute | solution.py:343
  2.0 4.8 %collective-permute-start = (f32[4,384]{1,0:T(4,128)S(1)}, f32[4,384]{1,0:T(4,128)S(1)}, u32[]{:S(2)}, u32[]{:S(2)}) collective-permute-start(f32[4,384]{1,0:T(4,128)S(1)} %get-tuple-element.40), channel_id=1, source_target_pairs={{0,2},{1,3},{2,0},{3,1},{4,6},{5,7},{6,4},{7,5},{8,10},{9,11},{10,... | collective-permute-start | bytes 18440 | tf_op jit(solution)/shard_map/ppermute | solution.py:343
  6.8 1.2 %collective-permute-start.1 = (f32[4,384]{1,0:T(4,128)S(1)}, f32[4,384]{1,0:T(4,128)S(1)}, u32[]{:S(2)}, u32[]{:S(2)}) collective-permute-start(f32[4,384]{1,0:T(4,128)S(1)} %gate.4), channel_id=1, source_target_pairs={{0,1},{1,0},{2,3},{3,2},{4,5},{5,4},{6,7},{7,6},{8,9},{9,8},{10,11... | collective-permute-start | bytes 18440 | tf_op jit(solution)/shard_map/ppermute | solution.py:343
  7.0 14.5 %collective-permute-start.7 = (s16[640,512]{1,0:T(8,128)(2,1)S(1)}, s16[640,512]{1,0:T(8,128)(2,1)S(1)}, u32[]{:S(2)}, u32[]{:S(2)}) collective-permute-start(s16[640,512]{1,0:T(8,128)(2,1)S(1)} %get-tuple-element.49), channel_id=1, source_target_pairs={{0,1},{1,0},{2,3},{3,2},{4,5},{5,4},{6,7},{7,6},{8,9},{9,8},{10,11... | collective-permute-start | bytes 1966088 | tf_op jit(solution)/shard_map/ppermute | solution.py:343
  8.2 11.1 %collective-permute-start.5 = (bf16[2,2,320,128]{3,2,1,0:T(8,128)(2,1)S(1)}, bf16[2,2,320,128]{3,2,1,0:T(8,128)(2,1)S(1)}, u32[]{:S(2)}, u32[]{:S(2)}) collective-permute-start(bf16[2,2,320,128]{3,2,1,0:T(8,128)(2,1)S(1)} %get-tuple-element.45), channel_id=1, source_target_pairs={{0,4},{4,0},{8,12},{12,8},{16,20},{20,16},{24,28},{28,24},{1,5},{5... | collective-permute-start | bytes 983048 | tf_op jit(solution)/shard_map/ppermute | solution.py:343
  9.7 17.3 %collective-permute-start.8 = (bf16[2,2,320,256]{3,2,1,0:T(8,128)(2,1)S(1)}, bf16[2,2,320,256]{3,2,1,0:T(8,128)(2,1)S(1)}, u32[]{:S(2)}, u32[]{:S(2)}) collective-permute-start(bf16[2,2,320,256]{3,2,1,0:T(8,128)(2,1)S(1)} %get-tuple-element.52), channel_id=1, source_target_pairs={{0,2},{1,3},{2,0},{3,1},{4,6},{5,7},{6,4},{7,5},{8,10},{9,11},{10,... | collective-permute-start | bytes 1966088 | tf_op jit(solution)/shard_map/ppermute | solution.py:343
  11.2 3.6 %collective-permute-start.2 = (f32[1,384]{1,0:T(1,128)S(1)}, f32[1,384]{1,0:T(1,128)S(1)}, u32[]{:S(2)}, u32[]{:S(2)}) collective-permute-start(f32[1,384]{1,0:T(1,128)S(1)} %get-tuple-element.77.token_ref), channel_id=1, source_target_pairs={{0,8},{4,12},{8,0},{12,4},{16,24},{20,28},{24,16},{28,20},{1,9},{5... | collective-permute-start | bytes 4616 | tf_op jit(solution)/shard_map/ppermute | solution.py:343
  14.7 4.5 %collective-permute-start.3 = (f32[1,384]{1,0:T(1,128)S(1)}, f32[1,384]{1,0:T(1,128)S(1)}, u32[]{:S(2)}, u32[]{:S(2)}) collective-permute-start(f32[1,384]{1,0:T(1,128)S(1)} %gate.5), channel_id=1, source_target_pairs={{0,16},{4,20},{8,24},{12,28},{16,0},{20,4},{24,8},{28,12},{1,17},{... | collective-permute-start | bytes 4616 | tf_op jit(solution)/shard_map/ppermute | solution.py:343
  19.2 3.7 %collective-permute-start.6 = (f32[3,384]{1,0:T(4,128)S(1)}, f32[3,384]{1,0:T(4,128)S(1)}, u32[]{:S(2)}, u32[]{:S(2)}) collective-permute-start(f32[3,384]{1,0:T(4,128)S(1)} %gate.6), channel_id=1, source_target_pairs={{0,4},{4,0},{8,12},{12,8},{16,20},{20,16},{24,28},{28,24},{1,5},{5... | collective-permute-start | bytes 13832 | tf_op jit(solution)/shard_map/ppermute | solution.py:343
  24.3 5.1 %collective-permute-start.12 = (bf16[256,256]{1,0:T(8,128)(2,1)S(1)}, bf16[256,256]{1,0:T(8,128)(2,1)S(1)}, u32[]{:S(2)}, u32[]{:S(2)}) collective-permute-start(bf16[256,256]{1,0:T(8,128)(2,1)S(1)} %get-tuple-element.69), channel_id=1, source_target_pairs={{0,2},{1,3},{2,0},{3,1},{4,6},{5,7},{6,4},{7,5},{8,10},{9,11},{10,... | collective-permute-start | bytes 393224 | tf_op jit(solution)/shard_map/ppermute | solution.py:343
  28.4 7.1 %collective-permute-start.9 = (bf16[256,512]{1,0:T(8,128)(2,1)S(1)}, bf16[256,512]{1,0:T(8,128)(2,1)S(1)}, u32[]{:S(2)}, u32[]{:S(2)}) collective-permute-start(bf16[256,512]{1,0:T(8,128)(2,1)S(1)} %beams_s.3), channel_id=1, source_target_pairs={{0,4},{4,0},{8,12},{12,8},{16,20},{20,16},{24,28},{28,24},{1,5},{5... | collective-permute-start | bytes 786440 | tf_op jit(solution)/shard_map/ppermute | solution.py:343
  29.5 6.1 %collective-permute-start.13 = (bf16[256,256]{1,0:T(8,128)(2,1)S(1)}, bf16[256,256]{1,0:T(8,128)(2,1)S(1)}, u32[]{:S(2)}, u32[]{:S(2)}) collective-permute-start(bf16[256,256]{1,0:T(8,128)(2,1)S(1)} %get-tuple-element.71), channel_id=1, source_target_pairs={{0,8},{4,12},{8,0},{12,4},{16,24},{20,28},{24,16},{28,20},{1,9},{5... | collective-permute-start | bytes 393224 | tf_op jit(solution)/shard_map/ppermute | solution.py:343
  35.6 7.4 %collective-permute-start.14 = (bf16[256,256]{1,0:T(8,128)(2,1)S(1)}, bf16[256,256]{1,0:T(8,128)(2,1)S(1)}, u32[]{:S(2)}, u32[]{:S(2)}) collective-permute-start(bf16[256,256]{1,0:T(8,128)(2,1)S(1)} %get-tuple-element.74), channel_id=1, source_target_pairs={{0,16},{4,20},{8,24},{12,28},{16,0},{20,4},{24,8},{28,12},{1,17},{... | collective-permute-start | bytes 393224 | tf_op jit(solution)/shard_map/ppermute | solution.py:343
  38.3 5.4 %collective-permute-start.10 = (bf16[128,512]{1,0:T(8,128)(2,1)S(1)}, bf16[128,512]{1,0:T(8,128)(2,1)S(1)}, u32[]{:S(2)}, u32[]{:S(2)}) collective-permute-start(bf16[128,512]{1,0:T(8,128)(2,1)S(1)} %get-tuple-element.65), channel_id=1, source_target_pairs={{0,8},{4,12},{8,0},{12,4},{16,24},{20,28},{24,16},{28,20},{1,9},{5... | collective-permute-start | bytes 393224 | tf_op jit(solution)/shard_map/ppermute | solution.py:343
  43.1 5.9 %collective-permute-start.15 = (bf16[256,256]{1,0:T(8,128)(2,1)S(1)}, bf16[256,256]{1,0:T(8,128)(2,1)S(1)}, u32[]{:S(2)}, u32[]{:S(2)}) collective-permute-start(bf16[256,256]{1,0:T(8,128)(2,1)S(1)} %step_r.5.near_r), channel_id=1, source_target_pairs={{0,4},{4,0},{8,12},{12,8},{16,20},{20,16},{24,28},{28,24},{1,5},{5... | collective-permute-start | bytes 393224 | tf_op jit(solution)/shard_map/ppermute | solution.py:343
  43.7 5.2 %collective-permute-start.11 = (bf16[64,512]{1,0:T(8,128)(2,1)S(1)}, bf16[64,512]{1,0:T(8,128)(2,1)S(1)}, u32[]{:S(2)}, u32[]{:S(2)}) collective-permute-start(bf16[64,512]{1,0:T(8,128)(2,1)S(1)} %get-tuple-element.67), channel_id=1, source_target_pairs={{0,16},{4,20},{8,24},{12,28},{16,0},{20,4},{24,8},{28,12},{1,17},{... | collective-permute-start | bytes 196616 | tf_op jit(solution)/shard_map/ppermute | solution.py:343
  49.3 1.3 %collective-permute-start.16 = (bf16[2,64,128]{2,1,0:T(8,128)(2,1)S(1)}, bf16[2,64,128]{2,1,0:T(8,128)(2,1)S(1)}, u32[]{:S(2)}, u32[]{:S(2)}) collective-permute-start(bf16[2,64,128]{2,1,0:T(8,128)(2,1)S(1)} %field.3), channel_id=1, source_target_pairs={{0,1},{1,0},{2,3},{3,2},{4,5},{5,4},{6,7},{7,6},{8,9},{9,8},{10,11... | collective-permute-start | bytes 98312 | tf_op jit(solution)/shard_map/ppermute | solution.py:343

commit v10 on v9

--- a/solution.py
+++ b/solution.py
@@ -199,7 +199,7 @@
 
 
 def steering_far(starts, per, blocks, token, delays, copied=(), block=None, head=()):
-    parts = 1
+    parts = math.gcd(per // CHUNK, 1 if block else 2)
     shape = (per * blocks, delays.shape[1])
     whole = (shape[0] + (head[0].shape[0] if head else 0), shape[1])
     return kernel_call(

time: 51.6 us -> 51.6 us (level)
  no operation moved by 1% of the time
where the time goes in v10:
time: 51.6 us; the launch traced here: 51.3 us
  starting transfers between devices  21.2 us (41%)
  Pallas kernels  16.6 us (32%)
  waiting for transfers between devices  12.5 us (24%)
  other arithmetic  0.72 us (1%)
    ppermute x17, starting transfers between devices, swap(): return lax.ppermute(value, axis, [(i, i ^ bit) for i in range(size)])  21.2 us
    pallas_call x23, Pallas kernels, kernel_call(): pl.pallas_call(body, out_shape=out, in_specs=[pl.BlockSpec(memory_space=s...  16.6 us
    ppermute x17, waiting for transfers between devices, swap(): return lax.ppermute(value, axis, [(i, i ^ bit) for i in range(size)])  12.5 us
  transfers between devices with their start and end apart: 17, of which 8 were waited for; matrix products, arithmetic and copies ran while one was open for 0% of the time, Pallas kernels for 29%

profile of v10, /device:TPU:0, one launch (start us, length us, event | category | flops | bytes accessed | tf_op | source)
XLA Modules:
  0.0 51.3 jit_solution(4445155444779298121)
XLA Ops:
  0.0 1.5 %power.1 = (f32[4,384]{1,0:T(4,128)S(1)}, bf16[2,320,256]{2,1,0:T(8,128)(2,1)S(1)}, bf16[2,320,256]{2,1,0:T(8,128)(2,1)S(1)}) custom-call(s32[2]{0:T(128)} %wl_ref.1, bf16[2,2,320,256]{3,2,1,0:T(8,128)(2,1)} %spec_ref.1), custom_call_target="tpu_custom_call" | custom-call | flops 1 | bytes 1 | tf_op jit(solution)/shard_map/power/pallas_call | solution.py:60
  1.5 0.5 %collective-permute-start.4 = (bf16[2,320,256]{2,1,0:T(8,128)(2,1)S(1)}, bf16[2,320,256]{2,1,0:T(8,128)(2,1)S(1)}, u32[]{:S(2)}, u32[]{:S(2)}) collective-permute-start(bf16[2,320,256]{2,1,0:T(8,128)(2,1)S(1)} %get-tuple-element.44), channel_id=1, source_target_pairs={{0,1},{1,0},{2,3},{3,2},{4,5},{5,4},{6,7},{7,6},{8,9},{9,8},{10,11... | collective-permute-start | bytes 983048 | tf_op jit(solution)/shard_map/ppermute | solution.py:343
  2.0 2.6 %collective-permute-start = (f32[4,384]{1,0:T(4,128)S(1)}, f32[4,384]{1,0:T(4,128)S(1)}, u32[]{:S(2)}, u32[]{:S(2)}) collective-permute-start(f32[4,384]{1,0:T(4,128)S(1)} %get-tuple-element.40), channel_id=1, source_target_pairs={{0,2},{1,3},{2,0},{3,1},{4,6},{5,7},{6,4},{7,5},{8,10},{9,11},{10,... | collective-permute-start | bytes 18440 | tf_op jit(solution)/shard_map/ppermute | solution.py:343
  4.6 2.1 %steering_far.5 = (bf16[640,512]{1,0:T(8,128)(2,1)S(1)}, bf16[640,512]{1,0:T(8,128)(2,1)S(1)}, f32[1,384]{1,0:T(1,128)S(1)}, s16[640,512]{1,0:T(8,128)(2,1)S(1)}) custom-call(f32[1,384]{1,0:T(1,128)S(1)} %slice.34.token_ref, s32[2560,512]{1,0:T(8,128)} %delays_ref.5), custom_call_target="tpu_custom_call" | custom-call | flops 1 | bytes 1 | tf_op jit(solution)/shard_map/steering_far/pallas_call | solution.py:60
  6.7 0.0 collective-permute-done
  6.7 0.2 collective-permute-start.1
  6.9 0.3 collective-permute-start.7
  7.3 0.7 %collective-permute-done.1 = f32[4,384]{1,0:T(4,128)S(1)} collective-permute-done((f32[4,384]{1,0:T(4,128)S(1)}, f32[4,384]{1,0:T(4,128)S(1)}, u32[]{:S(2)}, u32[]{:S(2)}) %collective-permute-start.1) | collective-permute-done | bytes 6176 | tf_op jit(solution)/shard_map/ppermute | solution.py:343
  7.9 0.0 collective-permute-done.4.other_ref
  8.0 0.1 send.1
  8.1 1.6 %collective-permute-start.5 = (bf16[2,2,320,128]{3,2,1,0:T(8,128)(2,1)S(1)}, bf16[2,2,320,128]{3,2,1,0:T(8,128)(2,1)S(1)}, u32[]{:S(2)}, u32[]{:S(2)}) collective-permute-start(bf16[2,2,320,128]{3,2,1,0:T(8,128)(2,1)S(1)} %get-tuple-element.45), channel_id=1, source_target_pairs={{0,4},{4,0},{8,12},{12,8},{16,20},{20,16},{24,28},{28,24},{1,5},{5... | collective-permute-start | bytes 983048 | tf_op jit(solution)/shard_map/ppermute | solution.py:343
  9.7 1.5 %collective-permute-start.8 = (bf16[2,2,320,256]{3,2,1,0:T(8,128)(2,1)S(1)}, bf16[2,2,320,256]{3,2,1,0:T(8,128)(2,1)S(1)}, u32[]{:S(2)}, u32[]{:S(2)}) collective-permute-start(bf16[2,2,320,256]{3,2,1,0:T(8,128)(2,1)S(1)} %get-tuple-element.52), channel_id=1, source_target_pairs={{0,2},{1,3},{2,0},{3,1},{4,6},{5,7},{6,4},{7,5},{8,10},{9,11},{10,... | collective-permute-start | bytes 1966088 | tf_op jit(solution)/shard_map/ppermute | solution.py:343
  11.2 1.6 %collective-permute-start.2 = (f32[1,384]{1,0:T(1,128)S(1)}, f32[1,384]{1,0:T(1,128)S(1)}, u32[]{:S(2)}, u32[]{:S(2)}) collective-permute-start(f32[1,384]{1,0:T(1,128)S(1)} %get-tuple-element.77.token_ref), channel_id=1, source_target_pairs={{0,8},{4,12},{8,0},{12,4},{16,24},{20,28},{24,16},{28,20},{1,9},{5... | collective-permute-start | bytes 4616 | tf_op jit(solution)/shard_map/ppermute | solution.py:343
  12.7 1.7 %steering_far.6 = (bf16[320,512]{1,0:T(8,128)(2,1)S(1)}, bf16[320,512]{1,0:T(8,128)(2,1)S(1)}, f32[1,384]{1,0:T(1,128)S(1)}) custom-call(f32[1,384]{1,0:T(1,128)S(1)} %get-tuple-element.77.token_ref, s32[1280,512]{1,0:T(8,128)} %delays_ref.9), custom_call_target="tpu_custom_call" | custom-call | flops 1 | bytes 1 | tf_op jit(solution)/shard_map/steering_far/pallas_call | solution.py:60
  14.4 0.3 collective-permute-done.2
  14.7 2.6 %collective-permute-start.3 = (f32[1,384]{1,0:T(1,128)S(1)}, f32[1,384]{1,0:T(1,128)S(1)}, u32[]{:S(2)}, u32[]{:S(2)}) collective-permute-start(f32[1,384]{1,0:T(1,128)S(1)} %gate.5), channel_id=1, source_target_pairs={{0,16},{4,20},{8,24},{12,28},{16,0},{20,4},{24,8},{28,12},{1,17},{... | collective-permute-start | bytes 4616 | tf_op jit(solution)/shard_map/ppermute | solution.py:343
  17.3 1.7 %steering_far.7 = (bf16[640,512]{1,0:T(8,128)(2,1)S(1)}, bf16[640,512]{1,0:T(8,128)(2,1)S(1)}, f32[1,384]{1,0:T(1,128)S(1)}) custom-call(f32[1,384]{1,0:T(1,128)S(1)} %add.21.refs_0_.token_ref, s32[1280,512]{1,0:T(8,128)} %delays_ref.9, bf16[320,512]{1,0:T(8,128)(2,1)S(1)} %get-tuple-element.46.refs_0_, bf16[320,512]{1,0:T(8,128)(2,1)S(1)} %get-tuple-element.47.refs_1_), custom_call_target="tpu_custom_call" | custom-call | flops 1 | bytes 1 | tf_op jit(solution)/shard_map/steering_far/pallas_call | solution.py:60
  19.1 0.2 collective-permute-done.3
  19.2 0.0 collective-permute-done.5.refs_2_.from_ref
  19.2 0.6 %collective-permute-start.6 = (f32[3,384]{1,0:T(4,128)S(1)}, f32[3,384]{1,0:T(4,128)S(1)}, u32[]{:S(2)}, u32[]{:S(2)}) collective-permute-start(f32[3,384]{1,0:T(4,128)S(1)} %gate.6), channel_id=1, source_target_pairs={{0,4},{4,0},{8,12},{12,8},{16,20},{20,16},{24,28},{28,24},{1,5},{5... | collective-permute-start | bytes 13832 | tf_op jit(solution)/shard_map/ppermute | solution.py:343
  19.8 1.7 %steering_far.8 = (bf16[320,512]{1,0:T(8,128)(2,1)S(1)}, bf16[320,512]{1,0:T(8,128)(2,1)S(1)}, f32[1,384]{1,0:T(1,128)S(1)}) custom-call(f32[1,384]{1,0:T(1,128)S(1)} %add.22.refs_1_.token_ref, s32[1280,512]{1,0:T(8,128)} %delays_ref.9), custom_call_target="tpu_custom_call" | custom-call | flops 1 | bytes 1 | tf_op jit(solution)/shard_map/steering_far/pallas_call | solution.py:60
  21.5 0.0 collective-permute-done.7.refs_0_
  21.5 1.1 %steering.1 = (bf16[640,512]{1,0:T(8,128)(2,1)S(1)}, bf16[640,512]{1,0:T(8,128)(2,1)S(1)}, f32[1,384]{1,0:T(1,128)S(1)}) custom-call(f32[1,384]{1,0:T(1,128)S(1)} %add.22.refs_1_.token_ref, s16[640,512]{1,0:T(8,128)(2,1)S(1)} %collective-permute-done.7.refs_0_), custom_call_target="tpu_custom_call" | custom-call | flops 1 | bytes 1 | tf_op jit(solution)/shard_map/steering/pallas_call | solution.py:60
  22.7 0.2 collective-permute-done.6.far_ref
  22.9 1.4 %beams_r.1 = (f32[256,256]{1,0:T(8,128)S(1)}, bf16[256,256]{1,0:T(8,128)(2,1)S(1)}, f32[1,384]{1,0:T(1,128)S(1)}) custom-call(f32[2,384]{1,0:T(2,128)S(1)} %pad_maximum_fusion.refs_0_.near_power_ref, f32[3,384]{1,0:T(4,128)S(1)} %collective-permute-done.6.far_ref, f32[1,384]{1,0:T(1,128)S(1)} %gate.7.level_ref.token_ref, ...), custom_call_target="tpu_custom_call" | custom-call | flops 1 | bytes 1 | tf_op jit(solution)/shard_map/beams_r/pallas_call | solution.py:60
  24.3 1.0 %collective-permute-start.12 = (bf16[256,256]{1,0:T(8,128)(2,1)S(1)}, bf16[256,256]{1,0:T(8,128)(2,1)S(1)}, u32[]{:S(2)}, u32[]{:S(2)}) collective-permute-start(bf16[256,256]{1,0:T(8,128)(2,1)S(1)} %get-tuple-element.69), channel_id=1, source_target_pairs={{0,2},{1,3},{2,0},{3,1},{4,6},{5,7},{6,4},{7,5},{8,10},{9,11},{10,... | collective-permute-start | bytes 393224 | tf_op jit(solution)/shard_map/ppermute | solution.py:343
  25.3 1.7 %steering_far.9 = (bf16[640,512]{1,0:T(8,128)(2,1)S(1)}, bf16[640,512]{1,0:T(8,128)(2,1)S(1)}, f32[1,384]{1,0:T(1,128)}) custom-call(f32[1,384]{1,0:T(1,128)S(1)} %get-tuple-element.59.token_ref, s32[1280,512]{1,0:T(8,128)} %delays_ref.9, bf16[320,512]{1,0:T(8,128)(2,1)S(1)} %get-tuple-element.60.refs_0_, bf16[320,512]{1,0:T(8,128)(2,1)S(1)} %get-tuple-element.61.refs_1_), custom_call_target="tpu_custom_call" | custom-call | flops 1 | bytes 1 | tf_op jit(solution)/shard_map/steering_far/pallas_call | solution.py:60
  27.0 0.0 collective-permute-done.8.from_ref
  27.1 1.3 %beams_s.3 = bf16[256,512]{1,0:T(8,128)(2,1)S(1)} custom-call(f32[2,384]{1,0:T(2,128)S(1)} %pad_maximum_fusion.refs_0_.near_power_ref, f32[2,384]{1,0:T(2,128)S(1)} %pad_maximum_fusion.1.far_ref, f32[1,384]{1,0:T(1,128)S(1)} %gate.7.level_ref.token_ref, bf16[2,320,256]{2,1,0:T(8,128)(2,1)S(1)} %get-tuple-element.43.own_ref, ...), custom_call_target="tpu_custom_call" | custom-call | flops 1 | bytes 1 | tf_op jit(solution)/shard_map/beams_s/pallas_call | solution.py:60
  28.4 1.0 %collective-permute-start.9 = (bf16[256,512]{1,0:T(8,128)(2,1)S(1)}, bf16[256,512]{1,0:T(8,128)(2,1)S(1)}, u32[]{:S(2)}, u32[]{:S(2)}) collective-permute-start(bf16[256,512]{1,0:T(8,128)(2,1)S(1)} %beams_s.3), channel_id=1, source_target_pairs={{0,4},{4,0},{8,12},{12,8},{16,20},{20,16},{24,28},{28,24},{1,5},{5... | collective-permute-start | bytes 786440 | tf_op jit(solution)/shard_map/ppermute | solution.py:343
  29.4 0.0 collective-permute-done.12.other_ref
  29.5 1.6 %collective-permute-start.13 = (bf16[256,256]{1,0:T(8,128)(2,1)S(1)}, bf16[256,256]{1,0:T(8,128)(2,1)S(1)}, u32[]{:S(2)}, u32[]{:S(2)}) collective-permute-start(bf16[256,256]{1,0:T(8,128)(2,1)S(1)} %get-tuple-element.71), channel_id=1, source_target_pairs={{0,8},{4,12},{8,0},{12,4},{16,24},{20,28},{24,16},{28,20},{1,9},{5... | collective-permute-start | bytes 393224 | tf_op jit(solution)/shard_map/ppermute | solution.py:343
  31.1 1.3 %beams_s.2.keep_ref = f32[256,512]{1,0:T(8,128)S(1)} custom-call(f32[2,384]{1,0:T(2,128)S(1)} %pad_maximum_fusion.refs_0_.near_power_ref, f32[2,384]{1,0:T(2,128)S(1)} %pad_maximum_fusion.1.far_ref, f32[1,384]{1,0:T(1,128)S(1)} %gate.7.level_ref.token_ref, bf16[2,320,256]{2,1,0:T(8,128)(2,1)S(1)} %get-tuple-element.43.own_ref, ...), custom_call_target="tpu_custom_call" | custom-call | flops 1 | bytes 1 | tf_op jit(solution)/shard_map/beams_s/pallas_call | solution.py:60
  32.4 3.0 %collective-permute-done.9.other_ref = bf16[256,512]{1,0:T(8,128)(2,1)S(1)} collective-permute-done((bf16[256,512]{1,0:T(8,128)(2,1)S(1)}, bf16[256,512]{1,0:T(8,128)(2,1)S(1)}, u32[]{:S(2)}, u32[]{:S(2)}) %collective-permute-start.9) | collective-permute-done | bytes 262176 | tf_op jit(solution)/shard_map/ppermute | solution.py:343
  35.5 0.1 step_s.3
  35.6 0.0 collective-permute-done.13.other_ref
  35.6 2.6 %collective-permute-start.14 = (bf16[256,256]{1,0:T(8,128)(2,1)S(1)}, bf16[256,256]{1,0:T(8,128)(2,1)S(1)}, u32[]{:S(2)}, u32[]{:S(2)}) collective-permute-start(bf16[256,256]{1,0:T(8,128)(2,1)S(1)} %get-tuple-element.74), channel_id=1, source_target_pairs={{0,16},{4,20},{8,24},{12,28},{16,0},{20,4},{24,8},{28,12},{1,17},{... | collective-permute-start | bytes 393224 | tf_op jit(solution)/shard_map/ppermute | solution.py:343
  38.3 1.6 %collective-permute-start.10 = (bf16[128,512]{1,0:T(8,128)(2,1)S(1)}, bf16[128,512]{1,0:T(8,128)(2,1)S(1)}, u32[]{:S(2)}, u32[]{:S(2)}) collective-permute-start(bf16[128,512]{1,0:T(8,128)(2,1)S(1)} %get-tuple-element.65), channel_id=1, source_target_pairs={{0,8},{4,12},{8,0},{12,4},{16,24},{20,28},{24,16},{28,20},{1,9},{5... | collective-permute-start | bytes 393224 | tf_op jit(solution)/shard_map/ppermute | solution.py:343
  39.9 3.2 %collective-permute-done.14.other_ref = bf16[256,256]{1,0:T(8,128)(2,1)S(1)} collective-permute-done((bf16[256,256]{1,0:T(8,128)(2,1)S(1)}, bf16[256,256]{1,0:T(8,128)(2,1)S(1)}, u32[]{:S(2)}, u32[]{:S(2)}) %collective-permute-start.14) | collective-permute-done | bytes 131104 | tf_op jit(solution)/shard_map/ppermute | solution.py:343
  43.1 0.6 %collective-permute-start.15 = (bf16[256,256]{1,0:T(8,128)(2,1)S(1)}, bf16[256,256]{1,0:T(8,128)(2,1)S(1)}, u32[]{:S(2)}, u32[]{:S(2)}) collective-permute-start(bf16[256,256]{1,0:T(8,128)(2,1)S(1)} %step_r.5.near_r), channel_id=1, source_target_pairs={{0,4},{4,0},{8,12},{12,8},{16,20},{20,16},{24,28},{28,24},{1,5},{5... | collective-permute-start | bytes 393224 | tf_op jit(solution)/shard_map/ppermute | solution.py:343
  43.7 0.0 collective-permute-done.10.other_ref
  43.7 1.2 %collective-permute-start.11 = (bf16[64,512]{1,0:T(8,128)(2,1)S(1)}, bf16[64,512]{1,0:T(8,128)(2,1)S(1)}, u32[]{:S(2)}, u32[]{:S(2)}) collective-permute-start(bf16[64,512]{1,0:T(8,128)(2,1)S(1)} %get-tuple-element.67), channel_id=1, source_target_pairs={{0,16},{4,20},{8,24},{12,28},{16,0},{20,4},{24,8},{28,12},{1,17},{... | collective-permute-start | bytes 196616 | tf_op jit(solution)/shard_map/ppermute | solution.py:343
  45.0 4.0 %collective-permute-done.11.other_ref = bf16[64,512]{1,0:T(8,128)(2,1)S(1)} collective-permute-done((bf16[64,512]{1,0:T(8,128)(2,1)S(1)}, bf16[64,512]{1,0:T(8,128)(2,1)S(1)}, u32[]{:S(2)}, u32[]{:S(2)}) %collective-permute-start.11) | collective-permute-done | bytes 65568 | tf_op jit(solution)/shard_map/ppermute | solution.py:343
  49.0 0.0 collective-permute-done.15.far_r
  49.0 0.3 field.3
  49.3 0.1 collective-permute-start.16
  49.4 0.3 field.2
  49.7 0.9 %collective-permute-done.16 = bf16[2,64,128]{2,1,0:T(8,128)(2,1)S(1)} collective-permute-done((bf16[2,64,128]{2,1,0:T(8,128)(2,1)S(1)}, bf16[2,64,128]{2,1,0:T(8,128)(2,1)S(1)}, u32[]{:S(2)}, u32[]{:S(2)}) %collective-permute-start.16) | collective-permute-done | bytes 32800 | tf_op jit(solution)/shard_map/ppermute | solution.py:343
  50.6 0.7 %maximum_bitcast_fusion = f32[2,2,128,64]{2,3,1,0:T(8,128)} fusion(f32[1,2,64,128]{3,2,1,0:T(8,128)S(1)} %get-tuple-element.76, f32[1,2,64,128]{3,2,1,0:T(8,128)S(1)} %get-tuple-element.75), kind=kLoop, calls=%fused_computation | loop fusion | flops 32768 | bytes 262144 | tf_op jit(solution)/shard_map/transpose | solution.py:475
  (19 shorter events, 0.3 us)
Async XLA Ops:
  1.5 6.5 %collective-permute-start.4 = (bf16[2,320,256]{2,1,0:T(8,128)(2,1)S(1)}, bf16[2,320,256]{2,1,0:T(8,128)(2,1)S(1)}, u32[]{:S(2)}, u32[]{:S(2)}) collective-permute-start(bf16[2,320,256]{2,1,0:T(8,128)(2,1)S(1)} %get-tuple-element.44), channel_id=1, source_target_pairs={{0,1},{1,0},{2,3},{3,2},{4,5},{5,4},{6,7},{7,6},{8,9},{9,8},{10,11... | collective-permute-start | bytes 983048 | tf_op jit(solution)/shard_map/ppermute | solution.py:343
  2.0 4.7 %collective-permute-start = (f32[4,384]{1,0:T(4,128)S(1)}, f32[4,384]{1,0:T(4,128)S(1)}, u32[]{:S(2)}, u32[]{:S(2)}) collective-permute-start(f32[4,384]{1,0:T(4,128)S(1)} %get-tuple-element.40), channel_id=1, source_target_pairs={{0,2},{1,3},{2,0},{3,1},{4,6},{5,7},{6,4},{7,5},{8,10},{9,11},{10,... | collective-permute-start | bytes 18440 | tf_op jit(solution)/shard_map/ppermute | solution.py:343
  6.7 1.2 %collective-permute-start.1 = (f32[4,384]{1,0:T(4,128)S(1)}, f32[4,384]{1,0:T(4,128)S(1)}, u32[]{:S(2)}, u32[]{:S(2)}) collective-permute-start(f32[4,384]{1,0:T(4,128)S(1)} %gate.4), channel_id=1, source_target_pairs={{0,1},{1,0},{2,3},{3,2},{4,5},{5,4},{6,7},{7,6},{8,9},{9,8},{10,11... | collective-permute-start | bytes 18440 | tf_op jit(solution)/shard_map/ppermute | solution.py:343
  6.9 14.6 %collective-permute-start.7 = (s16[640,512]{1,0:T(8,128)(2,1)S(1)}, s16[640,512]{1,0:T(8,128)(2,1)S(1)}, u32[]{:S(2)}, u32[]{:S(2)}) collective-permute-start(s16[640,512]{1,0:T(8,128)(2,1)S(1)} %get-tuple-element.49), channel_id=1, source_target_pairs={{0,1},{1,0},{2,3},{3,2},{4,5},{5,4},{6,7},{7,6},{8,9},{9,8},{10,11... | collective-permute-start | bytes 1966088 | tf_op jit(solution)/shard_map/ppermute | solution.py:343
  8.1 11.2 %collective-permute-start.5 = (bf16[2,2,320,128]{3,2,1,0:T(8,128)(2,1)S(1)}, bf16[2,2,320,128]{3,2,1,0:T(8,128)(2,1)S(1)}, u32[]{:S(2)}, u32[]{:S(2)}) collective-permute-start(bf16[2,2,320,128]{3,2,1,0:T(8,128)(2,1)S(1)} %get-tuple-element.45), channel_id=1, source_target_pairs={{0,4},{4,0},{8,12},{12,8},{16,20},{20,16},{24,28},{28,24},{1,5},{5... | collective-permute-start | bytes 983048 | tf_op jit(solution)/shard_map/ppermute | solution.py:343
  9.7 17.4 %collective-permute-start.8 = (bf16[2,2,320,256]{3,2,1,0:T(8,128)(2,1)S(1)}, bf16[2,2,320,256]{3,2,1,0:T(8,128)(2,1)S(1)}, u32[]{:S(2)}, u32[]{:S(2)}) collective-permute-start(bf16[2,2,320,256]{3,2,1,0:T(8,128)(2,1)S(1)} %get-tuple-element.52), channel_id=1, source_target_pairs={{0,2},{1,3},{2,0},{3,1},{4,6},{5,7},{6,4},{7,5},{8,10},{9,11},{10,... | collective-permute-start | bytes 1966088 | tf_op jit(solution)/shard_map/ppermute | solution.py:343
  11.2 3.6 %collective-permute-start.2 = (f32[1,384]{1,0:T(1,128)S(1)}, f32[1,384]{1,0:T(1,128)S(1)}, u32[]{:S(2)}, u32[]{:S(2)}) collective-permute-start(f32[1,384]{1,0:T(1,128)S(1)} %get-tuple-element.77.token_ref), channel_id=1, source_target_pairs={{0,8},{4,12},{8,0},{12,4},{16,24},{20,28},{24,16},{28,20},{1,9},{5... | collective-permute-start | bytes 4616 | tf_op jit(solution)/shard_map/ppermute | solution.py:343
  14.7 4.5 %collective-permute-start.3 = (f32[1,384]{1,0:T(1,128)S(1)}, f32[1,384]{1,0:T(1,128)S(1)}, u32[]{:S(2)}, u32[]{:S(2)}) collective-permute-start(f32[1,384]{1,0:T(1,128)S(1)} %gate.5), channel_id=1, source_target_pairs={{0,16},{4,20},{8,24},{12,28},{16,0},{20,4},{24,8},{28,12},{1,17},{... | collective-permute-start | bytes 4616 | tf_op jit(solution)/shard_map/ppermute | solution.py:343
  19.2 3.7 %collective-permute-start.6 = (f32[3,384]{1,0:T(4,128)S(1)}, f32[3,384]{1,0:T(4,128)S(1)}, u32[]{:S(2)}, u32[]{:S(2)}) collective-permute-start(f32[3,384]{1,0:T(4,128)S(1)} %gate.6), channel_id=1, source_target_pairs={{0,4},{4,0},{8,12},{12,8},{16,20},{20,16},{24,28},{28,24},{1,5},{5... | collective-permute-start | bytes 13832 | tf_op jit(solution)/shard_map/ppermute | solution.py:343
  24.3 5.1 %collective-permute-start.12 = (bf16[256,256]{1,0:T(8,128)(2,1)S(1)}, bf16[256,256]{1,0:T(8,128)(2,1)S(1)}, u32[]{:S(2)}, u32[]{:S(2)}) collective-permute-start(bf16[256,256]{1,0:T(8,128)(2,1)S(1)} %get-tuple-element.69), channel_id=1, source_target_pairs={{0,2},{1,3},{2,0},{3,1},{4,6},{5,7},{6,4},{7,5},{8,10},{9,11},{10,... | collective-permute-start | bytes 393224 | tf_op jit(solution)/shard_map/ppermute | solution.py:343
  28.4 7.1 %collective-permute-start.9 = (bf16[256,512]{1,0:T(8,128)(2,1)S(1)}, bf16[256,512]{1,0:T(8,128)(2,1)S(1)}, u32[]{:S(2)}, u32[]{:S(2)}) collective-permute-start(bf16[256,512]{1,0:T(8,128)(2,1)S(1)} %beams_s.3), channel_id=1, source_target_pairs={{0,4},{4,0},{8,12},{12,8},{16,20},{20,16},{24,28},{28,24},{1,5},{5... | collective-permute-start | bytes 786440 | tf_op jit(solution)/shard_map/ppermute | solution.py:343
  29.5 6.1 %collective-permute-start.13 = (bf16[256,256]{1,0:T(8,128)(2,1)S(1)}, bf16[256,256]{1,0:T(8,128)(2,1)S(1)}, u32[]{:S(2)}, u32[]{:S(2)}) collective-permute-start(bf16[256,256]{1,0:T(8,128)(2,1)S(1)} %get-tuple-element.71), channel_id=1, source_target_pairs={{0,8},{4,12},{8,0},{12,4},{16,24},{20,28},{24,16},{28,20},{1,9},{5... | collective-permute-start | bytes 393224 | tf_op jit(solution)/shard_map/ppermute | solution.py:343
  35.6 7.4 %collective-permute-start.14 = (bf16[256,256]{1,0:T(8,128)(2,1)S(1)}, bf16[256,256]{1,0:T(8,128)(2,1)S(1)}, u32[]{:S(2)}, u32[]{:S(2)}) collective-permute-start(bf16[256,256]{1,0:T(8,128)(2,1)S(1)} %get-tuple-element.74), channel_id=1, source_target_pairs={{0,16},{4,20},{8,24},{12,28},{16,0},{20,4},{24,8},{28,12},{1,17},{... | collective-permute-start | bytes 393224 | tf_op jit(solution)/shard_map/ppermute | solution.py:343
  38.3 5.4 %collective-permute-start.10 = (bf16[128,512]{1,0:T(8,128)(2,1)S(1)}, bf16[128,512]{1,0:T(8,128)(2,1)S(1)}, u32[]{:S(2)}, u32[]{:S(2)}) collective-permute-start(bf16[128,512]{1,0:T(8,128)(2,1)S(1)} %get-tuple-element.65), channel_id=1, source_target_pairs={{0,8},{4,12},{8,0},{12,4},{16,24},{20,28},{24,16},{28,20},{1,9},{5... | collective-permute-start | bytes 393224 | tf_op jit(solution)/shard_map/ppermute | solution.py:343
  43.1 5.9 %collective-permute-start.15 = (bf16[256,256]{1,0:T(8,128)(2,1)S(1)}, bf16[256,256]{1,0:T(8,128)(2,1)S(1)}, u32[]{:S(2)}, u32[]{:S(2)}) collective-permute-start(bf16[256,256]{1,0:T(8,128)(2,1)S(1)} %step_r.5.near_r), channel_id=1, source_target_pairs={{0,4},{4,0},{8,12},{12,8},{16,20},{20,16},{24,28},{28,24},{1,5},{5... | collective-permute-start | bytes 393224 | tf_op jit(solution)/shard_map/ppermute | solution.py:343
  43.7 5.2 %collective-permute-start.11 = (bf16[64,512]{1,0:T(8,128)(2,1)S(1)}, bf16[64,512]{1,0:T(8,128)(2,1)S(1)}, u32[]{:S(2)}, u32[]{:S(2)}) collective-permute-start(bf16[64,512]{1,0:T(8,128)(2,1)S(1)} %get-tuple-element.67), channel_id=1, source_target_pairs={{0,16},{4,20},{8,24},{12,28},{16,0},{20,4},{24,8},{28,12},{1,17},{... | collective-permute-start | bytes 196616 | tf_op jit(solution)/shard_map/ppermute | solution.py:343
  49.3 1.3 %collective-permute-start.16 = (bf16[2,64,128]{2,1,0:T(8,128)(2,1)S(1)}, bf16[2,64,128]{2,1,0:T(8,128)(2,1)S(1)}, u32[]{:S(2)}, u32[]{:S(2)}) collective-permute-start(bf16[2,64,128]{2,1,0:T(8,128)(2,1)S(1)} %field.3), channel_id=1, source_target_pairs={{0,1},{1,0},{2,3},{3,2},{4,5},{5,4},{6,7},{7,6},{8,9},{9,8},{10,11... | collective-permute-start | bytes 98312 | tf_op jit(solution)/shard_map/ppermute | solution.py:343
